TPU v7x, 32 devices: a whole 2x2x4 slice. The times are simulated.
32 devices in a mesh: samp: 4 (over y, core), feat: 8 (over z, x).
Axes of the slice: x: 2, y: 2, z: 4, core: 2. Of those that a mesh axis runs over, the one named last changes fastest.
Arguments:
- samples: bfloat16 [4096, 4096], P('samp', 'feat'), may hold values from -8 to 8
- precision: float32 [32, 6, 128, 128], P('feat'), may hold values from -1.2 to 2
- col_blocks: int32 [32, 6], P('feat'), may hold values from -1 to 31, as said below
Outputs:
- updated: float32 [32, 6, 128, 128], P('feat')
Inputs may be any that keep to these rules, and one draw needn't show every extreme that they name: `col_blocks`: slot 0 of block row j holds j; the other column blocks of a row follow in increasing order, then -1 fills the empty slots. The pattern is symmetric: row j names c exactly when row c names j. Block row j lies on index j // 4 of feat; for two different such indices, at most one block row of the one names a column block of the other, and the block rows of one index name column blocks of at most 6 other indices.
All inputs are finite; a program needn't handle non-finite values.
Results may differ from a plain program's by a relative error of at most 0.0028.
Values may be sent and summed in bfloat16 or wider, within the bound.
No kernel may reach another device: no remote copies, remote signals or barrier semaphores. Data moves between devices by JAX's collectives and lax.ppermute only.
A program may use at most 128 MiB of HBM per device.

v0:
```python
import jax
import jax.numpy as jnp
from jax import lax
from jax.sharding import PartitionSpec as P

ITERS = 3


step_size = 0.2
penalty = 0.25


def prox_step(current, gradient, keep_mask, on_diagonal):
    stepped = current - step_size * gradient
    shrunk = jnp.sign(stepped) * jnp.maximum(jnp.abs(stepped) - step_size * penalty, 0.0)
    rooted = 0.5 * (stepped + jnp.sqrt(stepped * stepped + 4.0 * step_size))
    return jnp.where(keep_mask, jnp.where(on_diagonal, rooted, shrunk), jnp.float32(0.0))


def mirror_outbound(flat_gram, send_slot, send_has):
    return jnp.where(
        send_has[:, None, None], jnp.take(flat_gram, send_slot, axis=0), jnp.float32(0.0)
    )


def mirror_inbound(inbound, flat_gram, holder, flat_local, remote):
    from_peer = jnp.take(inbound, holder, axis=0)
    from_self = jnp.take(flat_gram, flat_local, axis=0)
    return jnp.where(remote[:, :, None, None], from_peer, from_self)


def local(samples, precision, col_blocks):
    row_count = samples.shape[0]
    block_rows = precision.shape[0]
    slot_count = precision.shape[1]
    block_size = precision.shape[2]
    flat_count = block_rows * slot_count
    peer_count = lax.axis_size("feat")
    myself = lax.axis_index("feat")
    sample_total = row_count * lax.axis_size("samp")
    filled = col_blocks >= 0
    safe_cols = jnp.where(filled, col_blocks, 0)
    holder = safe_cols // block_rows
    locate = safe_cols % block_rows
    remote = filled & (holder != myself)
    xblocks = samples.reshape(row_count, block_rows, block_size)
    row_ids = myself * block_rows + jnp.arange(block_rows, dtype=jnp.int32)
    peer_ids = jnp.arange(peer_count, dtype=jnp.int32)
    slot_links = (holder[None] == peer_ids[:, None, None]) & remote[None]
    linked = jnp.any(slot_links, axis=2)
    has_link = jnp.any(linked, axis=1)
    source_row = jnp.argmax(linked, axis=1)
    outgoing = jnp.where(
        has_link[None, :, None], jnp.take(xblocks, source_row, axis=1), jnp.zeros((), samples.dtype)
    )
    flat_links = slot_links.reshape(peer_count, flat_count)
    send_slot = jnp.argmax(flat_links, axis=1)
    send_has = jnp.any(flat_links, axis=1)
    matching = col_blocks[locate] == row_ids[:, None, None]
    mate_slot = jnp.argmax(matching, axis=2)
    flat_local = locate * slot_count + mate_slot
    identity_mask = jnp.eye(block_size, dtype=bool)
    on_diagonal = (col_blocks == row_ids[:, None])[:, :, None, None] & identity_mask[None, None]
    keep_mask = filled[:, :, None, None]
    arrived = lax.all_to_all(outgoing, "feat", split_axis=1, concat_axis=1, tiled=True)
    joined = jnp.concatenate([arrived, xblocks], axis=1)
    source_index = jnp.where(remote, holder, peer_count + locate)
    stacked = jnp.take(joined, source_index, axis=1)
    current = jnp.where(keep_mask, precision, jnp.float32(0.0))
    weights = current.astype(jnp.bfloat16)
    share = flat_count // lax.axis_size("samp")
    share_start = lax.axis_index("samp") * share
    share_keep = lax.dynamic_slice_in_dim(
        keep_mask.reshape(flat_count, 1, 1), share_start, share, 0
    )
    share_diag = lax.dynamic_slice_in_dim(
        on_diagonal.reshape(flat_count, block_size, block_size), share_start, share, 0
    )
    share_current = lax.dynamic_slice_in_dim(
        current.reshape(flat_count, block_size, block_size), share_start, share, 0
    )
    for iteration in range(ITERS):
        running = jnp.einsum("rlkb,lkab->rla", stacked, weights, preferred_element_type=jnp.float32)
        projected = running.astype(jnp.bfloat16)
        partial_gram = jnp.einsum(
            "rla,rlkb->lkab", projected, stacked, preferred_element_type=jnp.float32
        )
        flat_partial = partial_gram.reshape(flat_count, block_size, block_size)
        inbound = lax.all_to_all(
            mirror_outbound(flat_partial, send_slot, send_has),
            "feat",
            split_axis=0,
            concat_axis=0,
            tiled=True,
        )
        mirror = mirror_inbound(inbound, flat_partial, holder, flat_local, remote)
        flat_term = (0.5 * (partial_gram + jnp.swapaxes(mirror, 2, 3)) / sample_total).reshape(
            flat_count, block_size, block_size
        )
        share_gradient = lax.psum_scatter(flat_term, "samp", scatter_dimension=0, tiled=True)
        share_current = prox_step(share_current, share_gradient, share_keep, share_diag)
        if iteration + 1 < ITERS:
            gathered = lax.all_gather(
                share_current.astype(jnp.bfloat16), "samp", axis=0, tiled=True
            )
            weights = gathered.reshape(block_rows, slot_count, block_size, block_size)
        else:
            gathered = lax.all_gather(share_current, "samp", axis=0, tiled=True)
            current = gathered.reshape(block_rows, slot_count, block_size, block_size)
    return current


def solution(mesh):
    return jax.shard_map(
        local,
        mesh=mesh,
        in_specs=(P("samp", "feat"), P("feat", None, None, None), P("feat", None)),
        out_specs=P("feat", None, None, None),
        check_vma=False,
    )
```

profile of v0, /device:TPU:0, one launch (start us, length us, event | category | flops | bytes accessed | tf_op | source)
XLA Modules:
  0.0 333.1 jit_solution(5778394578277752231)
XLA Ops:
  17.2 7.4 %all-to-all-start = ((bf16[1024,8,128]{2,0,1:T(8,128)(2,1)}), bf16[1024,8,128]{2,0,1:T(8,128)(2,1)}, u32[]{:S(2)}, u32[]{:S(2)}) async-start(bf16[1024,8,128]{2,0,1:T(8,128)(2,1)} %select_bitcast_fusion), calls=%async_computation | async-start | bytes 4194304 | tf_op jit(solution)/shard_map/all_to_all | solution.py:65
  26.2 46.8 %all-to-all-done = bf16[1024,8,128]{2,0,1:T(8,128)(2,1)} async-done(((bf16[1024,8,128]{2,0,1:T(8,128)(2,1)}), bf16[1024,8,128]{2,0,1:T(8,128)(2,1)}, u32[]{:S(2)}, u32[]{:S(2)}) %all-to-all-start) | async-done | bytes 2097184 | tf_op jit(solution)/shard_map/all_to_all | solution.py:65
  73.0 2.2 pad_maximum_fusion
  75.2 4.4 %gather_fusion.1 = bf16[24,1024,128]{2,1,0:T(8,128)(2,1)} fusion(bf16[1024,12,128]{2,0,1:T(8,128)(2,1)S(1)} %pad_maximum_fusion, s32[1024]{0:T(1024)S(1)} %pad_clamp_fusion.4), kind=kCustom, calls=%fused_computation.10 | custom fusion | bytes 12583008 | tf_op jit(solution)/shard_map/jit(_take)/gather | solution.py:68
  79.6 8.8 %copy.63 = bf16[4,6,1024,128]{2,3,1,0:T(8,128)(2,1)} copy(bf16[4,6,1024,128]{3,2,1,0:T(8,128)(2,1)} %bitcast.123) | data formatting | bytes 12582912 | tf_op jit(solution)/shard_map/jit(_take)/gather | solution.py:68
  88.3 7.5 %fusion.8 = f32[4,6,128,128]{3,2,1,0:T(8,128)S(1)} fusion(bf16[4,6,1024,128]{2,3,1,0:T(8,128)(2,1)} %copy.63, pred[4,6]{1,0:T(4,128)(4,1)S(1)} %get-tuple-element.29, f32[4,6,128,128]{3,2,1,0:T(8,128)S(1)} %copy-done.5), kind=kOutput, calls=%fused_computation.20 | convolution fusion | flops 1617821696 | bytes 9437208 | tf_op jit(solution)/shard_map/rla,rlkb->lkab/dot_general | solution.py:85
  98.4 2.0 select_select_fusion.5
  100.3 3.7 %all-to-all-start.1 = ((f32[8,128,128]{2,1,0:T(8,128)}), f32[8,128,128]{2,1,0:T(8,128)S(1)}, u32[]{:S(2)}, u32[]{:S(2)}) async-start(f32[8,128,128]{2,1,0:T(8,128)} %select_select_fusion.5), calls=%async_computation.1 | async-start | bytes 1048576 | tf_op jit(solution)/shard_map/all_to_all | solution.py:89
  104.3 1.9 gather_fusion.5
  106.1 12.5 %all-to-all-done.1 = f32[8,128,128]{2,1,0:T(8,128)S(1)} async-done(((f32[8,128,128]{2,1,0:T(8,128)}), f32[8,128,128]{2,1,0:T(8,128)S(1)}, u32[]{:S(2)}, u32[]{:S(2)}) %all-to-all-start.1) | async-done | bytes 524320 | tf_op jit(solution)/shard_map/all_to_all | solution.py:89
  118.7 1.8 gather_fusion.4
  120.5 2.3 fusion.20
  124.8 27.1 %reduce-scatter.4.cloned.1.call-done = f32[6,128,128]{2,1,0:T(8,128)} async-done(((f32[24,128,128]{2,1,0:T(8,128)}), f32[6,128,128]{2,1,0:T(8,128)}) %reduce-scatter.4.cloned.1.call-update) | async-done | bytes 393232 | tf_op jit(solution)/shard_map/reduce_scatter | solution.py:100
  151.9 2.3 fusion.55
  154.2 8.2 %all_gather.9 = bf16[24,128,128]{2,1,0:T(8,128)(2,1)S(1)} all-gather(bf16[6,128,128]{2,1,0:T(8,128)(2,1)S(1)} %get-tuple-element.18), channel_id=1, replica_groups=mesh['samp'=4,'feat'=8] {'samp'}, dimensions={0}, use_global_device_ids=true | all-gather | bytes 983040 | tf_op jit(solution)/shard_map/all_gather | solution.py:103
  162.4 7.6 %fusion.4 = f32[4,6,128,128]{3,2,1,0:T(8,128)S(1)} fusion(bf16[4,6,1024,128]{2,3,1,0:T(8,128)(2,1)} %copy.63, pred[4,6]{1,0:T(4,128)(4,1)S(1)} %get-tuple-element.29, bf16[4,6,128,128]{3,2,1,0:T(8,128)(2,1)S(1)} %bitcast.141), kind=kOutput, calls=%fused_computation.16 | convolution fusion | flops 1617428480 | bytes 8650776 | tf_op jit(solution)/shard_map/rla,rlkb->lkab/dot_general | solution.py:85
  171.9 2.0 select_select_fusion.4
  173.9 5.5 %all-to-all-start.2 = ((f32[8,128,128]{2,1,0:T(8,128)}), f32[8,128,128]{2,1,0:T(8,128)S(1)}, u32[]{:S(2)}, u32[]{:S(2)}) async-start(f32[8,128,128]{2,1,0:T(8,128)} %select_select_fusion.4), calls=%async_computation.3 | async-start | bytes 1048576 | tf_op jit(solution)/shard_map/all_to_all | solution.py:89
  181.4 3.0 copy.73
  184.5 9.9 %all-to-all-done.2 = f32[8,128,128]{2,1,0:T(8,128)S(1)} async-done(((f32[8,128,128]{2,1,0:T(8,128)}), f32[8,128,128]{2,1,0:T(8,128)S(1)}, u32[]{:S(2)}, u32[]{:S(2)}) %all-to-all-start.2) | async-done | bytes 524320 | tf_op jit(solution)/shard_map/all_to_all | solution.py:89
  196.2 2.3 fusion.19
  200.2 26.8 %reduce-scatter.6.cloned.1.call-done = f32[6,128,128]{2,1,0:T(8,128)} async-done(((f32[24,128,128]{2,1,0:T(8,128)}), f32[6,128,128]{2,1,0:T(8,128)}) %reduce-scatter.6.cloned.1.call-update) | async-done | bytes 393232 | tf_op jit(solution)/shard_map/reduce_scatter | solution.py:100
  228.4 8.2 %all_gather.10 = bf16[24,128,128]{2,1,0:T(8,128)(2,1)S(1)} all-gather(bf16[6,128,128]{2,1,0:T(8,128)(2,1)S(1)} %get-tuple-element.16), channel_id=1, replica_groups=mesh['samp'=4,'feat'=8] {'samp'}, dimensions={0}, use_global_device_ids=true | all-gather | bytes 983040 | tf_op jit(solution)/shard_map/all_gather | solution.py:103
  236.6 7.6 %fusion = f32[4,6,128,128]{3,2,1,0:T(8,128)S(1)} fusion(bf16[4,6,1024,128]{2,3,1,0:T(8,128)(2,1)} %copy.63, pred[4,6]{1,0:T(4,128)(4,1)S(1)} %copy-done.25, bf16[4,6,128,128]{3,2,1,0:T(8,128)(2,1)S(1)} %bitcast.140), kind=kOutput, calls=%fused_computation.12 | convolution fusion | flops 1617428480 | bytes 8650776 | tf_op jit(solution)/shard_map/rla,rlkb->lkab/dot_general | solution.py:85
  246.8 2.0 select_select_fusion.3
  248.8 5.5 %all-to-all-start.3 = ((f32[8,128,128]{2,1,0:T(8,128)}), f32[8,128,128]{2,1,0:T(8,128)S(1)}, u32[]{:S(2)}, u32[]{:S(2)}) async-start(f32[8,128,128]{2,1,0:T(8,128)} %select_select_fusion.3), calls=%async_computation.5 | async-start | bytes 1048576 | tf_op jit(solution)/shard_map/all_to_all | solution.py:89
  256.2 13.1 %all-to-all-done.3 = f32[8,128,128]{2,1,0:T(8,128)S(1)} async-done(((f32[8,128,128]{2,1,0:T(8,128)}), f32[8,128,128]{2,1,0:T(8,128)S(1)}, u32[]{:S(2)}, u32[]{:S(2)}) %all-to-all-start.3) | async-done | bytes 524320 | tf_op jit(solution)/shard_map/all_to_all | solution.py:89
  271.1 2.3 fusion.18
  275.1 26.8 %reduce-scatter.8.cloned.1.call-done = f32[6,128,128]{2,1,0:T(8,128)} async-done(((f32[24,128,128]{2,1,0:T(8,128)}), f32[6,128,128]{2,1,0:T(8,128)}) %reduce-scatter.8.cloned.1.call-update) | async-done | bytes 393232 | tf_op jit(solution)/shard_map/reduce_scatter | solution.py:100
  301.9 2.1 fusion.38
  304.1 19.8 %all-gather.2.cloned.1.call-done = f32[24,128,128]{2,1,0:T(8,128)} async-done(((f32[6,128,128]{2,1,0:T(8,128)}), f32[24,128,128]{2,1,0:T(8,128)}) %all-gather.2.cloned.1.call-update) | async-done | bytes 1572880 | tf_op jit(solution)/shard_map/all_gather | solution.py:108
  323.8 2.7 copy.96
  (113 shorter events, 33.6 us)
Async XLA Ops:
  7.2 189.0 %copy-start.15 = (pred[4,6]{1,0:T(4,128)(4,1)}, pred[4,6]{1,0:T(4,128)(4,1)S(1)}, u32[]{:S(2)}) copy-start(pred[4,6]{1,0:T(4,128)(4,1)S(1)} %get-tuple-element.20) | copy-start | bytes 76
  11.0 151.4 %copy-start.24 = (pred[4,6]{1,0:T(4,128)(4,1)}, pred[4,6]{1,0:T(4,128)(4,1)S(1)}, u32[]{:S(2)}) copy-start(pred[4,6]{1,0:T(4,128)(4,1)S(1)} %get-tuple-element.29) | copy-start | bytes 76
  11.0 185.2 %copy-start.13 = (pred[4,6]{1,0:T(4,128)(4,1)}, pred[4,6]{1,0:T(4,128)(4,1)S(1)}, u32[]{:S(2)}) copy-start(pred[4,6]{1,0:T(4,128)(4,1)S(1)} %get-tuple-element.22) | copy-start | bytes 76
  11.0 185.2 %copy-start.14 = (pred[4,6]{1,0:T(4,128)(4,1)}, pred[4,6]{1,0:T(4,128)(4,1)S(1)}, u32[]{:S(2)}) copy-start(pred[4,6]{1,0:T(4,128)(4,1)S(1)} %get-tuple-element.28) | copy-start | bytes 76
  12.5 159.4 %copy-start.12 = (pred[8]{0:T(512)(128)(4,1)}, pred[8]{0:T(512)(128)(4,1)S(1)}, u32[]{:S(2)}) copy-start(pred[8]{0:T(512)(128)(4,1)S(1)} %get-tuple-element.34) | copy-start | bytes 28
  17.2 7.6 %copy-start.6 = (f32[4,6,128,128]{3,2,1,0:T(8,128)S(1)}, f32[4,6,128,128]{3,2,1,0:T(8,128)}, u32[]{:S(2)}) copy-start(f32[4,6,128,128]{3,2,1,0:T(8,128)} %param.10) | copy-start | bytes 4718596
  17.2 55.7 %all-to-all-start = ((bf16[1024,8,128]{2,0,1:T(8,128)(2,1)}), bf16[1024,8,128]{2,0,1:T(8,128)(2,1)}, u32[]{:S(2)}, u32[]{:S(2)}) async-start(bf16[1024,8,128]{2,0,1:T(8,128)(2,1)} %select_bitcast_fusion), calls=%async_computation | async-start | bytes 4194304 | tf_op jit(solution)/shard_map/all_to_all | solution.py:65
  24.7 145.8 %copy-start.16 = (s32[1024]{0:T(1024)}, s32[1024]{0:T(1024)S(1)}, u32[]{:S(2)}) copy-start(s32[1024]{0:T(1024)S(1)} %pad_clamp_fusion.3) | copy-start | bytes 12292
  24.9 147.0 %copy-start.17 = (pred[8]{0:T(512)(128)(4,1)}, pred[8]{0:T(512)(128)(4,1)S(1)}, u32[]{:S(2)}) copy-start(pred[8]{0:T(512)(128)(4,1)S(1)} %fusion.45) | copy-start | bytes 28
  79.6 8.8 %copy-start.5 = (f32[4,6,128,128]{3,2,1,0:T(8,128)S(1)}, f32[4,6,128,128]{3,2,1,0:T(8,128)}, u32[]{:S(2)}) copy-start(f32[4,6,128,128]{3,2,1,0:T(8,128)} %broadcast_select_fusion.7) | copy-start | bytes 4718596
  95.8 1.1 copy-start.1
  100.3 18.3 %all-to-all-start.1 = ((f32[8,128,128]{2,1,0:T(8,128)}), f32[8,128,128]{2,1,0:T(8,128)S(1)}, u32[]{:S(2)}, u32[]{:S(2)}) async-start(f32[8,128,128]{2,1,0:T(8,128)} %select_select_fusion.5), calls=%async_computation.1 | async-start | bytes 1048576 | tf_op jit(solution)/shard_map/all_to_all | solution.py:89
  104.0 47.9 %reduce-scatter.4.cloned.1.call-start = ((), (), s32[]{:S(2)}) async-start(), calls=%async_computation.7 | async-start | bytes 1966080 | tf_op jit(solution)/shard_map/reduce_scatter | solution.py:100
  104.2 75.4 %copy-start.10 = (s32[1024]{0:T(1024)}, s32[1024]{0:T(1024)S(1)}, u32[]{:S(2)}) copy-start(s32[1024]{0:T(1024)S(1)} %pad_clamp_fusion) | copy-start | bytes 12292
  104.2 90.2 %copy-start.8 = (s32[1024]{0:T(1024)}, s32[1024]{0:T(1024)S(1)}, u32[]{:S(2)}) copy-start(s32[1024]{0:T(1024)S(1)} %pad_clamp_fusion.2) | copy-start | bytes 12292
  106.1 14.4 %copy-start.2 = (f32[4,6,128,128]{3,2,1,0:T(8,128)S(1)}, f32[4,6,128,128]{3,2,1,0:T(8,128)}, u32[]{:S(2)}) copy-start(f32[4,6,128,128]{3,2,1,0:T(8,128)} %copy-done.1) | copy-start | bytes 4718596
  124.7 45.3 %copy-start.18 = (pred[6]{0:T(512)(128)(4,1)}, pred[6]{0:T(512)(128)(4,1)S(1)}, u32[]{:S(2)}) copy-start(pred[6]{0:T(512)(128)(4,1)S(1)} %dynamic-slice) | copy-start | bytes 22
  124.8 45.3 %copy-start.21 = (pred[6]{0:T(512)(128)(4,1)}, pred[6]{0:T(512)(128)(4,1)S(1)}, u32[]{:S(2)}) copy-start(pred[6]{0:T(512)(128)(4,1)S(1)} %dynamic-slice_bitcast_fusion) | copy-start | bytes 22
  173.9 20.5 %all-to-all-start.2 = ((f32[8,128,128]{2,1,0:T(8,128)}), f32[8,128,128]{2,1,0:T(8,128)S(1)}, u32[]{:S(2)}, u32[]{:S(2)}) async-start(f32[8,128,128]{2,1,0:T(8,128)} %select_select_fusion.4), calls=%async_computation.3 | async-start | bytes 1048576 | tf_op jit(solution)/shard_map/all_to_all | solution.py:89
  179.4 47.6 %reduce-scatter.6.cloned.1.call-start = ((), (), s32[]{:S(2)}) async-start(), calls=%async_computation.8 | async-start | bytes 1966080 | tf_op jit(solution)/shard_map/reduce_scatter | solution.py:100
  200.1 26.9 %copy-start.7 = (f32[6,128,128]{2,1,0:T(8,128)S(1)}, f32[6,128,128]{2,1,0:T(8,128)}, u32[]{:S(2)}) copy-start(f32[6,128,128]{2,1,0:T(8,128)} %get-tuple-element.19) | copy-start | bytes 1179652
  200.1 26.9 %copy-start.19 = (pred[6]{0:T(512)(128)(4,1)S(1)}, pred[6]{0:T(512)(128)(4,1)}, u32[]{:S(2)}) copy-start(pred[6]{0:T(512)(128)(4,1)} %copy-done.18) | copy-start | bytes 22
  200.1 26.9 %copy-start.22 = (pred[6]{0:T(512)(128)(4,1)S(1)}, pred[6]{0:T(512)(128)(4,1)}, u32[]{:S(2)}) copy-start(pred[6]{0:T(512)(128)(4,1)} %copy-done.21) | copy-start | bytes 22
  200.2 36.4 %copy-start.25 = (pred[4,6]{1,0:T(4,128)(4,1)S(1)}, pred[4,6]{1,0:T(4,128)(4,1)}, u32[]{:S(2)}) copy-start(pred[4,6]{1,0:T(4,128)(4,1)} %copy-done.24) | copy-start | bytes 76
  246.8 7.6 %copy-start.11 = (s32[1024]{0:T(1024)S(1)}, s32[1024]{0:T(1024)}, u32[]{:S(2)}) copy-start(s32[1024]{0:T(1024)} %copy-done.10) | copy-start | bytes 12292
  248.8 20.5 %all-to-all-start.3 = ((f32[8,128,128]{2,1,0:T(8,128)}), f32[8,128,128]{2,1,0:T(8,128)S(1)}, u32[]{:S(2)}, u32[]{:S(2)}) async-start(f32[8,128,128]{2,1,0:T(8,128)} %select_select_fusion.3), calls=%async_computation.5 | async-start | bytes 1048576 | tf_op jit(solution)/shard_map/all_to_all | solution.py:89
  254.3 15.0 %copy-start.9 = (s32[1024]{0:T(1024)S(1)}, s32[1024]{0:T(1024)}, u32[]{:S(2)}) copy-start(s32[1024]{0:T(1024)} %copy-done.8) | copy-start | bytes 12292
  254.3 47.6 %reduce-scatter.8.cloned.1.call-start = ((), (), s32[]{:S(2)}) async-start(), calls=%async_computation.9 | async-start | bytes 1966080 | tf_op jit(solution)/shard_map/reduce_scatter | solution.py:100
  256.2 14.9 %copy-start.4 = (f32[4,6,128,128]{3,2,1,0:T(8,128)S(1)}, f32[4,6,128,128]{3,2,1,0:T(8,128)}, u32[]{:S(2)}) copy-start(f32[4,6,128,128]{3,2,1,0:T(8,128)} %copy-done.3) | copy-start | bytes 4718596
  275.1 26.9 %copy-start.20 = (pred[6]{0:T(512)(128)(4,1)S(1)}, pred[6]{0:T(512)(128)(4,1)}, u32[]{:S(2)}) copy-start(pred[6]{0:T(512)(128)(4,1)} %copy-done.18) | copy-start | bytes 22
  275.1 26.9 %copy-start.23 = (pred[6]{0:T(512)(128)(4,1)S(1)}, pred[6]{0:T(512)(128)(4,1)}, u32[]{:S(2)}) copy-start(pred[6]{0:T(512)(128)(4,1)} %copy-done.21) | copy-start | bytes 22
  275.1 48.8 %all-gather.2.cloned.1.call-start = ((), (), s32[]{:S(2)}) async-start(), calls=%async_computation.10 | async-start | bytes 1966080 | tf_op jit(solution)/shard_map/all_gather | solution.py:108
  (2 other events, 2.1 us)
Sparse Core Ops, SparseCore 0:
  124.6 27.3 reduce-scatter.3
  200.3 26.6 reduce-scatter.5
  275.2 26.6 reduce-scatter.7
  304.2 19.6 all-gather.1
where the time goes:
time: 334 us; the launch traced here: 333 us
  waiting for transfers between devices  183 us (55%)
  local copies, waits for them, and re-layouts  47.3 us (14%)
  other arithmetic  27.9 us (8%)
  matrix products  22.7 us (7%)
  starting transfers between devices  22.4 us (7%)
  blocking collectives  16.4 us (5%)
  between operations  13.4 us (4%)
    reduce_scatter x3, waiting for transfers between devices, local(): lax.psum_scatter(flat_term, 'samp', scatter_dimension=0, tiled=True)  80.7 us
    all_to_all x1, waiting for transfers between devices, local(): lax.all_to_all(outgoing, 'feat', split_axis=1, concat_axis=1, tiled=True)  46.8 us
    all_to_all x3, waiting for transfers between devices, local(): lax.all_to_all(mirror_outbound(flat_partial, send_slot, send_has), 'feat'...  35.6 us
    dot_general x3, matrix products, local(): jnp.einsum('rla,rlkb->lkab', projected, stacked, preferred_element_type=j...  22.7 us
    all_gather x1, waiting for transfers between devices, local(): gathered = lax.all_gather(share_current, 'samp', axis=0, tiled=True)  19.8 us
    all_gather x2, blocking collectives, local(): lax.all_gather(share_current.astype(jnp.bfloat16), 'samp', axis=0, tiled=...  16.4 us
    all_to_all x3, starting transfers between devices, local(): lax.all_to_all(mirror_outbound(flat_partial, send_slot, send_has), 'feat'...  14.7 us
    gather x2, local copies, waits for them, and re-layouts, local(): stacked = jnp.take(joined, source_index, axis=1)  13.2 us
  transfers between devices with their start and end apart: 8, of which 8 were waited for; matrix products, arithmetic and copies ran while one was open for 3% of the time, Pallas kernels for 0%

commit v1 on v0

v1 whole, which is shorter than its diff:
```python
import functools

import jax
import jax.numpy as jnp
from jax import lax
from jax.experimental import pallas as pl
from jax.experimental.pallas import tpu as pltpu
from jax.sharding import PartitionSpec as P

ITERS = 3
STEP = 0.2
SHRINK = 0.05

SMEM = pl.BlockSpec(memory_space=pltpu.SMEM)
VMEM = pl.BlockSpec(memory_space=pltpu.VMEM)


def params(mib):
    return pltpu.CompilerParams(vmem_limit_bytes=mib << 20)


def dot_nt(a, b):
    return lax.dot_general(a, b, (((1,), (1,)), ((), ())), preferred_element_type=jnp.float32)


def dot_nn(a, b):
    return lax.dot_general(a, b, (((1,), (0,)), ((), ())), preferred_element_type=jnp.float32)


def for_each(lo, hi, body):
    if hi - lo <= 8:
        for i in range(lo, hi):
            body(i)
    else:
        pl.loop(lo, hi)(body)


class Local:
    def __init__(self, cb_ref, block_rows, rounds):
        self.cb = cb_ref
        self.block_rows = block_rows
        self.slots = cb_ref.shape[1]
        self.me = lax.axis_index("feat")
        self.rounds = rounds

    def slot(self, j, k):
        c = self.cb[j, k]
        filled = c >= 0
        safe = jnp.maximum(c, 0)
        holder = lax.div(safe, self.block_rows)
        return filled, filled & (holder == self.me), lax.rem(safe, self.block_rows), holder

    def place(self, holder):
        return lax.bitwise_xor(holder, self.me) if self.rounds else holder

    def fill_links(self, tab_ref):
        for p in range(tab_ref.shape[1]):
            tab_ref[0, p] = -1
            tab_ref[1, p] = -1
        for j in range(self.block_rows):
            for k in range(1, self.slots):
                filled, own, _, holder = self.slot(j, k)

                @pl.when(filled & jnp.logical_not(own))
                def _(j=j, k=k, holder=holder):
                    p = self.place(holder)
                    tab_ref[0, p] = j
                    tab_ref[1, p] = k

    def count(self, j):
        total = jnp.int32(0)
        for k in range(self.slots):
            total = total + (self.cb[j, k] >= 0).astype(jnp.int32)
        return total

    def mate(self, row, j):
        found = jnp.int32(0)
        for m in range(1, self.slots):
            found = jnp.where(self.cb[row, m] == self.me * self.block_rows + j, m, found)
        return found


def pack_kernel(rounds, cb_ref, x_ref, own_ref, *rest):
    *send_refs, tab_ref = rest
    block_rows, block, _ = own_ref.shape
    here = Local(cb_ref, block_rows, rounds)
    here.fill_links(tab_ref)
    for b in range(block_rows):
        own_ref[b] = x_ref[:, b * block : (b + 1) * block].T
    if rounds:
        for r, send_ref in enumerate(send_refs, 1):
            send_ref[...] = own_ref[jnp.maximum(tab_ref[0, r], 0)]
    else:
        (send_ref,) = send_refs

        def copy(p):
            send_ref[p] = own_ref[jnp.maximum(tab_ref[0, p], 0)]

        for_each(0, send_ref.shape[0], copy)


def put_halves(core, value, index, keep_ref, send_ref):
    half = value.shape[0] // 2
    top, bottom = value[:half], value[half:]
    keep_ref[index] = jnp.where(core == 0, top, bottom)
    send_ref[index] = jnp.where(core == 0, bottom, top)


def own_gram_kernel(own_ref, keep_ref, send_ref):
    block_rows = own_ref.shape[0]
    core = lax.rem(lax.axis_index("samp"), 2)
    for a in range(block_rows):
        for b in range(block_rows):
            put_halves(core, dot_nt(own_ref[a], own_ref[b]), (a, b), keep_ref, send_ref)


def gram_kernel(rounds, first, last, cb_ref, own_ref, *rest):
    *arrived_refs, keep_ref, send_ref, tab_ref, all_ref = rest
    block_rows = own_ref.shape[0]
    core = lax.rem(lax.axis_index("samp"), 2)
    here = Local(cb_ref, block_rows, rounds)
    here.fill_links(tab_ref)
    all_ref[:block_rows] = own_ref[...]
    if rounds:
        for i, ref in enumerate(arrived_refs):
            all_ref[block_rows + i] = ref[...]
    else:
        all_ref[block_rows:] = arrived_refs[0][...]
    base = 1 if rounds else 0

    def body(p):
        row = tab_ref[0, p]

        @pl.when(row >= 0)
        def _():
            mine = all_ref[block_rows + p - base]
            for k in range(here.slots):
                filled, own, b, holder = here.slot(row, k)
                q = here.place(holder)

                @pl.when(filled & (own | (q <= p)))
                def _():
                    source = jnp.where(own, b, block_rows + q - base)
                    put_halves(core, dot_nt(mine, all_ref[source]), (p - first, k), keep_ref, send_ref)

    for_each(first, last, body)


def joined(core, mine, other):
    top = jnp.where(core == 0, mine, other)
    bottom = jnp.where(core == 0, other, mine)
    return jnp.concatenate([top, bottom], axis=0)


def products(here, block, w_ref, gram_ref, low_ref, v_ref):
    for j in range(here.block_rows):
        count = here.count(j)
        for wide in range(2, here.slots + 1, 2):

            @pl.when((count == wide) | (count == wide - 1))
            def _(j=j, wide=wide):
                width = wide * block
                v_ref[j, :, :width] = dot_nn(w_ref[j, :, :width], gram_ref[j, :width, :width])

        for k in range(here.slots):

            @pl.when(k < count)
            def _(j=j, k=k):
                at = slice(k * block, (k + 1) * block)
                v_ref[j, :, at] += dot_nn(w_ref[j, :, at], low_ref[j, k])


def step_and_send(here, block, scale, v_ref, next_ref, out_ref):
    for j in range(here.block_rows):
        for k in range(here.slots):
            filled, own, b, holder = here.slot(j, k)
            at = slice(k * block, (k + 1) * block)

            @pl.when(own)
            def _(j=j, k=k, b=b, at=at):
                m = here.mate(b, j) if k else 0
                column = pl.ds(pl.multiple_of(m * block, block), block)
                mirrored = v_ref[b, :, column].T
                next_ref[j, k] = next_ref[j, k] - scale * (v_ref[j, :, at] + mirrored)

            @pl.when(filled & jnp.logical_not(own))
            def _(j=j, k=k, holder=holder, at=at):
                value = v_ref[j, :, at]
                next_ref[j, k] = next_ref[j, k] - scale * value
                out_ref[holder] = value.T.astype(out_ref.dtype)


def first_kernel(rounds, groups, scale, cb_ref, prec_ref, *rest):
    count = 2 * (1 + len(groups))
    pieces, rest = rest[:count], rest[count:]
    gram_ref, low_ref, next_ref, out_ref, tab_ref, w_ref, v_ref = rest
    block_rows, slots, block, _ = prec_ref.shape
    core = lax.rem(lax.axis_index("samp"), 2)
    here = Local(cb_ref, block_rows, rounds)
    here.fill_links(tab_ref)
    mine_ref, other_ref = pieces[:2]

    def place_block(row, k, l, value):
        at_k = pl.ds(pl.multiple_of(k * block, block), block)
        at_l = pl.ds(pl.multiple_of(l * block, block), block)
        high = value.astype(jnp.bfloat16)
        gram_ref[row, at_k, at_l] = high
        return high, at_k, at_l

    def place_low(row, k, value, high):
        low_ref[row, k] = (value - high.astype(jnp.float32)).astype(jnp.bfloat16)

    for j in range(block_rows):
        n = here.count(j)

        def along(k, carry, j=j, n=n):
            _, own_k, a, _ = here.slot(j, k)

            @pl.when(own_k)
            def _():
                def across(l, carry):
                    _, own_l, b, _ = here.slot(j, l)

                    @pl.when(own_l)
                    def _():
                        value = joined(core, mine_ref[a, b], other_ref[a, b])
                        high, _, _ = place_block(j, k, l, value)

                        @pl.when(k == l)
                        def _():
                            place_low(j, k, value, high)

                    return carry

                lax.fori_loop(0, n, across, 0)

            return carry

        lax.fori_loop(0, n, along, 0)
        for odd in range(1, slots, 2):

            @pl.when(n == odd)
            def _(j=j, odd=odd):
                gram_ref[j, odd * block : (odd + 1) * block, :] = jnp.zeros(
                    (block, slots * block), gram_ref.dtype
                )

    for (first, last), mine_ref, other_ref in zip(groups, pieces[2::2], pieces[3::2]):

        def body(p, first=first, mine_ref=mine_ref, other_ref=other_ref):
            row, k = tab_ref[0, p], tab_ref[1, p]

            @pl.when(row >= 0)
            def _():
                for l in range(slots):
                    filled, own, _, holder = here.slot(row, l)

                    @pl.when(filled & (own | (here.place(holder) <= p)))
                    def _(l=l):
                        value = joined(core, mine_ref[p - first, l], other_ref[p - first, l])
                        high, at_k, at_l = place_block(row, k, l, value)

                        @pl.when(k == l)
                        def _():
                            place_low(row, k, value, high)

                        @pl.when(k != l)
                        def _():
                            gram_ref[row, at_l, at_k] = value.T.astype(jnp.bfloat16)

        for_each(first, last, body)

    for j in range(block_rows):
        for k in range(slots):
            filled = here.cb[j, k] >= 0

            @pl.when(filled)
            def _(j=j, k=k):
                value = prec_ref[j, k]
                next_ref[j, k] = value
                w_ref[j, :, k * block : (k + 1) * block] = value.astype(jnp.bfloat16)

            @pl.when(jnp.logical_not(filled))
            def _(j=j, k=k):
                next_ref[j, k] = jnp.zeros((block, block), jnp.float32)
                w_ref[j, :, k * block : (k + 1) * block] = jnp.zeros((block, block), jnp.bfloat16)

    products(here, block, w_ref, gram_ref, low_ref, v_ref)
    step_and_send(here, block, scale, v_ref, next_ref, out_ref)


def prox_blocks(here, block, scale, stepped_ref, in_ref, next_ref, w_ref):
    eye = lax.broadcasted_iota(jnp.int32, (block, block), 0) == lax.broadcasted_iota(
        jnp.int32, (block, block), 1
    )

    def finish(j, k, m):
        value = m - jnp.clip(m, -SHRINK, SHRINK)
        if k == 0:
            value = jnp.where(eye, 0.5 * (m + jnp.sqrt(m * m + 4.0 * STEP)), value)
        next_ref[j, k] = value
        if w_ref is not None:
            w_ref[j, :, k * block : (k + 1) * block] = value.astype(jnp.bfloat16)

    for j in range(here.block_rows):
        for k in range(here.slots):
            filled, own, _, holder = here.slot(j, k)

            @pl.when(own)
            def _(j=j, k=k):
                finish(j, k, stepped_ref[j, k])

            @pl.when(filled & jnp.logical_not(own))
            def _(j=j, k=k, holder=holder):
                finish(j, k, stepped_ref[j, k] - scale * in_ref[holder].astype(jnp.float32))

            @pl.when(jnp.logical_not(filled))
            def _(j=j, k=k):
                next_ref[j, k] = jnp.zeros((block, block), jnp.float32)
                if w_ref is not None:
                    w_ref[j, :, k * block : (k + 1) * block] = jnp.zeros((block, block), jnp.bfloat16)


def middle_kernel(scale, cb_ref, stepped_ref, in_ref, gram_ref, low_ref, next_ref, out_ref, w_ref, v_ref):
    block_rows, _, block, _ = stepped_ref.shape
    here = Local(cb_ref, block_rows, False)
    prox_blocks(here, block, scale, stepped_ref, in_ref, next_ref, w_ref)
    products(here, block, w_ref, gram_ref, low_ref, v_ref)
    step_and_send(here, block, scale, v_ref, next_ref, out_ref)


def last_kernel(scale, cb_ref, stepped_ref, in_ref, next_ref):
    block_rows, _, block, _ = stepped_ref.shape
    prox_blocks(Local(cb_ref, block_rows, False), block, scale, stepped_ref, in_ref, next_ref, None)


def call(kernel, inputs, outs, scratch, mib, smem=1, flops=0):
    moved = sum(x.size * x.dtype.itemsize for x in (*inputs, *outs))
    return pl.pallas_call(
        kernel,
        out_shape=outs,
        in_specs=[SMEM] * smem + [VMEM] * (len(inputs) - smem),
        out_specs=[VMEM] * len(outs),
        scratch_shapes=scratch,
        compiler_params=params(mib),
        cost_estimate=pl.CostEstimate(flops=flops, bytes_accessed=moved, transcendentals=0),
    )(*inputs)


def swap(x, bit):
    count = lax.axis_size("samp")
    return lax.ppermute(x, "samp", [(i, i ^ bit) for i in range(count)])


def sum_over_samp(keep, send):
    half = keep + swap(send, 1)
    bit = 2
    while bit < lax.axis_size("samp"):
        half = half + swap(half, bit)
        bit *= 2
    return half, swap(half, 1)


def local(samples, precision, col_blocks):
    row_count = samples.shape[0]
    block_rows, slots, block, _ = precision.shape
    peers = lax.axis_size("feat")
    scale = 0.5 * STEP / (row_count * lax.axis_size("samp"))
    rounds = peers <= 8
    groups = [(1, 4), (4, 6), (6, 8)] if rounds and peers == 8 else [(1 if rounds else 0, peers)]

    def shape(dims, dtype):
        return jax.ShapeDtypeStruct(dims, dtype)

    bf16, f32 = samples.dtype, jnp.float32
    tab = pltpu.SMEM((2, peers), jnp.int32)
    strip = (block, row_count)
    sends = [shape(strip, bf16)] * (peers - 1) if rounds else [shape((peers, *strip), bf16)]
    own, *sends = call(
        functools.partial(pack_kernel, rounds),
        (col_blocks, samples),
        [shape((block_rows, *strip), bf16), *sends],
        [tab],
        48,
    )
    if rounds:
        arrived = [
            lax.ppermute(x, "feat", [(i, i ^ r) for i in range(peers)])
            for r, x in enumerate(sends, 1)
        ]
    else:
        arrived = [lax.all_to_all(sends[0], "feat", 0, 0, tiled=True)]
    pieces = []
    halves = shape((block_rows, block_rows, block // 2, block), f32)
    pieces += sum_over_samp(*call(own_gram_kernel, (own,), [halves] * 2, [], 48, smem=0))
    for first, last in groups:
        known = arrived[: last - 1] if rounds else arrived
        halves = shape((last - first, slots, block // 2, block), f32)
        held = pltpu.VMEM((block_rows + (last - 1 if rounds else peers), *strip), bf16)
        pieces += sum_over_samp(
            *call(
                functools.partial(gram_kernel, rounds, first, last),
                (col_blocks, own, *known),
                [halves] * 2,
                [tab, held],
                60,
            )
        )
    blocks = shape(precision.shape, f32)
    swapped = shape((peers, block, block), bf16)
    work = [
        pltpu.VMEM((block_rows, block, slots * block), bf16),
        pltpu.VMEM((block_rows, block, slots * block), f32),
    ]
    gram, low, stepped, out = call(
        functools.partial(first_kernel, rounds, groups, scale),
        (col_blocks, precision, *pieces),
        [
            shape((block_rows, slots * block, slots * block), bf16),
            shape(precision.shape, bf16),
            blocks,
            swapped,
        ],
        [tab, *work],
        60,
    )
    for iteration in range(ITERS):
        mirrored = lax.all_to_all(out, "feat", 0, 0, tiled=True)
        if iteration + 1 < ITERS:
            stepped, out = call(
                functools.partial(middle_kernel, scale),
                (col_blocks, stepped, mirrored, gram, low),
                [blocks, swapped],
                work,
                60,
            )
    (updated,) = call(
        functools.partial(last_kernel, scale), (col_blocks, stepped, mirrored), [blocks], [], 48
    )
    return updated


def solution(mesh):
    return jax.shard_map(
        local,
        mesh=mesh,
        in_specs=(P("samp", "feat"), P("feat", None, None, None), P("feat", None)),
        out_specs=P("feat", None, None, None),
        check_vma=False,
    )
```

time: 334 us -> 208 us (0.62)
  waiting for transfers between devices: 183 us -> 77.6 us
  blocking collectives: 16.4 us -> 58.1 us
  local copies, waits for them, and re-layouts: 47.3 us -> 8.22 us
  Pallas kernels: 0 us -> 38.3 us
  other arithmetic: 27.9 us -> 1.49 us
  matrix products: 22.7 us -> 0 us
  between operations: 13.4 us -> 0.26 us
    all_to_all x4 -> x0, waiting for transfers between devices: 82.4 us -> none  [the longest x1 46.8 us: local(): lax.all_to_all(outgoing, 'feat', split_axis=1, concat_axis=1, tiled=True)]
    reduce_scatter x3 -> x0, waiting for transfers between devices: 80.7 us -> none  [local(): lax.psum_scatter(flat_term, 'samp', scatter_dimension=0, tiled=True)]
    ppermute x0 -> x19, waiting for transfers between devices: none -> 77.6 us  [the longest x12 39.1 us: swap(): return lax.ppermute(x, 'samp', [(i, i ^ bit) for i in range(count)])]
    all_to_all x0 -> x3, blocking collectives: none -> 58.1 us  [local(): mirrored = lax.all_to_all(out, 'feat', 0, 0, tiled=True)]
    pallas_call x0 -> x9, Pallas kernels: none -> 38.3 us  [call(): pl.pallas_call(kernel, out_shape=outs, in_specs=[SMEM] * smem + [VMEM] *...]
    gather x16 -> x0, local copies, waits for them, and re-layouts: 33.7 us -> none  [the longest x2 13.2 us: local(): stacked = jnp.take(joined, source_index, axis=1)]
    dot_general x3 -> x0, matrix products: 22.7 us -> none  [local(): jnp.einsum('rla,rlkb->lkab', projected, stacked, preferred_element_type=j...]
    all_to_all x4 -> x0, starting transfers between devices: 22.1 us -> none  [the longest x3 14.7 us: local(): lax.all_to_all(mirror_outbound(flat_partial, send_slot, send_has), 'feat'...]
  transfers between devices with their start and end apart: 8 -> 19, of which waited for: 8 -> 10; matrix products, arithmetic and copies ran while one was open for 3% -> 1% of each run, Pallas kernels for 0% -> 4%
where the time goes in v1:
time: 208 us; the launch traced here: 205 us
  waiting for transfers between devices  77.6 us (37%)
  blocking collectives  58.1 us (28%)
  Pallas kernels  38.3 us (18%)
  starting transfers between devices  21.4 us (10%)
  local copies, waits for them, and re-layouts  8.22 us (4%)
    all_to_all x3, blocking collectives, local(): mirrored = lax.all_to_all(out, 'feat', 0, 0, tiled=True)  58.1 us
    ppermute x12, waiting for transfers between devices, swap(): return lax.ppermute(x, 'samp', [(i, i ^ bit) for i in range(count)])  39.1 us
    ppermute x7, waiting for transfers between devices, local(): lax.ppermute(x, 'feat', [(i, i ^ r) for i in range(peers)])  38.5 us
    pallas_call x9, Pallas kernels, call(): pl.pallas_call(kernel, out_shape=outs, in_specs=[SMEM] * smem + [VMEM] *...  38.3 us
    ppermute x7, starting transfers between devices, local(): lax.ppermute(x, 'feat', [(i, i ^ r) for i in range(peers)])  16 us
    unnamed x46, local copies, waits for them, and re-layouts  8.22 us
    ppermute x12, starting transfers between devices, swap(): return lax.ppermute(x, 'samp', [(i, i ^ bit) for i in range(count)])  5.39 us
  transfers between devices with their start and end apart: 19, of which 10 were waited for; matrix products, arithmetic and copies ran while one was open for 1% of the time, Pallas kernels for 4%

profile of v1, /device:TPU:0, one launch (start us, length us, event | category | flops | bytes accessed | tf_op | source)
XLA Modules:
  0.0 205.3 jit_solution(12694074359595712047)
XLA Ops:
  0.0 1.2 copy-done.3
  3.9 2.9 %collective-permute-start.3 = (bf16[128,1024]{1,0:T(8,128)(2,1)S(1)}, bf16[128,1024]{1,0:T(8,128)(2,1)S(1)}, u32[]{:S(2)}, u32[]{:S(2)}) collective-permute-start(bf16[128,1024]{1,0:T(8,128)(2,1)S(1)} %get-tuple-element.32), channel_id=1, source_target_pairs={{0,1},{1,0},{2,3},{3,2},{4,5},{5,4},{6,7},{7,6},{8,9},{9,8},{10,11... | collective-permute-start | bytes 786440 | tf_op jit(solution)/shard_map/ppermute | solution.py:388
  6.8 1.6 collective-permute-start.4
  8.4 4.7 %collective-permute-done.3.rest_0_ = bf16[128,1024]{1,0:T(8,128)(2,1)S(1)} collective-permute-done((bf16[128,1024]{1,0:T(8,128)(2,1)S(1)}, bf16[128,1024]{1,0:T(8,128)(2,1)S(1)}, u32[]{:S(2)}, u32[]{:S(2)}) %collective-permute-start.3) | collective-permute-done | bytes 262176 | tf_op jit(solution)/shard_map/ppermute | solution.py:388
  13.1 2.9 %collective-permute-done.4.rest_1_ = bf16[128,1024]{1,0:T(8,128)(2,1)S(1)} collective-permute-done((bf16[128,1024]{1,0:T(8,128)(2,1)S(1)}, bf16[128,1024]{1,0:T(8,128)(2,1)S(1)}, u32[]{:S(2)}, u32[]{:S(2)}) %collective-permute-start.4) | collective-permute-done | bytes 262176 | tf_op jit(solution)/shard_map/ppermute | solution.py:388
  16.1 4.0 %collective-permute-done.5.rest_2_ = bf16[128,1024]{1,0:T(8,128)(2,1)S(1)} collective-permute-done((bf16[128,1024]{1,0:T(8,128)(2,1)S(1)}, bf16[128,1024]{1,0:T(8,128)(2,1)S(1)}, u32[]{:S(2)}, u32[]{:S(2)}) %collective-permute-start.5) | collective-permute-done | bytes 262176 | tf_op jit(solution)/shard_map/ppermute | solution.py:388
  20.7 3.1 %shard_map.39 = (f32[3,6,64,128]{3,2,1,0:T(8,128)}, f32[3,6,64,128]{3,2,1,0:T(8,128)}) custom-call(s32[4,6]{1,0:T(4,128)} %cb_ref.15, bf16[4,128,1024]{2,1,0:T(8,128)(2,1)} %copy-done, bf16[128,1024]{1,0:T(8,128)(2,1)} %copy-done.7, bf16[128,1024]{1,0:T(8,128)(2,1)} %copy-done.8, bf16[128,1024]{1,0:T(8,128)(2,1)} %copy-done.9), custom_call_target="tpu_custom_call" | custom-call | bytes 3014752 | tf_op jit(solution)/shard_map/pallas_call | solution.py:339
  23.9 3.0 %collective-permute-start.9 = (bf16[128,1024]{1,0:T(8,128)(2,1)S(1)}, bf16[128,1024]{1,0:T(8,128)(2,1)S(1)}, u32[]{:S(2)}, u32[]{:S(2)}) collective-permute-start(bf16[128,1024]{1,0:T(8,128)(2,1)S(1)} %get-tuple-element.37), channel_id=1, source_target_pairs={{0,4},{1,5},{2,6},{3,7},{4,0},{5,1},{6,2},{7,3},{8,12},{9,13},{10,... | collective-permute-start | bytes 786440 | tf_op jit(solution)/shard_map/ppermute | solution.py:388
  26.9 1.2 shard_map.38
  28.4 1.8 collective-permute-start.10
  30.2 2.7 %collective-permute-start.14 = (bf16[128,1024]{1,0:T(8,128)(2,1)S(1)}, bf16[128,1024]{1,0:T(8,128)(2,1)}, u32[]{:S(2)}, u32[]{:S(2)}) collective-permute-start(bf16[128,1024]{1,0:T(8,128)(2,1)S(1)} %get-tuple-element.41), channel_id=1, source_target_pairs={{0,6},{1,7},{2,4},{3,5},{4,2},{5,3},{6,0},{7,1},{8,14},{9,15},{10,... | collective-permute-start | bytes 786440 | tf_op jit(solution)/shard_map/ppermute | solution.py:388
  32.9 18.0 %collective-permute-done.9.rest_3_ = bf16[128,1024]{1,0:T(8,128)(2,1)S(1)} collective-permute-done((bf16[128,1024]{1,0:T(8,128)(2,1)S(1)}, bf16[128,1024]{1,0:T(8,128)(2,1)S(1)}, u32[]{:S(2)}, u32[]{:S(2)}) %collective-permute-start.9) | collective-permute-done | bytes 262176 | tf_op jit(solution)/shard_map/ppermute | solution.py:388
  50.9 4.0 %collective-permute-start.15 = (bf16[128,1024]{1,0:T(8,128)(2,1)S(1)}, bf16[128,1024]{1,0:T(8,128)(2,1)S(1)}, u32[]{:S(2)}, u32[]{:S(2)}) collective-permute-start(bf16[128,1024]{1,0:T(8,128)(2,1)S(1)} %get-tuple-element.42), channel_id=1, source_target_pairs={{0,7},{1,6},{2,5},{3,4},{4,3},{5,2},{6,1},{7,0},{8,15},{9,14},{10,... | collective-permute-start | bytes 786440 | tf_op jit(solution)/shard_map/ppermute | solution.py:388
  54.9 8.9 %collective-permute-done.10.rest_4_ = bf16[128,1024]{1,0:T(8,128)(2,1)S(1)} collective-permute-done((bf16[128,1024]{1,0:T(8,128)(2,1)S(1)}, bf16[128,1024]{1,0:T(8,128)(2,1)S(1)}, u32[]{:S(2)}, u32[]{:S(2)}) %collective-permute-start.10) | collective-permute-done | bytes 262176 | tf_op jit(solution)/shard_map/ppermute | solution.py:388
  64.5 3.2 %shard_map.40 = (f32[2,6,64,128]{3,2,1,0:T(8,128)}, f32[2,6,64,128]{3,2,1,0:T(8,128)}) custom-call(s32[4,6]{1,0:T(4,128)} %cb_ref.15, bf16[4,128,1024]{2,1,0:T(8,128)(2,1)} %copy-done, bf16[128,1024]{1,0:T(8,128)(2,1)} %copy-done.7, bf16[128,1024]{1,0:T(8,128)(2,1)} %copy-done.8, bf16[128,1024]{1,0:T(8,128)(2,1)} %copy-done.9, bf16[128,1024]{1,0:T(8,128)(2,1)} %copy-done.13, ...), custom_call_target="tpu_custom_call" | custom-call | bytes 3145824 | tf_op jit(solution)/shard_map/pallas_call | solution.py:339
  68.4 2.8 %shard_map.41 = (f32[2,6,64,128]{3,2,1,0:T(8,128)}, f32[2,6,64,128]{3,2,1,0:T(8,128)}) custom-call(s32[4,6]{1,0:T(4,128)} %cb_ref.15, bf16[4,128,1024]{2,1,0:T(8,128)(2,1)} %copy-done, bf16[128,1024]{1,0:T(8,128)(2,1)} %copy-done.7, bf16[128,1024]{1,0:T(8,128)(2,1)} %copy-done.8, bf16[128,1024]{1,0:T(8,128)(2,1)} %copy-done.9, bf16[128,1024]{1,0:T(8,128)(2,1)} %copy-done.13, ...), custom_call_target="tpu_custom_call" | custom-call | bytes 3670112 | tf_op jit(solution)/shard_map/pallas_call | solution.py:339
  71.9 1.6 collective-permute-start.7
  73.4 1.1 add.24
  75.2 1.6 collective-permute-start.12
  77.4 10.7 %collective-permute-done.7 = f32[3,6,64,128]{3,2,1,0:T(8,128)S(1)} collective-permute-done((f32[3,6,64,128]{3,2,1,0:T(8,128)S(1)}, f32[3,6,64,128]{3,2,1,0:T(8,128)S(1)}, u32[]{:S(2)}, u32[]{:S(2)}) %collective-permute-start.7) | collective-permute-done | bytes 589856 | tf_op jit(solution)/shard_map/ppermute | solution.py:352
  88.3 11.1 %collective-permute-done.1 = f32[4,4,64,128]{3,2,1,0:T(8,128)S(1)} collective-permute-done((f32[4,4,64,128]{3,2,1,0:T(8,128)S(1)}, f32[4,4,64,128]{3,2,1,0:T(8,128)S(1)}, u32[]{:S(2)}, u32[]{:S(2)}) %collective-permute-start.1) | collective-permute-done | bytes 524320 | tf_op jit(solution)/shard_map/ppermute | solution.py:352
  99.5 8.3 %collective-permute-done.12 = f32[2,6,64,128]{3,2,1,0:T(8,128)S(1)} collective-permute-done((f32[2,6,64,128]{3,2,1,0:T(8,128)S(1)}, f32[2,6,64,128]{3,2,1,0:T(8,128)S(1)}, u32[]{:S(2)}, u32[]{:S(2)}) %collective-permute-start.12) | collective-permute-done | bytes 393248 | tf_op jit(solution)/shard_map/ppermute | solution.py:352
  107.9 7.4 %collective-permute-done.17 = f32[2,6,64,128]{3,2,1,0:T(8,128)S(1)} collective-permute-done((f32[2,6,64,128]{3,2,1,0:T(8,128)S(1)}, f32[2,6,64,128]{3,2,1,0:T(8,128)S(1)}, u32[]{:S(2)}, u32[]{:S(2)}) %collective-permute-start.17) | collective-permute-done | bytes 393248 | tf_op jit(solution)/shard_map/ppermute | solution.py:352
  115.4 1.7 collective-permute-done.18.rest_7_
  119.0 9.5 %shard_map.42 = (bf16[4,768,768]{2,1,0:T(8,128)(2,1)}, bf16[4,6,128,128]{3,2,1,0:T(8,128)(2,1)}, f32[4,6,128,128]{3,2,1,0:T(8,128)}, bf16[8,128,128]{2,1,0:T(8,128)(2,1)}) custom-call(s32[4,6]{1,0:T(4,128)} %cb_ref.15, f32[4,6,128,128]{3,2,1,0:T(8,128)} %prec_ref.1, f32[4,4,64,128]{3,2,1,0:T(8,128)} %copy-done.10, f32[4,4,64,128]{3,2,1,0:T(8,128)} %copy-done.17, ...), custom_call_target="tpu_custom_call" | custom-call | bytes 12714080 | tf_op jit(solution)/shard_map/pallas_call | solution.py:339
  128.4 28.9 %all_to_all.15.in_ref = bf16[8,128,128]{2,1,0:T(8,128)(2,1)} all-to-all(bf16[8,128,128]{2,1,0:T(8,128)(2,1)} %get-tuple-element.46), channel_id=1, replica_groups=mesh['samp'=4,'feat'=8] {'feat'}, dimensions={0} | all-to-all | bytes 524288 | tf_op jit(solution)/shard_map/all_to_all | solution.py:428
  157.3 7.5 %shard_map.43 = (f32[4,6,128,128]{3,2,1,0:T(8,128)}, bf16[8,128,128]{2,1,0:T(8,128)(2,1)}) custom-call(s32[4,6]{1,0:T(4,128)} %cb_ref.15, f32[4,6,128,128]{3,2,1,0:T(8,128)} %get-tuple-element.45.stepped_ref, bf16[8,128,128]{2,1,0:T(8,128)(2,1)} %all_to_all.15.in_ref, bf16[4,768,768]{2,1,0:T(8,128)(2,1)} %get-tuple-element.47.gram_ref, ...), custom_call_target="tpu_custom_call" | custom-call | bytes 9175136 | tf_op jit(solution)/shard_map/pallas_call | solution.py:339
  164.9 15.1 %all_to_all.16.in_ref = bf16[8,128,128]{2,1,0:T(8,128)(2,1)} all-to-all(bf16[8,128,128]{2,1,0:T(8,128)(2,1)} %get-tuple-element.50), channel_id=1, replica_groups=mesh['samp'=4,'feat'=8] {'feat'}, dimensions={0} | all-to-all | bytes 524288 | tf_op jit(solution)/shard_map/all_to_all | solution.py:428
  180.0 7.6 %shard_map.44 = (f32[4,6,128,128]{3,2,1,0:T(8,128)}, bf16[8,128,128]{2,1,0:T(8,128)(2,1)}) custom-call(s32[4,6]{1,0:T(4,128)} %cb_ref.15, f32[4,6,128,128]{3,2,1,0:T(8,128)} %get-tuple-element.49.stepped_ref, bf16[8,128,128]{2,1,0:T(8,128)(2,1)} %all_to_all.16.in_ref, bf16[4,768,768]{2,1,0:T(8,128)(2,1)} %get-tuple-element.47.gram_ref, ...), custom_call_target="tpu_custom_call" | custom-call | bytes 9175136 | tf_op jit(solution)/shard_map/pallas_call | solution.py:339
  187.6 14.0 %all_to_all.17.in_ref = bf16[8,128,128]{2,1,0:T(8,128)(2,1)S(1)} all-to-all(bf16[8,128,128]{2,1,0:T(8,128)(2,1)} %get-tuple-element.52), channel_id=1, replica_groups=mesh['samp'=4,'feat'=8] {'feat'}, dimensions={0} | all-to-all | bytes 524288 | tf_op jit(solution)/shard_map/all_to_all | solution.py:428
  201.6 1.4 copy-done.2
  203.0 2.3 %shard_map.45 = f32[4,6,128,128]{3,2,1,0:T(8,128)} custom-call(s32[4,6]{1,0:T(4,128)S(1)} %copy-done.5, f32[4,6,128,128]{3,2,1,0:T(8,128)S(1)} %copy-done.2, bf16[8,128,128]{2,1,0:T(8,128)(2,1)S(1)} %all_to_all.17.in_ref), custom_call_target="tpu_custom_call" | custom-call | bytes 3407968 | tf_op jit(solution)/shard_map/pallas_call | solution.py:339
  (72 shorter events, 9.2 us)
Async XLA Ops:
  3.9 23.0 %copy-start.1 = (bf16[4,128,1024]{2,1,0:T(8,128)(2,1)S(1)}, bf16[4,128,1024]{2,1,0:T(8,128)(2,1)}, u32[]{:S(2)}) copy-start(bf16[4,128,1024]{2,1,0:T(8,128)(2,1)} %copy-done) | copy-start | bytes 3145732
  3.9 9.2 %collective-permute-start.3 = (bf16[128,1024]{1,0:T(8,128)(2,1)S(1)}, bf16[128,1024]{1,0:T(8,128)(2,1)S(1)}, u32[]{:S(2)}, u32[]{:S(2)}) collective-permute-start(bf16[128,1024]{1,0:T(8,128)(2,1)S(1)} %get-tuple-element.32), channel_id=1, source_target_pairs={{0,1},{1,0},{2,3},{3,2},{4,5},{5,4},{6,7},{7,6},{8,9},{9,8},{10,11... | collective-permute-start | bytes 786440 | tf_op jit(solution)/shard_map/ppermute | solution.py:388
  6.8 9.2 %collective-permute-start.4 = (bf16[128,1024]{1,0:T(8,128)(2,1)S(1)}, bf16[128,1024]{1,0:T(8,128)(2,1)S(1)}, u32[]{:S(2)}, u32[]{:S(2)}) collective-permute-start(bf16[128,1024]{1,0:T(8,128)(2,1)S(1)} %get-tuple-element.33), channel_id=1, source_target_pairs={{0,2},{1,3},{2,0},{3,1},{4,6},{5,7},{6,4},{7,5},{8,10},{9,11},{10,... | collective-permute-start | bytes 786440 | tf_op jit(solution)/shard_map/ppermute | solution.py:388
  8.4 11.6 %collective-permute-start.5 = (bf16[128,1024]{1,0:T(8,128)(2,1)S(1)}, bf16[128,1024]{1,0:T(8,128)(2,1)S(1)}, u32[]{:S(2)}, u32[]{:S(2)}) collective-permute-start(bf16[128,1024]{1,0:T(8,128)(2,1)S(1)} %get-tuple-element.34), channel_id=1, source_target_pairs={{0,3},{1,2},{2,1},{3,0},{4,7},{5,6},{6,5},{7,4},{8,11},{9,10},{10,... | collective-permute-start | bytes 786440 | tf_op jit(solution)/shard_map/ppermute | solution.py:388
  13.1 6.9 %copy-start.7 = (bf16[128,1024]{1,0:T(8,128)(2,1)}, bf16[128,1024]{1,0:T(8,128)(2,1)S(1)}, u32[]{:S(2)}) copy-start(bf16[128,1024]{1,0:T(8,128)(2,1)S(1)} %collective-permute-done.3.rest_0_) | copy-start | bytes 786436
  16.1 4.0 %copy-start.8 = (bf16[128,1024]{1,0:T(8,128)(2,1)}, bf16[128,1024]{1,0:T(8,128)(2,1)S(1)}, u32[]{:S(2)}) copy-start(bf16[128,1024]{1,0:T(8,128)(2,1)S(1)} %collective-permute-done.4.rest_1_) | copy-start | bytes 786436
  23.9 47.9 %collective-permute-start.6 = (f32[3,6,64,128]{3,2,1,0:T(8,128)}, f32[3,6,64,128]{3,2,1,0:T(8,128)S(1)}, u32[]{:S(2)}, u32[]{:S(2)}) collective-permute-start(f32[3,6,64,128]{3,2,1,0:T(8,128)} %get-tuple-element.36), channel_id=1, source_target_pairs={{0,8},{8,0},{16,24},{24,16},{1,9},{9,1},{17,25},{25,17},{2,10},{10... | collective-permute-start | bytes 1769480 | tf_op jit(solution)/shard_map/ppermute | solution.py:352
  23.9 27.0 %collective-permute-start.9 = (bf16[128,1024]{1,0:T(8,128)(2,1)S(1)}, bf16[128,1024]{1,0:T(8,128)(2,1)S(1)}, u32[]{:S(2)}, u32[]{:S(2)}) collective-permute-start(bf16[128,1024]{1,0:T(8,128)(2,1)S(1)} %get-tuple-element.37), channel_id=1, source_target_pairs={{0,4},{1,5},{2,6},{3,7},{4,0},{5,1},{6,2},{7,3},{8,12},{9,13},{10,... | collective-permute-start | bytes 786440 | tf_op jit(solution)/shard_map/ppermute | solution.py:388
  28.2 45.3 %collective-permute-start = (f32[4,4,64,128]{3,2,1,0:T(8,128)S(1)}, f32[4,4,64,128]{3,2,1,0:T(8,128)}, u32[]{:S(2)}, u32[]{:S(2)}) collective-permute-start(f32[4,4,64,128]{3,2,1,0:T(8,128)S(1)} %get-tuple-element.31), channel_id=1, source_target_pairs={{0,8},{8,0},{16,24},{24,16},{1,9},{9,1},{17,25},{25,17},{2,10},{10... | collective-permute-start | bytes 1572872 | tf_op jit(solution)/shard_map/ppermute | solution.py:352
  28.4 35.4 %collective-permute-start.10 = (bf16[128,1024]{1,0:T(8,128)(2,1)S(1)}, bf16[128,1024]{1,0:T(8,128)(2,1)S(1)}, u32[]{:S(2)}, u32[]{:S(2)}) collective-permute-start(bf16[128,1024]{1,0:T(8,128)(2,1)S(1)} %get-tuple-element.38), channel_id=1, source_target_pairs={{0,5},{1,4},{2,7},{3,6},{4,1},{5,0},{6,3},{7,2},{8,13},{9,12},{10,... | collective-permute-start | bytes 786440 | tf_op jit(solution)/shard_map/ppermute | solution.py:388
  30.2 37.5 %collective-permute-start.14 = (bf16[128,1024]{1,0:T(8,128)(2,1)S(1)}, bf16[128,1024]{1,0:T(8,128)(2,1)}, u32[]{:S(2)}, u32[]{:S(2)}) collective-permute-start(bf16[128,1024]{1,0:T(8,128)(2,1)S(1)} %get-tuple-element.41), channel_id=1, source_target_pairs={{0,6},{1,7},{2,4},{3,5},{4,2},{5,3},{6,0},{7,1},{8,14},{9,15},{10,... | collective-permute-start | bytes 786440 | tf_op jit(solution)/shard_map/ppermute | solution.py:388
  50.9 12.9 %copy-start.13 = (bf16[128,1024]{1,0:T(8,128)(2,1)}, bf16[128,1024]{1,0:T(8,128)(2,1)S(1)}, u32[]{:S(2)}) copy-start(bf16[128,1024]{1,0:T(8,128)(2,1)S(1)} %collective-permute-done.9.rest_3_) | copy-start | bytes 786436
  50.9 16.8 %collective-permute-start.15 = (bf16[128,1024]{1,0:T(8,128)(2,1)S(1)}, bf16[128,1024]{1,0:T(8,128)(2,1)S(1)}, u32[]{:S(2)}, u32[]{:S(2)}) collective-permute-start(bf16[128,1024]{1,0:T(8,128)(2,1)S(1)} %get-tuple-element.42), channel_id=1, source_target_pairs={{0,7},{1,6},{2,5},{3,4},{4,3},{5,2},{6,1},{7,0},{8,15},{9,14},{10,... | collective-permute-start | bytes 786440 | tf_op jit(solution)/shard_map/ppermute | solution.py:388
  67.7 4.1 %copy-start.16 = (f32[3,6,64,128]{3,2,1,0:T(8,128)S(1)}, f32[3,6,64,128]{3,2,1,0:T(8,128)}, u32[]{:S(2)}) copy-start(f32[3,6,64,128]{3,2,1,0:T(8,128)} %get-tuple-element.35) | copy-start | bytes 1769476
  67.7 7.4 %collective-permute-start.11 = (f32[2,6,64,128]{3,2,1,0:T(8,128)}, f32[2,6,64,128]{3,2,1,0:T(8,128)S(1)}, u32[]{:S(2)}, u32[]{:S(2)}) collective-permute-start(f32[2,6,64,128]{3,2,1,0:T(8,128)} %get-tuple-element.40), channel_id=1, source_target_pairs={{0,8},{8,0},{16,24},{24,16},{1,9},{9,1},{17,25},{25,17},{2,10},{10... | collective-permute-start | bytes 1179656 | tf_op jit(solution)/shard_map/ppermute | solution.py:352
  71.3 5.5 %collective-permute-start.16 = (f32[2,6,64,128]{3,2,1,0:T(8,128)}, f32[2,6,64,128]{3,2,1,0:T(8,128)S(1)}, u32[]{:S(2)}, u32[]{:S(2)}) collective-permute-start(f32[2,6,64,128]{3,2,1,0:T(8,128)} %get-tuple-element.44), channel_id=1, source_target_pairs={{0,8},{8,0},{16,24},{24,16},{1,9},{9,1},{17,25},{25,17},{2,10},{10... | collective-permute-start | bytes 1179656 | tf_op jit(solution)/shard_map/ppermute | solution.py:352
  71.8 3.4 %copy-start.20 = (f32[2,6,64,128]{3,2,1,0:T(8,128)S(1)}, f32[2,6,64,128]{3,2,1,0:T(8,128)}, u32[]{:S(2)}) copy-start(f32[2,6,64,128]{3,2,1,0:T(8,128)} %get-tuple-element.39) | copy-start | bytes 1179652
  71.8 4.9 %copy-start.21 = (f32[2,6,64,128]{3,2,1,0:T(8,128)S(1)}, f32[2,6,64,128]{3,2,1,0:T(8,128)}, u32[]{:S(2)}) copy-start(f32[2,6,64,128]{3,2,1,0:T(8,128)} %get-tuple-element.43) | copy-start | bytes 1179652
  71.9 16.3 %collective-permute-start.7 = (f32[3,6,64,128]{3,2,1,0:T(8,128)S(1)}, f32[3,6,64,128]{3,2,1,0:T(8,128)S(1)}, u32[]{:S(2)}, u32[]{:S(2)}) collective-permute-start(f32[3,6,64,128]{3,2,1,0:T(8,128)S(1)} %add.26), channel_id=1, source_target_pairs={{0,16},{8,24},{16,0},{24,8},{1,17},{9,25},{17,1},{25,9},{2,18},{10... | collective-permute-start | bytes 1769480 | tf_op jit(solution)/shard_map/ppermute | solution.py:352
  74.5 24.8 %collective-permute-start.1 = (f32[4,4,64,128]{3,2,1,0:T(8,128)S(1)}, f32[4,4,64,128]{3,2,1,0:T(8,128)S(1)}, u32[]{:S(2)}, u32[]{:S(2)}) collective-permute-start(f32[4,4,64,128]{3,2,1,0:T(8,128)S(1)} %add.24), channel_id=1, source_target_pairs={{0,16},{8,24},{16,0},{24,8},{1,17},{9,25},{17,1},{25,9},{2,18},{10... | collective-permute-start | bytes 1572872 | tf_op jit(solution)/shard_map/ppermute | solution.py:352
  75.2 32.6 %collective-permute-start.12 = (f32[2,6,64,128]{3,2,1,0:T(8,128)S(1)}, f32[2,6,64,128]{3,2,1,0:T(8,128)S(1)}, u32[]{:S(2)}, u32[]{:S(2)}) collective-permute-start(f32[2,6,64,128]{3,2,1,0:T(8,128)S(1)} %add.28), channel_id=1, source_target_pairs={{0,16},{8,24},{16,0},{24,8},{1,17},{9,25},{17,1},{25,9},{2,18},{10... | collective-permute-start | bytes 1179656 | tf_op jit(solution)/shard_map/ppermute | solution.py:352
  76.8 38.5 %collective-permute-start.17 = (f32[2,6,64,128]{3,2,1,0:T(8,128)S(1)}, f32[2,6,64,128]{3,2,1,0:T(8,128)S(1)}, u32[]{:S(2)}, u32[]{:S(2)}) collective-permute-start(f32[2,6,64,128]{3,2,1,0:T(8,128)S(1)} %add.30), channel_id=1, source_target_pairs={{0,16},{8,24},{16,0},{24,8},{1,17},{9,25},{17,1},{25,9},{2,18},{10... | collective-permute-start | bytes 1179656 | tf_op jit(solution)/shard_map/ppermute | solution.py:352
  88.2 27.1 %copy-start.6 = (f32[3,6,64,128]{3,2,1,0:T(8,128)}, f32[3,6,64,128]{3,2,1,0:T(8,128)S(1)}, u32[]{:S(2)}) copy-start(f32[3,6,64,128]{3,2,1,0:T(8,128)S(1)} %add.27.rest_2_) | copy-start | bytes 1769476
  88.2 28.9 %collective-permute-start.8 = (f32[3,6,64,128]{3,2,1,0:T(8,128)S(1)}, f32[3,6,64,128]{3,2,1,0:T(8,128)S(1)}, u32[]{:S(2)}, u32[]{:S(2)}) collective-permute-start(f32[3,6,64,128]{3,2,1,0:T(8,128)S(1)} %add.27.rest_2_), channel_id=1, source_target_pairs={{0,8},{8,0},{16,24},{24,16},{1,9},{9,1},{17,25},{25,17},{2,10},{10... | collective-permute-start | bytes 1769480 | tf_op jit(solution)/shard_map/ppermute | solution.py:352
  99.4 17.7 %copy-start.10 = (f32[4,4,64,128]{3,2,1,0:T(8,128)}, f32[4,4,64,128]{3,2,1,0:T(8,128)S(1)}, u32[]{:S(2)}) copy-start(f32[4,4,64,128]{3,2,1,0:T(8,128)S(1)} %add.25.rest_0_) | copy-start | bytes 1572868
  99.4 17.7 %collective-permute-start.2 = (f32[4,4,64,128]{3,2,1,0:T(8,128)S(1)}, f32[4,4,64,128]{3,2,1,0:T(8,128)S(1)}, u32[]{:S(2)}, u32[]{:S(2)}) collective-permute-start(f32[4,4,64,128]{3,2,1,0:T(8,128)S(1)} %add.25.rest_0_), channel_id=1, source_target_pairs={{0,8},{8,0},{16,24},{24,16},{1,9},{9,1},{17,25},{25,17},{2,10},{10... | collective-permute-start | bytes 1572872 | tf_op jit(solution)/shard_map/ppermute | solution.py:352
  107.8 9.3 %copy-start.11 = (f32[2,6,64,128]{3,2,1,0:T(8,128)}, f32[2,6,64,128]{3,2,1,0:T(8,128)S(1)}, u32[]{:S(2)}) copy-start(f32[2,6,64,128]{3,2,1,0:T(8,128)S(1)} %add.29.rest_4_) | copy-start | bytes 1179652
  107.8 7.6 %collective-permute-start.13 = (f32[2,6,64,128]{3,2,1,0:T(8,128)S(1)}, f32[2,6,64,128]{3,2,1,0:T(8,128)S(1)}, u32[]{:S(2)}, u32[]{:S(2)}) collective-permute-start(f32[2,6,64,128]{3,2,1,0:T(8,128)S(1)} %add.29.rest_4_), channel_id=1, source_target_pairs={{0,8},{8,0},{16,24},{24,16},{1,9},{9,1},{17,25},{25,17},{2,10},{10... | collective-permute-start | bytes 1179656 | tf_op jit(solution)/shard_map/ppermute | solution.py:352
  115.3 1.8 copy-start.12
  115.3 1.8 collective-permute-start.18
  115.4 1.7 copy-start.18
  180.0 21.6 %copy-start.5 = (s32[4,6]{1,0:T(4,128)S(1)}, s32[4,6]{1,0:T(4,128)}, u32[]{:S(2)}) copy-start(s32[4,6]{1,0:T(4,128)} %cb_ref.15) | copy-start | bytes 292
  (10 other events, 9.0 us)

commit v2 on v1

v2 whole, which is shorter than its diff:
```python
import functools
import math

import jax
import jax.numpy as jnp
from jax import lax
from jax.experimental import pallas as pl
from jax.experimental.pallas import tpu as pltpu
from jax.sharding import PartitionSpec as P

ITERS = 3
STEP = 0.2
SHRINK = 0.05

SMEM = pl.BlockSpec(memory_space=pltpu.SMEM)
VMEM = pl.BlockSpec(memory_space=pltpu.VMEM)


def dot_nt(a, b):
    return lax.dot_general(a, b, (((1,), (1,)), ((), ())), preferred_element_type=jnp.float32)


def dot_nn(a, b):
    return lax.dot_general(a, b, (((1,), (0,)), ((), ())), preferred_element_type=jnp.float32)


def for_each(lo, hi, body):
    if hi - lo <= 8:
        for i in range(lo, hi):
            body(i)
    else:
        pl.loop(lo, hi)(body)


class Local:
    def __init__(self, cb_ref, block_rows, rounds):
        self.cb = cb_ref
        self.block_rows = block_rows
        self.slots = cb_ref.shape[1]
        self.me = lax.axis_index("feat")
        self.core = lax.rem(lax.axis_index("samp"), 2)
        self.rounds = rounds

    def slot(self, j, k):
        c = self.cb[j, k]
        filled = c >= 0
        safe = jnp.maximum(c, 0)
        holder = lax.div(safe, self.block_rows)
        return filled, filled & (holder == self.me), lax.rem(safe, self.block_rows), holder

    def place(self, holder):
        return lax.bitwise_xor(holder, self.me) if self.rounds else holder

    def fill_links(self, tab_ref):
        for p in range(tab_ref.shape[1]):
            tab_ref[0, p] = -1
            tab_ref[1, p] = -1
        @pl.loop(0, self.block_rows)
        def _(j):
            for k in range(1, self.slots):
                filled, own, _, holder = self.slot(j, k)

                @pl.when(filled & jnp.logical_not(own))
                def _(k=k, holder=holder):
                    p = self.place(holder)
                    tab_ref[0, p] = j
                    tab_ref[1, p] = k

    def count(self, j):
        total = jnp.int32(0)
        for k in range(self.slots):
            total = total + (self.cb[j, k] >= 0).astype(jnp.int32)
        return total

    def mate(self, row, j):
        found = jnp.int32(0)
        for m in range(1, self.slots):
            found = jnp.where(self.cb[row, m] == self.me * self.block_rows + j, m, found)
        return found


def aligned(index, block):
    return pl.ds(pl.multiple_of(index * block, block), block)


def pack_kernel(rounds, cb_ref, x_ref, own_ref, *rest):
    *send_refs, tab_ref = rest
    block_rows, block, _ = own_ref.shape
    here = Local(cb_ref, block_rows, rounds)
    here.fill_links(tab_ref)
    for b in range(block_rows):
        own_ref[b] = x_ref[:, b * block : (b + 1) * block].T
    if rounds:
        for r, send_ref in enumerate(send_refs, 1):
            send_ref[...] = own_ref[jnp.maximum(tab_ref[0, r], 0)]
    else:
        (send_ref,) = send_refs

        def copy(p):
            send_ref[p] = own_ref[jnp.maximum(tab_ref[0, p], 0)]

        for_each(0, send_ref.shape[0], copy)


def eye_of(block):
    return lax.broadcasted_iota(jnp.int32, (block, block), 0) == lax.broadcasted_iota(
        jnp.int32, (block, block), 1
    )


def low_diagonal(value, high):
    rest = value - high.astype(jnp.float32)
    return jnp.sum(jnp.where(eye_of(value.shape[0]), rest, 0.0), axis=0, keepdims=True)


def put_block(out_ref, i, position, value, diagonal):
    block = value.shape[0]
    high = value.astype(jnp.bfloat16)
    out_ref[i, aligned(position, block)] = high

    @pl.when(diagonal)
    def _():
        low = jnp.broadcast_to(low_diagonal(value, high), (16, block))
        out_ref[i, out_ref.shape[1] - 16 :] = low.astype(jnp.bfloat16)


def own_gram_kernel(mine_ref, other_ref, out_ref):
    block_rows = mine_ref.shape[0]
    core = lax.rem(lax.axis_index("samp"), 2)
    for i in range(block_rows // 2):
        a = 2 * i + core
        for b in range(block_rows):
            value = dot_nt(mine_ref[a], mine_ref[b]) + dot_nt(other_ref[a], other_ref[b])
            put_block(out_ref, i, b, value, a == b)


def position_of(k, l):
    return jnp.where(l == k, 0, jnp.where(l == 0, k, l))


def gram_kernel(rounds, first, last, cb_ref, mine_ref, other_ref, *rest):
    *arrived_refs, out_ref, tab_ref, held_ref = rest
    block_rows = mine_ref.shape[0]
    here = Local(cb_ref, block_rows, rounds)
    here.fill_links(tab_ref)
    count = len(arrived_refs) // 2
    known = last if rounds else tab_ref.shape[1]

    def pair(q):
        if rounds:
            return arrived_refs[q - 1][...], arrived_refs[count + q - 1][...]
        return arrived_refs[0][q], arrived_refs[1][q]

    def body(p):
        row, k = tab_ref[0, p], tab_ref[1, p]

        @pl.when((row >= 0) & (lax.rem(p, 2) == here.core))
        def _():
            held_ref[0], held_ref[1] = pair(p)
            i = (p - first) // 2

            def put(l, a, b):
                value = dot_nt(held_ref[0], a) + dot_nt(held_ref[1], b)
                put_block(out_ref, i, position_of(k, l), value, l == k)

            @pl.loop(0, here.slots)
            def _(l):
                _, own, b, _ = here.slot(row, l)

                @pl.when(own)
                def _():
                    put(l, mine_ref[b], other_ref[b])

            def with_arrival(q):
                @pl.when((tab_ref[0, q] == row) & (q <= p))
                def _():
                    put(tab_ref[1, q], *pair(q))

            if rounds:
                for q in range(1, p + 1):
                    with_arrival(q)
            else:
                pl.loop(0, known)(with_arrival)

    if rounds:
        for p in range(max(first, 1), last):
            body(p)
    else:
        pl.loop(first, last)(body)


def read_part(parts, mine, index):
    half = len(parts) // 2
    terms = [
        jnp.where(mine, a[index], b[index]).astype(jnp.float32)
        for a, b in zip(parts[:half], parts[half:])
    ]
    while len(terms) > 1:
        terms = [a + b for a, b in zip(terms[::2], terms[1::2])]
    return terms[0]


def place_block(gram_ref, low_ref, row, k, l, value, lows):
    block = value.shape[0]
    high = value.astype(jnp.bfloat16)
    gram_ref[row, aligned(k, block), aligned(l, block)] = high

    @pl.when(k == l)
    def _():
        low_ref[row, pl.ds(k, 1)] = low_diagonal(value, high) + lows()


def place_arrivals(here, first, last, parts, tab_ref, gram_ref, low_ref):
    block = parts[0].shape[2]
    slots = here.slots

    def body(p):
        row, k = tab_ref[0, p], tab_ref[1, p]

        @pl.when(row >= 0)
        def _():
            mine = lax.rem(p, 2) == here.core
            i = (p - first) // 2

            def lows():
                return read_part(parts, mine, (i, pl.ds(slots * block, 1)))

            @pl.loop(0, slots)
            def _(l):
                filled, own, _, holder = here.slot(row, l)

                @pl.when(filled & (own | (here.place(holder) <= p)))
                def _():
                    value = read_part(parts, mine, (i, aligned(position_of(k, l), block)))
                    place_block(gram_ref, low_ref, row, k, l, value, lows)

                    @pl.when(k != l)
                    def _():
                        flipped = value.T.astype(jnp.bfloat16)
                        gram_ref[row, aligned(l, block), aligned(k, block)] = flipped

    pl.loop(first, last)(body)


def place_own(here, block, parts, gram_ref, low_ref):
    slots = here.slots
    @pl.loop(0, here.block_rows)
    def _(j):
        n = here.count(j)

        def along(k, carry):
            _, own_k, a, _ = here.slot(j, k)

            @pl.when(own_k)
            def _():
                mine = lax.rem(a, 2) == here.core
                i = lax.div(a, 2)

                def lows():
                    return read_part(parts, mine, (i, pl.ds(here.block_rows * block, 1)))

                def across(l, carry):
                    _, own_l, b, _ = here.slot(j, l)

                    @pl.when(own_l)
                    def _():
                        value = read_part(parts, mine, (i, aligned(b, block)))
                        place_block(gram_ref, low_ref, j, k, l, value, lows)

                    return carry

                lax.fori_loop(0, n, across, 0)

            return carry

        lax.fori_loop(0, n, along, 0)
        for odd in range(1, slots, 2):

            @pl.when(n == odd)
            def _(odd=odd):
                gram_ref[j, odd * block : (odd + 1) * block, :] = jnp.zeros(
                    (block, slots * block), gram_ref.dtype
                )


def gather_kernel(rounds, groups, ways, cb_ref, *rest):
    count = 2 * ways
    parts, (gram_ref, low_ref, tab_ref) = rest[:-3], rest[-3:]
    block_rows, wide, _ = gram_ref.shape
    here = Local(cb_ref, block_rows, rounds)
    here.fill_links(tab_ref)
    place_own(here, wide // here.slots, parts[:count], gram_ref, low_ref)
    for g, (first, last) in enumerate(groups, 1):
        place_arrivals(here, first, last, parts[g * count : (g + 1) * count], tab_ref, gram_ref, low_ref)


def products(here, block, w_ref, gram_ref, low_ref, v_ref):
    @pl.loop(0, here.block_rows)
    def _(j):
        count = here.count(j)
        for wide in range(2, here.slots + 1, 2):

            @pl.when((count == wide) | (count == wide - 1))
            def _(wide=wide):
                width = wide * block
                v_ref[j, :, :width] = dot_nn(w_ref[j, :, :width], gram_ref[j, :width, :width])
                for k in range(wide):
                    at = slice(k * block, (k + 1) * block)
                    v_ref[j, :, at] += w_ref[j, :, at].astype(jnp.float32) * low_ref[j, k : k + 1]


def step_and_send(here, block, scale, v_ref, next_ref, out_ref):
    @pl.loop(0, here.block_rows)
    def _(j):
        for k in range(here.slots):
            filled, own, b, holder = here.slot(j, k)
            at = slice(k * block, (k + 1) * block)

            @pl.when(own)
            def _(k=k, b=b, at=at):
                m = here.mate(b, j) if k else 0
                mirrored = v_ref[b, :, aligned(m, block)].T
                next_ref[j, k] = next_ref[j, k] - scale * (v_ref[j, :, at] + mirrored)

            @pl.when(filled & jnp.logical_not(own))
            def _(k=k, holder=holder, at=at):
                value = v_ref[j, :, at]
                next_ref[j, k] = next_ref[j, k] - scale * value
                out_ref[holder] = value.astype(out_ref.dtype).T


def first_kernel(rounds, group, ways, scale, cb_ref, prec_ref, gram_in_ref, low_in_ref, *rest):
    parts, rest = rest[: 2 * ways], rest[2 * ways :]
    gram_ref, low_ref, next_ref, out_ref, tab_ref, w_ref, v_ref = rest
    block_rows, slots, block, _ = prec_ref.shape
    here = Local(cb_ref, block_rows, rounds)
    here.fill_links(tab_ref)
    low_ref[...] = low_in_ref[...]

    @pl.loop(0, block_rows * slots)
    def _(i):
        at = (lax.div(i, slots), aligned(lax.rem(i, slots), block))
        gram_ref[at] = gram_in_ref[at]

    place_arrivals(here, *group, parts, tab_ref, gram_ref, low_ref)
    @pl.loop(0, block_rows)
    def _(j):
        for k in range(slots):
            filled = here.cb[j, k] >= 0
            value = jnp.where(filled, prec_ref[j, k], 0.0)
            next_ref[j, k] = value
            w_ref[j, :, k * block : (k + 1) * block] = value.astype(jnp.bfloat16)
    products(here, block, w_ref, gram_ref, low_ref, v_ref)
    step_and_send(here, block, scale, v_ref, next_ref, out_ref)


def prox_blocks(here, block, scale, stepped_ref, in_ref, next_ref, w_ref):
    eye = eye_of(block)

    def finish(j, k, m):
        value = m - jnp.clip(m, -SHRINK, SHRINK)
        if k == 0:
            value = jnp.where(eye, 0.5 * (m + jnp.sqrt(m * m + 4.0 * STEP)), value)
        next_ref[j, k] = value
        if w_ref is not None:
            w_ref[j, :, k * block : (k + 1) * block] = value.astype(jnp.bfloat16)

    @pl.loop(0, here.block_rows)
    def _(j):
        for k in range(here.slots):
            filled, own, _, holder = here.slot(j, k)

            @pl.when(own)
            def _(k=k):
                finish(j, k, stepped_ref[j, k])

            @pl.when(filled & jnp.logical_not(own))
            def _(k=k, holder=holder):
                finish(j, k, stepped_ref[j, k] - scale * in_ref[holder].astype(jnp.float32))

            @pl.when(jnp.logical_not(filled))
            def _(k=k):
                next_ref[j, k] = jnp.zeros((block, block), jnp.float32)
                if w_ref is not None:
                    w_ref[j, :, k * block : (k + 1) * block] = jnp.zeros((block, block), jnp.bfloat16)


def middle_kernel(scale, cb_ref, stepped_ref, in_ref, gram_ref, low_ref, next_ref, out_ref, w_ref, v_ref):
    block_rows, _, block, _ = stepped_ref.shape
    here = Local(cb_ref, block_rows, False)
    prox_blocks(here, block, scale, stepped_ref, in_ref, next_ref, w_ref)
    products(here, block, w_ref, gram_ref, low_ref, v_ref)
    step_and_send(here, block, scale, v_ref, next_ref, out_ref)


def last_kernel(scale, cb_ref, stepped_ref, in_ref, next_ref):
    block_rows, _, block, _ = stepped_ref.shape
    prox_blocks(Local(cb_ref, block_rows, False), block, scale, stepped_ref, in_ref, next_ref, None)


def call(kernel, inputs, outs, scratch, smem=1):
    arrays = (*inputs, *outs, *scratch)
    size = sum(math.prod(x.shape) * jnp.dtype(x.dtype).itemsize for x in arrays)
    return pl.pallas_call(
        kernel,
        out_shape=outs,
        in_specs=[SMEM] * smem + [VMEM] * (len(inputs) - smem),
        out_specs=[VMEM] * len(outs),
        scratch_shapes=scratch,
        compiler_params=pltpu.CompilerParams(vmem_limit_bytes=size + (6 << 20)),
        cost_estimate=pl.CostEstimate(flops=1, bytes_accessed=1, transcendentals=0),
    )(*inputs)


def swap(x, bit):
    count = lax.axis_size("samp")
    return lax.ppermute(x, "samp", [(i, i ^ bit) for i in range(count)])


def everywhere(x):
    mine = [x] + [swap(x, bit) for bit in range(2, lax.axis_size("samp"), 2)]
    return mine + [swap(part, 1) for part in mine]


def after(x, *earlier):
    return lax.optimization_barrier((x, *earlier))[0]


def local(samples, precision, col_blocks):
    row_count = samples.shape[0]
    block_rows, slots, block, _ = precision.shape
    peers = lax.axis_size("feat")
    ways = lax.axis_size("samp") // 2
    scale = 0.5 * STEP / (row_count * lax.axis_size("samp"))
    rounds = peers == 8
    groups = [(0, 4), (4, 6), (6, 8)] if rounds else [(0, peers)]

    def shape(dims, dtype):
        return jax.ShapeDtypeStruct(dims, dtype)

    bf16, f32 = samples.dtype, jnp.float32
    tab = pltpu.SMEM((2, peers), jnp.int32)
    strip = (block, row_count)
    sends = [shape(strip, bf16)] * (peers - 1) if rounds else [shape((peers, *strip), bf16)]
    own, *sends = call(
        functools.partial(pack_kernel, rounds),
        (col_blocks, samples),
        [shape((block_rows, *strip), bf16), *sends],
        [tab],
    )

    def exchange(x, r):
        return lax.ppermute(x, "feat", [(i, i ^ r) for i in range(peers)])

    if rounds:
        arrived = [exchange(sends[r - 1], r) for r in range(1, 6)]
        arrived += [exchange(after(sends[r - 1], arrived[r - 3]), r) for r in (6, 7)]
    else:
        arrived = [lax.all_to_all(sends[0], "feat", 0, 0, tiled=True)]
    own_pair = (own, swap(own, 1))
    over = [swap(x, 1) for x in arrived]
    lists = [
        everywhere(
            call(
                own_gram_kernel,
                own_pair,
                [shape((block_rows // 2, block_rows * block + 16, block), bf16)],
                [],
                smem=0,
            )[0]
        )
    ]
    for first, last in groups:
        known = last - 1 if rounds else 1
        lists.append(
            everywhere(
                call(
                    functools.partial(gram_kernel, rounds, first, last),
                    (col_blocks, *own_pair, *arrived[:known], *over[:known]),
                    [shape(((last - first) // 2, slots * block + 16, block), bf16)],
                    [tab, pltpu.VMEM((2, *strip), bf16)],
                )[0]
            )
        )
    grams = [
        shape((block_rows, slots * block, slots * block), bf16),
        shape((block_rows, 8, block), f32),
    ]
    blocks = shape(precision.shape, f32)
    swapped = shape((peers, block, block), bf16)
    work = [
        pltpu.VMEM((block_rows, block, slots * block), bf16),
        pltpu.VMEM((block_rows, block, slots * block), f32),
    ]
    gram, low = call(
        functools.partial(gather_kernel, rounds, groups[:-1], ways),
        (col_blocks, *sum(lists[:-1], [])),
        grams,
        [tab],
    )
    gram, low, stepped, out = call(
        functools.partial(first_kernel, rounds, groups[-1], ways, scale),
        (col_blocks, precision, gram, low, *lists[-1]),
        [*grams, blocks, swapped],
        [tab, *work],
    )
    for iteration in range(ITERS):
        mirrored = lax.all_to_all(out, "feat", 0, 0, tiled=True)
        if iteration + 1 < ITERS:
            stepped, out = call(
                functools.partial(middle_kernel, scale),
                (col_blocks, stepped, mirrored, gram, low),
                [blocks, swapped],
                work,
            )
    (updated,) = call(functools.partial(last_kernel, scale), (col_blocks, stepped, mirrored), [blocks], [])
    return updated


def solution(mesh):
    return jax.shard_map(
        local,
        mesh=mesh,
        in_specs=(P("samp", "feat"), P("feat", None, None, None), P("feat", None)),
        out_specs=P("feat", None, None, None),
        check_vma=False,
    )
```

time: 208 us -> 149 us (0.72); the launches traced: 205 us -> 149 us
  waiting for transfers between devices: 77.6 us -> 45.5 us
  Pallas kernels: 38.3 us -> 21.9 us
  local copies, waits for them, and re-layouts: 8.22 us -> 2.6 us
  blocking collectives: 58.1 us -> 55.1 us
  starting transfers between devices: 21.4 us -> 23.7 us
    ppermute x12 -> x20, waiting for transfers between devices: 39.1 us -> 16.2 us  [swap(): return lax.ppermute(x, 'samp', [(i, i ^ bit) for i in range(count)])]
    pallas_call x9 -> x10, Pallas kernels: 38.3 us -> 21.9 us  [call(): pl.pallas_call(kernel, out_shape=outs, in_specs=[SMEM] * smem + [VMEM] *...]
    ppermute x7, waiting for transfers between devices: 38.5 us -> 29.3 us  [exchange(): return lax.ppermute(x, 'feat', [(i, i ^ r) for i in range(peers)])]
    unnamed x46 -> x10, local copies, waits for them, and re-layouts: 8.22 us -> 2.6 us
    all_to_all x3, blocking collectives: 58.1 us -> 55.1 us  [local(): mirrored = lax.all_to_all(out, 'feat', 0, 0, tiled=True)]
    ppermute x12 -> x20, starting transfers between devices: 5.39 us -> 7.96 us  [swap(): return lax.ppermute(x, 'samp', [(i, i ^ bit) for i in range(count)])]
  transfers between devices with their start and end apart: 19 -> 27, of which waited for: 10 -> 10; matrix products, arithmetic and copies ran while one was open for 1% -> 0% of each run, Pallas kernels for 4% -> 6%
where the time goes in v2:
time: 149 us
  blocking collectives  55.1 us (37%)
  waiting for transfers between devices  45.5 us (31%)
  starting transfers between devices  23.7 us (16%)
  Pallas kernels  21.9 us (15%)
  local copies, waits for them, and re-layouts  2.6 us (2%)
    all_to_all x3, blocking collectives, local(): mirrored = lax.all_to_all(out, 'feat', 0, 0, tiled=True)  55.1 us
    ppermute x7, waiting for transfers between devices, exchange(): return lax.ppermute(x, 'feat', [(i, i ^ r) for i in range(peers)])  29.3 us
    pallas_call x10, Pallas kernels, call(): pl.pallas_call(kernel, out_shape=outs, in_specs=[SMEM] * smem + [VMEM] *...  21.9 us
    ppermute x20, waiting for transfers between devices, swap(): return lax.ppermute(x, 'samp', [(i, i ^ bit) for i in range(count)])  16.2 us
    ppermute x7, starting transfers between devices, exchange(): return lax.ppermute(x, 'feat', [(i, i ^ r) for i in range(peers)])  15.8 us
    ppermute x20, starting transfers between devices, swap(): return lax.ppermute(x, 'samp', [(i, i ^ bit) for i in range(count)])  7.96 us
  transfers between devices with their start and end apart: 27, of which 10 were waited for; matrix products, arithmetic and copies ran while one was open for 0% of the time, Pallas kernels for 6%

profile of v2, /device:TPU:0, one launch (start us, length us, event | category | flops | bytes accessed | tf_op | source)
XLA Modules:
  0.0 149.1 jit_solution(11313845455083075147)
XLA Ops:
  0.0 1.2 copy-done.1
  1.9 1.1 shard_map.37
  3.6 2.6 %collective-permute-start.4 = (bf16[128,1024]{1,0:T(8,128)(2,1)S(1)}, bf16[128,1024]{1,0:T(8,128)(2,1)S(1)}, u32[]{:S(2)}, u32[]{:S(2)}) collective-permute-start(bf16[128,1024]{1,0:T(8,128)(2,1)S(1)} %get-tuple-element.26), channel_id=1, source_target_pairs={{0,1},{1,0},{2,3},{3,2},{4,5},{5,4},{6,7},{7,6},{8,9},{9,8},{10,11... | collective-permute-start | bytes 786440 | tf_op jit(solution)/shard_map/ppermute | solution.py:453
  6.1 1.6 %collective-permute-start.5 = (bf16[128,1024]{1,0:T(8,128)(2,1)S(1)}, bf16[128,1024]{1,0:T(8,128)(2,1)S(1)}, u32[]{:S(2)}, u32[]{:S(2)}) collective-permute-start(bf16[128,1024]{1,0:T(8,128)(2,1)S(1)} %get-tuple-element.27), channel_id=1, source_target_pairs={{0,2},{1,3},{2,0},{3,1},{4,6},{5,7},{6,4},{7,5},{8,10},{9,11},{10,... | collective-permute-start | bytes 786440 | tf_op jit(solution)/shard_map/ppermute | solution.py:453
  7.7 3.0 %collective-permute-start.13 = (bf16[128,1024]{1,0:T(8,128)(2,1)S(1)}, bf16[128,1024]{1,0:T(8,128)(2,1)S(1)}, u32[]{:S(2)}, u32[]{:S(2)}) collective-permute-start(bf16[128,1024]{1,0:T(8,128)(2,1)S(1)} %get-tuple-element.29), channel_id=1, source_target_pairs={{0,4},{1,5},{2,6},{3,7},{4,0},{5,1},{6,2},{7,3},{8,12},{9,13},{10,... | collective-permute-start | bytes 786440 | tf_op jit(solution)/shard_map/ppermute | solution.py:453
  10.7 2.3 %collective-permute-done.4.rest_0_ = bf16[128,1024]{1,0:T(8,128)(2,1)S(1)} collective-permute-done((bf16[128,1024]{1,0:T(8,128)(2,1)S(1)}, bf16[128,1024]{1,0:T(8,128)(2,1)S(1)}, u32[]{:S(2)}, u32[]{:S(2)}) %collective-permute-start.4) | collective-permute-done | bytes 262176 | tf_op jit(solution)/shard_map/ppermute | solution.py:453
  13.0 3.8 %collective-permute-start.14 = (bf16[128,1024]{1,0:T(8,128)(2,1)S(1)}, bf16[128,1024]{1,0:T(8,128)(2,1)S(1)}, u32[]{:S(2)}, u32[]{:S(2)}) collective-permute-start(bf16[128,1024]{1,0:T(8,128)(2,1)S(1)} %get-tuple-element.30), channel_id=1, source_target_pairs={{0,5},{1,4},{2,7},{3,6},{4,1},{5,0},{6,3},{7,2},{8,13},{9,12},{10,... | collective-permute-start | bytes 786440 | tf_op jit(solution)/shard_map/ppermute | solution.py:453
  16.8 8.9 %collective-permute-done.5.rest_1_ = bf16[128,1024]{1,0:T(8,128)(2,1)S(1)} collective-permute-done((bf16[128,1024]{1,0:T(8,128)(2,1)S(1)}, bf16[128,1024]{1,0:T(8,128)(2,1)S(1)}, u32[]{:S(2)}, u32[]{:S(2)}) %collective-permute-start.5) | collective-permute-done | bytes 262176 | tf_op jit(solution)/shard_map/ppermute | solution.py:453
  25.8 4.2 %collective-permute-done.6.rest_2_ = bf16[128,1024]{1,0:T(8,128)(2,1)S(1)} collective-permute-done((bf16[128,1024]{1,0:T(8,128)(2,1)S(1)}, bf16[128,1024]{1,0:T(8,128)(2,1)S(1)}, u32[]{:S(2)}, u32[]{:S(2)}) %collective-permute-start.6) | collective-permute-done | bytes 262176 | tf_op jit(solution)/shard_map/ppermute | solution.py:453
  30.5 4.2 %collective-permute-done.14.rest_4_ = bf16[128,1024]{1,0:T(8,128)(2,1)S(1)} collective-permute-done((bf16[128,1024]{1,0:T(8,128)(2,1)S(1)}, bf16[128,1024]{1,0:T(8,128)(2,1)S(1)}, u32[]{:S(2)}, u32[]{:S(2)}) %collective-permute-start.14) | collective-permute-done | bytes 262176 | tf_op jit(solution)/shard_map/ppermute | solution.py:453
  34.7 3.9 %collective-permute-start.20 = (bf16[128,1024]{1,0:T(8,128)(2,1)S(1)}, bf16[128,1024]{1,0:T(8,128)(2,1)S(1)}, u32[]{:S(2)}, u32[]{:S(2)}) collective-permute-start(bf16[128,1024]{1,0:T(8,128)(2,1)S(1)} %get-tuple-element.34), channel_id=1, source_target_pairs={{0,6},{1,7},{2,4},{3,5},{4,2},{5,3},{6,0},{7,1},{8,14},{9,15},{10,... | collective-permute-start | bytes 786440 | tf_op jit(solution)/shard_map/ppermute | solution.py:453
  38.6 0.9 collective-permute-start.21
  40.0 5.8 %collective-permute-done.20.rest_5_ = bf16[128,1024]{1,0:T(8,128)(2,1)S(1)} collective-permute-done((bf16[128,1024]{1,0:T(8,128)(2,1)S(1)}, bf16[128,1024]{1,0:T(8,128)(2,1)S(1)}, u32[]{:S(2)}, u32[]{:S(2)}) %collective-permute-start.20) | collective-permute-done | bytes 262176 | tf_op jit(solution)/shard_map/ppermute | solution.py:453
  45.9 3.8 %collective-permute-done.21.rest_6_ = bf16[128,1024]{1,0:T(8,128)(2,1)S(1)} collective-permute-done((bf16[128,1024]{1,0:T(8,128)(2,1)S(1)}, bf16[128,1024]{1,0:T(8,128)(2,1)S(1)}, u32[]{:S(2)}, u32[]{:S(2)}) %collective-permute-start.21) | collective-permute-done | bytes 262176 | tf_op jit(solution)/shard_map/ppermute | solution.py:453
  50.4 1.5 %shard_map.39.rest_4_ = bf16[2,784,128]{2,1,0:T(8,128)(2,1)S(1)} custom-call(s32[4,6]{1,0:T(4,128)S(1)} %copy-done.3, bf16[4,128,1024]{2,1,0:T(8,128)(2,1)S(1)} %get-tuple-element.25.mine_ref, bf16[4,128,1024]{2,1,0:T(8,128)(2,1)S(1)} %collective-permute-done.other_ref, bf16[128,1024]{1,0:T(8,128)(2,1)S(1)} %collective-permute-done.4.rest_0_, ...), custom_call_target="tpu_custom_call" | custom-call | flops 1 | bytes 1 | tf_op jit(solution)/shard_map/pallas_call | solution.py:404
  51.9 1.6 %collective-permute-start.10 = (bf16[2,784,128]{2,1,0:T(8,128)(2,1)S(1)}, bf16[2,784,128]{2,1,0:T(8,128)(2,1)S(1)}, u32[]{:S(2)}, u32[]{:S(2)}) collective-permute-start(bf16[2,784,128]{2,1,0:T(8,128)(2,1)S(1)} %shard_map.39.rest_4_), channel_id=1, source_target_pairs={{0,16},{8,24},{16,0},{24,8},{1,17},{9,25},{17,1},{25,9},{2,18},{10... | collective-permute-start | bytes 1204232 | tf_op jit(solution)/shard_map/ppermute | solution.py:417
  54.3 1.1 collective-permute-start.18
  55.8 0.7 shard_map.42.rest_0_
  56.6 1.6 %collective-permute-start.24 = (bf16[1,784,128]{2,1,0:T(8,128)(2,1)S(1)}, bf16[1,784,128]{2,1,0:T(8,128)(2,1)S(1)}, u32[]{:S(2)}, u32[]{:S(2)}) collective-permute-start(bf16[1,784,128]{2,1,0:T(8,128)(2,1)S(1)} %shard_map.42.rest_0_), channel_id=1, source_target_pairs={{0,16},{8,24},{16,0},{24,8},{1,17},{9,25},{17,1},{25,9},{2,18},{10... | collective-permute-start | bytes 602120 | tf_op jit(solution)/shard_map/ppermute | solution.py:417
  58.2 3.6 %shard_map.38.rest_0_ = bf16[2,528,128]{2,1,0:T(8,128)(2,1)S(1)} custom-call(bf16[4,128,1024]{2,1,0:T(8,128)(2,1)S(1)} %get-tuple-element.25.mine_ref, bf16[4,128,1024]{2,1,0:T(8,128)(2,1)S(1)} %collective-permute-done.other_ref), custom_call_target="tpu_custom_call" | custom-call | flops 1 | bytes 1 | tf_op jit(solution)/shard_map/pallas_call | solution.py:404
  62.3 6.0 %collective-permute-done.17.rest_9_ = bf16[1,784,128]{2,1,0:T(8,128)(2,1)S(1)} collective-permute-done((bf16[1,784,128]{2,1,0:T(8,128)(2,1)S(1)}, bf16[1,784,128]{2,1,0:T(8,128)(2,1)S(1)}, u32[]{:S(2)}, u32[]{:S(2)}) %collective-permute-start.17) | collective-permute-done | bytes 200736 | tf_op jit(solution)/shard_map/ppermute | solution.py:417
  68.9 3.8 %collective-permute-done.24.rest_1_ = bf16[1,784,128]{2,1,0:T(8,128)(2,1)S(1)} collective-permute-done((bf16[1,784,128]{2,1,0:T(8,128)(2,1)S(1)}, bf16[1,784,128]{2,1,0:T(8,128)(2,1)S(1)}, u32[]{:S(2)}, u32[]{:S(2)}) %collective-permute-start.24) | collective-permute-done | bytes 200736 | tf_op jit(solution)/shard_map/ppermute | solution.py:417
  72.7 5.4 %collective-permute-done.1.rest_1_ = bf16[2,528,128]{2,1,0:T(8,128)(2,1)S(1)} collective-permute-done((bf16[2,528,128]{2,1,0:T(8,128)(2,1)S(1)}, bf16[2,528,128]{2,1,0:T(8,128)(2,1)S(1)}, u32[]{:S(2)}, u32[]{:S(2)}) %collective-permute-start.1) | collective-permute-done | bytes 270368 | tf_op jit(solution)/shard_map/ppermute | solution.py:417
  78.7 1.0 collective-permute-done.3.rest_3_
  79.6 2.2 %shard_map.41 = (bf16[4,768,768]{2,1,0:T(8,128)(2,1)S(1)}, f32[4,8,128]{2,1,0:T(8,128)S(1)}) custom-call(s32[4,6]{1,0:T(4,128)S(1)} %copy-done.4, bf16[2,528,128]{2,1,0:T(8,128)(2,1)S(1)} %shard_map.38.rest_0_, bf16[2,528,128]{2,1,0:T(8,128)(2,1)S(1)} %collective-permute-done.1.rest_1_, bf16[2,528,128]{2,1,0:T(8,128)(2,1)S(1)} %collective-permute-done.2.rest_2_, ...), custom_call_target="tpu_custom_call" | custom-call | flops 1 | bytes 1 | tf_op jit(solution)/shard_map/pallas_call | solution.py:404
  81.9 3.3 %shard_map.43 = (bf16[4,768,768]{2,1,0:T(8,128)(2,1)S(1)}, f32[4,8,128]{2,1,0:T(8,128)S(1)}, f32[4,6,128,128]{3,2,1,0:T(8,128)S(1)}, bf16[8,128,128]{2,1,0:T(8,128)(2,1)S(1)}) custom-call(s32[4,6]{1,0:T(4,128)S(1)} %copy-done.4, f32[4,6,128,128]{3,2,1,0:T(8,128)S(1)} %copy-done, bf16[4,768,768]{2,1,0:T(8,128)(2,1)S(1)} %get-tuple-element.31.gram_in_ref, ...), custom_call_target="tpu_custom_call" | custom-call | flops 1 | bytes 1 | tf_op jit(solution)/shard_map/pallas_call | solution.py:404
  85.2 30.2 %all_to_all.15.in_ref = bf16[8,128,128]{2,1,0:T(8,128)(2,1)S(1)} all-to-all(bf16[8,128,128]{2,1,0:T(8,128)(2,1)S(1)} %get-tuple-element.38), channel_id=1, replica_groups=mesh['samp'=4,'feat'=8] {'feat'}, dimensions={0} | all-to-all | bytes 524288 | tf_op jit(solution)/shard_map/all_to_all | solution.py:508
  115.4 3.1 %shard_map.44 = (f32[4,6,128,128]{3,2,1,0:T(8,128)S(1)}, bf16[8,128,128]{2,1,0:T(8,128)(2,1)S(1)}) custom-call(s32[4,6]{1,0:T(4,128)S(1)} %copy-done.4, f32[4,6,128,128]{3,2,1,0:T(8,128)S(1)} %get-tuple-element.37.stepped_ref, bf16[8,128,128]{2,1,0:T(8,128)(2,1)S(1)} %all_to_all.15.in_ref, bf16[4,768,768]{2,1,0:T(8,128)(2,1)S(1)} %get-tuple-element.39.gram_ref, ...), custom_call_target="tpu_custom_call" | custom-call | flops 1 | bytes 1 | tf_op jit(solution)/shard_map/pallas_call | solution.py:404
  118.6 12.5 %all_to_all.16.in_ref = bf16[8,128,128]{2,1,0:T(8,128)(2,1)S(1)} all-to-all(bf16[8,128,128]{2,1,0:T(8,128)(2,1)S(1)} %get-tuple-element.42), channel_id=1, replica_groups=mesh['samp'=4,'feat'=8] {'feat'}, dimensions={0} | all-to-all | bytes 524288 | tf_op jit(solution)/shard_map/all_to_all | solution.py:508
  131.0 3.1 %shard_map.45 = (f32[4,6,128,128]{3,2,1,0:T(8,128)S(1)}, bf16[8,128,128]{2,1,0:T(8,128)(2,1)S(1)}) custom-call(s32[4,6]{1,0:T(4,128)S(1)} %copy-done.4, f32[4,6,128,128]{3,2,1,0:T(8,128)S(1)} %get-tuple-element.41.stepped_ref, bf16[8,128,128]{2,1,0:T(8,128)(2,1)S(1)} %all_to_all.16.in_ref, bf16[4,768,768]{2,1,0:T(8,128)(2,1)S(1)} %get-tuple-element.39.gram_ref, ...), custom_call_target="tpu_custom_call" | custom-call | flops 1 | bytes 1 | tf_op jit(solution)/shard_map/pallas_call | solution.py:404
  134.2 12.5 %all_to_all.17.in_ref = bf16[8,128,128]{2,1,0:T(8,128)(2,1)S(1)} all-to-all(bf16[8,128,128]{2,1,0:T(8,128)(2,1)S(1)} %get-tuple-element.44), channel_id=1, replica_groups=mesh['samp'=4,'feat'=8] {'feat'}, dimensions={0} | all-to-all | bytes 524288 | tf_op jit(solution)/shard_map/all_to_all | solution.py:508
  146.6 2.4 %shard_map.46 = f32[4,6,128,128]{3,2,1,0:T(8,128)} custom-call(s32[4,6]{1,0:T(4,128)S(1)} %copy-done.4, f32[4,6,128,128]{3,2,1,0:T(8,128)S(1)} %get-tuple-element.43.stepped_ref, bf16[8,128,128]{2,1,0:T(8,128)(2,1)S(1)} %all_to_all.17.in_ref), custom_call_target="tpu_custom_call" | custom-call | flops 1 | bytes 1 | tf_op jit(solution)/shard_map/pallas_call | solution.py:404
  (45 shorter events, 5.9 us)
Async XLA Ops:
  0.0 1.2 copy-start.1
  1.2 0.7 copy-start.2
  3.1 46.6 %collective-permute-start = (bf16[4,128,1024]{2,1,0:T(8,128)(2,1)S(1)}, bf16[4,128,1024]{2,1,0:T(8,128)(2,1)S(1)}, u32[]{:S(2)}, u32[]{:S(2)}) collective-permute-start(bf16[4,128,1024]{2,1,0:T(8,128)(2,1)S(1)} %get-tuple-element.25.mine_ref), channel_id=1, source_target_pairs={{0,8},{8,0},{16,24},{24,16},{1,9},{9,1},{17,25},{25,17},{2,10},{10... | collective-permute-start | bytes 3145736 | tf_op jit(solution)/shard_map/ppermute | solution.py:417
  3.6 9.5 %collective-permute-start.4 = (bf16[128,1024]{1,0:T(8,128)(2,1)S(1)}, bf16[128,1024]{1,0:T(8,128)(2,1)S(1)}, u32[]{:S(2)}, u32[]{:S(2)}) collective-permute-start(bf16[128,1024]{1,0:T(8,128)(2,1)S(1)} %get-tuple-element.26), channel_id=1, source_target_pairs={{0,1},{1,0},{2,3},{3,2},{4,5},{5,4},{6,7},{7,6},{8,9},{9,8},{10,11... | collective-permute-start | bytes 786440 | tf_op jit(solution)/shard_map/ppermute | solution.py:453
  6.1 19.6 %collective-permute-start.5 = (bf16[128,1024]{1,0:T(8,128)(2,1)S(1)}, bf16[128,1024]{1,0:T(8,128)(2,1)S(1)}, u32[]{:S(2)}, u32[]{:S(2)}) collective-permute-start(bf16[128,1024]{1,0:T(8,128)(2,1)S(1)} %get-tuple-element.27), channel_id=1, source_target_pairs={{0,2},{1,3},{2,0},{3,1},{4,6},{5,7},{6,4},{7,5},{8,10},{9,11},{10,... | collective-permute-start | bytes 786440 | tf_op jit(solution)/shard_map/ppermute | solution.py:453
  7.7 22.2 %collective-permute-start.6 = (bf16[128,1024]{1,0:T(8,128)(2,1)S(1)}, bf16[128,1024]{1,0:T(8,128)(2,1)S(1)}, u32[]{:S(2)}, u32[]{:S(2)}) collective-permute-start(bf16[128,1024]{1,0:T(8,128)(2,1)S(1)} %get-tuple-element.28), channel_id=1, source_target_pairs={{0,3},{1,2},{2,1},{3,0},{4,7},{5,6},{6,5},{7,4},{8,11},{9,10},{10,... | collective-permute-start | bytes 786440 | tf_op jit(solution)/shard_map/ppermute | solution.py:453
  7.7 22.2 %collective-permute-start.13 = (bf16[128,1024]{1,0:T(8,128)(2,1)S(1)}, bf16[128,1024]{1,0:T(8,128)(2,1)S(1)}, u32[]{:S(2)}, u32[]{:S(2)}) collective-permute-start(bf16[128,1024]{1,0:T(8,128)(2,1)S(1)} %get-tuple-element.29), channel_id=1, source_target_pairs={{0,4},{1,5},{2,6},{3,7},{4,0},{5,1},{6,2},{7,3},{8,12},{9,13},{10,... | collective-permute-start | bytes 786440 | tf_op jit(solution)/shard_map/ppermute | solution.py:453
  13.0 21.6 %collective-permute-start.14 = (bf16[128,1024]{1,0:T(8,128)(2,1)S(1)}, bf16[128,1024]{1,0:T(8,128)(2,1)S(1)}, u32[]{:S(2)}, u32[]{:S(2)}) collective-permute-start(bf16[128,1024]{1,0:T(8,128)(2,1)S(1)} %get-tuple-element.30), channel_id=1, source_target_pairs={{0,5},{1,4},{2,7},{3,6},{4,1},{5,0},{6,3},{7,2},{8,13},{9,12},{10,... | collective-permute-start | bytes 786440 | tf_op jit(solution)/shard_map/ppermute | solution.py:453
  25.7 12.8 %collective-permute-start.7 = (bf16[128,1024]{1,0:T(8,128)(2,1)S(1)}, bf16[128,1024]{1,0:T(8,128)(2,1)S(1)}, u32[]{:S(2)}, u32[]{:S(2)}) collective-permute-start(bf16[128,1024]{1,0:T(8,128)(2,1)S(1)} %collective-permute-done.4.rest_0_), channel_id=1, source_target_pairs={{0,8},{8,0},{16,24},{24,16},{1,9},{9,1},{17,25},{25,17},{2,10},{10... | collective-permute-start | bytes 786440 | tf_op jit(solution)/shard_map/ppermute | solution.py:417
  30.0 9.6 %collective-permute-start.8 = (bf16[128,1024]{1,0:T(8,128)(2,1)S(1)}, bf16[128,1024]{1,0:T(8,128)(2,1)S(1)}, u32[]{:S(2)}, u32[]{:S(2)}) collective-permute-start(bf16[128,1024]{1,0:T(8,128)(2,1)S(1)} %collective-permute-done.5.rest_1_), channel_id=1, source_target_pairs={{0,8},{8,0},{16,24},{24,16},{1,9},{9,1},{17,25},{25,17},{2,10},{10... | collective-permute-start | bytes 786440 | tf_op jit(solution)/shard_map/ppermute | solution.py:417
  30.0 9.6 %collective-permute-start.9 = (bf16[128,1024]{1,0:T(8,128)(2,1)S(1)}, bf16[128,1024]{1,0:T(8,128)(2,1)S(1)}, u32[]{:S(2)}, u32[]{:S(2)}) collective-permute-start(bf16[128,1024]{1,0:T(8,128)(2,1)S(1)} %collective-permute-done.6.rest_2_), channel_id=1, source_target_pairs={{0,8},{8,0},{16,24},{24,16},{1,9},{9,1},{17,25},{25,17},{2,10},{10... | collective-permute-start | bytes 786440 | tf_op jit(solution)/shard_map/ppermute | solution.py:417
  34.7 11.2 %collective-permute-start.20 = (bf16[128,1024]{1,0:T(8,128)(2,1)S(1)}, bf16[128,1024]{1,0:T(8,128)(2,1)S(1)}, u32[]{:S(2)}, u32[]{:S(2)}) collective-permute-start(bf16[128,1024]{1,0:T(8,128)(2,1)S(1)} %get-tuple-element.34), channel_id=1, source_target_pairs={{0,6},{1,7},{2,4},{3,5},{4,2},{5,3},{6,0},{7,1},{8,14},{9,15},{10,... | collective-permute-start | bytes 786440 | tf_op jit(solution)/shard_map/ppermute | solution.py:453
  38.6 11.1 %collective-permute-start.21 = (bf16[128,1024]{1,0:T(8,128)(2,1)S(1)}, bf16[128,1024]{1,0:T(8,128)(2,1)S(1)}, u32[]{:S(2)}, u32[]{:S(2)}) collective-permute-start(bf16[128,1024]{1,0:T(8,128)(2,1)S(1)} %get-tuple-element.36), channel_id=1, source_target_pairs={{0,7},{1,6},{2,5},{3,4},{4,3},{5,2},{6,1},{7,0},{8,15},{9,14},{10,... | collective-permute-start | bytes 786440 | tf_op jit(solution)/shard_map/ppermute | solution.py:453
  39.5 14.0 %collective-permute-start.15 = (bf16[128,1024]{1,0:T(8,128)(2,1)S(1)}, bf16[128,1024]{1,0:T(8,128)(2,1)S(1)}, u32[]{:S(2)}, u32[]{:S(2)}) collective-permute-start(bf16[128,1024]{1,0:T(8,128)(2,1)S(1)} %collective-permute-done.13.rest_3_), channel_id=1, source_target_pairs={{0,8},{8,0},{16,24},{24,16},{1,9},{9,1},{17,25},{25,17},{2,10},{10... | collective-permute-start | bytes 786440 | tf_op jit(solution)/shard_map/ppermute | solution.py:417
  39.5 14.0 %collective-permute-start.16 = (bf16[128,1024]{1,0:T(8,128)(2,1)S(1)}, bf16[128,1024]{1,0:T(8,128)(2,1)S(1)}, u32[]{:S(2)}, u32[]{:S(2)}) collective-permute-start(bf16[128,1024]{1,0:T(8,128)(2,1)S(1)} %collective-permute-done.14.rest_4_), channel_id=1, source_target_pairs={{0,8},{8,0},{16,24},{24,16},{1,9},{9,1},{17,25},{25,17},{2,10},{10... | collective-permute-start | bytes 786440 | tf_op jit(solution)/shard_map/ppermute | solution.py:417
  45.9 10.0 %collective-permute-start.22 = (bf16[128,1024]{1,0:T(8,128)(2,1)S(1)}, bf16[128,1024]{1,0:T(8,128)(2,1)S(1)}, u32[]{:S(2)}, u32[]{:S(2)}) collective-permute-start(bf16[128,1024]{1,0:T(8,128)(2,1)S(1)} %collective-permute-done.20.rest_5_), channel_id=1, source_target_pairs={{0,8},{8,0},{16,24},{24,16},{1,9},{9,1},{17,25},{25,17},{2,10},{10... | collective-permute-start | bytes 786440 | tf_op jit(solution)/shard_map/ppermute | solution.py:417
  49.7 6.1 %collective-permute-start.23 = (bf16[128,1024]{1,0:T(8,128)(2,1)S(1)}, bf16[128,1024]{1,0:T(8,128)(2,1)S(1)}, u32[]{:S(2)}, u32[]{:S(2)}) collective-permute-start(bf16[128,1024]{1,0:T(8,128)(2,1)S(1)} %collective-permute-done.21.rest_6_), channel_id=1, source_target_pairs={{0,8},{8,0},{16,24},{24,16},{1,9},{9,1},{17,25},{25,17},{2,10},{10... | collective-permute-start | bytes 786440 | tf_op jit(solution)/shard_map/ppermute | solution.py:417
  49.7 0.7 copy-start.3
  51.9 3.9 %copy-start.4 = (s32[4,6]{1,0:T(4,128)S(1)}, s32[4,6]{1,0:T(4,128)}, u32[]{:S(2)}) copy-start(s32[4,6]{1,0:T(4,128)} %cb_ref.17) | copy-start | bytes 292
  51.9 16.5 %collective-permute-start.10 = (bf16[2,784,128]{2,1,0:T(8,128)(2,1)S(1)}, bf16[2,784,128]{2,1,0:T(8,128)(2,1)S(1)}, u32[]{:S(2)}, u32[]{:S(2)}) collective-permute-start(bf16[2,784,128]{2,1,0:T(8,128)(2,1)S(1)} %shard_map.39.rest_4_), channel_id=1, source_target_pairs={{0,16},{8,24},{16,0},{24,8},{1,17},{9,25},{17,1},{25,9},{2,18},{10... | collective-permute-start | bytes 1204232 | tf_op jit(solution)/shard_map/ppermute | solution.py:417
  54.3 8.1 %collective-permute-start.18 = (bf16[1,784,128]{2,1,0:T(8,128)(2,1)S(1)}, bf16[1,784,128]{2,1,0:T(8,128)(2,1)S(1)}, u32[]{:S(2)}, u32[]{:S(2)}) collective-permute-start(bf16[1,784,128]{2,1,0:T(8,128)(2,1)S(1)} %shard_map.40.rest_8_), channel_id=1, source_target_pairs={{0,8},{8,0},{16,24},{24,16},{1,9},{9,1},{17,25},{25,17},{2,10},{10... | collective-permute-start | bytes 602120 | tf_op jit(solution)/shard_map/ppermute | solution.py:417
  55.3 13.0 %collective-permute-start.17 = (bf16[1,784,128]{2,1,0:T(8,128)(2,1)S(1)}, bf16[1,784,128]{2,1,0:T(8,128)(2,1)S(1)}, u32[]{:S(2)}, u32[]{:S(2)}) collective-permute-start(bf16[1,784,128]{2,1,0:T(8,128)(2,1)S(1)} %shard_map.40.rest_8_), channel_id=1, source_target_pairs={{0,16},{8,24},{16,0},{24,8},{1,17},{9,25},{17,1},{25,9},{2,18},{10... | collective-permute-start | bytes 602120 | tf_op jit(solution)/shard_map/ppermute | solution.py:417
  56.6 16.1 %collective-permute-start.24 = (bf16[1,784,128]{2,1,0:T(8,128)(2,1)S(1)}, bf16[1,784,128]{2,1,0:T(8,128)(2,1)S(1)}, u32[]{:S(2)}, u32[]{:S(2)}) collective-permute-start(bf16[1,784,128]{2,1,0:T(8,128)(2,1)S(1)} %shard_map.42.rest_0_), channel_id=1, source_target_pairs={{0,16},{8,24},{16,0},{24,8},{1,17},{9,25},{17,1},{25,9},{2,18},{10... | collective-permute-start | bytes 602120 | tf_op jit(solution)/shard_map/ppermute | solution.py:417
  61.8 20.1 %copy-start = (f32[4,6,128,128]{3,2,1,0:T(8,128)S(1)}, f32[4,6,128,128]{3,2,1,0:T(8,128)}, u32[]{:S(2)}) copy-start(f32[4,6,128,128]{3,2,1,0:T(8,128)} %prec_ref.1) | copy-start | bytes 4718596
  61.8 16.3 %collective-permute-start.1 = (bf16[2,528,128]{2,1,0:T(8,128)(2,1)S(1)}, bf16[2,528,128]{2,1,0:T(8,128)(2,1)S(1)}, u32[]{:S(2)}, u32[]{:S(2)}) collective-permute-start(bf16[2,528,128]{2,1,0:T(8,128)(2,1)S(1)} %shard_map.38.rest_0_), channel_id=1, source_target_pairs={{0,16},{8,24},{16,0},{24,8},{1,17},{9,25},{17,1},{25,9},{2,18},{10... | collective-permute-start | bytes 811016 | tf_op jit(solution)/shard_map/ppermute | solution.py:417
  62.3 15.7 %collective-permute-start.2 = (bf16[2,528,128]{2,1,0:T(8,128)(2,1)S(1)}, bf16[2,528,128]{2,1,0:T(8,128)(2,1)S(1)}, u32[]{:S(2)}, u32[]{:S(2)}) collective-permute-start(bf16[2,528,128]{2,1,0:T(8,128)(2,1)S(1)} %shard_map.38.rest_0_), channel_id=1, source_target_pairs={{0,8},{8,0},{16,24},{24,16},{1,9},{9,1},{17,25},{25,17},{2,10},{10... | collective-permute-start | bytes 811016 | tf_op jit(solution)/shard_map/ppermute | solution.py:417
  68.4 10.3 %collective-permute-start.11 = (bf16[2,784,128]{2,1,0:T(8,128)(2,1)S(1)}, bf16[2,784,128]{2,1,0:T(8,128)(2,1)S(1)}, u32[]{:S(2)}, u32[]{:S(2)}) collective-permute-start(bf16[2,784,128]{2,1,0:T(8,128)(2,1)S(1)} %shard_map.39.rest_4_), channel_id=1, source_target_pairs={{0,8},{8,0},{16,24},{24,16},{1,9},{9,1},{17,25},{25,17},{2,10},{10... | collective-permute-start | bytes 1204232 | tf_op jit(solution)/shard_map/ppermute | solution.py:417
  68.4 11.2 %collective-permute-start.12 = (bf16[2,784,128]{2,1,0:T(8,128)(2,1)S(1)}, bf16[2,784,128]{2,1,0:T(8,128)(2,1)S(1)}, u32[]{:S(2)}, u32[]{:S(2)}) collective-permute-start(bf16[2,784,128]{2,1,0:T(8,128)(2,1)S(1)} %collective-permute-done.10.rest_5_), channel_id=1, source_target_pairs={{0,8},{8,0},{16,24},{24,16},{1,9},{9,1},{17,25},{25,17},{2,10},{10... | collective-permute-start | bytes 1204232 | tf_op jit(solution)/shard_map/ppermute | solution.py:417
  72.7 5.9 %collective-permute-start.19 = (bf16[1,784,128]{2,1,0:T(8,128)(2,1)S(1)}, bf16[1,784,128]{2,1,0:T(8,128)(2,1)S(1)}, u32[]{:S(2)}, u32[]{:S(2)}) collective-permute-start(bf16[1,784,128]{2,1,0:T(8,128)(2,1)S(1)} %collective-permute-done.17.rest_9_), channel_id=1, source_target_pairs={{0,8},{8,0},{16,24},{24,16},{1,9},{9,1},{17,25},{25,17},{2,10},{10... | collective-permute-start | bytes 602120 | tf_op jit(solution)/shard_map/ppermute | solution.py:417
  78.1 1.5 %collective-permute-start.3 = (bf16[2,528,128]{2,1,0:T(8,128)(2,1)S(1)}, bf16[2,528,128]{2,1,0:T(8,128)(2,1)S(1)}, u32[]{:S(2)}, u32[]{:S(2)}) collective-permute-start(bf16[2,528,128]{2,1,0:T(8,128)(2,1)S(1)} %collective-permute-done.1.rest_1_), channel_id=1, source_target_pairs={{0,8},{8,0},{16,24},{24,16},{1,9},{9,1},{17,25},{25,17},{2,10},{10... | collective-permute-start | bytes 811016 | tf_op jit(solution)/shard_map/ppermute | solution.py:417
  78.1 3.8 %collective-permute-start.25 = (bf16[1,784,128]{2,1,0:T(8,128)(2,1)S(1)}, bf16[1,784,128]{2,1,0:T(8,128)(2,1)S(1)}, u32[]{:S(2)}, u32[]{:S(2)}) collective-permute-start(bf16[1,784,128]{2,1,0:T(8,128)(2,1)S(1)} %shard_map.42.rest_0_), channel_id=1, source_target_pairs={{0,8},{8,0},{16,24},{24,16},{1,9},{9,1},{17,25},{25,17},{2,10},{10... | collective-permute-start | bytes 602120 | tf_op jit(solution)/shard_map/ppermute | solution.py:417
  78.6 3.3 %collective-permute-start.26 = (bf16[1,784,128]{2,1,0:T(8,128)(2,1)S(1)}, bf16[1,784,128]{2,1,0:T(8,128)(2,1)S(1)}, u32[]{:S(2)}, u32[]{:S(2)}) collective-permute-start(bf16[1,784,128]{2,1,0:T(8,128)(2,1)S(1)} %collective-permute-done.24.rest_1_), channel_id=1, source_target_pairs={{0,8},{8,0},{16,24},{24,16},{1,9},{9,1},{17,25},{25,17},{2,10},{10... | collective-permute-start | bytes 602120 | tf_op jit(solution)/shard_map/ppermute | solution.py:417

commit v3 on v0

v3 whole, which is shorter than its diff:
```python
import functools
import math

import jax
import jax.numpy as jnp
from jax import lax
from jax.experimental import pallas as pl
from jax.experimental.pallas import tpu as pltpu
from jax.sharding import PartitionSpec as P

ITERS = 3
STEP = 0.2
SHRINK = 0.05

SMEM = pl.BlockSpec(memory_space=pltpu.SMEM)
VMEM = pl.BlockSpec(memory_space=pltpu.VMEM)


def dot_nt(a, b):
    return lax.dot_general(a, b, (((1,), (1,)), ((), ())), preferred_element_type=jnp.float32)


def dot_nn(a, b):
    return lax.dot_general(a, b, (((1,), (0,)), ((), ())), preferred_element_type=jnp.float32)


class Pattern:
    def __init__(self, table, block_rows, slots):
        self.table = table
        self.block_rows = block_rows
        self.slots = slots

    def link(self, place):
        return self.table[0, place], self.table[1, place]

    def sent(self, peer):
        return self.table[2, peer], self.table[3, peer]

    def source(self, j, k):
        return self.table[4, j * self.slots + k]

    def peer(self, j, k):
        return self.table[5, j * self.slots + k]

    def mate(self, j, k):
        return self.table[6, j * self.slots + k], self.table[7, j * self.slots + k]

    def known(self, source, place):
        return (source >= 0) & (source - self.block_rows <= place)


def find(cb_ref, block_rows, rounds, c):
    me = lax.axis_index("feat")
    safe = jnp.maximum(c, 0)
    holder = lax.div(safe, block_rows)
    place = lax.bitwise_xor(holder, me) if rounds else holder
    return c >= 0, (c >= 0) & (holder == me), lax.rem(safe, block_rows), holder, place


def pattern_kernel(rounds, peers, cb_ref, table_ref):
    block_rows, slots = cb_ref.shape
    me = lax.axis_index("feat")
    for p in range(peers):
        table_ref[0, p] = -1
        table_ref[1, p] = -1
        table_ref[2, p] = 0
        table_ref[3, p] = slots

    @pl.loop(0, block_rows)
    def _(j):
        for k in range(slots):
            filled, own, b, holder, place = find(cb_ref, block_rows, rounds, cb_ref[j, k])
            m = jnp.int32(0)
            for other in range(1, slots):
                m = jnp.where(cb_ref[b, other] == me * block_rows + j, other, m)
            i = j * slots + k
            table_ref[4, i] = jnp.where(filled, jnp.where(own, b, block_rows + place), -1)
            table_ref[5, i] = jnp.where(filled & jnp.logical_not(own), holder, me)
            table_ref[6, i] = jnp.where(own, b, 0)
            table_ref[7, i] = jnp.where(own, m, slots)

            @pl.when(filled & jnp.logical_not(own))
            def _(k=k, holder=holder, place=place):
                table_ref[0, place] = j
                table_ref[1, place] = k
                table_ref[2, holder] = j
                table_ref[3, holder] = k


def aligned(index, block):
    return pl.ds(pl.multiple_of(index * block, block), block)


def span(k, block):
    return slice(k * block, (k + 1) * block)


def pack_kernel(rounds, cb_ref, x_ref, own_ref, *rest):
    *send_refs, row_ref = rest
    block_rows, block, _ = own_ref.shape
    peers = row_ref.shape[0]
    for p in range(peers):
        row_ref[p] = 0

    @pl.loop(0, block_rows)
    def _(j):
        for k in range(1, cb_ref.shape[1]):
            filled, own, _, _, place = find(cb_ref, block_rows, rounds, cb_ref[j, k])

            @pl.when(filled & jnp.logical_not(own))
            def _(place=place):
                row_ref[place] = j

    for b in range(block_rows):
        own_ref[b] = x_ref[:, span(b, block)].T
    if rounds:
        for r, send_ref in enumerate(send_refs, 1):
            send_ref[...] = own_ref[row_ref[r]]
    else:
        (send_ref,) = send_refs

        @pl.loop(0, peers)
        def _(p):
            send_ref[p] = own_ref[row_ref[p]]


def eye_of(block):
    return lax.broadcasted_iota(jnp.int32, (block, block), 0) == lax.broadcasted_iota(
        jnp.int32, (block, block), 1
    )


def low_diagonal(value, high):
    rest = value - high.astype(jnp.float32)
    return jnp.sum(jnp.where(eye_of(value.shape[0]), rest, 0.0), axis=0, keepdims=True)


def put_low(out_ref, i, value, high):
    low = jnp.broadcast_to(low_diagonal(value, high), (16, value.shape[1]))
    out_ref[i, out_ref.shape[1] - 16 :] = low.astype(jnp.bfloat16)


def own_pairs(block_rows):
    pairs = [(a, b) for a in range(block_rows) for b in range(a, block_rows)]
    return list(zip(pairs[::2], pairs[1::2]))


def own_gram_kernel(mine_ref, other_ref, out_ref):
    core = lax.rem(lax.axis_index("samp"), 2)
    block = mine_ref.shape[1]
    for i, ((a, b), (c, d)) in enumerate(own_pairs(mine_ref.shape[0])):
        x, y = jnp.where(core == 0, a, c), jnp.where(core == 0, b, d)
        value = dot_nt(mine_ref[x], mine_ref[y]) + dot_nt(other_ref[x], other_ref[y])
        high = value.astype(jnp.bfloat16)
        out_ref[i, :block] = high
        put_low(out_ref, i, value, high)


def slot_at(k, position):
    return k if position == 0 else jnp.where(k == position, 0, position)


def gram_kernel(rounds, first, last, table_ref, mine_ref, other_ref, *rest):
    *arrived_refs, out_ref, beside_ref = rest
    block_rows, block, samples = mine_ref.shape
    slots = 2 * (beside_ref.shape[1] // block)
    core = lax.rem(lax.axis_index("samp"), 2)
    here = Pattern(table_ref, block_rows, slots)
    count = len(arrived_refs) // 2

    def arrival(q):
        if rounds:
            return arrived_refs[q - 1][...], arrived_refs[count + q - 1][...]
        return arrived_refs[0][q], arrived_refs[1][q]

    def body(p):
        row, k = here.link(p)

        @pl.when(row >= 0)
        def _():
            for i in range(slots // 2):
                l = jnp.where(core == 0, slot_at(k, 2 * i), slot_at(k, 2 * i + 1))
                source = here.source(row, l)
                at = span(i, block)
                near = jnp.clip(source, 0, block_rows - 1)
                beside_ref[0, at] = mine_ref[near]
                beside_ref[1, at] = other_ref[near]

                def from_arrival(q, at=at, source=source):
                    @pl.when(source == block_rows + q)
                    def _():
                        beside_ref[0, at], beside_ref[1, at] = arrival(q)

                if rounds:
                    for q in range(1, p + 1):
                        from_arrival(q)
                else:

                    @pl.when((source >= block_rows) & (source <= block_rows + p))
                    def _(at=at, source=source):
                        beside_ref[0, at], beside_ref[1, at] = arrival(source - block_rows)

            mine, other = arrival(p)
            value = dot_nt(beside_ref[0], mine) + dot_nt(beside_ref[1], other)
            high = value.astype(jnp.bfloat16)
            out_ref[p - first, : slots // 2 * block] = high
            put_low(out_ref, p - first, value[:block], high[:block])

    if rounds:
        for p in range(first, last):
            body(p)
    else:
        pl.loop(first, last)(body)


def read_part(parts, mine, index):
    half = len(parts) // 2
    terms = [
        jnp.where(mine, a[index], b[index]).astype(jnp.float32)
        for a, b in zip(parts[:half], parts[half:])
    ]
    while len(terms) > 1:
        terms = [a + b for a, b in zip(terms[::2], terms[1::2])]
    return terms[0]


def place_arrivals(here, first, last, parts, gram_ref, low_ref):
    block = parts[0].shape[2]
    slots = here.slots
    core = lax.rem(lax.axis_index("samp"), 2)

    @pl.loop(first, last)
    def _(p):
        row, k = here.link(p)

        @pl.when(row >= 0)
        def _():
            i = p - first
            for position in range(slots):
                l = slot_at(k, position)
                mine = core == position % 2
                value = read_part(parts, mine, (i, span(position // 2, block)))
                value = jnp.where(here.known(here.source(row, l), p), value, 0.0)
                high = value.astype(jnp.bfloat16)
                gram_ref[row, aligned(l, block), aligned(k, block)] = high
                if position:
                    gram_ref[row, aligned(k, block), aligned(l, block)] = high.T
                else:
                    lows = read_part(parts, mine, (i, pl.ds(slots // 2 * block, 1)))
                    low_ref[row, pl.ds(k, 1)] = low_diagonal(value, high) + lows


def gather_own_kernel(slots, table_ref, *rest):
    *parts, gram_ref, low_ref, sum_ref, row_ref = rest
    block_rows = gram_ref.shape[0]
    block = parts[0].shape[2]
    core = lax.rem(lax.axis_index("samp"), 2)
    here = Pattern(table_ref, block_rows, slots)
    sum_ref[block_rows] = jnp.zeros(sum_ref.shape[1:], sum_ref.dtype)
    row_ref[...] = jnp.zeros(row_ref.shape, row_ref.dtype)
    low_ref[...] = jnp.zeros(low_ref.shape, low_ref.dtype)
    for a in range(block_rows):
        sum_ref[a, block_rows] = jnp.zeros((block, block), sum_ref.dtype)
    for i, two in enumerate(own_pairs(block_rows)):
        for maker, (a, b) in enumerate(two):
            value = read_part(parts, core == maker, (i, slice(0, block)))
            high = value.astype(jnp.bfloat16)
            sum_ref[a, b] = high
            if a == b:
                lows = read_part(parts, core == maker, (i, slice(block, block + 1)))
                row_ref[a : a + 1] = low_diagonal(value, high) + lows
            else:
                sum_ref[b, a] = high.T

    @pl.loop(0, block_rows)
    def _(j):
        sources = [here.source(j, k) for k in range(slots)]
        rows = [
            jnp.where((x >= 0) & (x < block_rows), x, block_rows) for x in sources
        ]
        for k, a in enumerate(rows):
            low_ref[j, k : k + 1] = row_ref[pl.ds(a, 1)]
            for l, b in enumerate(rows):
                gram_ref[j, span(k, block), span(l, block)] = sum_ref[a, b]


def gather_kernel(groups, ways, slots, table_ref, gram_in_ref, low_in_ref, *rest):
    *parts, gram_ref, low_ref, sem = rest
    copy = pltpu.make_async_copy(gram_in_ref, gram_ref, sem)
    copy.start()
    low_ref[...] = low_in_ref[...]
    here = Pattern(table_ref, gram_ref.shape[0], slots)
    copy.wait()
    for g, (first, last) in enumerate(groups):
        at = slice(2 * ways * g, 2 * ways * (g + 1))
        place_arrivals(here, first, last, parts[at], gram_ref, low_ref)


def multiply_and_step(here, scale, w_ref, gram_ref, low_ref, v_ref, next_ref, out_ref):
    block_rows, slots, block, _ = next_ref.shape
    v_ref[:, :, slots * block :] = jnp.zeros((block_rows, block, block), jnp.float32)

    @pl.loop(0, block_rows)
    def _(j):
        value = dot_nn(w_ref[j], gram_ref[j])
        for k in range(slots):
            at = span(k, block)
            low = w_ref[j, :, at].astype(jnp.float32) * low_ref[j, k : k + 1]
            v_ref[j, :, at] = value[:, at] + low

    for p in range(out_ref.shape[0]) if out_ref.shape[0] <= 8 else ():
        row, column = here.sent(p)
        out_ref[p] = v_ref[row, :, aligned(column, block)].astype(out_ref.dtype).T
    if out_ref.shape[0] > 8:

        @pl.loop(0, out_ref.shape[0])
        def _(p):
            row, column = here.sent(p)
            out_ref[p] = v_ref[row, :, aligned(column, block)].astype(out_ref.dtype).T

    @pl.loop(0, block_rows)
    def _(j):
        for k in range(slots):
            row, column = here.mate(j, k)
            mirrored = v_ref[row, :, aligned(column, block)].T
            next_ref[j, k] = next_ref[j, k] - scale * (v_ref[j, :, span(k, block)] + mirrored)


def first_kernel(group, ways, scale, table_ref, prec_ref, gram_in_ref, low_in_ref, *rest):
    parts, rest = rest[: 2 * ways], rest[2 * ways :]
    gram_ref, low_ref, next_ref, out_ref, w_ref, v_ref, sem = rest
    copy = pltpu.make_async_copy(gram_in_ref, gram_ref, sem)
    copy.start()
    low_ref[...] = low_in_ref[...]
    block_rows, slots, block, _ = prec_ref.shape
    here = Pattern(table_ref, block_rows, slots)

    @pl.loop(0, block_rows)
    def _(j):
        for k in range(slots):
            value = jnp.where(here.source(j, k) >= 0, prec_ref[j, k], 0.0)
            next_ref[j, k] = value
            w_ref[j, :, span(k, block)] = value.astype(jnp.bfloat16)

    copy.wait()
    place_arrivals(here, *group, parts, gram_ref, low_ref)
    multiply_and_step(here, scale, w_ref, gram_ref, low_ref, v_ref, next_ref, out_ref)


def soft(m):
    return m - jnp.clip(m, -SHRINK, SHRINK)


def next_omega(here, j, scale, stepped_ref, in_ref, put):
    block = stepped_ref.shape[2]
    for k in range(here.slots):
        m = stepped_ref[j, k]
        if k == 0:
            root = 0.5 * (m + jnp.sqrt(m * m + 4.0 * STEP))
            put(k, jnp.where(eye_of(block), root, soft(m)))
        else:
            arrived = in_ref[here.peer(j, k)].astype(jnp.float32)
            put(k, soft(m - scale * arrived))


def middle_kernel(scale, table_ref, stepped_ref, in_ref, gram_ref, low_ref, next_ref, out_ref, w_ref, v_ref):
    block_rows, slots, block, _ = stepped_ref.shape
    here = Pattern(table_ref, block_rows, slots)

    @pl.loop(0, block_rows)
    def _(j):
        def put(k, value):
            next_ref[j, k] = value
            w_ref[j, :, span(k, block)] = value.astype(jnp.bfloat16)

        next_omega(here, j, scale, stepped_ref, in_ref, put)

    multiply_and_step(here, scale, w_ref, gram_ref, low_ref, v_ref, next_ref, out_ref)


def last_kernel(scale, table_ref, stepped_ref, in_ref, next_ref):
    block_rows, slots, block, _ = stepped_ref.shape
    here = Pattern(table_ref, block_rows, slots)

    @pl.loop(0, block_rows)
    def _(j):
        def put(k, value):
            next_ref[j, k] = value

        next_omega(here, j, scale, stepped_ref, in_ref, put)


def call(kernel, inputs, outs, scratch, smem=1, left=(), sems=(), out_space=VMEM):
    arrays = (*inputs, *outs, *scratch)
    size = sum(math.prod(x.shape) * jnp.dtype(x.dtype).itemsize for x in arrays)
    specs = [SMEM] * smem + [VMEM] * (len(inputs) - smem)
    for i in left:
        specs[i] = pl.BlockSpec(memory_space=pl.ANY)
    return pl.pallas_call(
        kernel,
        out_shape=outs,
        in_specs=specs,
        out_specs=[out_space] * len(outs),
        scratch_shapes=[*scratch, *sems],
        compiler_params=pltpu.CompilerParams(vmem_limit_bytes=size + (6 << 20)),
        cost_estimate=pl.CostEstimate(flops=1, bytes_accessed=1, transcendentals=0),
    )(*inputs)


def swap(x, bit):
    count = lax.axis_size("samp")
    return lax.ppermute(x, "samp", [(i, i ^ bit) for i in range(count)])


def from_ys(x):
    return [x] + [swap(x, bit) for bit in range(2, lax.axis_size("samp"), 2)]


def both_cores(parts):
    return (*parts, *(swap(x, 1) for x in parts))


def after(x, *earlier):
    return lax.optimization_barrier((x, *earlier))[0]


def fenced(col_blocks, part, *args):
    def nothing(*args):
        return jax.tree.map(lambda x: jnp.zeros(x.shape, x.dtype), jax.eval_shape(part, *args))

    return lax.cond(col_blocks[0, 0] >= 0, part, nothing, *args)


def local(samples, precision, col_blocks):
    row_count = samples.shape[0]
    block_rows, slots, block, _ = precision.shape
    peers = lax.axis_size("feat")
    ways = lax.axis_size("samp") // 2
    scale = 0.5 * STEP / (row_count * lax.axis_size("samp"))
    rounds = peers == 8 and ways == 2
    groups = [(1, 6), (6, 8)] if rounds else [(0, peers)]

    def shape(dims, dtype):
        return jax.ShapeDtypeStruct(dims, dtype)

    bf16, f32 = samples.dtype, jnp.float32
    strip = (block, row_count)
    sem = pltpu.SemaphoreType.DMA(())
    sends = [shape(strip, bf16)] * (peers - 1) if rounds else [shape((peers, *strip), bf16)]
    own, *sends = call(
        functools.partial(pack_kernel, rounds),
        (col_blocks, samples),
        [shape((block_rows, *strip), bf16), *sends],
        [pltpu.SMEM((peers,), jnp.int32)],
    )

    def exchange(x, r):
        return lax.ppermute(x, "feat", [(i, i ^ r) for i in range(peers)])

    grams = [
        shape((block_rows, slots * block, slots * block), bf16),
        shape((block_rows, 8, block), f32),
    ]

    def pattern():
        width = max(peers, block_rows * slots)
        return call(
            functools.partial(pattern_kernel, rounds, peers),
            (col_blocks,),
            [shape((8, width), jnp.int32)],
            [],
            out_space=SMEM,
        )[0]

    def own_list(own, other):
        return call(
            own_gram_kernel,
            (own, other),
            [shape((block_rows * (block_rows + 1) // 4, block + 16, block), bf16)],
            [],
            smem=0,
        )[0]

    def arrival_list(first, last, table, own_pair, arrived, over):
        return call(
            functools.partial(gram_kernel, rounds, first, last),
            (table, *own_pair, *arrived, *over),
            [shape((last - first, slots // 2 * block + 16, block), bf16)],
            [pltpu.VMEM((2, slots // 2 * block, row_count), bf16)],
        )[0]

    def gather_own(table, *parts):
        return call(
            functools.partial(gather_own_kernel, slots),
            (table, *parts),
            grams,
            [
                pltpu.VMEM((block_rows + 1, block_rows + 1, block, block), bf16),
                pltpu.VMEM((8, block), f32),
            ],
        )

    def gather(table, gram, low, *lists):
        return call(
            functools.partial(gather_kernel, groups[:-1], ways, slots),
            (table, gram, low, *sum(lists, ())),
            grams,
            [],
            left=[1],
            sems=[sem],
        )

    def over_of(blocks, earlier):
        return [swap(after(x, earlier), 1) for x in blocks]

    if rounds:
        other = swap(own, 1)
        own_pair = (own, other)
        ready = [*sends[:2], after(sends[2], other), *sends[3:]]
        arrived = [exchange(ready[r - 1], r) for r in (1, 2, 3, 4, 5)]

        def begin(own, other):
            return own_list(own, other), pattern()

        step, table = fenced(col_blocks, begin, own, other)
        over = over_of(arrived, step)
        arrived += [exchange(after(sends[r - 1], arrived[r - 3]), r) for r in (6, 7)]

        def own_part(table, own_list, own_y):
            return gather_own(table, own_list, own_y, swap(own_list, 1), swap(own_y, 1))

        def most(table, own_pair, arrived, over, own_list):
            own_y = swap(own_list, 2)
            out = after(arrival_list(1, 6, table, own_pair, arrived, over), own_y)
            out_y, own_y = swap(out, 2), after(own_y, out)
            gram, low = fenced(col_blocks, own_part, table, own_list, own_y)
            out_core = swap(after(out, gram), 1)
            out_both = swap(after(out_y, gram), 1)
            return gram, low, (out, out_y, out_core, out_both)

        gram, low, *lists = fenced(col_blocks, most, table, own_pair, arrived[:5], over, step)
        over += over_of(arrived[5:], gram)
        step = arrival_list(6, 8, table, own_pair, arrived, over)
        gram, low = gather(table, after(gram, step), low, *lists)
        last_list = both_cores([step, after(from_ys(step)[1], gram)])
    else:
        other = swap(own, 1)
        table = pattern()
        arrived = lax.all_to_all(sends[0], "feat", 0, 0, tiled=True)
        gram, low = gather_own(table, *both_cores(from_ys(own_list(own, other))))
        last_list = both_cores(
            from_ys(arrival_list(0, peers, table, (own, other), [arrived], [swap(arrived, 1)]))
        )
    blocks = shape(precision.shape, f32)
    swapped = shape((peers, block, block), bf16)
    work = [
        pltpu.VMEM((block_rows, block, slots * block), bf16),
        pltpu.VMEM((block_rows, block, (slots + 1) * block), f32),
    ]
    gram, low, stepped, out = call(
        functools.partial(first_kernel, groups[-1], ways, scale),
        (table, precision, gram, low, *last_list),
        [*grams, blocks, swapped],
        work,
        left=[2],
        sems=[sem],
    )
    for iteration in range(ITERS):
        mirrored = lax.all_to_all(out, "feat", 0, 0, tiled=True)
        if iteration + 1 < ITERS:
            stepped, out = call(
                functools.partial(middle_kernel, scale),
                (table, stepped, mirrored, gram, low),
                [blocks, swapped],
                work,
            )
    (updated,) = call(functools.partial(last_kernel, scale), (table, stepped, mirrored), [blocks], [])
    return updated


def solution(mesh):
    return jax.shard_map(
        local,
        mesh=mesh,
        in_specs=(P("samp", "feat"), P("feat", None, None, None), P("feat", None)),
        out_specs=P("feat", None, None, None),
        check_vma=False,
    )
```

time: 334 us -> 124 us (0.37)
  waiting for transfers between devices: 183 us -> 26.1 us
  local copies, waits for them, and re-layouts: 47.3 us -> 3.68 us
  Pallas kernels: 0 us -> 34.2 us
  other arithmetic: 27.9 us -> 0 us
  matrix products: 22.7 us -> 0 us
  blocking collectives: 16.4 us -> 38.3 us
  between operations: 13.4 us -> 0.77 us
    all_to_all x4 -> x0, waiting for transfers between devices: 82.4 us -> none  [the longest x1 46.8 us: local(): lax.all_to_all(outgoing, 'feat', split_axis=1, concat_axis=1, tiled=True)]
    reduce_scatter x3 -> x0, waiting for transfers between devices: 80.7 us -> none  [local(): lax.psum_scatter(flat_term, 'samp', scatter_dimension=0, tiled=True)]
    all_to_all x0 -> x3, blocking collectives: none -> 38.3 us  [local(): mirrored = lax.all_to_all(out, 'feat', 0, 0, tiled=True)]
    pallas_call x0 -> x11, Pallas kernels: none -> 34.2 us  [call(): pl.pallas_call(kernel, out_shape=outs, in_specs=specs, out_specs=[out_spa...]
    gather x16 -> x0, local copies, waits for them, and re-layouts: 33.7 us -> none  [the longest x2 13.2 us: local(): stacked = jnp.take(joined, source_index, axis=1)]
    ppermute x0 -> x24, waiting for transfers between devices: none -> 26.1 us  [the longest x7 15 us: exchange(): return lax.ppermute(x, 'feat', [(i, i ^ r) for i in range(peers)])]
    dot_general x3 -> x0, matrix products: 22.7 us -> none  [local(): jnp.einsum('rla,rlkb->lkab', projected, stacked, preferred_element_type=j...]
    all_to_all x4 -> x0, starting transfers between devices: 22.1 us -> none  [the longest x3 14.7 us: local(): lax.all_to_all(mirror_outbound(flat_partial, send_slot, send_has), 'feat'...]
  transfers between devices with their start and end apart: 8 -> 24, of which waited for: 8 -> 11; matrix products, arithmetic and copies ran while one was open for 3% -> 2% of each run, Pallas kernels for 0% -> 15%
where the time goes in v3:
time: 124 us
  blocking collectives  38.3 us (31%)
  Pallas kernels  34.2 us (28%)
  waiting for transfers between devices  26.1 us (21%)
  starting transfers between devices  20.4 us (16%)
  local copies, waits for them, and re-layouts  3.68 us (3%)
    all_to_all x3, blocking collectives, local(): mirrored = lax.all_to_all(out, 'feat', 0, 0, tiled=True)  38.3 us
    pallas_call x11, Pallas kernels, call(): pl.pallas_call(kernel, out_shape=outs, in_specs=specs, out_specs=[out_spa...  34.2 us
    ppermute x7, waiting for transfers between devices, exchange(): return lax.ppermute(x, 'feat', [(i, i ^ r) for i in range(peers)])  15 us
    ppermute x7, starting transfers between devices, exchange(): return lax.ppermute(x, 'feat', [(i, i ^ r) for i in range(peers)])  13.3 us
    ppermute x17, waiting for transfers between devices, swap(): return lax.ppermute(x, 'samp', [(i, i ^ bit) for i in range(count)])  11.1 us
    ppermute x17, starting transfers between devices, swap(): return lax.ppermute(x, 'samp', [(i, i ^ bit) for i in range(count)])  7.05 us
  transfers between devices with their start and end apart: 24, of which 11 were waited for; matrix products, arithmetic and copies ran while one was open for 2% of the time, Pallas kernels for 15%

profile of v3, /device:TPU:0, one launch (start us, length us, event | category | flops | bytes accessed | tf_op | source)
XLA Modules:
  0.0 124.1 jit_solution(8339537549658670332)
XLA Ops:
  1.2 1.2 shard_map.37
  3.0 2.6 %collective-permute-start.7 = (bf16[128,1024]{1,0:T(8,128)(2,1)S(1)}, bf16[128,1024]{1,0:T(8,128)(2,1)S(1)}, u32[]{:S(2)}, u32[]{:S(2)}) collective-permute-start(bf16[128,1024]{1,0:T(8,128)(2,1)S(1)} %get-tuple-element.115), channel_id=1, source_target_pairs={{0,1},{1,0},{2,3},{3,2},{4,5},{5,4},{6,7},{7,6},{8,9},{9,8},{10,11... | collective-permute-start | bytes 786440 | tf_op jit(solution)/shard_map/ppermute | solution.py:458
  5.6 1.6 %collective-permute-start.8 = (bf16[128,1024]{1,0:T(8,128)(2,1)S(1)}, bf16[128,1024]{1,0:T(8,128)(2,1)S(1)}, u32[]{:S(2)}, u32[]{:S(2)}) collective-permute-start(bf16[128,1024]{1,0:T(8,128)(2,1)S(1)} %get-tuple-element.116), channel_id=1, source_target_pairs={{0,2},{1,3},{2,0},{3,1},{4,6},{5,7},{6,4},{7,5},{8,10},{9,11},{10,... | collective-permute-start | bytes 786440 | tf_op jit(solution)/shard_map/ppermute | solution.py:458
  7.1 2.6 %collective-permute-start.10 = (bf16[128,1024]{1,0:T(8,128)(2,1)S(1)}, bf16[128,1024]{1,0:T(8,128)(2,1)}, u32[]{:S(2)}, u32[]{:S(2)}) collective-permute-start(bf16[128,1024]{1,0:T(8,128)(2,1)S(1)} %get-tuple-element.119), channel_id=1, source_target_pairs={{0,4},{1,5},{2,6},{3,7},{4,0},{5,1},{6,2},{7,3},{8,12},{9,13},{10,... | collective-permute-start | bytes 786440 | tf_op jit(solution)/shard_map/ppermute | solution.py:458
  11.9 1.4 %collective-permute-start.9 = (bf16[128,1024]{1,0:T(8,128)(2,1)S(1)}, bf16[128,1024]{1,0:T(8,128)(2,1)}, u32[]{:S(2)}, u32[]{:S(2)}) collective-permute-start(bf16[128,1024]{1,0:T(8,128)(2,1)S(1)} %get-tuple-element.118), channel_id=1, source_target_pairs={{0,3},{1,2},{2,1},{3,0},{4,7},{5,6},{6,5},{7,4},{8,11},{9,10},{10,... | collective-permute-start | bytes 786440 | tf_op jit(solution)/shard_map/ppermute | solution.py:458
  13.3 4.6 %conditional.3 = (bf16[5,144,128]{2,1,0:T(8,128)(2,1)}, s32[8,24]{1,0:T(8,128)S(1)}) conditional(s32[]{:T(128)} %bitcast.1, () %tuple.44, (bf16[4,128,1024]{2,1,0:T(8,128)(2,1)S(1)}, bf16[4,128,1024]{2,1,0:T(8,128)(2,1)}, s32[4,6]{1,0:T(4,128)}) %tuple.45), branch_computations={%region_0.0_spmd, %region_1.0_spmd} | conditional | flops 2 | bytes 185110 | solution.py:431
  13.3 2.8 %branch_1_fun.4 = bf16[5,144,128]{2,1,0:T(8,128)(2,1)} custom-call(bf16[4,128,1024]{2,1,0:T(8,128)(2,1)S(1)} %get-tuple-element.47.mine_ref, bf16[4,128,1024]{2,1,0:T(8,128)(2,1)} %get-tuple-element.48.other_ref), custom_call_target="tpu_custom_call" | custom-call | flops 1 | bytes 1 | tf_op jit(solution)/shard_map/cond/branch_1_fun/pallas_call | solution.py:399
  16.1 1.9 %branch_1_fun.5 = s32[8,24]{1,0:T(8,128)S(1)} custom-call(s32[4,6]{1,0:T(4,128)} %get-tuple-element.49.cb_ref), custom_call_target="tpu_custom_call" | custom-call | flops 1 | bytes 1 | tf_op jit(solution)/shard_map/cond/branch_1_fun/pallas_call | solution.py:399
  18.1 2.1 %collective-permute-done.8.rest_1_ = bf16[128,1024]{1,0:T(8,128)(2,1)S(1)} collective-permute-done((bf16[128,1024]{1,0:T(8,128)(2,1)S(1)}, bf16[128,1024]{1,0:T(8,128)(2,1)S(1)}, u32[]{:S(2)}, u32[]{:S(2)}) %collective-permute-start.8) | collective-permute-done | bytes 262176 | tf_op jit(solution)/shard_map/ppermute | solution.py:458
  20.2 12.9 %collective-permute-done.11.rest_4_ = bf16[128,1024]{1,0:T(8,128)(2,1)} collective-permute-done((bf16[128,1024]{1,0:T(8,128)(2,1)S(1)}, bf16[128,1024]{1,0:T(8,128)(2,1)}, u32[]{:S(2)}, u32[]{:S(2)}) %collective-permute-start.11) | collective-permute-done | bytes 262176 | tf_op jit(solution)/shard_map/ppermute | solution.py:458
  33.6 3.5 %collective-permute-start.18 = (bf16[128,1024]{1,0:T(8,128)(2,1)S(1)}, bf16[128,1024]{1,0:T(8,128)(2,1)S(1)}, u32[]{:S(2)}, u32[]{:S(2)}) collective-permute-start(bf16[128,1024]{1,0:T(8,128)(2,1)S(1)} %get-tuple-element.130), channel_id=1, source_target_pairs={{0,7},{1,6},{2,5},{3,4},{4,3},{5,2},{6,1},{7,0},{8,15},{9,14},{10,... | collective-permute-start | bytes 786440 | tf_op jit(solution)/shard_map/ppermute | solution.py:458
  37.1 1.4 %collective-permute-start.17 = (bf16[128,1024]{1,0:T(8,128)(2,1)S(1)}, bf16[128,1024]{1,0:T(8,128)(2,1)S(1)}, u32[]{:S(2)}, u32[]{:S(2)}) collective-permute-start(bf16[128,1024]{1,0:T(8,128)(2,1)S(1)} %get-tuple-element.128), channel_id=1, source_target_pairs={{0,6},{1,7},{2,4},{3,5},{4,2},{5,3},{6,0},{7,1},{8,14},{9,15},{10,... | collective-permute-start | bytes 786440 | tf_op jit(solution)/shard_map/ppermute | solution.py:458
  38.5 21.9 %conditional.4 = (bf16[4,768,768]{2,1,0:T(8,128)(2,1)}, f32[4,8,128]{2,1,0:T(8,128)}, bf16[5,400,128]{2,1,0:T(8,128)(2,1)}, bf16[5,400,128]{2,1,0:T(8,128)(2,1)}...) conditional(s32[]{:T(128)} %bitcast.1, () %tuple.46, (s32[4,6]{1,0:T(4,128)}, ...), branch_computations={%region_2.0_spmd, %region_3.0_spmd} | conditional | flops 4 | bytes 11616541 | solution.py:431
  38.5 1.6 %collective-permute-start.2 = (bf16[5,144,128]{2,1,0:T(8,128)(2,1)}, bf16[5,144,128]{2,1,0:T(8,128)(2,1)S(1)}, u32[]{:S(2)}, u32[]{:S(2)}) collective-permute-start(bf16[5,144,128]{2,1,0:T(8,128)(2,1)} %get-tuple-element.54), channel_id=1, source_target_pairs={{0,16},{8,24},{16,0},{24,8},{1,17},{9,25},{17,1},{25,9},{2,18},{10... | collective-permute-start | bytes 552968 | tf_op jit(solution)/shard_map/cond/branch_1_fun/ppermute | solution.py:412
  40.1 4.7 %branch_1_fun.7 = bf16[5,400,128]{2,1,0:T(8,128)(2,1)} custom-call(s32[8,24]{1,0:T(8,128)S(1)} %get-tuple-element.55.table_ref, bf16[4,128,1024]{2,1,0:T(8,128)(2,1)S(1)} %get-tuple-element.56.mine_ref, bf16[4,128,1024]{2,1,0:T(8,128)(2,1)} %get-tuple-element.57.other_ref, bf16[128,1024]{1,0:T(8,128)(2,1)S(1)} %get-tuple-element.58.rest_0_, ...), custom_call_target="tpu_custom_call" | custom-call | flops 1 | bytes 1 | tf_op jit(solution)/shard_map/cond/branch_1_fun/pallas_call | solution.py:399
  45.2 1.5 %collective-permute-start.3 = (bf16[5,400,128]{2,1,0:T(8,128)(2,1)}, bf16[5,400,128]{2,1,0:T(8,128)(2,1)}, u32[]{:S(2)}, u32[]{:S(2)}) collective-permute-start(bf16[5,400,128]{2,1,0:T(8,128)(2,1)} %branch_1_fun.7), channel_id=1, source_target_pairs={{0,16},{8,24},{16,0},{24,8},{1,17},{9,25},{17,1},{25,9},{2,18},{10... | collective-permute-start | bytes 1536008 | tf_op jit(solution)/shard_map/cond/branch_1_fun/ppermute | solution.py:412
  46.7 1.3 %slice.1 = s32[1,1]{1,0:T(1,128)} slice(s32[4,6]{1,0:T(4,128)} %get-tuple-element.53), slice={[0:1], [0:1]} | slice | bytes 8 | tf_op jit(solution)/shard_map/cond/branch_1_fun/slice | solution.py:431
  48.6 6.1 %conditional = ((bf16[4,768,768]{2,1,0:T(8,128)(2,1)}, f32[4,8,128]{2,1,0:T(8,128)})) conditional(s32[]{:T(128)} %bitcast, () %tuple.21, (bf16[5,144,128]{2,1,0:T(8,128)(2,1)}, bf16[5,144,128]{2,1,0:T(8,128)(2,1)S(1)}, s32[8,24]{1,0:T(8,128)S(1)}) %tuple.24), branch_computations={%region_4.0_spmd, %region_5.0_spmd} | conditional | flops 1 | bytes 4735006 | solution.py:431
  50.4 4.3 %branch_1_fun.6 = (bf16[4,768,768]{2,1,0:T(8,128)(2,1)}, f32[4,8,128]{2,1,0:T(8,128)}) custom-call(s32[8,24]{1,0:T(8,128)S(1)} %get-tuple-element.50.table_ref, bf16[5,144,128]{2,1,0:T(8,128)(2,1)} %get-tuple-element.51.rest_0_, bf16[5,144,128]{2,1,0:T(8,128)(2,1)S(1)} %get-tuple-element.52.rest_1_, bf16[5,144,128]{2,1,0:T(8,128)(2,1)S(1)} %collective-permute-done.rest_2_, ...), custom_call_target="tpu_custom_call" | custom-call | flops 1 | bytes 1 | tf_op jit(solution)/shard_map/cond/branch_1_fun/cond/branch_1_fun/pallas_call | solution.py:399
  54.9 3.2 %collective-permute-done.3 = bf16[5,400,128]{2,1,0:T(8,128)(2,1)} collective-permute-done((bf16[5,400,128]{2,1,0:T(8,128)(2,1)}, bf16[5,400,128]{2,1,0:T(8,128)(2,1)}, u32[]{:S(2)}, u32[]{:S(2)}) %collective-permute-start.3) | collective-permute-done | bytes 512032 | tf_op jit(solution)/shard_map/cond/branch_1_fun/ppermute | solution.py:412
  58.2 2.2 %collective-permute-done.5 = bf16[5,400,128]{2,1,0:T(8,128)(2,1)} collective-permute-done((bf16[5,400,128]{2,1,0:T(8,128)(2,1)}, bf16[5,400,128]{2,1,0:T(8,128)(2,1)}, u32[]{:S(2)}, u32[]{:S(2)}) %collective-permute-start.5) | collective-permute-done | bytes 512032 | tf_op jit(solution)/shard_map/cond/branch_1_fun/ppermute | solution.py:412
  62.3 2.6 %shard_map.38.rest_0_ = bf16[2,400,128]{2,1,0:T(8,128)(2,1)S(1)} custom-call(s32[8,24]{1,0:T(8,128)S(1)} %get-tuple-element.113.table_ref, bf16[4,128,1024]{2,1,0:T(8,128)(2,1)S(1)} %get-tuple-element.112.mine_ref, bf16[4,128,1024]{2,1,0:T(8,128)(2,1)} %collective-permute-done.6.other_ref, bf16[128,1024]{1,0:T(8,128)(2,1)S(1)} %collective-permute-done.7.rest_0_, ...), custom_call_target="tpu_custom_call" | custom-call | flops 1 | bytes 1 | tf_op jit(solution)/shard_map/pallas_call | solution.py:399
  65.0 1.5 %collective-permute-start.21 = (bf16[2,400,128]{2,1,0:T(8,128)(2,1)S(1)}, bf16[2,400,128]{2,1,0:T(8,128)(2,1)S(1)}, u32[]{:S(2)}, u32[]{:S(2)}) collective-permute-start(bf16[2,400,128]{2,1,0:T(8,128)(2,1)S(1)} %shard_map.38.rest_0_), channel_id=1, source_target_pairs={{0,16},{8,24},{16,0},{24,8},{1,17},{9,25},{17,1},{25,9},{2,18},{10... | collective-permute-start | bytes 614408 | tf_op jit(solution)/shard_map/ppermute | solution.py:412
  66.5 4.4 %shard_map.39 = (bf16[4,768,768]{2,1,0:T(8,128)(2,1)S(1)}, f32[4,8,128]{2,1,0:T(8,128)S(1)}) custom-call(s32[8,24]{1,0:T(8,128)S(1)} %get-tuple-element.113.table_ref, bf16[4,768,768]{2,1,0:T(8,128)(2,1)} %get-tuple-element.133.gram_in_ref, f32[4,8,128]{2,1,0:T(8,128)} %get-tuple-element.134.low_in_ref, bf16[5,400,128]{2,1,0:T(8,128)(2,1)} %get-tuple-element.135.rest_0_, ...), custom_call_target="tpu_custom_call" | custom-call | flops 1 | bytes 1 | tf_op jit(solution)/shard_map/pallas_call | solution.py:399
  72.1 1.4 %collective-permute-done.23.rest_3_ = bf16[2,400,128]{2,1,0:T(8,128)(2,1)S(1)} collective-permute-done((bf16[2,400,128]{2,1,0:T(8,128)(2,1)S(1)}, bf16[2,400,128]{2,1,0:T(8,128)(2,1)S(1)}, u32[]{:S(2)}, u32[]{:S(2)}) %collective-permute-start.23) | collective-permute-done | bytes 204832 | tf_op jit(solution)/shard_map/ppermute | solution.py:412
  73.6 3.6 %shard_map.40 = (bf16[4,768,768]{2,1,0:T(8,128)(2,1)S(1)}, f32[4,8,128]{2,1,0:T(8,128)S(1)}, f32[4,6,128,128]{3,2,1,0:T(8,128)S(1)}, bf16[8,128,128]{2,1,0:T(8,128)(2,1)S(1)}) custom-call(s32[8,24]{1,0:T(8,128)S(1)} %get-tuple-element.113.table_ref, f32[4,6,128,128]{3,2,1,0:T(8,128)S(1)} %copy-done, bf16[4,768,768]{2,1,0:T(8,128)(2,1)S(1)} %get-tuple-element.139.gram_in_ref, ...), custom_call_target="tpu_custom_call" | custom-call | flops 1 | bytes 1 | tf_op jit(solution)/shard_map/pallas_call | solution.py:399
  77.2 14.5 %all_to_all.15.in_ref = bf16[8,128,128]{2,1,0:T(8,128)(2,1)S(1)} all-to-all(bf16[8,128,128]{2,1,0:T(8,128)(2,1)S(1)} %get-tuple-element.143), channel_id=1, replica_groups=mesh['samp'=4,'feat'=8] {'feat'}, dimensions={0} | all-to-all | bytes 524288 | tf_op jit(solution)/shard_map/all_to_all | solution.py:569
  91.6 3.2 %shard_map.41 = (f32[4,6,128,128]{3,2,1,0:T(8,128)S(1)}, bf16[8,128,128]{2,1,0:T(8,128)(2,1)S(1)}) custom-call(s32[8,24]{1,0:T(8,128)S(1)} %get-tuple-element.113.table_ref, f32[4,6,128,128]{3,2,1,0:T(8,128)S(1)} %get-tuple-element.142.stepped_ref, bf16[8,128,128]{2,1,0:T(8,128)(2,1)S(1)} %all_to_all.15.in_ref, ...), custom_call_target="tpu_custom_call" | custom-call | flops 1 | bytes 1 | tf_op jit(solution)/shard_map/pallas_call | solution.py:399
  94.9 12.0 %all_to_all.16.in_ref = bf16[8,128,128]{2,1,0:T(8,128)(2,1)S(1)} all-to-all(bf16[8,128,128]{2,1,0:T(8,128)(2,1)S(1)} %get-tuple-element.147), channel_id=1, replica_groups=mesh['samp'=4,'feat'=8] {'feat'}, dimensions={0} | all-to-all | bytes 524288 | tf_op jit(solution)/shard_map/all_to_all | solution.py:569
  106.8 3.3 %shard_map.42 = (f32[4,6,128,128]{3,2,1,0:T(8,128)S(1)}, bf16[8,128,128]{2,1,0:T(8,128)(2,1)S(1)}) custom-call(s32[8,24]{1,0:T(8,128)S(1)} %get-tuple-element.113.table_ref, f32[4,6,128,128]{3,2,1,0:T(8,128)S(1)} %get-tuple-element.146.stepped_ref, bf16[8,128,128]{2,1,0:T(8,128)(2,1)S(1)} %all_to_all.16.in_ref, ...), custom_call_target="tpu_custom_call" | custom-call | flops 1 | bytes 1 | tf_op jit(solution)/shard_map/pallas_call | solution.py:399
  110.1 11.9 %all_to_all.17.in_ref = bf16[8,128,128]{2,1,0:T(8,128)(2,1)S(1)} all-to-all(bf16[8,128,128]{2,1,0:T(8,128)(2,1)S(1)} %get-tuple-element.149), channel_id=1, replica_groups=mesh['samp'=4,'feat'=8] {'feat'}, dimensions={0} | all-to-all | bytes 524288 | tf_op jit(solution)/shard_map/all_to_all | solution.py:569
  122.0 2.1 %shard_map.43 = f32[4,6,128,128]{3,2,1,0:T(8,128)} custom-call(s32[8,24]{1,0:T(8,128)S(1)} %get-tuple-element.113.table_ref, f32[4,6,128,128]{3,2,1,0:T(8,128)S(1)} %get-tuple-element.148.stepped_ref, bf16[8,128,128]{2,1,0:T(8,128)(2,1)S(1)} %all_to_all.17.in_ref), custom_call_target="tpu_custom_call" | custom-call | flops 1 | bytes 1 | tf_op jit(solution)/shard_map/pallas_call | solution.py:399
  (39 shorter events, 9.4 us)
Async XLA Ops:
  0.0 1.2 copy-start.1
  2.5 9.4 %collective-permute-start.6 = (bf16[4,128,1024]{2,1,0:T(8,128)(2,1)S(1)}, bf16[4,128,1024]{2,1,0:T(8,128)(2,1)}, u32[]{:S(2)}, u32[]{:S(2)}) collective-permute-start(bf16[4,128,1024]{2,1,0:T(8,128)(2,1)S(1)} %get-tuple-element.112.mine_ref), channel_id=1, source_target_pairs={{0,8},{8,0},{16,24},{24,16},{1,9},{9,1},{17,25},{25,17},{2,10},{10... | collective-permute-start | bytes 3145736 | tf_op jit(solution)/shard_map/ppermute | solution.py:412
  3.0 15.0 %collective-permute-start.7 = (bf16[128,1024]{1,0:T(8,128)(2,1)S(1)}, bf16[128,1024]{1,0:T(8,128)(2,1)S(1)}, u32[]{:S(2)}, u32[]{:S(2)}) collective-permute-start(bf16[128,1024]{1,0:T(8,128)(2,1)S(1)} %get-tuple-element.115), channel_id=1, source_target_pairs={{0,1},{1,0},{2,3},{3,2},{4,5},{5,4},{6,7},{7,6},{8,9},{9,8},{10,11... | collective-permute-start | bytes 786440 | tf_op jit(solution)/shard_map/ppermute | solution.py:458
  5.6 14.7 %collective-permute-start.8 = (bf16[128,1024]{1,0:T(8,128)(2,1)S(1)}, bf16[128,1024]{1,0:T(8,128)(2,1)S(1)}, u32[]{:S(2)}, u32[]{:S(2)}) collective-permute-start(bf16[128,1024]{1,0:T(8,128)(2,1)S(1)} %get-tuple-element.116), channel_id=1, source_target_pairs={{0,2},{1,3},{2,0},{3,1},{4,6},{5,7},{6,4},{7,5},{8,10},{9,11},{10,... | collective-permute-start | bytes 786440 | tf_op jit(solution)/shard_map/ppermute | solution.py:458
  7.1 26.0 %collective-permute-start.10 = (bf16[128,1024]{1,0:T(8,128)(2,1)S(1)}, bf16[128,1024]{1,0:T(8,128)(2,1)}, u32[]{:S(2)}, u32[]{:S(2)}) collective-permute-start(bf16[128,1024]{1,0:T(8,128)(2,1)S(1)} %get-tuple-element.119), channel_id=1, source_target_pairs={{0,4},{1,5},{2,6},{3,7},{4,0},{5,1},{6,2},{7,3},{8,12},{9,13},{10,... | collective-permute-start | bytes 786440 | tf_op jit(solution)/shard_map/ppermute | solution.py:458
  9.7 23.4 %collective-permute-start.11 = (bf16[128,1024]{1,0:T(8,128)(2,1)S(1)}, bf16[128,1024]{1,0:T(8,128)(2,1)}, u32[]{:S(2)}, u32[]{:S(2)}) collective-permute-start(bf16[128,1024]{1,0:T(8,128)(2,1)S(1)} %get-tuple-element.120), channel_id=1, source_target_pairs={{0,5},{1,4},{2,7},{3,6},{4,1},{5,0},{6,3},{7,2},{8,13},{9,12},{10,... | collective-permute-start | bytes 786440 | tf_op jit(solution)/shard_map/ppermute | solution.py:458
  11.9 21.7 %collective-permute-start.9 = (bf16[128,1024]{1,0:T(8,128)(2,1)S(1)}, bf16[128,1024]{1,0:T(8,128)(2,1)}, u32[]{:S(2)}, u32[]{:S(2)}) collective-permute-start(bf16[128,1024]{1,0:T(8,128)(2,1)S(1)} %get-tuple-element.118), channel_id=1, source_target_pairs={{0,3},{1,2},{2,1},{3,0},{4,7},{5,6},{6,5},{7,4},{8,11},{9,10},{10,... | collective-permute-start | bytes 786440 | tf_op jit(solution)/shard_map/ppermute | solution.py:458
  18.0 15.6 %collective-permute-start.12 = (bf16[128,1024]{1,0:T(8,128)(2,1)S(1)}, bf16[128,1024]{1,0:T(8,128)(2,1)S(1)}, u32[]{:S(2)}, u32[]{:S(2)}) collective-permute-start(bf16[128,1024]{1,0:T(8,128)(2,1)S(1)} %collective-permute-done.7.rest_0_), channel_id=1, source_target_pairs={{0,8},{8,0},{16,24},{24,16},{1,9},{9,1},{17,25},{25,17},{2,10},{10... | collective-permute-start | bytes 786440 | tf_op jit(solution)/shard_map/ppermute | solution.py:412
  20.2 16.9 %collective-permute-start.13 = (bf16[128,1024]{1,0:T(8,128)(2,1)S(1)}, bf16[128,1024]{1,0:T(8,128)(2,1)S(1)}, u32[]{:S(2)}, u32[]{:S(2)}) collective-permute-start(bf16[128,1024]{1,0:T(8,128)(2,1)S(1)} %collective-permute-done.8.rest_1_), channel_id=1, source_target_pairs={{0,8},{8,0},{16,24},{24,16},{1,9},{9,1},{17,25},{25,17},{2,10},{10... | collective-permute-start | bytes 786440 | tf_op jit(solution)/shard_map/ppermute | solution.py:412
  33.1 5.4 %collective-permute-start.15 = (bf16[128,1024]{1,0:T(8,128)(2,1)}, bf16[128,1024]{1,0:T(8,128)(2,1)S(1)}, u32[]{:S(2)}, u32[]{:S(2)}) collective-permute-start(bf16[128,1024]{1,0:T(8,128)(2,1)} %collective-permute-done.10.rest_3_), channel_id=1, source_target_pairs={{0,8},{8,0},{16,24},{24,16},{1,9},{9,1},{17,25},{25,17},{2,10},{10... | collective-permute-start | bytes 786440 | tf_op jit(solution)/shard_map/ppermute | solution.py:412
  33.1 5.4 %collective-permute-start.16 = (bf16[128,1024]{1,0:T(8,128)(2,1)}, bf16[128,1024]{1,0:T(8,128)(2,1)}, u32[]{:S(2)}, u32[]{:S(2)}) collective-permute-start(bf16[128,1024]{1,0:T(8,128)(2,1)} %collective-permute-done.11.rest_4_), channel_id=1, source_target_pairs={{0,8},{8,0},{16,24},{24,16},{1,9},{9,1},{17,25},{25,17},{2,10},{10... | collective-permute-start | bytes 786440 | tf_op jit(solution)/shard_map/ppermute | solution.py:412
  33.6 4.8 %collective-permute-start.14 = (bf16[128,1024]{1,0:T(8,128)(2,1)}, bf16[128,1024]{1,0:T(8,128)(2,1)}, u32[]{:S(2)}, u32[]{:S(2)}) collective-permute-start(bf16[128,1024]{1,0:T(8,128)(2,1)} %collective-permute-done.9.rest_2_), channel_id=1, source_target_pairs={{0,8},{8,0},{16,24},{24,16},{1,9},{9,1},{17,25},{25,17},{2,10},{10... | collective-permute-start | bytes 786440 | tf_op jit(solution)/shard_map/ppermute | solution.py:412
  33.6 26.8 %collective-permute-start.18 = (bf16[128,1024]{1,0:T(8,128)(2,1)S(1)}, bf16[128,1024]{1,0:T(8,128)(2,1)S(1)}, u32[]{:S(2)}, u32[]{:S(2)}) collective-permute-start(bf16[128,1024]{1,0:T(8,128)(2,1)S(1)} %get-tuple-element.130), channel_id=1, source_target_pairs={{0,7},{1,6},{2,5},{3,4},{4,3},{5,2},{6,1},{7,0},{8,15},{9,14},{10,... | collective-permute-start | bytes 786440 | tf_op jit(solution)/shard_map/ppermute | solution.py:458
  37.1 23.3 %collective-permute-start.17 = (bf16[128,1024]{1,0:T(8,128)(2,1)S(1)}, bf16[128,1024]{1,0:T(8,128)(2,1)S(1)}, u32[]{:S(2)}, u32[]{:S(2)}) collective-permute-start(bf16[128,1024]{1,0:T(8,128)(2,1)S(1)} %get-tuple-element.128), channel_id=1, source_target_pairs={{0,6},{1,7},{2,4},{3,5},{4,2},{5,3},{6,0},{7,1},{8,14},{9,15},{10,... | collective-permute-start | bytes 786440 | tf_op jit(solution)/shard_map/ppermute | solution.py:458
  38.5 6.7 %collective-permute-start.2 = (bf16[5,144,128]{2,1,0:T(8,128)(2,1)}, bf16[5,144,128]{2,1,0:T(8,128)(2,1)S(1)}, u32[]{:S(2)}, u32[]{:S(2)}) collective-permute-start(bf16[5,144,128]{2,1,0:T(8,128)(2,1)} %get-tuple-element.54), channel_id=1, source_target_pairs={{0,16},{8,24},{16,0},{24,8},{1,17},{9,25},{17,1},{25,9},{2,18},{10... | collective-permute-start | bytes 552968 | tf_op jit(solution)/shard_map/cond/branch_1_fun/ppermute | solution.py:412
  45.2 13.0 %collective-permute-start.3 = (bf16[5,400,128]{2,1,0:T(8,128)(2,1)}, bf16[5,400,128]{2,1,0:T(8,128)(2,1)}, u32[]{:S(2)}, u32[]{:S(2)}) collective-permute-start(bf16[5,400,128]{2,1,0:T(8,128)(2,1)} %branch_1_fun.7), channel_id=1, source_target_pairs={{0,16},{8,24},{16,0},{24,8},{1,17},{9,25},{17,1},{25,9},{2,18},{10... | collective-permute-start | bytes 1536008 | tf_op jit(solution)/shard_map/cond/branch_1_fun/ppermute | solution.py:412
  48.6 1.7 %collective-permute-start = (bf16[5,144,128]{2,1,0:T(8,128)(2,1)}, bf16[5,144,128]{2,1,0:T(8,128)(2,1)S(1)}, u32[]{:S(2)}, u32[]{:S(2)}) collective-permute-start(bf16[5,144,128]{2,1,0:T(8,128)(2,1)} %get-tuple-element.51.rest_0_), channel_id=1, source_target_pairs={{0,8},{8,0},{16,24},{24,16},{1,9},{9,1},{17,25},{25,17},{2,10},{10... | collective-permute-start | bytes 552968 | tf_op jit(solution)/shard_map/cond/branch_1_fun/cond/branch_1_fun/ppermute | solution.py:412
  48.7 1.7 %collective-permute-start.1 = (bf16[5,144,128]{2,1,0:T(8,128)(2,1)S(1)}, bf16[5,144,128]{2,1,0:T(8,128)(2,1)S(1)}, u32[]{:S(2)}, u32[]{:S(2)}) collective-permute-start(bf16[5,144,128]{2,1,0:T(8,128)(2,1)S(1)} %get-tuple-element.52.rest_1_), channel_id=1, source_target_pairs={{0,8},{8,0},{16,24},{24,16},{1,9},{9,1},{17,25},{25,17},{2,10},{10... | collective-permute-start | bytes 552968 | tf_op jit(solution)/shard_map/cond/branch_1_fun/cond/branch_1_fun/ppermute | solution.py:412
  54.7 3.5 %collective-permute-start.4 = (bf16[5,400,128]{2,1,0:T(8,128)(2,1)}, bf16[5,400,128]{2,1,0:T(8,128)(2,1)}, u32[]{:S(2)}, u32[]{:S(2)}) collective-permute-start(bf16[5,400,128]{2,1,0:T(8,128)(2,1)} %branch_1_fun.7), channel_id=1, source_target_pairs={{0,8},{8,0},{16,24},{24,16},{1,9},{9,1},{17,25},{25,17},{2,10},{10... | collective-permute-start | bytes 1536008 | tf_op jit(solution)/shard_map/cond/branch_1_fun/ppermute | solution.py:412
  58.2 2.2 %collective-permute-start.5 = (bf16[5,400,128]{2,1,0:T(8,128)(2,1)}, bf16[5,400,128]{2,1,0:T(8,128)(2,1)}, u32[]{:S(2)}, u32[]{:S(2)}) collective-permute-start(bf16[5,400,128]{2,1,0:T(8,128)(2,1)} %collective-permute-done.3), channel_id=1, source_target_pairs={{0,8},{8,0},{16,24},{24,16},{1,9},{9,1},{17,25},{25,17},{2,10},{10... | collective-permute-start | bytes 1536008 | tf_op jit(solution)/shard_map/cond/branch_1_fun/ppermute | solution.py:412
  60.4 1.5 %collective-permute-start.19 = (bf16[128,1024]{1,0:T(8,128)(2,1)S(1)}, bf16[128,1024]{1,0:T(8,128)(2,1)S(1)}, u32[]{:S(2)}, u32[]{:S(2)}) collective-permute-start(bf16[128,1024]{1,0:T(8,128)(2,1)S(1)} %collective-permute-done.17.rest_5_), channel_id=1, source_target_pairs={{0,8},{8,0},{16,24},{24,16},{1,9},{9,1},{17,25},{25,17},{2,10},{10... | collective-permute-start | bytes 786440 | tf_op jit(solution)/shard_map/ppermute | solution.py:412
  60.5 1.8 %collective-permute-start.20 = (bf16[128,1024]{1,0:T(8,128)(2,1)S(1)}, bf16[128,1024]{1,0:T(8,128)(2,1)S(1)}, u32[]{:S(2)}, u32[]{:S(2)}) collective-permute-start(bf16[128,1024]{1,0:T(8,128)(2,1)S(1)} %collective-permute-done.18.rest_6_), channel_id=1, source_target_pairs={{0,8},{8,0},{16,24},{24,16},{1,9},{9,1},{17,25},{25,17},{2,10},{10... | collective-permute-start | bytes 786440 | tf_op jit(solution)/shard_map/ppermute | solution.py:412
  65.0 8.6 %copy-start = (f32[4,6,128,128]{3,2,1,0:T(8,128)S(1)}, f32[4,6,128,128]{3,2,1,0:T(8,128)}, u32[]{:S(2)}) copy-start(f32[4,6,128,128]{3,2,1,0:T(8,128)} %prec_ref.1) | copy-start | bytes 4718596
  65.0 7.2 %collective-permute-start.21 = (bf16[2,400,128]{2,1,0:T(8,128)(2,1)S(1)}, bf16[2,400,128]{2,1,0:T(8,128)(2,1)S(1)}, u32[]{:S(2)}, u32[]{:S(2)}) collective-permute-start(bf16[2,400,128]{2,1,0:T(8,128)(2,1)S(1)} %shard_map.38.rest_0_), channel_id=1, source_target_pairs={{0,16},{8,24},{16,0},{24,8},{1,17},{9,25},{17,1},{25,9},{2,18},{10... | collective-permute-start | bytes 614408 | tf_op jit(solution)/shard_map/ppermute | solution.py:412
  66.5 5.7 %collective-permute-start.22 = (bf16[2,400,128]{2,1,0:T(8,128)(2,1)S(1)}, bf16[2,400,128]{2,1,0:T(8,128)(2,1)S(1)}, u32[]{:S(2)}, u32[]{:S(2)}) collective-permute-start(bf16[2,400,128]{2,1,0:T(8,128)(2,1)S(1)} %shard_map.38.rest_0_), channel_id=1, source_target_pairs={{0,8},{8,0},{16,24},{24,16},{1,9},{9,1},{17,25},{25,17},{2,10},{10... | collective-permute-start | bytes 614408 | tf_op jit(solution)/shard_map/ppermute | solution.py:412
  72.1 1.5 %collective-permute-start.23 = (bf16[2,400,128]{2,1,0:T(8,128)(2,1)S(1)}, bf16[2,400,128]{2,1,0:T(8,128)(2,1)S(1)}, u32[]{:S(2)}, u32[]{:S(2)}) collective-permute-start(bf16[2,400,128]{2,1,0:T(8,128)(2,1)S(1)} %collective-permute-done.21.rest_1_), channel_id=1, source_target_pairs={{0,8},{8,0},{16,24},{24,16},{1,9},{9,1},{17,25},{25,17},{2,10},{10... | collective-permute-start | bytes 614408 | tf_op jit(solution)/shard_map/ppermute | solution.py:412

commit v4 on v3

--- a/solution.py
+++ b/solution.py
@@ -10,6 +10,7 @@
 
 ITERS = 3
 STEP = 0.2
+TURNS = ((2, 7), (3, 5), (2, 6), (1, 4))
 SHRINK = 0.05
 
 SMEM = pl.BlockSpec(memory_space=pltpu.SMEM)
@@ -75,16 +76,17 @@
                 m = jnp.where(cb_ref[b, other] == me * block_rows + j, other, m)
             i = j * slots + k
             table_ref[4, i] = jnp.where(filled, jnp.where(own, b, block_rows + place), -1)
-            table_ref[5, i] = jnp.where(filled & jnp.logical_not(own), holder, me)
+            peer, nobody = (place, 0) if rounds else (holder, me)
+            table_ref[5, i] = jnp.where(filled & jnp.logical_not(own), peer, nobody)
             table_ref[6, i] = jnp.where(own, b, 0)
             table_ref[7, i] = jnp.where(own, m, slots)
 
             @pl.when(filled & jnp.logical_not(own))
-            def _(k=k, holder=holder, place=place):
+            def _(k=k, peer=peer, place=place):
                 table_ref[0, place] = j
                 table_ref[1, place] = k
-                table_ref[2, holder] = j
-                table_ref[3, holder] = k
+                table_ref[2, peer] = j
+                table_ref[3, peer] = k
 
 
 def aligned(index, block):
@@ -296,7 +298,35 @@
         place_arrivals(here, first, last, parts[at], gram_ref, low_ref)
 
 
-def multiply_and_step(here, scale, w_ref, gram_ref, low_ref, v_ref, next_ref, out_ref):
+def send(here, v_ref, out_refs):
+    block = v_ref.shape[1]
+
+    def put(out_ref, index, peer):
+        row, column = here.sent(peer)
+        out_ref[index] = v_ref[row, :, aligned(column, block)].astype(out_ref.dtype).T
+
+    if len(out_refs) > 1:
+        core = lax.rem(lax.axis_index("samp"), 2)
+        for out_ref, (a, b) in zip(out_refs, TURNS):
+            put(out_ref, ..., jnp.where(core == 0, a, b))
+    else:
+
+        @pl.loop(0, out_refs[0].shape[0])
+        def _(p):
+            put(out_refs[0], p, p)
+
+
+def receive(in_refs, all_ref):
+    core = lax.rem(lax.axis_index("samp"), 2)
+    mine_ref, other_ref = in_refs
+    for turn, (a, b) in enumerate(TURNS):
+        mine, other = mine_ref[turn], other_ref[turn]
+        all_ref[a] = jnp.where(core == 0, mine, other)
+        all_ref[b] = jnp.where(core == 0, other, mine)
+    all_ref[0] = jnp.zeros(all_ref.shape[1:], all_ref.dtype)
+
+
+def multiply_and_step(here, scale, w_ref, gram_ref, low_ref, v_ref, next_ref, out_refs):
     block_rows, slots, block, _ = next_ref.shape
     v_ref[:, :, slots * block :] = jnp.zeros((block_rows, block, block), jnp.float32)
 
@@ -308,15 +338,7 @@
             low = w_ref[j, :, at].astype(jnp.float32) * low_ref[j, k : k + 1]
             v_ref[j, :, at] = value[:, at] + low
 
-    for p in range(out_ref.shape[0]) if out_ref.shape[0] <= 8 else ():
-        row, column = here.sent(p)
-        out_ref[p] = v_ref[row, :, aligned(column, block)].astype(out_ref.dtype).T
-    if out_ref.shape[0] > 8:
-
-        @pl.loop(0, out_ref.shape[0])
-        def _(p):
-            row, column = here.sent(p)
-            out_ref[p] = v_ref[row, :, aligned(column, block)].astype(out_ref.dtype).T
+    send(here, v_ref, out_refs)
 
     @pl.loop(0, block_rows)
     def _(j):
@@ -328,7 +350,7 @@
 
 def first_kernel(group, ways, scale, table_ref, prec_ref, gram_in_ref, low_in_ref, *rest):
     parts, rest = rest[: 2 * ways], rest[2 * ways :]
-    gram_ref, low_ref, next_ref, out_ref, w_ref, v_ref, sem = rest
+    gram_ref, low_ref, next_ref, *out_refs, w_ref, v_ref, sem = rest
     copy = pltpu.make_async_copy(gram_in_ref, gram_ref, sem)
     copy.start()
     low_ref[...] = low_in_ref[...]
@@ -344,7 +366,7 @@
 
     copy.wait()
     place_arrivals(here, *group, parts, gram_ref, low_ref)
-    multiply_and_step(here, scale, w_ref, gram_ref, low_ref, v_ref, next_ref, out_ref)
+    multiply_and_step(here, scale, w_ref, gram_ref, low_ref, v_ref, next_ref, out_refs)
 
 
 def soft(m):
@@ -363,9 +385,13 @@
             put(k, soft(m - scale * arrived))
 
 
-def middle_kernel(scale, table_ref, stepped_ref, in_ref, gram_ref, low_ref, next_ref, out_ref, w_ref, v_ref):
+def middle_kernel(count, scale, table_ref, stepped_ref, *rest):
+    in_refs, rest = rest[:count], rest[count:]
+    gram_ref, low_ref, next_ref, *out_refs, w_ref, v_ref, all_ref = rest
     block_rows, slots, block, _ = stepped_ref.shape
     here = Pattern(table_ref, block_rows, slots)
+    if count > 1:
+        receive(in_refs, all_ref)
 
     @pl.loop(0, block_rows)
     def _(j):
@@ -373,21 +399,24 @@
             next_ref[j, k] = value
             w_ref[j, :, span(k, block)] = value.astype(jnp.bfloat16)
 
-        next_omega(here, j, scale, stepped_ref, in_ref, put)
-
-    multiply_and_step(here, scale, w_ref, gram_ref, low_ref, v_ref, next_ref, out_ref)
-
-
-def last_kernel(scale, table_ref, stepped_ref, in_ref, next_ref):
+        next_omega(here, j, scale, stepped_ref, all_ref if count > 1 else in_refs[0], put)
+
+    multiply_and_step(here, scale, w_ref, gram_ref, low_ref, v_ref, next_ref, out_refs)
+
+
+def last_kernel(count, scale, table_ref, stepped_ref, *rest):
+    *in_refs, next_ref, all_ref = rest
     block_rows, slots, block, _ = stepped_ref.shape
     here = Pattern(table_ref, block_rows, slots)
+    if count > 1:
+        receive(in_refs, all_ref)
 
     @pl.loop(0, block_rows)
     def _(j):
         def put(k, value):
             next_ref[j, k] = value
 
-        next_omega(here, j, scale, stepped_ref, in_ref, put)
+        next_omega(here, j, scale, stepped_ref, all_ref if count > 1 else in_refs[0], put)
 
 
 def call(kernel, inputs, outs, scratch, smem=1, left=(), sems=(), out_space=VMEM):
@@ -424,11 +453,11 @@
     return lax.optimization_barrier((x, *earlier))[0]
 
 
-def fenced(col_blocks, part, *args):
+def fenced(always, part, *args):
     def nothing(*args):
         return jax.tree.map(lambda x: jnp.zeros(x.shape, x.dtype), jax.eval_shape(part, *args))
 
-    return lax.cond(col_blocks[0, 0] >= 0, part, nothing, *args)
+    return lax.cond(always, part, nothing, *args)
 
 
 def local(samples, precision, col_blocks):
@@ -513,6 +542,7 @@
     def over_of(blocks, earlier):
         return [swap(after(x, earlier), 1) for x in blocks]
 
+    always = col_blocks[0, 0] >= 0
     if rounds:
         other = swap(own, 1)
         own_pair = (own, other)
@@ -522,7 +552,7 @@
         def begin(own, other):
             return own_list(own, other), pattern()
 
-        step, table = fenced(col_blocks, begin, own, other)
+        step, table = fenced(always, begin, own, other)
         over = over_of(arrived, step)
         arrived += [exchange(after(sends[r - 1], arrived[r - 3]), r) for r in (6, 7)]
 
@@ -533,12 +563,12 @@
             own_y = swap(own_list, 2)
             out = after(arrival_list(1, 6, table, own_pair, arrived, over), own_y)
             out_y, own_y = swap(out, 2), after(own_y, out)
-            gram, low = fenced(col_blocks, own_part, table, own_list, own_y)
+            gram, low = fenced(always, own_part, table, own_list, own_y)
             out_core = swap(after(out, gram), 1)
             out_both = swap(after(out_y, gram), 1)
             return gram, low, (out, out_y, out_core, out_both)
 
-        gram, low, *lists = fenced(col_blocks, most, table, own_pair, arrived[:5], over, step)
+        gram, low, *lists = fenced(always, most, table, own_pair, arrived[:5], over, step)
         over += over_of(arrived[5:], gram)
         step = arrival_list(6, 8, table, own_pair, arrived, over)
         gram, low = gather(table, after(gram, step), low, *lists)
@@ -552,29 +582,52 @@
             from_ys(arrival_list(0, peers, table, (own, other), [arrived], [swap(arrived, 1)]))
         )
     blocks = shape(precision.shape, f32)
-    swapped = shape((peers, block, block), bf16)
+    swapped = [shape((block, block) if rounds else (peers, block, block), bf16)]
+    if rounds:
+        swapped *= len(TURNS)
+    all_in = pltpu.VMEM((peers, block, block) if rounds else (8, 128), bf16)
+
+    def trade(out):
+        if not rounds:
+            return [lax.all_to_all(out[0], "feat", 0, 0, tiled=True)]
+        got = []
+        for x, turn in zip(out, TURNS):
+            pairs = [
+                (s * peers + f, s * peers + (f ^ turn[s % 2]))
+                for s in range(lax.axis_size("samp"))
+                for f in range(peers)
+            ]
+            got.append(lax.ppermute(x, ("samp", "feat"), pairs))
+        got = jnp.stack(got)
+        return [got, swap(got, 1)]
+
     work = [
         pltpu.VMEM((block_rows, block, slots * block), bf16),
         pltpu.VMEM((block_rows, block, (slots + 1) * block), f32),
     ]
-    gram, low, stepped, out = call(
+    gram, low, stepped, *out = call(
         functools.partial(first_kernel, groups[-1], ways, scale),
         (table, precision, gram, low, *last_list),
-        [*grams, blocks, swapped],
+        [*grams, blocks, *swapped],
         work,
         left=[2],
         sems=[sem],
     )
     for iteration in range(ITERS):
-        mirrored = lax.all_to_all(out, "feat", 0, 0, tiled=True)
+        mirrored = trade(out)
         if iteration + 1 < ITERS:
-            stepped, out = call(
-                functools.partial(middle_kernel, scale),
-                (table, stepped, mirrored, gram, low),
-                [blocks, swapped],
-                work,
+            stepped, *out = call(
+                functools.partial(middle_kernel, len(mirrored), scale),
+                (table, stepped, *mirrored, gram, low),
+                [blocks, *swapped],
+                [*work, all_in],
             )
-    (updated,) = call(functools.partial(last_kernel, scale), (table, stepped, mirrored), [blocks], [])
+    (updated,) = call(
+        functools.partial(last_kernel, len(mirrored), scale),
+        (table, stepped, *mirrored),
+        [blocks],
+        [all_in],
+    )
     return updated
 
 

time: 124 us -> 116 us (0.935)
  blocking collectives: 38.3 us -> 0 us
  starting transfers between devices: 20.4 us -> 38.1 us
  waiting for transfers between devices: 26.1 us -> 40.4 us
  local copies, waits for them, and re-layouts: 3.68 us -> 2.42 us
    all_to_all x3 -> x0, blocking collectives: 38.3 us -> none  [local(): mirrored = lax.all_to_all(out, 'feat', 0, 0, tiled=True)]
    ppermute x0 -> x12, starting transfers between devices: none -> 14.9 us  [trade(): got.append(lax.ppermute(x, ('samp', 'feat'), pairs))]
    ppermute x0 -> x12, waiting for transfers between devices: none -> 9.33 us  [trade(): got.append(lax.ppermute(x, ('samp', 'feat'), pairs))]
    ppermute x17 -> x20, waiting for transfers between devices: 11.1 us -> 15.9 us  [swap(): return lax.ppermute(x, 'samp', [(i, i ^ bit) for i in range(count)])]
    ppermute x17 -> x20, starting transfers between devices: 7.05 us -> 9.87 us  [swap(): return lax.ppermute(x, 'samp', [(i, i ^ bit) for i in range(count)])]
    slice x2 -> x1, local copies, waits for them, and re-layouts: 2.45 us -> 1.19 us  [local(): always = col_blocks[0, 0] >= 0]
  transfers between devices with their start and end apart: 24 -> 39, of which waited for: 11 -> 20; matrix products, arithmetic and copies ran while one was open for 2% -> 1% of each run, Pallas kernels for 15% -> 16%
where the time goes in v4:
time: 116 us; the launch traced here: 115 us
  waiting for transfers between devices  40.4 us (35%)
  starting transfers between devices  38.1 us (33%)
  Pallas kernels  33.3 us (29%)
  local copies, waits for them, and re-layouts  2.42 us (2%)
    pallas_call x11, Pallas kernels, call(): pl.pallas_call(kernel, out_shape=outs, in_specs=specs, out_specs=[out_spa...  33.3 us
    ppermute x20, waiting for transfers between devices, swap(): return lax.ppermute(x, 'samp', [(i, i ^ bit) for i in range(count)])  15.9 us
    ppermute x7, waiting for transfers between devices, exchange(): return lax.ppermute(x, 'feat', [(i, i ^ r) for i in range(peers)])  15.1 us
    ppermute x12, starting transfers between devices, trade(): got.append(lax.ppermute(x, ('samp', 'feat'), pairs))  14.9 us
    ppermute x7, starting transfers between devices, exchange(): return lax.ppermute(x, 'feat', [(i, i ^ r) for i in range(peers)])  13.3 us
    ppermute x20, starting transfers between devices, swap(): return lax.ppermute(x, 'samp', [(i, i ^ bit) for i in range(count)])  9.87 us
    ppermute x12, waiting for transfers between devices, trade(): got.append(lax.ppermute(x, ('samp', 'feat'), pairs))  9.33 us
  transfers between devices with their start and end apart: 39, of which 20 were waited for; matrix products, arithmetic and copies ran while one was open for 1% of the time, Pallas kernels for 16%

profile of v4, /device:TPU:0, one launch (start us, length us, event | category | flops | bytes accessed | tf_op | source)
XLA Modules:
  0.0 115.0 jit_solution(17917937619454092927)
XLA Ops:
  3.0 2.6 %collective-permute-start.7 = (bf16[128,1024]{1,0:T(8,128)(2,1)S(1)}, bf16[128,1024]{1,0:T(8,128)(2,1)S(1)}, u32[]{:S(2)}, u32[]{:S(2)}) collective-permute-start(bf16[128,1024]{1,0:T(8,128)(2,1)S(1)} %get-tuple-element.124), channel_id=1, source_target_pairs={{0,1},{1,0},{2,3},{3,2},{4,5},{5,4},{6,7},{7,6},{8,9},{9,8},{10,11... | collective-permute-start | bytes 786440 | tf_op jit(solution)/shard_map/ppermute | solution.py:487
  5.6 1.6 %collective-permute-start.8 = (bf16[128,1024]{1,0:T(8,128)(2,1)S(1)}, bf16[128,1024]{1,0:T(8,128)(2,1)S(1)}, u32[]{:S(2)}, u32[]{:S(2)}) collective-permute-start(bf16[128,1024]{1,0:T(8,128)(2,1)S(1)} %get-tuple-element.125), channel_id=1, source_target_pairs={{0,2},{1,3},{2,0},{3,1},{4,6},{5,7},{6,4},{7,5},{8,10},{9,11},{10,... | collective-permute-start | bytes 786440 | tf_op jit(solution)/shard_map/ppermute | solution.py:487
  7.1 2.6 %collective-permute-start.10 = (bf16[128,1024]{1,0:T(8,128)(2,1)S(1)}, bf16[128,1024]{1,0:T(8,128)(2,1)}, u32[]{:S(2)}, u32[]{:S(2)}) collective-permute-start(bf16[128,1024]{1,0:T(8,128)(2,1)S(1)} %get-tuple-element.128), channel_id=1, source_target_pairs={{0,4},{1,5},{2,6},{3,7},{4,0},{5,1},{6,2},{7,3},{8,12},{9,13},{10,... | collective-permute-start | bytes 786440 | tf_op jit(solution)/shard_map/ppermute | solution.py:487
  11.9 1.4 %collective-permute-start.9 = (bf16[128,1024]{1,0:T(8,128)(2,1)S(1)}, bf16[128,1024]{1,0:T(8,128)(2,1)}, u32[]{:S(2)}, u32[]{:S(2)}) collective-permute-start(bf16[128,1024]{1,0:T(8,128)(2,1)S(1)} %get-tuple-element.127), channel_id=1, source_target_pairs={{0,3},{1,2},{2,1},{3,0},{4,7},{5,6},{6,5},{7,4},{8,11},{9,10},{10,... | collective-permute-start | bytes 786440 | tf_op jit(solution)/shard_map/ppermute | solution.py:487
  13.3 4.6 %conditional.3 = (bf16[5,144,128]{2,1,0:T(8,128)(2,1)}, s32[8,24]{1,0:T(8,128)S(1)}) conditional(s32[]{:T(128)} %convert_element_type.7, () %tuple.44, (bf16[4,128,1024]{2,1,0:T(8,128)(2,1)S(1)}, bf16[4,128,1024]{2,1,0:T(8,128)(2,1)}, s32[4,6]{1,0:T(4,128)}) %tuple.45), branch_computations={%region_0.0_spmd, %region_1.0_spmd} | conditional | flops 2 | bytes 185110 | solution.py:460
  13.3 2.8 %branch_1_fun.4 = bf16[5,144,128]{2,1,0:T(8,128)(2,1)} custom-call(bf16[4,128,1024]{2,1,0:T(8,128)(2,1)S(1)} %get-tuple-element.47.mine_ref, bf16[4,128,1024]{2,1,0:T(8,128)(2,1)} %get-tuple-element.48.other_ref), custom_call_target="tpu_custom_call" | custom-call | flops 1 | bytes 1 | tf_op jit(solution)/shard_map/cond/branch_1_fun/pallas_call | solution.py:428
  16.1 1.8 %branch_1_fun.5 = s32[8,24]{1,0:T(8,128)S(1)} custom-call(s32[4,6]{1,0:T(4,128)} %get-tuple-element.49.cb_ref), custom_call_target="tpu_custom_call" | custom-call | flops 1 | bytes 1 | tf_op jit(solution)/shard_map/cond/branch_1_fun/pallas_call | solution.py:428
  18.0 2.2 %collective-permute-done.8.rest_1_ = bf16[128,1024]{1,0:T(8,128)(2,1)S(1)} collective-permute-done((bf16[128,1024]{1,0:T(8,128)(2,1)S(1)}, bf16[128,1024]{1,0:T(8,128)(2,1)S(1)}, u32[]{:S(2)}, u32[]{:S(2)}) %collective-permute-start.8) | collective-permute-done | bytes 262176 | tf_op jit(solution)/shard_map/ppermute | solution.py:487
  20.2 12.9 %collective-permute-done.11.rest_4_ = bf16[128,1024]{1,0:T(8,128)(2,1)} collective-permute-done((bf16[128,1024]{1,0:T(8,128)(2,1)S(1)}, bf16[128,1024]{1,0:T(8,128)(2,1)}, u32[]{:S(2)}, u32[]{:S(2)}) %collective-permute-start.11) | collective-permute-done | bytes 262176 | tf_op jit(solution)/shard_map/ppermute | solution.py:487
  33.6 3.5 %collective-permute-start.18 = (bf16[128,1024]{1,0:T(8,128)(2,1)S(1)}, bf16[128,1024]{1,0:T(8,128)(2,1)S(1)}, u32[]{:S(2)}, u32[]{:S(2)}) collective-permute-start(bf16[128,1024]{1,0:T(8,128)(2,1)S(1)} %get-tuple-element.139), channel_id=1, source_target_pairs={{0,7},{1,6},{2,5},{3,4},{4,3},{5,2},{6,1},{7,0},{8,15},{9,14},{10,... | collective-permute-start | bytes 786440 | tf_op jit(solution)/shard_map/ppermute | solution.py:487
  38.5 22.0 %conditional.4 = (bf16[4,768,768]{2,1,0:T(8,128)(2,1)}, f32[4,8,128]{2,1,0:T(8,128)}, bf16[5,400,128]{2,1,0:T(8,128)(2,1)}, bf16[5,400,128]{2,1,0:T(8,128)(2,1)}...) conditional(s32[]{:T(128)} %convert_element_type.7, () %tuple.46, (pred[]{:T(512)}, ...), branch_computations={%region_2.0_spmd, %region_3.0_spmd} | conditional | flops 3 | bytes 11616524 | solution.py:460
  38.5 1.6 %collective-permute-start.2 = (bf16[5,144,128]{2,1,0:T(8,128)(2,1)}, bf16[5,144,128]{2,1,0:T(8,128)(2,1)}, u32[]{:S(2)}, u32[]{:S(2)}) collective-permute-start(bf16[5,144,128]{2,1,0:T(8,128)(2,1)} %get-tuple-element.54), channel_id=1, source_target_pairs={{0,16},{8,24},{16,0},{24,8},{1,17},{9,25},{17,1},{25,9},{2,18},{10... | collective-permute-start | bytes 552968 | tf_op jit(solution)/shard_map/cond/branch_1_fun/ppermute | solution.py:441
  40.1 4.7 %branch_1_fun.7 = bf16[5,400,128]{2,1,0:T(8,128)(2,1)} custom-call(s32[8,24]{1,0:T(8,128)S(1)} %get-tuple-element.55.table_ref, bf16[4,128,1024]{2,1,0:T(8,128)(2,1)S(1)} %get-tuple-element.56.mine_ref, bf16[4,128,1024]{2,1,0:T(8,128)(2,1)} %get-tuple-element.57.other_ref, bf16[128,1024]{1,0:T(8,128)(2,1)S(1)} %get-tuple-element.58.rest_0_, ...), custom_call_target="tpu_custom_call" | custom-call | flops 1 | bytes 1 | tf_op jit(solution)/shard_map/cond/branch_1_fun/pallas_call | solution.py:428
  45.3 1.5 %collective-permute-start.3 = (bf16[5,400,128]{2,1,0:T(8,128)(2,1)}, bf16[5,400,128]{2,1,0:T(8,128)(2,1)}, u32[]{:S(2)}, u32[]{:S(2)}) collective-permute-start(bf16[5,400,128]{2,1,0:T(8,128)(2,1)} %branch_1_fun.7), channel_id=1, source_target_pairs={{0,16},{8,24},{16,0},{24,8},{1,17},{9,25},{17,1},{25,9},{2,18},{10... | collective-permute-start | bytes 1536008 | tf_op jit(solution)/shard_map/cond/branch_1_fun/ppermute | solution.py:441
  46.8 6.3 %conditional = ((bf16[4,768,768]{2,1,0:T(8,128)(2,1)}, f32[4,8,128]{2,1,0:T(8,128)})) conditional(s32[]{:T(128)} %convert_element_type.1, () %tuple.21, (bf16[5,144,128]{2,1,0:T(8,128)(2,1)}, bf16[5,144,128]{2,1,0:T(8,128)(2,1)}, s32[8,24]{1,0:T(8,128)S(1)}) %tuple.24), branch_computations={%region_4.0_spmd, %region_5.0_spmd} | conditional | flops 1 | bytes 4735006 | solution.py:460
  48.7 4.4 %branch_1_fun.6 = (bf16[4,768,768]{2,1,0:T(8,128)(2,1)}, f32[4,8,128]{2,1,0:T(8,128)}) custom-call(s32[8,24]{1,0:T(8,128)S(1)} %get-tuple-element.50.table_ref, bf16[5,144,128]{2,1,0:T(8,128)(2,1)} %get-tuple-element.51.rest_0_, bf16[5,144,128]{2,1,0:T(8,128)(2,1)} %get-tuple-element.52.rest_1_, bf16[5,144,128]{2,1,0:T(8,128)(2,1)S(1)} %collective-permute-done.rest_2_, ...), custom_call_target="tpu_custom_call" | custom-call | flops 1 | bytes 1 | tf_op jit(solution)/shard_map/cond/branch_1_fun/cond/branch_1_fun/pallas_call | solution.py:428
  53.4 4.8 %collective-permute-done.3 = bf16[5,400,128]{2,1,0:T(8,128)(2,1)} collective-permute-done((bf16[5,400,128]{2,1,0:T(8,128)(2,1)}, bf16[5,400,128]{2,1,0:T(8,128)(2,1)}, u32[]{:S(2)}, u32[]{:S(2)}) %collective-permute-start.3) | collective-permute-done | bytes 512032 | tf_op jit(solution)/shard_map/cond/branch_1_fun/ppermute | solution.py:441
  58.2 2.2 %collective-permute-done.5 = bf16[5,400,128]{2,1,0:T(8,128)(2,1)} collective-permute-done((bf16[5,400,128]{2,1,0:T(8,128)(2,1)}, bf16[5,400,128]{2,1,0:T(8,128)(2,1)}, u32[]{:S(2)}, u32[]{:S(2)}) %collective-permute-start.5) | collective-permute-done | bytes 512032 | tf_op jit(solution)/shard_map/cond/branch_1_fun/ppermute | solution.py:441
  62.4 1.8 %shard_map.38.rest_0_ = bf16[2,400,128]{2,1,0:T(8,128)(2,1)S(1)} custom-call(s32[8,24]{1,0:T(8,128)S(1)} %get-tuple-element.122.table_ref, bf16[4,128,1024]{2,1,0:T(8,128)(2,1)S(1)} %get-tuple-element.121.mine_ref, bf16[4,128,1024]{2,1,0:T(8,128)(2,1)} %collective-permute-done.6.other_ref, bf16[128,1024]{1,0:T(8,128)(2,1)S(1)} %collective-permute-done.7.rest_0_, ...), custom_call_target="tpu_custom_call" | custom-call | flops 1 | bytes 1 | tf_op jit(solution)/shard_map/pallas_call | solution.py:428
  64.2 1.6 %collective-permute-start.21 = (bf16[2,400,128]{2,1,0:T(8,128)(2,1)S(1)}, bf16[2,400,128]{2,1,0:T(8,128)(2,1)S(1)}, u32[]{:S(2)}, u32[]{:S(2)}) collective-permute-start(bf16[2,400,128]{2,1,0:T(8,128)(2,1)S(1)} %shard_map.38.rest_0_), channel_id=1, source_target_pairs={{0,16},{8,24},{16,0},{24,8},{1,17},{9,25},{17,1},{25,9},{2,18},{10... | collective-permute-start | bytes 614408 | tf_op jit(solution)/shard_map/ppermute | solution.py:441
  65.7 4.4 %shard_map.39 = (bf16[4,768,768]{2,1,0:T(8,128)(2,1)S(1)}, f32[4,8,128]{2,1,0:T(8,128)S(1)}) custom-call(s32[8,24]{1,0:T(8,128)S(1)} %get-tuple-element.122.table_ref, bf16[4,768,768]{2,1,0:T(8,128)(2,1)} %get-tuple-element.142.gram_in_ref, f32[4,8,128]{2,1,0:T(8,128)} %get-tuple-element.143.low_in_ref, bf16[5,400,128]{2,1,0:T(8,128)(2,1)} %get-tuple-element.144.rest_0_, ...), custom_call_target="tpu_custom_call" | custom-call | flops 1 | bytes 1 | tf_op jit(solution)/shard_map/pallas_call | solution.py:428
  71.4 1.4 %collective-permute-done.23.rest_3_ = bf16[2,400,128]{2,1,0:T(8,128)(2,1)S(1)} collective-permute-done((bf16[2,400,128]{2,1,0:T(8,128)(2,1)S(1)}, bf16[2,400,128]{2,1,0:T(8,128)(2,1)S(1)}, u32[]{:S(2)}, u32[]{:S(2)}) %collective-permute-start.23) | collective-permute-done | bytes 204832 | tf_op jit(solution)/shard_map/ppermute | solution.py:441
  72.8 3.4 %shard_map.40 = (bf16[4,768,768]{2,1,0:T(8,128)(2,1)S(1)}, f32[4,8,128]{2,1,0:T(8,128)S(1)}, f32[4,6,128,128]{3,2,1,0:T(8,128)S(1)}, bf16[128,128]{1,0:T(8,128)(...) custom-call(s32[8,24]{1,0:T(8,128)S(1)} %get-tuple-element.122.table_ref, ...), custom_call_target="tpu_custom_call" | custom-call | flops 1 | bytes 1 | tf_op jit(solution)/shard_map/pallas_call | solution.py:428
  76.8 4.1 %collective-permute-start.25 = (bf16[128,128]{1,0:T(8,128)(2,1)S(1)}, bf16[128,128]{1,0:T(8,128)(2,1)S(1)}, u32[]{:S(2)}, u32[]{:S(2)}) collective-permute-start(bf16[128,128]{1,0:T(8,128)(2,1)S(1)} %get-tuple-element.153), channel_id=1, source_target_pairs={{0,3},{1,2},{2,1},{3,0},{4,7},{5,6},{6,5},{7,4},{8,13},{9,12},{10,... | collective-permute-start | bytes 98312 | tf_op jit(solution)/shard_map/ppermute | solution.py:600
  81.5 1.7 %collective-permute-done.25 = bf16[128,128]{1,0:T(8,128)(2,1)S(1)} collective-permute-done((bf16[128,128]{1,0:T(8,128)(2,1)S(1)}, bf16[128,128]{1,0:T(8,128)(2,1)S(1)}, u32[]{:S(2)}, u32[]{:S(2)}) %collective-permute-start.25) | collective-permute-done | bytes 32800 | tf_op jit(solution)/shard_map/ppermute | solution.py:600
  83.2 2.1 %collective-permute-done.26 = bf16[128,128]{1,0:T(8,128)(2,1)S(1)} collective-permute-done((bf16[128,128]{1,0:T(8,128)(2,1)S(1)}, bf16[128,128]{1,0:T(8,128)(2,1)S(1)}, u32[]{:S(2)}, u32[]{:S(2)}) %collective-permute-start.26) | collective-permute-done | bytes 32800 | tf_op jit(solution)/shard_map/ppermute | solution.py:600
  87.1 3.3 %shard_map.41 = (f32[4,6,128,128]{3,2,1,0:T(8,128)S(1)}, bf16[128,128]{1,0:T(8,128)(2,1)S(1)}, bf16[128,128]{1,0:T(8,128)(2,1)S(1)}, bf16[128,128]{1,0:T(8,128)(2,1)S(1)}, bf16[128,128]{1,0:T(8,128)(2,1)S(1)}) custom-call(s32[8,24]{1,0:T(8,128)S(1)} %get-tuple-element.122.table_ref, f32[4,6,128,128]{3,2,1,0:T(8,128)S(1)} %get-tuple-element.151.stepped_ref, ...), custom_call_target="tpu_custom_call" | custom-call | flops 1 | bytes 1 | tf_op jit(solution)/shard_map/pallas_call | solution.py:428
  95.1 1.6 %collective-permute-done.30 = bf16[128,128]{1,0:T(8,128)(2,1)S(1)} collective-permute-done((bf16[128,128]{1,0:T(8,128)(2,1)S(1)}, bf16[128,128]{1,0:T(8,128)(2,1)S(1)}, u32[]{:S(2)}, u32[]{:S(2)}) %collective-permute-start.30) | collective-permute-done | bytes 32800 | tf_op jit(solution)/shard_map/ppermute | solution.py:600
  99.6 3.3 %shard_map.42 = (f32[4,6,128,128]{3,2,1,0:T(8,128)S(1)}, bf16[128,128]{1,0:T(8,128)(2,1)S(1)}, bf16[128,128]{1,0:T(8,128)(2,1)S(1)}, bf16[128,128]{1,0:T(8,128)(2,1)S(1)}, bf16[128,128]{1,0:T(8,128)(2,1)S(1)}) custom-call(s32[8,24]{1,0:T(8,128)S(1)} %get-tuple-element.122.table_ref, f32[4,6,128,128]{3,2,1,0:T(8,128)S(1)} %get-tuple-element.158.stepped_ref, ...), custom_call_target="tpu_custom_call" | custom-call | flops 1 | bytes 1 | tf_op jit(solution)/shard_map/pallas_call | solution.py:428
  104.2 2.2 %collective-permute-start.35 = (bf16[128,128]{1,0:T(8,128)(2,1)S(1)}, bf16[128,128]{1,0:T(8,128)(2,1)S(1)}, u32[]{:S(2)}, u32[]{:S(2)}) collective-permute-start(bf16[128,128]{1,0:T(8,128)(2,1)S(1)} %get-tuple-element.165), channel_id=1, source_target_pairs={{0,3},{1,2},{2,1},{3,0},{4,7},{5,6},{6,5},{7,4},{8,13},{9,12},{10,... | collective-permute-start | bytes 98312 | tf_op jit(solution)/shard_map/ppermute | solution.py:600
  107.7 1.6 %collective-permute-done.35 = bf16[128,128]{1,0:T(8,128)(2,1)S(1)} collective-permute-done((bf16[128,128]{1,0:T(8,128)(2,1)S(1)}, bf16[128,128]{1,0:T(8,128)(2,1)S(1)}, u32[]{:S(2)}, u32[]{:S(2)}) %collective-permute-start.35) | collective-permute-done | bytes 32800 | tf_op jit(solution)/shard_map/ppermute | solution.py:600
  112.8 2.2 %shard_map.43 = f32[4,6,128,128]{3,2,1,0:T(8,128)} custom-call(s32[8,24]{1,0:T(8,128)S(1)} %get-tuple-element.122.table_ref, f32[4,6,128,128]{3,2,1,0:T(8,128)S(1)} %get-tuple-element.163.stepped_ref, bf16[4,128,128]{2,1,0:T(8,128)(2,1)S(1)} %pad_maximum_fusion.2.rest_0_, bf16[4,128,128]{2,1,0:T(8,128)(2,1)S(1)} %collective-permute-done.38.rest_1_), custom_call_target="tpu_custom_call" | custom-call | flops 1 | bytes 1 | tf_op jit(solution)/shard_map/pallas_call | solution.py:428
  (68 shorter events, 28.9 us)
Async XLA Ops:
  2.5 9.4 %collective-permute-start.6 = (bf16[4,128,1024]{2,1,0:T(8,128)(2,1)S(1)}, bf16[4,128,1024]{2,1,0:T(8,128)(2,1)}, u32[]{:S(2)}, u32[]{:S(2)}) collective-permute-start(bf16[4,128,1024]{2,1,0:T(8,128)(2,1)S(1)} %get-tuple-element.121.mine_ref), channel_id=1, source_target_pairs={{0,8},{8,0},{16,24},{24,16},{1,9},{9,1},{17,25},{25,17},{2,10},{10... | collective-permute-start | bytes 3145736 | tf_op jit(solution)/shard_map/ppermute | solution.py:441
  3.0 14.9 %collective-permute-start.7 = (bf16[128,1024]{1,0:T(8,128)(2,1)S(1)}, bf16[128,1024]{1,0:T(8,128)(2,1)S(1)}, u32[]{:S(2)}, u32[]{:S(2)}) collective-permute-start(bf16[128,1024]{1,0:T(8,128)(2,1)S(1)} %get-tuple-element.124), channel_id=1, source_target_pairs={{0,1},{1,0},{2,3},{3,2},{4,5},{5,4},{6,7},{7,6},{8,9},{9,8},{10,11... | collective-permute-start | bytes 786440 | tf_op jit(solution)/shard_map/ppermute | solution.py:487
  5.6 14.7 %collective-permute-start.8 = (bf16[128,1024]{1,0:T(8,128)(2,1)S(1)}, bf16[128,1024]{1,0:T(8,128)(2,1)S(1)}, u32[]{:S(2)}, u32[]{:S(2)}) collective-permute-start(bf16[128,1024]{1,0:T(8,128)(2,1)S(1)} %get-tuple-element.125), channel_id=1, source_target_pairs={{0,2},{1,3},{2,0},{3,1},{4,6},{5,7},{6,4},{7,5},{8,10},{9,11},{10,... | collective-permute-start | bytes 786440 | tf_op jit(solution)/shard_map/ppermute | solution.py:487
  7.1 26.0 %collective-permute-start.10 = (bf16[128,1024]{1,0:T(8,128)(2,1)S(1)}, bf16[128,1024]{1,0:T(8,128)(2,1)}, u32[]{:S(2)}, u32[]{:S(2)}) collective-permute-start(bf16[128,1024]{1,0:T(8,128)(2,1)S(1)} %get-tuple-element.128), channel_id=1, source_target_pairs={{0,4},{1,5},{2,6},{3,7},{4,0},{5,1},{6,2},{7,3},{8,12},{9,13},{10,... | collective-permute-start | bytes 786440 | tf_op jit(solution)/shard_map/ppermute | solution.py:487
  9.7 23.4 %collective-permute-start.11 = (bf16[128,1024]{1,0:T(8,128)(2,1)S(1)}, bf16[128,1024]{1,0:T(8,128)(2,1)}, u32[]{:S(2)}, u32[]{:S(2)}) collective-permute-start(bf16[128,1024]{1,0:T(8,128)(2,1)S(1)} %get-tuple-element.129), channel_id=1, source_target_pairs={{0,5},{1,4},{2,7},{3,6},{4,1},{5,0},{6,3},{7,2},{8,13},{9,12},{10,... | collective-permute-start | bytes 786440 | tf_op jit(solution)/shard_map/ppermute | solution.py:487
  11.9 21.7 %collective-permute-start.9 = (bf16[128,1024]{1,0:T(8,128)(2,1)S(1)}, bf16[128,1024]{1,0:T(8,128)(2,1)}, u32[]{:S(2)}, u32[]{:S(2)}) collective-permute-start(bf16[128,1024]{1,0:T(8,128)(2,1)S(1)} %get-tuple-element.127), channel_id=1, source_target_pairs={{0,3},{1,2},{2,1},{3,0},{4,7},{5,6},{6,5},{7,4},{8,11},{9,10},{10,... | collective-permute-start | bytes 786440 | tf_op jit(solution)/shard_map/ppermute | solution.py:487
  17.9 15.7 %collective-permute-start.12 = (bf16[128,1024]{1,0:T(8,128)(2,1)S(1)}, bf16[128,1024]{1,0:T(8,128)(2,1)S(1)}, u32[]{:S(2)}, u32[]{:S(2)}) collective-permute-start(bf16[128,1024]{1,0:T(8,128)(2,1)S(1)} %collective-permute-done.7.rest_0_), channel_id=1, source_target_pairs={{0,8},{8,0},{16,24},{24,16},{1,9},{9,1},{17,25},{25,17},{2,10},{10... | collective-permute-start | bytes 786440 | tf_op jit(solution)/shard_map/ppermute | solution.py:441
  20.2 16.9 %collective-permute-start.13 = (bf16[128,1024]{1,0:T(8,128)(2,1)S(1)}, bf16[128,1024]{1,0:T(8,128)(2,1)S(1)}, u32[]{:S(2)}, u32[]{:S(2)}) collective-permute-start(bf16[128,1024]{1,0:T(8,128)(2,1)S(1)} %collective-permute-done.8.rest_1_), channel_id=1, source_target_pairs={{0,8},{8,0},{16,24},{24,16},{1,9},{9,1},{17,25},{25,17},{2,10},{10... | collective-permute-start | bytes 786440 | tf_op jit(solution)/shard_map/ppermute | solution.py:441
  33.1 5.4 %collective-permute-start.15 = (bf16[128,1024]{1,0:T(8,128)(2,1)}, bf16[128,1024]{1,0:T(8,128)(2,1)S(1)}, u32[]{:S(2)}, u32[]{:S(2)}) collective-permute-start(bf16[128,1024]{1,0:T(8,128)(2,1)} %collective-permute-done.10.rest_3_), channel_id=1, source_target_pairs={{0,8},{8,0},{16,24},{24,16},{1,9},{9,1},{17,25},{25,17},{2,10},{10... | collective-permute-start | bytes 786440 | tf_op jit(solution)/shard_map/ppermute | solution.py:441
  33.1 5.4 %collective-permute-start.16 = (bf16[128,1024]{1,0:T(8,128)(2,1)}, bf16[128,1024]{1,0:T(8,128)(2,1)}, u32[]{:S(2)}, u32[]{:S(2)}) collective-permute-start(bf16[128,1024]{1,0:T(8,128)(2,1)} %collective-permute-done.11.rest_4_), channel_id=1, source_target_pairs={{0,8},{8,0},{16,24},{24,16},{1,9},{9,1},{17,25},{25,17},{2,10},{10... | collective-permute-start | bytes 786440 | tf_op jit(solution)/shard_map/ppermute | solution.py:441
  33.6 4.8 %collective-permute-start.14 = (bf16[128,1024]{1,0:T(8,128)(2,1)}, bf16[128,1024]{1,0:T(8,128)(2,1)}, u32[]{:S(2)}, u32[]{:S(2)}) collective-permute-start(bf16[128,1024]{1,0:T(8,128)(2,1)} %collective-permute-done.9.rest_2_), channel_id=1, source_target_pairs={{0,8},{8,0},{16,24},{24,16},{1,9},{9,1},{17,25},{25,17},{2,10},{10... | collective-permute-start | bytes 786440 | tf_op jit(solution)/shard_map/ppermute | solution.py:441
  33.6 26.8 %collective-permute-start.18 = (bf16[128,1024]{1,0:T(8,128)(2,1)S(1)}, bf16[128,1024]{1,0:T(8,128)(2,1)S(1)}, u32[]{:S(2)}, u32[]{:S(2)}) collective-permute-start(bf16[128,1024]{1,0:T(8,128)(2,1)S(1)} %get-tuple-element.139), channel_id=1, source_target_pairs={{0,7},{1,6},{2,5},{3,4},{4,3},{5,2},{6,1},{7,0},{8,15},{9,14},{10,... | collective-permute-start | bytes 786440 | tf_op jit(solution)/shard_map/ppermute | solution.py:487
  37.1 23.3 %collective-permute-start.17 = (bf16[128,1024]{1,0:T(8,128)(2,1)S(1)}, bf16[128,1024]{1,0:T(8,128)(2,1)S(1)}, u32[]{:S(2)}, u32[]{:S(2)}) collective-permute-start(bf16[128,1024]{1,0:T(8,128)(2,1)S(1)} %get-tuple-element.137), channel_id=1, source_target_pairs={{0,6},{1,7},{2,4},{3,5},{4,2},{5,3},{6,0},{7,1},{8,14},{9,15},{10,... | collective-permute-start | bytes 786440 | tf_op jit(solution)/shard_map/ppermute | solution.py:487
  38.5 6.8 %collective-permute-start.2 = (bf16[5,144,128]{2,1,0:T(8,128)(2,1)}, bf16[5,144,128]{2,1,0:T(8,128)(2,1)}, u32[]{:S(2)}, u32[]{:S(2)}) collective-permute-start(bf16[5,144,128]{2,1,0:T(8,128)(2,1)} %get-tuple-element.54), channel_id=1, source_target_pairs={{0,16},{8,24},{16,0},{24,8},{1,17},{9,25},{17,1},{25,9},{2,18},{10... | collective-permute-start | bytes 552968 | tf_op jit(solution)/shard_map/cond/branch_1_fun/ppermute | solution.py:441
  45.3 12.9 %collective-permute-start.3 = (bf16[5,400,128]{2,1,0:T(8,128)(2,1)}, bf16[5,400,128]{2,1,0:T(8,128)(2,1)}, u32[]{:S(2)}, u32[]{:S(2)}) collective-permute-start(bf16[5,400,128]{2,1,0:T(8,128)(2,1)} %branch_1_fun.7), channel_id=1, source_target_pairs={{0,16},{8,24},{16,0},{24,8},{1,17},{9,25},{17,1},{25,9},{2,18},{10... | collective-permute-start | bytes 1536008 | tf_op jit(solution)/shard_map/cond/branch_1_fun/ppermute | solution.py:441
  53.1 5.1 %collective-permute-start.4 = (bf16[5,400,128]{2,1,0:T(8,128)(2,1)}, bf16[5,400,128]{2,1,0:T(8,128)(2,1)}, u32[]{:S(2)}, u32[]{:S(2)}) collective-permute-start(bf16[5,400,128]{2,1,0:T(8,128)(2,1)} %branch_1_fun.7), channel_id=1, source_target_pairs={{0,8},{8,0},{16,24},{24,16},{1,9},{9,1},{17,25},{25,17},{2,10},{10... | collective-permute-start | bytes 1536008 | tf_op jit(solution)/shard_map/cond/branch_1_fun/ppermute | solution.py:441
  58.2 2.2 %collective-permute-start.5 = (bf16[5,400,128]{2,1,0:T(8,128)(2,1)}, bf16[5,400,128]{2,1,0:T(8,128)(2,1)}, u32[]{:S(2)}, u32[]{:S(2)}) collective-permute-start(bf16[5,400,128]{2,1,0:T(8,128)(2,1)} %collective-permute-done.3), channel_id=1, source_target_pairs={{0,8},{8,0},{16,24},{24,16},{1,9},{9,1},{17,25},{25,17},{2,10},{10... | collective-permute-start | bytes 1536008 | tf_op jit(solution)/shard_map/cond/branch_1_fun/ppermute | solution.py:441
  64.2 7.2 %collective-permute-start.21 = (bf16[2,400,128]{2,1,0:T(8,128)(2,1)S(1)}, bf16[2,400,128]{2,1,0:T(8,128)(2,1)S(1)}, u32[]{:S(2)}, u32[]{:S(2)}) collective-permute-start(bf16[2,400,128]{2,1,0:T(8,128)(2,1)S(1)} %shard_map.38.rest_0_), channel_id=1, source_target_pairs={{0,16},{8,24},{16,0},{24,8},{1,17},{9,25},{17,1},{25,9},{2,18},{10... | collective-permute-start | bytes 614408 | tf_op jit(solution)/shard_map/ppermute | solution.py:441
  65.7 5.6 %collective-permute-start.22 = (bf16[2,400,128]{2,1,0:T(8,128)(2,1)S(1)}, bf16[2,400,128]{2,1,0:T(8,128)(2,1)S(1)}, u32[]{:S(2)}, u32[]{:S(2)}) collective-permute-start(bf16[2,400,128]{2,1,0:T(8,128)(2,1)S(1)} %shard_map.38.rest_0_), channel_id=1, source_target_pairs={{0,8},{8,0},{16,24},{24,16},{1,9},{9,1},{17,25},{25,17},{2,10},{10... | collective-permute-start | bytes 614408 | tf_op jit(solution)/shard_map/ppermute | solution.py:441
  76.2 5.3 %collective-permute-start.24 = (bf16[128,128]{1,0:T(8,128)(2,1)S(1)}, bf16[128,128]{1,0:T(8,128)(2,1)S(1)}, u32[]{:S(2)}, u32[]{:S(2)}) collective-permute-start(bf16[128,128]{1,0:T(8,128)(2,1)S(1)} %get-tuple-element.152), channel_id=1, source_target_pairs={{0,2},{1,3},{2,0},{3,1},{4,6},{5,7},{6,4},{7,5},{8,15},{9,14},{10,... | collective-permute-start | bytes 98312 | tf_op jit(solution)/shard_map/ppermute | solution.py:600
  76.8 6.3 %collective-permute-start.25 = (bf16[128,128]{1,0:T(8,128)(2,1)S(1)}, bf16[128,128]{1,0:T(8,128)(2,1)S(1)}, u32[]{:S(2)}, u32[]{:S(2)}) collective-permute-start(bf16[128,128]{1,0:T(8,128)(2,1)S(1)} %get-tuple-element.153), channel_id=1, source_target_pairs={{0,3},{1,2},{2,1},{3,0},{4,7},{5,6},{6,5},{7,4},{8,13},{9,12},{10,... | collective-permute-start | bytes 98312 | tf_op jit(solution)/shard_map/ppermute | solution.py:600
  80.9 4.3 %collective-permute-start.26 = (bf16[128,128]{1,0:T(8,128)(2,1)S(1)}, bf16[128,128]{1,0:T(8,128)(2,1)S(1)}, u32[]{:S(2)}, u32[]{:S(2)}) collective-permute-start(bf16[128,128]{1,0:T(8,128)(2,1)S(1)} %get-tuple-element.154), channel_id=1, source_target_pairs={{0,2},{1,3},{2,0},{3,1},{4,6},{5,7},{6,4},{7,5},{8,14},{9,15},{10,... | collective-permute-start | bytes 98312 | tf_op jit(solution)/shard_map/ppermute | solution.py:600
  81.0 4.3 %collective-permute-start.27 = (bf16[128,128]{1,0:T(8,128)(2,1)S(1)}, bf16[128,128]{1,0:T(8,128)(2,1)S(1)}, u32[]{:S(2)}, u32[]{:S(2)}) collective-permute-start(bf16[128,128]{1,0:T(8,128)(2,1)S(1)} %get-tuple-element.155), channel_id=1, source_target_pairs={{0,1},{1,0},{2,3},{3,2},{4,5},{5,4},{6,7},{7,6},{8,12},{9,13},{10,... | collective-permute-start | bytes 98312 | tf_op jit(solution)/shard_map/ppermute | solution.py:600
  90.3 4.8 %collective-permute-start.29 = (bf16[128,128]{1,0:T(8,128)(2,1)S(1)}, bf16[128,128]{1,0:T(8,128)(2,1)S(1)}, u32[]{:S(2)}, u32[]{:S(2)}) collective-permute-start(bf16[128,128]{1,0:T(8,128)(2,1)S(1)} %get-tuple-element.159), channel_id=1, source_target_pairs={{0,2},{1,3},{2,0},{3,1},{4,6},{5,7},{6,4},{7,5},{8,15},{9,14},{10,... | collective-permute-start | bytes 98312 | tf_op jit(solution)/shard_map/ppermute | solution.py:600
  91.6 5.1 %collective-permute-start.30 = (bf16[128,128]{1,0:T(8,128)(2,1)S(1)}, bf16[128,128]{1,0:T(8,128)(2,1)S(1)}, u32[]{:S(2)}, u32[]{:S(2)}) collective-permute-start(bf16[128,128]{1,0:T(8,128)(2,1)S(1)} %get-tuple-element.160), channel_id=1, source_target_pairs={{0,3},{1,2},{2,1},{3,0},{4,7},{5,6},{6,5},{7,4},{8,13},{9,12},{10,... | collective-permute-start | bytes 98312 | tf_op jit(solution)/shard_map/ppermute | solution.py:600
  92.8 4.0 %collective-permute-start.31 = (bf16[128,128]{1,0:T(8,128)(2,1)S(1)}, bf16[128,128]{1,0:T(8,128)(2,1)S(1)}, u32[]{:S(2)}, u32[]{:S(2)}) collective-permute-start(bf16[128,128]{1,0:T(8,128)(2,1)S(1)} %get-tuple-element.161), channel_id=1, source_target_pairs={{0,2},{1,3},{2,0},{3,1},{4,6},{5,7},{6,4},{7,5},{8,14},{9,15},{10,... | collective-permute-start | bytes 98312 | tf_op jit(solution)/shard_map/ppermute | solution.py:600
  93.9 3.9 %collective-permute-start.32 = (bf16[128,128]{1,0:T(8,128)(2,1)S(1)}, bf16[128,128]{1,0:T(8,128)(2,1)S(1)}, u32[]{:S(2)}, u32[]{:S(2)}) collective-permute-start(bf16[128,128]{1,0:T(8,128)(2,1)S(1)} %get-tuple-element.162), channel_id=1, source_target_pairs={{0,1},{1,0},{2,3},{3,2},{4,5},{5,4},{6,7},{7,6},{8,12},{9,13},{10,... | collective-permute-start | bytes 98312 | tf_op jit(solution)/shard_map/ppermute | solution.py:600
  102.9 4.8 %collective-permute-start.34 = (bf16[128,128]{1,0:T(8,128)(2,1)S(1)}, bf16[128,128]{1,0:T(8,128)(2,1)S(1)}, u32[]{:S(2)}, u32[]{:S(2)}) collective-permute-start(bf16[128,128]{1,0:T(8,128)(2,1)S(1)} %get-tuple-element.164), channel_id=1, source_target_pairs={{0,2},{1,3},{2,0},{3,1},{4,6},{5,7},{6,4},{7,5},{8,15},{9,14},{10,... | collective-permute-start | bytes 98312 | tf_op jit(solution)/shard_map/ppermute | solution.py:600
  104.2 5.1 %collective-permute-start.35 = (bf16[128,128]{1,0:T(8,128)(2,1)S(1)}, bf16[128,128]{1,0:T(8,128)(2,1)S(1)}, u32[]{:S(2)}, u32[]{:S(2)}) collective-permute-start(bf16[128,128]{1,0:T(8,128)(2,1)S(1)} %get-tuple-element.165), channel_id=1, source_target_pairs={{0,3},{1,2},{2,1},{3,0},{4,7},{5,6},{6,5},{7,4},{8,13},{9,12},{10,... | collective-permute-start | bytes 98312 | tf_op jit(solution)/shard_map/ppermute | solution.py:600
  106.5 4.1 %collective-permute-start.36 = (bf16[128,128]{1,0:T(8,128)(2,1)S(1)}, bf16[128,128]{1,0:T(8,128)(2,1)S(1)}, u32[]{:S(2)}, u32[]{:S(2)}) collective-permute-start(bf16[128,128]{1,0:T(8,128)(2,1)S(1)} %get-tuple-element.166), channel_id=1, source_target_pairs={{0,2},{1,3},{2,0},{3,1},{4,6},{5,7},{6,4},{7,5},{8,14},{9,15},{10,... | collective-permute-start | bytes 98312 | tf_op jit(solution)/shard_map/ppermute | solution.py:600
  106.6 4.1 %collective-permute-start.37 = (bf16[128,128]{1,0:T(8,128)(2,1)S(1)}, bf16[128,128]{1,0:T(8,128)(2,1)S(1)}, u32[]{:S(2)}, u32[]{:S(2)}) collective-permute-start(bf16[128,128]{1,0:T(8,128)(2,1)S(1)} %get-tuple-element.167), channel_id=1, source_target_pairs={{0,1},{1,0},{2,3},{3,2},{4,5},{5,4},{6,7},{7,6},{8,12},{9,13},{10,... | collective-permute-start | bytes 98312 | tf_op jit(solution)/shard_map/ppermute | solution.py:600
  110.6 2.2 %collective-permute-start.38 = (bf16[4,128,128]{2,1,0:T(8,128)(2,1)S(1)}, bf16[4,128,128]{2,1,0:T(8,128)(2,1)S(1)}, u32[]{:S(2)}, u32[]{:S(2)}) collective-permute-start(bf16[4,128,128]{2,1,0:T(8,128)(2,1)S(1)} %pad_maximum_fusion.2.rest_0_), channel_id=1, source_target_pairs={{0,8},{8,0},{16,24},{24,16},{1,9},{9,1},{17,25},{25,17},{2,10},{10... | collective-permute-start | bytes 393224 | tf_op jit(solution)/shard_map/ppermute | solution.py:441
  (9 other events, 21.8 us)

commit v5 on v4

--- a/solution.py
+++ b/solution.py
@@ -326,8 +326,8 @@
     all_ref[0] = jnp.zeros(all_ref.shape[1:], all_ref.dtype)
 
 
-def multiply_and_step(here, scale, w_ref, gram_ref, low_ref, v_ref, next_ref, out_refs):
-    block_rows, slots, block, _ = next_ref.shape
+def multiply_and_send(here, w_ref, gram_ref, low_ref, v_ref, out_refs):
+    block_rows, slots, block = here.block_rows, here.slots, v_ref.shape[1]
     v_ref[:, :, slots * block :] = jnp.zeros((block_rows, block, block), jnp.float32)
 
     @pl.loop(0, block_rows)
@@ -340,17 +340,25 @@
 
     send(here, v_ref, out_refs)
 
+
+def step_kernel(first, scale, table_ref, omega_ref, v_ref, stepped_ref):
+    block_rows, slots, block, _ = omega_ref.shape
+    here = Pattern(table_ref, block_rows, slots)
+
     @pl.loop(0, block_rows)
     def _(j):
         for k in range(slots):
             row, column = here.mate(j, k)
+            omega = omega_ref[j, k]
+            if first:
+                omega = jnp.where(here.source(j, k) >= 0, omega, 0.0)
             mirrored = v_ref[row, :, aligned(column, block)].T
-            next_ref[j, k] = next_ref[j, k] - scale * (v_ref[j, :, span(k, block)] + mirrored)
-
-
-def first_kernel(group, ways, scale, table_ref, prec_ref, gram_in_ref, low_in_ref, *rest):
+            stepped_ref[j, k] = omega - scale * (v_ref[j, :, span(k, block)] + mirrored)
+
+
+def first_kernel(group, ways, table_ref, prec_ref, gram_in_ref, low_in_ref, *rest):
     parts, rest = rest[: 2 * ways], rest[2 * ways :]
-    gram_ref, low_ref, next_ref, *out_refs, w_ref, v_ref, sem = rest
+    gram_ref, low_ref, v_ref, *out_refs, w_ref, sem = rest
     copy = pltpu.make_async_copy(gram_in_ref, gram_ref, sem)
     copy.start()
     low_ref[...] = low_in_ref[...]
@@ -361,12 +369,11 @@
     def _(j):
         for k in range(slots):
             value = jnp.where(here.source(j, k) >= 0, prec_ref[j, k], 0.0)
-            next_ref[j, k] = value
             w_ref[j, :, span(k, block)] = value.astype(jnp.bfloat16)
 
     copy.wait()
     place_arrivals(here, *group, parts, gram_ref, low_ref)
-    multiply_and_step(here, scale, w_ref, gram_ref, low_ref, v_ref, next_ref, out_refs)
+    multiply_and_send(here, w_ref, gram_ref, low_ref, v_ref, out_refs)
 
 
 def soft(m):
@@ -387,7 +394,7 @@
 
 def middle_kernel(count, scale, table_ref, stepped_ref, *rest):
     in_refs, rest = rest[:count], rest[count:]
-    gram_ref, low_ref, next_ref, *out_refs, w_ref, v_ref, all_ref = rest
+    gram_ref, low_ref, next_ref, v_ref, *out_refs, w_ref, all_ref = rest
     block_rows, slots, block, _ = stepped_ref.shape
     here = Pattern(table_ref, block_rows, slots)
     if count > 1:
@@ -401,7 +408,7 @@
 
         next_omega(here, j, scale, stepped_ref, all_ref if count > 1 else in_refs[0], put)
 
-    multiply_and_step(here, scale, w_ref, gram_ref, low_ref, v_ref, next_ref, out_refs)
+    multiply_and_send(here, w_ref, gram_ref, low_ref, v_ref, out_refs)
 
 
 def last_kernel(count, scale, table_ref, stepped_ref, *rest):
@@ -601,26 +608,28 @@
         got = jnp.stack(got)
         return [got, swap(got, 1)]
 
-    work = [
-        pltpu.VMEM((block_rows, block, slots * block), bf16),
-        pltpu.VMEM((block_rows, block, (slots + 1) * block), f32),
-    ]
-    gram, low, stepped, *out = call(
-        functools.partial(first_kernel, groups[-1], ways, scale),
+    weights = pltpu.VMEM((block_rows, block, slots * block), bf16)
+    wide = shape((block_rows, block, (slots + 1) * block), f32)
+    gram, low, v, *out = call(
+        functools.partial(first_kernel, groups[-1], ways),
         (table, precision, gram, low, *last_list),
-        [*grams, blocks, *swapped],
-        work,
+        [*grams, wide, *swapped],
+        [weights],
         left=[2],
         sems=[sem],
     )
+    omega = precision
     for iteration in range(ITERS):
         mirrored = trade(out)
+        (stepped,) = call(
+            functools.partial(step_kernel, iteration == 0, scale), (table, omega, v), [blocks], []
+        )
         if iteration + 1 < ITERS:
-            stepped, *out = call(
+            omega, v, *out = call(
                 functools.partial(middle_kernel, len(mirrored), scale),
                 (table, stepped, *mirrored, gram, low),
-                [blocks, *swapped],
-                [*work, all_in],
+                [blocks, wide, *swapped],
+                [weights, all_in],
             )
     (updated,) = call(
         functools.partial(last_kernel, len(mirrored), scale),

time: 116 us -> 114 us (0.983); the launches traced: 115 us -> 114 us
  Pallas kernels: 33.3 us -> 37.9 us
  waiting for transfers between devices: 40.4 us -> 36.9 us
  starting transfers between devices: 38.1 us -> 35.3 us
    pallas_call x11 -> x14, Pallas kernels: 33.3 us -> 37.9 us  [call(): pl.pallas_call(kernel, out_shape=outs, in_specs=specs, out_specs=[out_spa...]
    ppermute x20, waiting for transfers between devices: 15.9 us -> 13.1 us  [swap(): return lax.ppermute(x, 'samp', [(i, i ^ bit) for i in range(count)])]
    ppermute x12, starting transfers between devices: 14.9 us -> 12.8 us  [trade(): got.append(lax.ppermute(x, ('samp', 'feat'), pairs))]
  transfers between devices with their start and end apart: 39 -> 39, of which waited for: 20 -> 21; matrix products, arithmetic and copies ran while one was open for 1% -> 1% of each run, Pallas kernels for 16% -> 20%
where the time goes in v5:
time: 114 us
  Pallas kernels  37.9 us (33%)
  waiting for transfers between devices  36.9 us (32%)
  starting transfers between devices  35.3 us (31%)
  local copies, waits for them, and re-layouts  3.23 us (3%)
    pallas_call x14, Pallas kernels, call(): pl.pallas_call(kernel, out_shape=outs, in_specs=specs, out_specs=[out_spa...  37.9 us
    ppermute x7, waiting for transfers between devices, exchange(): return lax.ppermute(x, 'feat', [(i, i ^ r) for i in range(peers)])  15.2 us
    ppermute x7, starting transfers between devices, exchange(): return lax.ppermute(x, 'feat', [(i, i ^ r) for i in range(peers)])  13.3 us
    ppermute x20, waiting for transfers between devices, swap(): return lax.ppermute(x, 'samp', [(i, i ^ bit) for i in range(count)])  13.1 us
    ppermute x12, starting transfers between devices, trade(): got.append(lax.ppermute(x, ('samp', 'feat'), pairs))  12.8 us
    ppermute x20, starting transfers between devices, swap(): return lax.ppermute(x, 'samp', [(i, i ^ bit) for i in range(count)])  9.28 us
    ppermute x12, waiting for transfers between devices, trade(): got.append(lax.ppermute(x, ('samp', 'feat'), pairs))  8.65 us
  transfers between devices with their start and end apart: 39, of which 21 were waited for; matrix products, arithmetic and copies ran while one was open for 1% of the time, Pallas kernels for 20%

profile of v5, /device:TPU:0, one launch (start us, length us, event | category | flops | bytes accessed | tf_op | source)
XLA Modules:
  0.0 114.3 jit_solution(15486310268795755387)
XLA Ops:
  3.0 2.6 %collective-permute-start.7 = (bf16[128,1024]{1,0:T(8,128)(2,1)S(1)}, bf16[128,1024]{1,0:T(8,128)(2,1)S(1)}, u32[]{:S(2)}, u32[]{:S(2)}) collective-permute-start(bf16[128,1024]{1,0:T(8,128)(2,1)S(1)} %get-tuple-element.126), channel_id=1, source_target_pairs={{0,1},{1,0},{2,3},{3,2},{4,5},{5,4},{6,7},{7,6},{8,9},{9,8},{10,11... | collective-permute-start | bytes 786440 | tf_op jit(solution)/shard_map/ppermute | solution.py:494
  5.6 1.6 %collective-permute-start.8 = (bf16[128,1024]{1,0:T(8,128)(2,1)S(1)}, bf16[128,1024]{1,0:T(8,128)(2,1)S(1)}, u32[]{:S(2)}, u32[]{:S(2)}) collective-permute-start(bf16[128,1024]{1,0:T(8,128)(2,1)S(1)} %get-tuple-element.127), channel_id=1, source_target_pairs={{0,2},{1,3},{2,0},{3,1},{4,6},{5,7},{6,4},{7,5},{8,10},{9,11},{10,... | collective-permute-start | bytes 786440 | tf_op jit(solution)/shard_map/ppermute | solution.py:494
  7.1 2.6 %collective-permute-start.10 = (bf16[128,1024]{1,0:T(8,128)(2,1)S(1)}, bf16[128,1024]{1,0:T(8,128)(2,1)}, u32[]{:S(2)}, u32[]{:S(2)}) collective-permute-start(bf16[128,1024]{1,0:T(8,128)(2,1)S(1)} %get-tuple-element.130), channel_id=1, source_target_pairs={{0,4},{1,5},{2,6},{3,7},{4,0},{5,1},{6,2},{7,3},{8,12},{9,13},{10,... | collective-permute-start | bytes 786440 | tf_op jit(solution)/shard_map/ppermute | solution.py:494
  11.9 1.4 %collective-permute-start.9 = (bf16[128,1024]{1,0:T(8,128)(2,1)S(1)}, bf16[128,1024]{1,0:T(8,128)(2,1)}, u32[]{:S(2)}, u32[]{:S(2)}) collective-permute-start(bf16[128,1024]{1,0:T(8,128)(2,1)S(1)} %get-tuple-element.129), channel_id=1, source_target_pairs={{0,3},{1,2},{2,1},{3,0},{4,7},{5,6},{6,5},{7,4},{8,11},{9,10},{10,... | collective-permute-start | bytes 786440 | tf_op jit(solution)/shard_map/ppermute | solution.py:494
  13.3 4.5 %conditional.3 = (bf16[5,144,128]{2,1,0:T(8,128)(2,1)}, s32[8,24]{1,0:T(8,128)S(1)}) conditional(s32[]{:T(128)} %convert_element_type.7, () %tuple.44, (bf16[4,128,1024]{2,1,0:T(8,128)(2,1)S(1)}, bf16[4,128,1024]{2,1,0:T(8,128)(2,1)}, s32[4,6]{1,0:T(4,128)}) %tuple.45), branch_computations={%region_0.0_spmd, %region_1.0_spmd} | conditional | flops 2 | bytes 185110 | solution.py:467
  13.3 2.8 %branch_1_fun.4 = bf16[5,144,128]{2,1,0:T(8,128)(2,1)} custom-call(bf16[4,128,1024]{2,1,0:T(8,128)(2,1)S(1)} %get-tuple-element.47.mine_ref, bf16[4,128,1024]{2,1,0:T(8,128)(2,1)} %get-tuple-element.48.other_ref), custom_call_target="tpu_custom_call" | custom-call | flops 1 | bytes 1 | tf_op jit(solution)/shard_map/cond/branch_1_fun/pallas_call | solution.py:435
  16.1 1.7 %branch_1_fun.5 = s32[8,24]{1,0:T(8,128)S(1)} custom-call(s32[4,6]{1,0:T(4,128)S(1)} %copy-done.4), custom_call_target="tpu_custom_call" | custom-call | flops 1 | bytes 1 | tf_op jit(solution)/shard_map/cond/branch_1_fun/pallas_call | solution.py:435
  17.9 2.3 %collective-permute-done.8.rest_1_ = bf16[128,1024]{1,0:T(8,128)(2,1)S(1)} collective-permute-done((bf16[128,1024]{1,0:T(8,128)(2,1)S(1)}, bf16[128,1024]{1,0:T(8,128)(2,1)S(1)}, u32[]{:S(2)}, u32[]{:S(2)}) %collective-permute-start.8) | collective-permute-done | bytes 262176 | tf_op jit(solution)/shard_map/ppermute | solution.py:494
  20.2 12.9 %collective-permute-done.11.rest_4_ = bf16[128,1024]{1,0:T(8,128)(2,1)} collective-permute-done((bf16[128,1024]{1,0:T(8,128)(2,1)S(1)}, bf16[128,1024]{1,0:T(8,128)(2,1)}, u32[]{:S(2)}, u32[]{:S(2)}) %collective-permute-start.11) | collective-permute-done | bytes 262176 | tf_op jit(solution)/shard_map/ppermute | solution.py:494
  33.6 3.5 %collective-permute-start.18 = (bf16[128,1024]{1,0:T(8,128)(2,1)S(1)}, bf16[128,1024]{1,0:T(8,128)(2,1)S(1)}, u32[]{:S(2)}, u32[]{:S(2)}) collective-permute-start(bf16[128,1024]{1,0:T(8,128)(2,1)S(1)} %get-tuple-element.141), channel_id=1, source_target_pairs={{0,7},{1,6},{2,5},{3,4},{4,3},{5,2},{6,1},{7,0},{8,15},{9,14},{10,... | collective-permute-start | bytes 786440 | tf_op jit(solution)/shard_map/ppermute | solution.py:494
  37.1 1.4 %collective-permute-start.17 = (bf16[128,1024]{1,0:T(8,128)(2,1)S(1)}, bf16[128,1024]{1,0:T(8,128)(2,1)S(1)}, u32[]{:S(2)}, u32[]{:S(2)}) collective-permute-start(bf16[128,1024]{1,0:T(8,128)(2,1)S(1)} %get-tuple-element.139), channel_id=1, source_target_pairs={{0,6},{1,7},{2,4},{3,5},{4,2},{5,3},{6,0},{7,1},{8,14},{9,15},{10,... | collective-permute-start | bytes 786440 | tf_op jit(solution)/shard_map/ppermute | solution.py:494
  39.3 22.4 %conditional.4 = (bf16[4,768,768]{2,1,0:T(8,128)(2,1)}, f32[4,8,128]{2,1,0:T(8,128)}, bf16[5,400,128]{2,1,0:T(8,128)(2,1)}, bf16[5,400,128]{2,1,0:T(8,128)(2,1)}...) conditional(s32[]{:T(128)} %convert_element_type.7, () %tuple.46, (pred[]{:T(512)}, ...), branch_computations={%region_2.0_spmd, %region_3.0_spmd} | conditional | flops 3 | bytes 11616524 | solution.py:467
  39.3 1.5 %collective-permute-start.2 = (bf16[5,144,128]{2,1,0:T(8,128)(2,1)}, bf16[5,144,128]{2,1,0:T(8,128)(2,1)}, u32[]{:S(2)}, u32[]{:S(2)}) collective-permute-start(bf16[5,144,128]{2,1,0:T(8,128)(2,1)} %get-tuple-element.54), channel_id=1, source_target_pairs={{0,16},{8,24},{16,0},{24,8},{1,17},{9,25},{17,1},{25,9},{2,18},{10... | collective-permute-start | bytes 552968 | tf_op jit(solution)/shard_map/cond/branch_1_fun/ppermute | solution.py:448
  40.8 5.3 %branch_1_fun.7 = bf16[5,400,128]{2,1,0:T(8,128)(2,1)} custom-call(s32[8,24]{1,0:T(8,128)S(1)} %get-tuple-element.55.table_ref, bf16[4,128,1024]{2,1,0:T(8,128)(2,1)S(1)} %get-tuple-element.56.mine_ref, bf16[4,128,1024]{2,1,0:T(8,128)(2,1)} %get-tuple-element.57.other_ref, bf16[128,1024]{1,0:T(8,128)(2,1)S(1)} %get-tuple-element.58.rest_0_, ...), custom_call_target="tpu_custom_call" | custom-call | flops 1 | bytes 1 | tf_op jit(solution)/shard_map/cond/branch_1_fun/pallas_call | solution.py:435
  46.1 1.5 %collective-permute-start.3 = (bf16[5,400,128]{2,1,0:T(8,128)(2,1)}, bf16[5,400,128]{2,1,0:T(8,128)(2,1)}, u32[]{:S(2)}, u32[]{:S(2)}) collective-permute-start(bf16[5,400,128]{2,1,0:T(8,128)(2,1)} %branch_1_fun.7), channel_id=1, source_target_pairs={{0,16},{8,24},{16,0},{24,8},{1,17},{9,25},{17,1},{25,9},{2,18},{10... | collective-permute-start | bytes 1536008 | tf_op jit(solution)/shard_map/cond/branch_1_fun/ppermute | solution.py:448
  47.6 6.3 %conditional = ((bf16[4,768,768]{2,1,0:T(8,128)(2,1)}, f32[4,8,128]{2,1,0:T(8,128)})) conditional(s32[]{:T(128)} %convert_element_type.1, () %tuple.21, (bf16[5,144,128]{2,1,0:T(8,128)(2,1)}, bf16[5,144,128]{2,1,0:T(8,128)(2,1)}, s32[8,24]{1,0:T(8,128)S(1)}) %tuple.24), branch_computations={%region_4.0_spmd, %region_5.0_spmd} | conditional | flops 1 | bytes 4735006 | solution.py:467
  49.5 4.4 %branch_1_fun.6 = (bf16[4,768,768]{2,1,0:T(8,128)(2,1)}, f32[4,8,128]{2,1,0:T(8,128)}) custom-call(s32[8,24]{1,0:T(8,128)S(1)} %get-tuple-element.50.table_ref, bf16[5,144,128]{2,1,0:T(8,128)(2,1)} %get-tuple-element.51.rest_0_, bf16[5,144,128]{2,1,0:T(8,128)(2,1)} %get-tuple-element.52.rest_1_, bf16[5,144,128]{2,1,0:T(8,128)(2,1)S(1)} %collective-permute-done.rest_2_, ...), custom_call_target="tpu_custom_call" | custom-call | flops 1 | bytes 1 | tf_op jit(solution)/shard_map/cond/branch_1_fun/cond/branch_1_fun/pallas_call | solution.py:435
  54.1 5.3 %collective-permute-done.3 = bf16[5,400,128]{2,1,0:T(8,128)(2,1)} collective-permute-done((bf16[5,400,128]{2,1,0:T(8,128)(2,1)}, bf16[5,400,128]{2,1,0:T(8,128)(2,1)}, u32[]{:S(2)}, u32[]{:S(2)}) %collective-permute-start.3) | collective-permute-done | bytes 512032 | tf_op jit(solution)/shard_map/cond/branch_1_fun/ppermute | solution.py:448
  59.5 2.2 %collective-permute-done.5 = bf16[5,400,128]{2,1,0:T(8,128)(2,1)} collective-permute-done((bf16[5,400,128]{2,1,0:T(8,128)(2,1)}, bf16[5,400,128]{2,1,0:T(8,128)(2,1)}, u32[]{:S(2)}, u32[]{:S(2)}) %collective-permute-start.5) | collective-permute-done | bytes 512032 | tf_op jit(solution)/shard_map/cond/branch_1_fun/ppermute | solution.py:448
  63.6 3.5 %shard_map.38.rest_0_ = bf16[2,400,128]{2,1,0:T(8,128)(2,1)S(1)} custom-call(s32[8,24]{1,0:T(8,128)S(1)} %get-tuple-element.124.table_ref, bf16[4,128,1024]{2,1,0:T(8,128)(2,1)S(1)} %get-tuple-element.123.mine_ref, bf16[4,128,1024]{2,1,0:T(8,128)(2,1)} %collective-permute-done.6.other_ref, bf16[128,1024]{1,0:T(8,128)(2,1)S(1)} %collective-permute-done.7.rest_0_, ...), custom_call_target="tpu_custom_call" | custom-call | flops 1 | bytes 1 | tf_op jit(solution)/shard_map/pallas_call | solution.py:435
  68.2 4.7 %shard_map.39 = (bf16[4,768,768]{2,1,0:T(8,128)(2,1)S(1)}, f32[4,8,128]{2,1,0:T(8,128)S(1)}) custom-call(s32[8,24]{1,0:T(8,128)S(1)} %get-tuple-element.124.table_ref, bf16[4,768,768]{2,1,0:T(8,128)(2,1)} %get-tuple-element.144.gram_in_ref, f32[4,8,128]{2,1,0:T(8,128)} %get-tuple-element.145.low_in_ref, bf16[5,400,128]{2,1,0:T(8,128)(2,1)} %get-tuple-element.146.rest_0_, ...), custom_call_target="tpu_custom_call" | custom-call | flops 1 | bytes 1 | tf_op jit(solution)/shard_map/pallas_call | solution.py:435
  74.2 1.4 %collective-permute-done.23.rest_3_ = bf16[2,400,128]{2,1,0:T(8,128)(2,1)S(1)} collective-permute-done((bf16[2,400,128]{2,1,0:T(8,128)(2,1)S(1)}, bf16[2,400,128]{2,1,0:T(8,128)(2,1)S(1)}, u32[]{:S(2)}, u32[]{:S(2)}) %collective-permute-start.23) | collective-permute-done | bytes 204832 | tf_op jit(solution)/shard_map/ppermute | solution.py:448
  75.6 3.0 %shard_map.40 = (bf16[4,768,768]{2,1,0:T(8,128)(2,1)S(1)}, f32[4,8,128]{2,1,0:T(8,128)S(1)}, f32[4,128,896]{2,1,0:T(8,128)S(1)}, bf16[128,128]{1,0:T(8,128)(2,1)...) custom-call(s32[8,24]{1,0:T(8,128)S(1)} %get-tuple-element.124.table_ref, ...), custom_call_target="tpu_custom_call" | custom-call | flops 1 | bytes 1 | tf_op jit(solution)/shard_map/pallas_call | solution.py:435
  78.7 1.5 %collective-permute-start.25 = (bf16[128,128]{1,0:T(8,128)(2,1)S(1)}, bf16[128,128]{1,0:T(8,128)(2,1)S(1)}, u32[]{:S(2)}, u32[]{:S(2)}) collective-permute-start(bf16[128,128]{1,0:T(8,128)(2,1)S(1)} %get-tuple-element.155), channel_id=1, source_target_pairs={{0,3},{1,2},{2,1},{3,0},{4,7},{5,6},{6,5},{7,4},{8,13},{9,12},{10,... | collective-permute-start | bytes 98312 | tf_op jit(solution)/shard_map/ppermute | solution.py:607
  80.7 1.5 %collective-permute-start.27 = (bf16[128,128]{1,0:T(8,128)(2,1)S(1)}, bf16[128,128]{1,0:T(8,128)(2,1)S(1)}, u32[]{:S(2)}, u32[]{:S(2)}) collective-permute-start(bf16[128,128]{1,0:T(8,128)(2,1)S(1)} %get-tuple-element.157), channel_id=1, source_target_pairs={{0,1},{1,0},{2,3},{3,2},{4,5},{5,4},{6,7},{7,6},{8,12},{9,13},{10,... | collective-permute-start | bytes 98312 | tf_op jit(solution)/shard_map/ppermute | solution.py:607
  86.2 1.4 %shard_map.41.stepped_ref = f32[4,6,128,128]{3,2,1,0:T(8,128)S(1)} custom-call(s32[8,24]{1,0:T(8,128)S(1)} %get-tuple-element.124.table_ref, f32[4,6,128,128]{3,2,1,0:T(8,128)S(1)} %copy-done, f32[4,128,896]{2,1,0:T(8,128)S(1)} %get-tuple-element.153.v_ref), custom_call_target="tpu_custom_call" | custom-call | flops 1 | bytes 1 | tf_op jit(solution)/shard_map/pallas_call | solution.py:435
  87.6 2.5 %shard_map.42 = (f32[4,6,128,128]{3,2,1,0:T(8,128)S(1)}, f32[4,128,896]{2,1,0:T(8,128)S(1)}, bf16[128,128]{1,0:T(8,128)(2,1)S(1)}, bf16[128,128]{1,0:T(8,128)(2,...) custom-call(s32[8,24]{1,0:T(8,128)S(1)} %get-tuple-element.124.table_ref, ...), custom_call_target="tpu_custom_call" | custom-call | flops 1 | bytes 1 | tf_op jit(solution)/shard_map/pallas_call | solution.py:435
  90.1 1.9 %collective-permute-start.29 = (bf16[128,128]{1,0:T(8,128)(2,1)S(1)}, bf16[128,128]{1,0:T(8,128)(2,1)S(1)}, u32[]{:S(2)}, u32[]{:S(2)}) collective-permute-start(bf16[128,128]{1,0:T(8,128)(2,1)S(1)} %get-tuple-element.162), channel_id=1, source_target_pairs={{0,2},{1,3},{2,0},{3,1},{4,6},{5,7},{6,4},{7,5},{8,15},{9,14},{10,... | collective-permute-start | bytes 98312 | tf_op jit(solution)/shard_map/ppermute | solution.py:607
  94.0 1.5 %collective-permute-start.32 = (bf16[128,128]{1,0:T(8,128)(2,1)S(1)}, bf16[128,128]{1,0:T(8,128)(2,1)S(1)}, u32[]{:S(2)}, u32[]{:S(2)}) collective-permute-start(bf16[128,128]{1,0:T(8,128)(2,1)S(1)} %get-tuple-element.165), channel_id=1, source_target_pairs={{0,1},{1,0},{2,3},{3,2},{4,5},{5,4},{6,7},{7,6},{8,12},{9,13},{10,... | collective-permute-start | bytes 98312 | tf_op jit(solution)/shard_map/ppermute | solution.py:607
  100.6 2.5 %shard_map.44 = (f32[4,6,128,128]{3,2,1,0:T(8,128)S(1)}, f32[4,128,896]{2,1,0:T(8,128)S(1)}, bf16[128,128]{1,0:T(8,128)(2,1)S(1)}, bf16[128,128]{1,0:T(8,128)(2,...) custom-call(s32[8,24]{1,0:T(8,128)S(1)} %get-tuple-element.124.table_ref, ...), custom_call_target="tpu_custom_call" | custom-call | flops 1 | bytes 1 | tf_op jit(solution)/shard_map/pallas_call | solution.py:435
  103.4 2.0 %collective-permute-start.35 = (bf16[128,128]{1,0:T(8,128)(2,1)S(1)}, bf16[128,128]{1,0:T(8,128)(2,1)S(1)}, u32[]{:S(2)}, u32[]{:S(2)}) collective-permute-start(bf16[128,128]{1,0:T(8,128)(2,1)S(1)} %get-tuple-element.169), channel_id=1, source_target_pairs={{0,3},{1,2},{2,1},{3,0},{4,7},{5,6},{6,5},{7,4},{8,13},{9,12},{10,... | collective-permute-start | bytes 98312 | tf_op jit(solution)/shard_map/ppermute | solution.py:607
  112.1 2.2 %shard_map.46 = f32[4,6,128,128]{3,2,1,0:T(8,128)} custom-call(s32[8,24]{1,0:T(8,128)S(1)} %get-tuple-element.124.table_ref, f32[4,6,128,128]{3,2,1,0:T(8,128)S(1)} %shard_map.45.stepped_ref, bf16[4,128,128]{2,1,0:T(8,128)(2,1)S(1)} %pad_maximum_fusion.2.rest_0_, bf16[4,128,128]{2,1,0:T(8,128)(2,1)S(1)} %collective-permute-done.38.rest_1_), custom_call_target="tpu_custom_call" | custom-call | flops 1 | bytes 1 | tf_op jit(solution)/shard_map/pallas_call | solution.py:435
  (77 shorter events, 31.0 us)
Async XLA Ops:
  2.5 9.4 %collective-permute-start.6 = (bf16[4,128,1024]{2,1,0:T(8,128)(2,1)S(1)}, bf16[4,128,1024]{2,1,0:T(8,128)(2,1)}, u32[]{:S(2)}, u32[]{:S(2)}) collective-permute-start(bf16[4,128,1024]{2,1,0:T(8,128)(2,1)S(1)} %get-tuple-element.123.mine_ref), channel_id=1, source_target_pairs={{0,8},{8,0},{16,24},{24,16},{1,9},{9,1},{17,25},{25,17},{2,10},{10... | collective-permute-start | bytes 3145736 | tf_op jit(solution)/shard_map/ppermute | solution.py:448
  3.0 14.8 %collective-permute-start.7 = (bf16[128,1024]{1,0:T(8,128)(2,1)S(1)}, bf16[128,1024]{1,0:T(8,128)(2,1)S(1)}, u32[]{:S(2)}, u32[]{:S(2)}) collective-permute-start(bf16[128,1024]{1,0:T(8,128)(2,1)S(1)} %get-tuple-element.126), channel_id=1, source_target_pairs={{0,1},{1,0},{2,3},{3,2},{4,5},{5,4},{6,7},{7,6},{8,9},{9,8},{10,11... | collective-permute-start | bytes 786440 | tf_op jit(solution)/shard_map/ppermute | solution.py:494
  5.6 14.7 %collective-permute-start.8 = (bf16[128,1024]{1,0:T(8,128)(2,1)S(1)}, bf16[128,1024]{1,0:T(8,128)(2,1)S(1)}, u32[]{:S(2)}, u32[]{:S(2)}) collective-permute-start(bf16[128,1024]{1,0:T(8,128)(2,1)S(1)} %get-tuple-element.127), channel_id=1, source_target_pairs={{0,2},{1,3},{2,0},{3,1},{4,6},{5,7},{6,4},{7,5},{8,10},{9,11},{10,... | collective-permute-start | bytes 786440 | tf_op jit(solution)/shard_map/ppermute | solution.py:494
  7.1 26.0 %collective-permute-start.10 = (bf16[128,1024]{1,0:T(8,128)(2,1)S(1)}, bf16[128,1024]{1,0:T(8,128)(2,1)}, u32[]{:S(2)}, u32[]{:S(2)}) collective-permute-start(bf16[128,1024]{1,0:T(8,128)(2,1)S(1)} %get-tuple-element.130), channel_id=1, source_target_pairs={{0,4},{1,5},{2,6},{3,7},{4,0},{5,1},{6,2},{7,3},{8,12},{9,13},{10,... | collective-permute-start | bytes 786440 | tf_op jit(solution)/shard_map/ppermute | solution.py:494
  9.7 23.4 %collective-permute-start.11 = (bf16[128,1024]{1,0:T(8,128)(2,1)S(1)}, bf16[128,1024]{1,0:T(8,128)(2,1)}, u32[]{:S(2)}, u32[]{:S(2)}) collective-permute-start(bf16[128,1024]{1,0:T(8,128)(2,1)S(1)} %get-tuple-element.131), channel_id=1, source_target_pairs={{0,5},{1,4},{2,7},{3,6},{4,1},{5,0},{6,3},{7,2},{8,13},{9,12},{10,... | collective-permute-start | bytes 786440 | tf_op jit(solution)/shard_map/ppermute | solution.py:494
  11.9 21.7 %collective-permute-start.9 = (bf16[128,1024]{1,0:T(8,128)(2,1)S(1)}, bf16[128,1024]{1,0:T(8,128)(2,1)}, u32[]{:S(2)}, u32[]{:S(2)}) collective-permute-start(bf16[128,1024]{1,0:T(8,128)(2,1)S(1)} %get-tuple-element.129), channel_id=1, source_target_pairs={{0,3},{1,2},{2,1},{3,0},{4,7},{5,6},{6,5},{7,4},{8,11},{9,10},{10,... | collective-permute-start | bytes 786440 | tf_op jit(solution)/shard_map/ppermute | solution.py:494
  17.8 15.8 %collective-permute-start.12 = (bf16[128,1024]{1,0:T(8,128)(2,1)S(1)}, bf16[128,1024]{1,0:T(8,128)(2,1)S(1)}, u32[]{:S(2)}, u32[]{:S(2)}) collective-permute-start(bf16[128,1024]{1,0:T(8,128)(2,1)S(1)} %collective-permute-done.7.rest_0_), channel_id=1, source_target_pairs={{0,8},{8,0},{16,24},{24,16},{1,9},{9,1},{17,25},{25,17},{2,10},{10... | collective-permute-start | bytes 786440 | tf_op jit(solution)/shard_map/ppermute | solution.py:448
  20.2 16.9 %collective-permute-start.13 = (bf16[128,1024]{1,0:T(8,128)(2,1)S(1)}, bf16[128,1024]{1,0:T(8,128)(2,1)S(1)}, u32[]{:S(2)}, u32[]{:S(2)}) collective-permute-start(bf16[128,1024]{1,0:T(8,128)(2,1)S(1)} %collective-permute-done.8.rest_1_), channel_id=1, source_target_pairs={{0,8},{8,0},{16,24},{24,16},{1,9},{9,1},{17,25},{25,17},{2,10},{10... | collective-permute-start | bytes 786440 | tf_op jit(solution)/shard_map/ppermute | solution.py:448
  33.1 5.4 %collective-permute-start.15 = (bf16[128,1024]{1,0:T(8,128)(2,1)}, bf16[128,1024]{1,0:T(8,128)(2,1)S(1)}, u32[]{:S(2)}, u32[]{:S(2)}) collective-permute-start(bf16[128,1024]{1,0:T(8,128)(2,1)} %collective-permute-done.10.rest_3_), channel_id=1, source_target_pairs={{0,8},{8,0},{16,24},{24,16},{1,9},{9,1},{17,25},{25,17},{2,10},{10... | collective-permute-start | bytes 786440 | tf_op jit(solution)/shard_map/ppermute | solution.py:448
  33.1 5.4 %collective-permute-start.16 = (bf16[128,1024]{1,0:T(8,128)(2,1)}, bf16[128,1024]{1,0:T(8,128)(2,1)S(1)}, u32[]{:S(2)}, u32[]{:S(2)}) collective-permute-start(bf16[128,1024]{1,0:T(8,128)(2,1)} %collective-permute-done.11.rest_4_), channel_id=1, source_target_pairs={{0,8},{8,0},{16,24},{24,16},{1,9},{9,1},{17,25},{25,17},{2,10},{10... | collective-permute-start | bytes 786440 | tf_op jit(solution)/shard_map/ppermute | solution.py:448
  33.6 4.8 %collective-permute-start.14 = (bf16[128,1024]{1,0:T(8,128)(2,1)}, bf16[128,1024]{1,0:T(8,128)(2,1)S(1)}, u32[]{:S(2)}, u32[]{:S(2)}) collective-permute-start(bf16[128,1024]{1,0:T(8,128)(2,1)} %collective-permute-done.9.rest_2_), channel_id=1, source_target_pairs={{0,8},{8,0},{16,24},{24,16},{1,9},{9,1},{17,25},{25,17},{2,10},{10... | collective-permute-start | bytes 786440 | tf_op jit(solution)/shard_map/ppermute | solution.py:448
  33.6 28.1 %collective-permute-start.18 = (bf16[128,1024]{1,0:T(8,128)(2,1)S(1)}, bf16[128,1024]{1,0:T(8,128)(2,1)S(1)}, u32[]{:S(2)}, u32[]{:S(2)}) collective-permute-start(bf16[128,1024]{1,0:T(8,128)(2,1)S(1)} %get-tuple-element.141), channel_id=1, source_target_pairs={{0,7},{1,6},{2,5},{3,4},{4,3},{5,2},{6,1},{7,0},{8,15},{9,14},{10,... | collective-permute-start | bytes 786440 | tf_op jit(solution)/shard_map/ppermute | solution.py:494
  37.1 24.6 %collective-permute-start.17 = (bf16[128,1024]{1,0:T(8,128)(2,1)S(1)}, bf16[128,1024]{1,0:T(8,128)(2,1)S(1)}, u32[]{:S(2)}, u32[]{:S(2)}) collective-permute-start(bf16[128,1024]{1,0:T(8,128)(2,1)S(1)} %get-tuple-element.139), channel_id=1, source_target_pairs={{0,6},{1,7},{2,4},{3,5},{4,2},{5,3},{6,0},{7,1},{8,14},{9,15},{10,... | collective-permute-start | bytes 786440 | tf_op jit(solution)/shard_map/ppermute | solution.py:494
  39.3 6.8 %collective-permute-start.2 = (bf16[5,144,128]{2,1,0:T(8,128)(2,1)}, bf16[5,144,128]{2,1,0:T(8,128)(2,1)}, u32[]{:S(2)}, u32[]{:S(2)}) collective-permute-start(bf16[5,144,128]{2,1,0:T(8,128)(2,1)} %get-tuple-element.54), channel_id=1, source_target_pairs={{0,16},{8,24},{16,0},{24,8},{1,17},{9,25},{17,1},{25,9},{2,18},{10... | collective-permute-start | bytes 552968 | tf_op jit(solution)/shard_map/cond/branch_1_fun/ppermute | solution.py:448
  46.1 13.4 %collective-permute-start.3 = (bf16[5,400,128]{2,1,0:T(8,128)(2,1)}, bf16[5,400,128]{2,1,0:T(8,128)(2,1)}, u32[]{:S(2)}, u32[]{:S(2)}) collective-permute-start(bf16[5,400,128]{2,1,0:T(8,128)(2,1)} %branch_1_fun.7), channel_id=1, source_target_pairs={{0,16},{8,24},{16,0},{24,8},{1,17},{9,25},{17,1},{25,9},{2,18},{10... | collective-permute-start | bytes 1536008 | tf_op jit(solution)/shard_map/cond/branch_1_fun/ppermute | solution.py:448
  53.9 5.6 %collective-permute-start.4 = (bf16[5,400,128]{2,1,0:T(8,128)(2,1)}, bf16[5,400,128]{2,1,0:T(8,128)(2,1)}, u32[]{:S(2)}, u32[]{:S(2)}) collective-permute-start(bf16[5,400,128]{2,1,0:T(8,128)(2,1)} %branch_1_fun.7), channel_id=1, source_target_pairs={{0,8},{8,0},{16,24},{24,16},{1,9},{9,1},{17,25},{25,17},{2,10},{10... | collective-permute-start | bytes 1536008 | tf_op jit(solution)/shard_map/cond/branch_1_fun/ppermute | solution.py:448
  67.1 7.1 %collective-permute-start.21 = (bf16[2,400,128]{2,1,0:T(8,128)(2,1)S(1)}, bf16[2,400,128]{2,1,0:T(8,128)(2,1)S(1)}, u32[]{:S(2)}, u32[]{:S(2)}) collective-permute-start(bf16[2,400,128]{2,1,0:T(8,128)(2,1)S(1)} %shard_map.38.rest_0_), channel_id=1, source_target_pairs={{0,16},{8,24},{16,0},{24,8},{1,17},{9,25},{17,1},{25,9},{2,18},{10... | collective-permute-start | bytes 614408 | tf_op jit(solution)/shard_map/ppermute | solution.py:448
  68.2 6.0 %collective-permute-start.22 = (bf16[2,400,128]{2,1,0:T(8,128)(2,1)S(1)}, bf16[2,400,128]{2,1,0:T(8,128)(2,1)S(1)}, u32[]{:S(2)}, u32[]{:S(2)}) collective-permute-start(bf16[2,400,128]{2,1,0:T(8,128)(2,1)S(1)} %shard_map.38.rest_0_), channel_id=1, source_target_pairs={{0,8},{8,0},{16,24},{24,16},{1,9},{9,1},{17,25},{25,17},{2,10},{10... | collective-permute-start | bytes 614408 | tf_op jit(solution)/shard_map/ppermute | solution.py:448
  78.6 4.0 %collective-permute-start.24 = (bf16[128,128]{1,0:T(8,128)(2,1)S(1)}, bf16[128,128]{1,0:T(8,128)(2,1)S(1)}, u32[]{:S(2)}, u32[]{:S(2)}) collective-permute-start(bf16[128,128]{1,0:T(8,128)(2,1)S(1)} %get-tuple-element.154), channel_id=1, source_target_pairs={{0,2},{1,3},{2,0},{3,1},{4,6},{5,7},{6,4},{7,5},{8,15},{9,14},{10,... | collective-permute-start | bytes 98312 | tf_op jit(solution)/shard_map/ppermute | solution.py:607
  78.7 4.9 %collective-permute-start.25 = (bf16[128,128]{1,0:T(8,128)(2,1)S(1)}, bf16[128,128]{1,0:T(8,128)(2,1)S(1)}, u32[]{:S(2)}, u32[]{:S(2)}) collective-permute-start(bf16[128,128]{1,0:T(8,128)(2,1)S(1)} %get-tuple-element.155), channel_id=1, source_target_pairs={{0,3},{1,2},{2,1},{3,0},{4,7},{5,6},{6,5},{7,4},{8,13},{9,12},{10,... | collective-permute-start | bytes 98312 | tf_op jit(solution)/shard_map/ppermute | solution.py:607
  80.2 3.9 %collective-permute-start.26 = (bf16[128,128]{1,0:T(8,128)(2,1)S(1)}, bf16[128,128]{1,0:T(8,128)(2,1)S(1)}, u32[]{:S(2)}, u32[]{:S(2)}) collective-permute-start(bf16[128,128]{1,0:T(8,128)(2,1)S(1)} %get-tuple-element.156), channel_id=1, source_target_pairs={{0,2},{1,3},{2,0},{3,1},{4,6},{5,7},{6,4},{7,5},{8,14},{9,15},{10,... | collective-permute-start | bytes 98312 | tf_op jit(solution)/shard_map/ppermute | solution.py:607
  80.7 4.1 %collective-permute-start.27 = (bf16[128,128]{1,0:T(8,128)(2,1)S(1)}, bf16[128,128]{1,0:T(8,128)(2,1)S(1)}, u32[]{:S(2)}, u32[]{:S(2)}) collective-permute-start(bf16[128,128]{1,0:T(8,128)(2,1)S(1)} %get-tuple-element.157), channel_id=1, source_target_pairs={{0,1},{1,0},{2,3},{3,2},{4,5},{5,4},{6,7},{7,6},{8,12},{9,13},{10,... | collective-permute-start | bytes 98312 | tf_op jit(solution)/shard_map/ppermute | solution.py:607
  84.9 2.7 %collective-permute-start.28 = (bf16[4,128,128]{2,1,0:T(8,128)(2,1)S(1)}, bf16[4,128,128]{2,1,0:T(8,128)(2,1)S(1)}, u32[]{:S(2)}, u32[]{:S(2)}) collective-permute-start(bf16[4,128,128]{2,1,0:T(8,128)(2,1)S(1)} %pad_maximum_fusion.rest_0_), channel_id=1, source_target_pairs={{0,8},{8,0},{16,24},{24,16},{1,9},{9,1},{17,25},{25,17},{2,10},{10... | collective-permute-start | bytes 393224 | tf_op jit(solution)/shard_map/ppermute | solution.py:448
  90.1 5.4 %collective-permute-start.29 = (bf16[128,128]{1,0:T(8,128)(2,1)S(1)}, bf16[128,128]{1,0:T(8,128)(2,1)S(1)}, u32[]{:S(2)}, u32[]{:S(2)}) collective-permute-start(bf16[128,128]{1,0:T(8,128)(2,1)S(1)} %get-tuple-element.162), channel_id=1, source_target_pairs={{0,2},{1,3},{2,0},{3,1},{4,6},{5,7},{6,4},{7,5},{8,15},{9,14},{10,... | collective-permute-start | bytes 98312 | tf_op jit(solution)/shard_map/ppermute | solution.py:607
  92.0 4.8 %collective-permute-start.30 = (bf16[128,128]{1,0:T(8,128)(2,1)S(1)}, bf16[128,128]{1,0:T(8,128)(2,1)S(1)}, u32[]{:S(2)}, u32[]{:S(2)}) collective-permute-start(bf16[128,128]{1,0:T(8,128)(2,1)S(1)} %get-tuple-element.163), channel_id=1, source_target_pairs={{0,3},{1,2},{2,1},{3,0},{4,7},{5,6},{6,5},{7,4},{8,13},{9,12},{10,... | collective-permute-start | bytes 98312 | tf_op jit(solution)/shard_map/ppermute | solution.py:607
  92.7 4.2 %collective-permute-start.31 = (bf16[128,128]{1,0:T(8,128)(2,1)S(1)}, bf16[128,128]{1,0:T(8,128)(2,1)S(1)}, u32[]{:S(2)}, u32[]{:S(2)}) collective-permute-start(bf16[128,128]{1,0:T(8,128)(2,1)S(1)} %get-tuple-element.164), channel_id=1, source_target_pairs={{0,2},{1,3},{2,0},{3,1},{4,6},{5,7},{6,4},{7,5},{8,14},{9,15},{10,... | collective-permute-start | bytes 98312 | tf_op jit(solution)/shard_map/ppermute | solution.py:607
  94.0 3.9 %collective-permute-start.32 = (bf16[128,128]{1,0:T(8,128)(2,1)S(1)}, bf16[128,128]{1,0:T(8,128)(2,1)S(1)}, u32[]{:S(2)}, u32[]{:S(2)}) collective-permute-start(bf16[128,128]{1,0:T(8,128)(2,1)S(1)} %get-tuple-element.165), channel_id=1, source_target_pairs={{0,1},{1,0},{2,3},{3,2},{4,5},{5,4},{6,7},{7,6},{8,12},{9,13},{10,... | collective-permute-start | bytes 98312 | tf_op jit(solution)/shard_map/ppermute | solution.py:607
  98.0 2.6 %collective-permute-start.33 = (bf16[4,128,128]{2,1,0:T(8,128)(2,1)S(1)}, bf16[4,128,128]{2,1,0:T(8,128)(2,1)S(1)}, u32[]{:S(2)}, u32[]{:S(2)}) collective-permute-start(bf16[4,128,128]{2,1,0:T(8,128)(2,1)S(1)} %pad_maximum_fusion.1.rest_0_), channel_id=1, source_target_pairs={{0,8},{8,0},{16,24},{24,16},{1,9},{9,1},{17,25},{25,17},{2,10},{10... | collective-permute-start | bytes 393224 | tf_op jit(solution)/shard_map/ppermute | solution.py:448
  103.1 4.0 %collective-permute-start.34 = (bf16[128,128]{1,0:T(8,128)(2,1)S(1)}, bf16[128,128]{1,0:T(8,128)(2,1)S(1)}, u32[]{:S(2)}, u32[]{:S(2)}) collective-permute-start(bf16[128,128]{1,0:T(8,128)(2,1)S(1)} %get-tuple-element.168), channel_id=1, source_target_pairs={{0,2},{1,3},{2,0},{3,1},{4,6},{5,7},{6,4},{7,5},{8,15},{9,14},{10,... | collective-permute-start | bytes 98312 | tf_op jit(solution)/shard_map/ppermute | solution.py:607
  103.4 4.8 %collective-permute-start.35 = (bf16[128,128]{1,0:T(8,128)(2,1)S(1)}, bf16[128,128]{1,0:T(8,128)(2,1)S(1)}, u32[]{:S(2)}, u32[]{:S(2)}) collective-permute-start(bf16[128,128]{1,0:T(8,128)(2,1)S(1)} %get-tuple-element.169), channel_id=1, source_target_pairs={{0,3},{1,2},{2,1},{3,0},{4,7},{5,6},{6,5},{7,4},{8,13},{9,12},{10,... | collective-permute-start | bytes 98312 | tf_op jit(solution)/shard_map/ppermute | solution.py:607
  105.3 3.9 %collective-permute-start.36 = (bf16[128,128]{1,0:T(8,128)(2,1)S(1)}, bf16[128,128]{1,0:T(8,128)(2,1)S(1)}, u32[]{:S(2)}, u32[]{:S(2)}) collective-permute-start(bf16[128,128]{1,0:T(8,128)(2,1)S(1)} %get-tuple-element.170), channel_id=1, source_target_pairs={{0,2},{1,3},{2,0},{3,1},{4,6},{5,7},{6,4},{7,5},{8,14},{9,15},{10,... | collective-permute-start | bytes 98312 | tf_op jit(solution)/shard_map/ppermute | solution.py:607
  106.3 4.2 %collective-permute-start.37 = (bf16[128,128]{1,0:T(8,128)(2,1)S(1)}, bf16[128,128]{1,0:T(8,128)(2,1)S(1)}, u32[]{:S(2)}, u32[]{:S(2)}) collective-permute-start(bf16[128,128]{1,0:T(8,128)(2,1)S(1)} %get-tuple-element.171), channel_id=1, source_target_pairs={{0,1},{1,0},{2,3},{3,2},{4,5},{5,4},{6,7},{7,6},{8,12},{9,13},{10,... | collective-permute-start | bytes 98312 | tf_op jit(solution)/shard_map/ppermute | solution.py:607
  (12 other events, 25.2 us)

commit v6 on v5

--- a/solution.py
+++ b/solution.py
@@ -248,8 +248,8 @@
                 if position:
                     gram_ref[row, aligned(k, block), aligned(l, block)] = high.T
                 else:
-                    lows = read_part(parts, mine, (i, pl.ds(slots // 2 * block, 1)))
-                    low_ref[row, pl.ds(k, 1)] = low_diagonal(value, high) + lows
+                    lows = read_part(parts, mine, (i, pl.ds(slots // 2 * block, 16)))
+                    low_ref[row, pl.ds(k, 1)] = low_diagonal(value, high) + lows[:1]
 
 
 def gather_own_kernel(slots, table_ref, *rest):
@@ -269,8 +269,8 @@
             high = value.astype(jnp.bfloat16)
             sum_ref[a, b] = high
             if a == b:
-                lows = read_part(parts, core == maker, (i, slice(block, block + 1)))
-                row_ref[a : a + 1] = low_diagonal(value, high) + lows
+                lows = read_part(parts, core == maker, (i, slice(block, block + 16)))
+                row_ref[a : a + 1] = low_diagonal(value, high) + lows[:1]
             else:
                 sum_ref[b, a] = high.T
 
@@ -412,18 +412,26 @@
 
 
 def last_kernel(count, scale, table_ref, stepped_ref, *rest):
-    *in_refs, next_ref, all_ref = rest
+    *in_refs, out_ref, all_ref, row_ref, sems = rest
     block_rows, slots, block, _ = stepped_ref.shape
     here = Pattern(table_ref, block_rows, slots)
     if count > 1:
         receive(in_refs, all_ref)
 
+    def copy(j):
+        return pltpu.make_async_copy(row_ref.at[j], out_ref.at[j], sems.at[j])
+
     @pl.loop(0, block_rows)
     def _(j):
         def put(k, value):
-            next_ref[j, k] = value
+            row_ref[j, k] = value
 
         next_omega(here, j, scale, stepped_ref, all_ref if count > 1 else in_refs[0], put)
+        copy(j).start()
+
+    @pl.loop(0, block_rows)
+    def _(j):
+        copy(j).wait()
 
 
 def call(kernel, inputs, outs, scratch, smem=1, left=(), sems=(), out_space=VMEM):
@@ -635,7 +643,9 @@
         functools.partial(last_kernel, len(mirrored), scale),
         (table, stepped, *mirrored),
         [blocks],
-        [all_in],
+        [all_in, pltpu.VMEM(precision.shape, f32)],
+        sems=[pltpu.SemaphoreType.DMA((block_rows,))],
+        out_space=pl.BlockSpec(memory_space=pl.ANY),
     )
     return updated
 

time: 114 us -> 114 us (level)
  Pallas kernels: 37.9 us -> 35.7 us
    pallas_call x14, Pallas kernels: 37.9 us -> 35.7 us  [call(): pl.pallas_call(kernel, out_shape=outs, in_specs=specs, out_specs=[out_spa...]
  transfers between devices with their start and end apart: 39 -> 39, of which waited for: 21 -> 19; matrix products, arithmetic and copies ran while one was open for 1% -> 1% of each run, Pallas kernels for 20% -> 19%
where the time goes in v6:
time: 114 us
  waiting for transfers between devices  37.6 us (33%)
  starting transfers between devices  36.1 us (32%)
  Pallas kernels  35.7 us (31%)
  local copies, waits for them, and re-layouts  3.23 us (3%)
    pallas_call x14, Pallas kernels, call(): pl.pallas_call(kernel, out_shape=outs, in_specs=specs, out_specs=[out_spa...  35.7 us
    ppermute x7, waiting for transfers between devices, exchange(): return lax.ppermute(x, 'feat', [(i, i ^ r) for i in range(peers)])  15.2 us
    ppermute x12, starting transfers between devices, trade(): got.append(lax.ppermute(x, ('samp', 'feat'), pairs))  13.4 us
    ppermute x7, starting transfers between devices, exchange(): return lax.ppermute(x, 'feat', [(i, i ^ r) for i in range(peers)])  13.3 us
    ppermute x20, waiting for transfers between devices, swap(): return lax.ppermute(x, 'samp', [(i, i ^ bit) for i in range(count)])  12.9 us
    ppermute x12, waiting for transfers between devices, trade(): got.append(lax.ppermute(x, ('samp', 'feat'), pairs))  9.51 us
    ppermute x20, starting transfers between devices, swap(): return lax.ppermute(x, 'samp', [(i, i ^ bit) for i in range(count)])  9.36 us
  transfers between devices with their start and end apart: 39, of which 19 were waited for; matrix products, arithmetic and copies ran while one was open for 1% of the time, Pallas kernels for 19%

profile of v6, /device:TPU:0, one launch (start us, length us, event | category | flops | bytes accessed | tf_op | source)
XLA Modules:
  0.0 113.8 jit_solution(7953693738750905040)
XLA Ops:
  3.0 2.6 %collective-permute-start.7 = (bf16[128,1024]{1,0:T(8,128)(2,1)S(1)}, bf16[128,1024]{1,0:T(8,128)(2,1)S(1)}, u32[]{:S(2)}, u32[]{:S(2)}) collective-permute-start(bf16[128,1024]{1,0:T(8,128)(2,1)S(1)} %get-tuple-element.126), channel_id=1, source_target_pairs={{0,1},{1,0},{2,3},{3,2},{4,5},{5,4},{6,7},{7,6},{8,9},{9,8},{10,11... | collective-permute-start | bytes 786440 | tf_op jit(solution)/shard_map/ppermute | solution.py:502
  5.6 1.6 %collective-permute-start.8 = (bf16[128,1024]{1,0:T(8,128)(2,1)S(1)}, bf16[128,1024]{1,0:T(8,128)(2,1)S(1)}, u32[]{:S(2)}, u32[]{:S(2)}) collective-permute-start(bf16[128,1024]{1,0:T(8,128)(2,1)S(1)} %get-tuple-element.127), channel_id=1, source_target_pairs={{0,2},{1,3},{2,0},{3,1},{4,6},{5,7},{6,4},{7,5},{8,10},{9,11},{10,... | collective-permute-start | bytes 786440 | tf_op jit(solution)/shard_map/ppermute | solution.py:502
  7.1 2.6 %collective-permute-start.10 = (bf16[128,1024]{1,0:T(8,128)(2,1)S(1)}, bf16[128,1024]{1,0:T(8,128)(2,1)}, u32[]{:S(2)}, u32[]{:S(2)}) collective-permute-start(bf16[128,1024]{1,0:T(8,128)(2,1)S(1)} %get-tuple-element.130), channel_id=1, source_target_pairs={{0,4},{1,5},{2,6},{3,7},{4,0},{5,1},{6,2},{7,3},{8,12},{9,13},{10,... | collective-permute-start | bytes 786440 | tf_op jit(solution)/shard_map/ppermute | solution.py:502
  13.3 4.5 %conditional.3 = (bf16[5,144,128]{2,1,0:T(8,128)(2,1)}, s32[8,24]{1,0:T(8,128)S(1)}) conditional(s32[]{:T(128)} %convert_element_type.7, () %tuple.44, (bf16[4,128,1024]{2,1,0:T(8,128)(2,1)S(1)}, bf16[4,128,1024]{2,1,0:T(8,128)(2,1)}, s32[4,6]{1,0:T(4,128)}) %tuple.45), branch_computations={%region_0.0_spmd, %region_1.0_spmd} | conditional | flops 2 | bytes 185110 | solution.py:475
  13.3 2.8 %branch_1_fun.4 = bf16[5,144,128]{2,1,0:T(8,128)(2,1)} custom-call(bf16[4,128,1024]{2,1,0:T(8,128)(2,1)S(1)} %get-tuple-element.47.mine_ref, bf16[4,128,1024]{2,1,0:T(8,128)(2,1)} %get-tuple-element.48.other_ref), custom_call_target="tpu_custom_call" | custom-call | flops 1 | bytes 1 | tf_op jit(solution)/shard_map/cond/branch_1_fun/pallas_call | solution.py:443
  16.1 1.7 %branch_1_fun.5 = s32[8,24]{1,0:T(8,128)S(1)} custom-call(s32[4,6]{1,0:T(4,128)S(1)} %copy-done.4), custom_call_target="tpu_custom_call" | custom-call | flops 1 | bytes 1 | tf_op jit(solution)/shard_map/cond/branch_1_fun/pallas_call | solution.py:443
  17.9 2.3 %collective-permute-done.8.rest_1_ = bf16[128,1024]{1,0:T(8,128)(2,1)S(1)} collective-permute-done((bf16[128,1024]{1,0:T(8,128)(2,1)S(1)}, bf16[128,1024]{1,0:T(8,128)(2,1)S(1)}, u32[]{:S(2)}, u32[]{:S(2)}) %collective-permute-start.8) | collective-permute-done | bytes 262176 | tf_op jit(solution)/shard_map/ppermute | solution.py:502
  20.2 12.9 %collective-permute-done.11.rest_4_ = bf16[128,1024]{1,0:T(8,128)(2,1)} collective-permute-done((bf16[128,1024]{1,0:T(8,128)(2,1)S(1)}, bf16[128,1024]{1,0:T(8,128)(2,1)}, u32[]{:S(2)}, u32[]{:S(2)}) %collective-permute-start.11) | collective-permute-done | bytes 262176 | tf_op jit(solution)/shard_map/ppermute | solution.py:502
  33.6 3.5 %collective-permute-start.18 = (bf16[128,1024]{1,0:T(8,128)(2,1)S(1)}, bf16[128,1024]{1,0:T(8,128)(2,1)S(1)}, u32[]{:S(2)}, u32[]{:S(2)}) collective-permute-start(bf16[128,1024]{1,0:T(8,128)(2,1)S(1)} %get-tuple-element.141), channel_id=1, source_target_pairs={{0,7},{1,6},{2,5},{3,4},{4,3},{5,2},{6,1},{7,0},{8,15},{9,14},{10,... | collective-permute-start | bytes 786440 | tf_op jit(solution)/shard_map/ppermute | solution.py:502
  39.3 21.9 %conditional.4 = (bf16[4,768,768]{2,1,0:T(8,128)(2,1)}, f32[4,8,128]{2,1,0:T(8,128)}, bf16[5,400,128]{2,1,0:T(8,128)(2,1)}, bf16[5,400,128]{2,1,0:T(8,128)(2,1)}...) conditional(s32[]{:T(128)} %convert_element_type.7, () %tuple.46, (pred[]{:T(512)}, ...), branch_computations={%region_2.0_spmd, %region_3.0_spmd} | conditional | flops 3 | bytes 11616524 | solution.py:475
  39.3 1.5 %collective-permute-start.2 = (bf16[5,144,128]{2,1,0:T(8,128)(2,1)}, bf16[5,144,128]{2,1,0:T(8,128)(2,1)}, u32[]{:S(2)}, u32[]{:S(2)}) collective-permute-start(bf16[5,144,128]{2,1,0:T(8,128)(2,1)} %get-tuple-element.54), channel_id=1, source_target_pairs={{0,16},{8,24},{16,0},{24,8},{1,17},{9,25},{17,1},{25,9},{2,18},{10... | collective-permute-start | bytes 552968 | tf_op jit(solution)/shard_map/cond/branch_1_fun/ppermute | solution.py:456
  40.8 4.6 %branch_1_fun.7 = bf16[5,400,128]{2,1,0:T(8,128)(2,1)} custom-call(s32[8,24]{1,0:T(8,128)S(1)} %get-tuple-element.55.table_ref, bf16[4,128,1024]{2,1,0:T(8,128)(2,1)S(1)} %get-tuple-element.56.mine_ref, bf16[4,128,1024]{2,1,0:T(8,128)(2,1)} %get-tuple-element.57.other_ref, bf16[128,1024]{1,0:T(8,128)(2,1)S(1)} %get-tuple-element.58.rest_0_, ...), custom_call_target="tpu_custom_call" | custom-call | flops 1 | bytes 1 | tf_op jit(solution)/shard_map/cond/branch_1_fun/pallas_call | solution.py:443
  46.0 1.5 %collective-permute-start.3 = (bf16[5,400,128]{2,1,0:T(8,128)(2,1)}, bf16[5,400,128]{2,1,0:T(8,128)(2,1)}, u32[]{:S(2)}, u32[]{:S(2)}) collective-permute-start(bf16[5,400,128]{2,1,0:T(8,128)(2,1)} %branch_1_fun.7), channel_id=1, source_target_pairs={{0,16},{8,24},{16,0},{24,8},{1,17},{9,25},{17,1},{25,9},{2,18},{10... | collective-permute-start | bytes 1536008 | tf_op jit(solution)/shard_map/cond/branch_1_fun/ppermute | solution.py:456
  47.6 6.3 %conditional = ((bf16[4,768,768]{2,1,0:T(8,128)(2,1)}, f32[4,8,128]{2,1,0:T(8,128)})) conditional(s32[]{:T(128)} %convert_element_type.1, () %tuple.21, (bf16[5,144,128]{2,1,0:T(8,128)(2,1)}, bf16[5,144,128]{2,1,0:T(8,128)(2,1)}, s32[8,24]{1,0:T(8,128)S(1)}) %tuple.24), branch_computations={%region_4.0_spmd, %region_5.0_spmd} | conditional | flops 1 | bytes 4735006 | solution.py:475
  49.5 4.4 %branch_1_fun.6 = (bf16[4,768,768]{2,1,0:T(8,128)(2,1)}, f32[4,8,128]{2,1,0:T(8,128)}) custom-call(s32[8,24]{1,0:T(8,128)S(1)} %get-tuple-element.50.table_ref, bf16[5,144,128]{2,1,0:T(8,128)(2,1)} %get-tuple-element.51.rest_0_, bf16[5,144,128]{2,1,0:T(8,128)(2,1)} %get-tuple-element.52.rest_1_, bf16[5,144,128]{2,1,0:T(8,128)(2,1)S(1)} %collective-permute-done.rest_2_, ...), custom_call_target="tpu_custom_call" | custom-call | flops 1 | bytes 1 | tf_op jit(solution)/shard_map/cond/branch_1_fun/cond/branch_1_fun/pallas_call | solution.py:443
  54.1 4.8 %collective-permute-done.3 = bf16[5,400,128]{2,1,0:T(8,128)(2,1)} collective-permute-done((bf16[5,400,128]{2,1,0:T(8,128)(2,1)}, bf16[5,400,128]{2,1,0:T(8,128)(2,1)}, u32[]{:S(2)}, u32[]{:S(2)}) %collective-permute-start.3) | collective-permute-done | bytes 512032 | tf_op jit(solution)/shard_map/cond/branch_1_fun/ppermute | solution.py:456
  58.9 2.2 %collective-permute-done.5 = bf16[5,400,128]{2,1,0:T(8,128)(2,1)} collective-permute-done((bf16[5,400,128]{2,1,0:T(8,128)(2,1)}, bf16[5,400,128]{2,1,0:T(8,128)(2,1)}, u32[]{:S(2)}, u32[]{:S(2)}) %collective-permute-start.5) | collective-permute-done | bytes 512032 | tf_op jit(solution)/shard_map/cond/branch_1_fun/ppermute | solution.py:456
  63.1 2.6 %shard_map.38.rest_0_ = bf16[2,400,128]{2,1,0:T(8,128)(2,1)S(1)} custom-call(s32[8,24]{1,0:T(8,128)S(1)} %get-tuple-element.124.table_ref, bf16[4,128,1024]{2,1,0:T(8,128)(2,1)S(1)} %get-tuple-element.123.mine_ref, bf16[4,128,1024]{2,1,0:T(8,128)(2,1)} %collective-permute-done.6.other_ref, bf16[128,1024]{1,0:T(8,128)(2,1)S(1)} %collective-permute-done.7.rest_0_, ...), custom_call_target="tpu_custom_call" | custom-call | flops 1 | bytes 1 | tf_op jit(solution)/shard_map/pallas_call | solution.py:443
  65.7 1.6 %collective-permute-start.21 = (bf16[2,400,128]{2,1,0:T(8,128)(2,1)S(1)}, bf16[2,400,128]{2,1,0:T(8,128)(2,1)S(1)}, u32[]{:S(2)}, u32[]{:S(2)}) collective-permute-start(bf16[2,400,128]{2,1,0:T(8,128)(2,1)S(1)} %shard_map.38.rest_0_), channel_id=1, source_target_pairs={{0,16},{8,24},{16,0},{24,8},{1,17},{9,25},{17,1},{25,9},{2,18},{10... | collective-permute-start | bytes 614408 | tf_op jit(solution)/shard_map/ppermute | solution.py:456
  67.3 4.6 %shard_map.39 = (bf16[4,768,768]{2,1,0:T(8,128)(2,1)S(1)}, f32[4,8,128]{2,1,0:T(8,128)S(1)}) custom-call(s32[8,24]{1,0:T(8,128)S(1)} %get-tuple-element.124.table_ref, bf16[4,768,768]{2,1,0:T(8,128)(2,1)} %get-tuple-element.144.gram_in_ref, f32[4,8,128]{2,1,0:T(8,128)} %get-tuple-element.145.low_in_ref, bf16[5,400,128]{2,1,0:T(8,128)(2,1)} %get-tuple-element.146.rest_0_, ...), custom_call_target="tpu_custom_call" | custom-call | flops 1 | bytes 1 | tf_op jit(solution)/shard_map/pallas_call | solution.py:443
  72.9 1.4 %collective-permute-done.23.rest_3_ = bf16[2,400,128]{2,1,0:T(8,128)(2,1)S(1)} collective-permute-done((bf16[2,400,128]{2,1,0:T(8,128)(2,1)S(1)}, bf16[2,400,128]{2,1,0:T(8,128)(2,1)S(1)}, u32[]{:S(2)}, u32[]{:S(2)}) %collective-permute-start.23) | collective-permute-done | bytes 204832 | tf_op jit(solution)/shard_map/ppermute | solution.py:456
  74.3 2.8 %shard_map.40 = (bf16[4,768,768]{2,1,0:T(8,128)(2,1)S(1)}, f32[4,8,128]{2,1,0:T(8,128)S(1)}, f32[4,128,896]{2,1,0:T(8,128)S(1)}, bf16[128,128]{1,0:T(8,128)(2,1)...) custom-call(s32[8,24]{1,0:T(8,128)S(1)} %get-tuple-element.124.table_ref, ...), custom_call_target="tpu_custom_call" | custom-call | flops 1 | bytes 1 | tf_op jit(solution)/shard_map/pallas_call | solution.py:443
  77.2 3.6 %collective-permute-start.25 = (bf16[128,128]{1,0:T(8,128)(2,1)S(1)}, bf16[128,128]{1,0:T(8,128)(2,1)S(1)}, u32[]{:S(2)}, u32[]{:S(2)}) collective-permute-start(bf16[128,128]{1,0:T(8,128)(2,1)S(1)} %get-tuple-element.155), channel_id=1, source_target_pairs={{0,3},{1,2},{2,1},{3,0},{4,7},{5,6},{6,5},{7,4},{8,13},{9,12},{10,... | collective-permute-start | bytes 98312 | tf_op jit(solution)/shard_map/ppermute | solution.py:615
  81.4 2.0 %collective-permute-done.25 = bf16[128,128]{1,0:T(8,128)(2,1)S(1)} collective-permute-done((bf16[128,128]{1,0:T(8,128)(2,1)S(1)}, bf16[128,128]{1,0:T(8,128)(2,1)S(1)}, u32[]{:S(2)}, u32[]{:S(2)}) %collective-permute-start.25) | collective-permute-done | bytes 32800 | tf_op jit(solution)/shard_map/ppermute | solution.py:615
  87.3 2.5 %shard_map.42 = (f32[4,6,128,128]{3,2,1,0:T(8,128)S(1)}, f32[4,128,896]{2,1,0:T(8,128)S(1)}, bf16[128,128]{1,0:T(8,128)(2,1)S(1)}, bf16[128,128]{1,0:T(8,128)(2,...) custom-call(s32[8,24]{1,0:T(8,128)S(1)} %get-tuple-element.124.table_ref, ...), custom_call_target="tpu_custom_call" | custom-call | flops 1 | bytes 1 | tf_op jit(solution)/shard_map/pallas_call | solution.py:443
  92.3 1.7 %collective-permute-start.31 = (bf16[128,128]{1,0:T(8,128)(2,1)S(1)}, bf16[128,128]{1,0:T(8,128)(2,1)S(1)}, u32[]{:S(2)}, u32[]{:S(2)}) collective-permute-start(bf16[128,128]{1,0:T(8,128)(2,1)S(1)} %get-tuple-element.164), channel_id=1, source_target_pairs={{0,2},{1,3},{2,0},{3,1},{4,6},{5,7},{6,4},{7,5},{8,14},{9,15},{10,... | collective-permute-start | bytes 98312 | tf_op jit(solution)/shard_map/ppermute | solution.py:615
  96.3 1.6 %collective-permute-done.32 = bf16[128,128]{1,0:T(8,128)(2,1)S(1)} collective-permute-done((bf16[128,128]{1,0:T(8,128)(2,1)S(1)}, bf16[128,128]{1,0:T(8,128)(2,1)S(1)}, u32[]{:S(2)}, u32[]{:S(2)}) %collective-permute-start.32) | collective-permute-done | bytes 32800 | tf_op jit(solution)/shard_map/ppermute | solution.py:615
  99.8 2.5 %shard_map.44 = (f32[4,6,128,128]{3,2,1,0:T(8,128)S(1)}, f32[4,128,896]{2,1,0:T(8,128)S(1)}, bf16[128,128]{1,0:T(8,128)(2,1)S(1)}, bf16[128,128]{1,0:T(8,128)(2,...) custom-call(s32[8,24]{1,0:T(8,128)S(1)} %get-tuple-element.124.table_ref, ...), custom_call_target="tpu_custom_call" | custom-call | flops 1 | bytes 1 | tf_op jit(solution)/shard_map/pallas_call | solution.py:443
  103.3 1.9 %collective-permute-start.35 = (bf16[128,128]{1,0:T(8,128)(2,1)S(1)}, bf16[128,128]{1,0:T(8,128)(2,1)S(1)}, u32[]{:S(2)}, u32[]{:S(2)}) collective-permute-start(bf16[128,128]{1,0:T(8,128)(2,1)S(1)} %get-tuple-element.169), channel_id=1, source_target_pairs={{0,3},{1,2},{2,1},{3,0},{4,7},{5,6},{6,5},{7,4},{8,13},{9,12},{10,... | collective-permute-start | bytes 98312 | tf_op jit(solution)/shard_map/ppermute | solution.py:615
  105.4 1.5 %collective-permute-start.37 = (bf16[128,128]{1,0:T(8,128)(2,1)S(1)}, bf16[128,128]{1,0:T(8,128)(2,1)S(1)}, u32[]{:S(2)}, u32[]{:S(2)}) collective-permute-start(bf16[128,128]{1,0:T(8,128)(2,1)S(1)} %get-tuple-element.171), channel_id=1, source_target_pairs={{0,1},{1,0},{2,3},{3,2},{4,5},{5,4},{6,7},{7,6},{8,12},{9,13},{10,... | collective-permute-start | bytes 98312 | tf_op jit(solution)/shard_map/ppermute | solution.py:615
  106.8 1.7 %collective-permute-done.35 = bf16[128,128]{1,0:T(8,128)(2,1)S(1)} collective-permute-done((bf16[128,128]{1,0:T(8,128)(2,1)S(1)}, bf16[128,128]{1,0:T(8,128)(2,1)S(1)}, u32[]{:S(2)}, u32[]{:S(2)}) %collective-permute-start.35) | collective-permute-done | bytes 32800 | tf_op jit(solution)/shard_map/ppermute | solution.py:615
  111.7 1.9 %shard_map.46 = f32[4,6,128,128]{3,2,1,0:T(8,128)} custom-call(s32[8,24]{1,0:T(8,128)S(1)} %get-tuple-element.124.table_ref, f32[4,6,128,128]{3,2,1,0:T(8,128)S(1)} %shard_map.45.stepped_ref, bf16[4,128,128]{2,1,0:T(8,128)(2,1)S(1)} %pad_maximum_fusion.2.rest_0_, bf16[4,128,128]{2,1,0:T(8,128)(2,1)S(1)} %collective-permute-done.38.rest_1_), custom_call_target="tpu_custom_call" | custom-call | flops 1 | bytes 1 | tf_op jit(solution)/shard_map/pallas_call | solution.py:443
  (77 shorter events, 29.7 us)
Async XLA Ops:
  2.5 9.4 %collective-permute-start.6 = (bf16[4,128,1024]{2,1,0:T(8,128)(2,1)S(1)}, bf16[4,128,1024]{2,1,0:T(8,128)(2,1)}, u32[]{:S(2)}, u32[]{:S(2)}) collective-permute-start(bf16[4,128,1024]{2,1,0:T(8,128)(2,1)S(1)} %get-tuple-element.123.mine_ref), channel_id=1, source_target_pairs={{0,8},{8,0},{16,24},{24,16},{1,9},{9,1},{17,25},{25,17},{2,10},{10... | collective-permute-start | bytes 3145736 | tf_op jit(solution)/shard_map/ppermute | solution.py:456
  3.0 14.8 %collective-permute-start.7 = (bf16[128,1024]{1,0:T(8,128)(2,1)S(1)}, bf16[128,1024]{1,0:T(8,128)(2,1)S(1)}, u32[]{:S(2)}, u32[]{:S(2)}) collective-permute-start(bf16[128,1024]{1,0:T(8,128)(2,1)S(1)} %get-tuple-element.126), channel_id=1, source_target_pairs={{0,1},{1,0},{2,3},{3,2},{4,5},{5,4},{6,7},{7,6},{8,9},{9,8},{10,11... | collective-permute-start | bytes 786440 | tf_op jit(solution)/shard_map/ppermute | solution.py:502
  5.6 14.7 %collective-permute-start.8 = (bf16[128,1024]{1,0:T(8,128)(2,1)S(1)}, bf16[128,1024]{1,0:T(8,128)(2,1)S(1)}, u32[]{:S(2)}, u32[]{:S(2)}) collective-permute-start(bf16[128,1024]{1,0:T(8,128)(2,1)S(1)} %get-tuple-element.127), channel_id=1, source_target_pairs={{0,2},{1,3},{2,0},{3,1},{4,6},{5,7},{6,4},{7,5},{8,10},{9,11},{10,... | collective-permute-start | bytes 786440 | tf_op jit(solution)/shard_map/ppermute | solution.py:502
  7.1 26.0 %collective-permute-start.10 = (bf16[128,1024]{1,0:T(8,128)(2,1)S(1)}, bf16[128,1024]{1,0:T(8,128)(2,1)}, u32[]{:S(2)}, u32[]{:S(2)}) collective-permute-start(bf16[128,1024]{1,0:T(8,128)(2,1)S(1)} %get-tuple-element.130), channel_id=1, source_target_pairs={{0,4},{1,5},{2,6},{3,7},{4,0},{5,1},{6,2},{7,3},{8,12},{9,13},{10,... | collective-permute-start | bytes 786440 | tf_op jit(solution)/shard_map/ppermute | solution.py:502
  9.7 23.4 %collective-permute-start.11 = (bf16[128,1024]{1,0:T(8,128)(2,1)S(1)}, bf16[128,1024]{1,0:T(8,128)(2,1)}, u32[]{:S(2)}, u32[]{:S(2)}) collective-permute-start(bf16[128,1024]{1,0:T(8,128)(2,1)S(1)} %get-tuple-element.131), channel_id=1, source_target_pairs={{0,5},{1,4},{2,7},{3,6},{4,1},{5,0},{6,3},{7,2},{8,13},{9,12},{10,... | collective-permute-start | bytes 786440 | tf_op jit(solution)/shard_map/ppermute | solution.py:502
  11.9 21.7 %collective-permute-start.9 = (bf16[128,1024]{1,0:T(8,128)(2,1)S(1)}, bf16[128,1024]{1,0:T(8,128)(2,1)}, u32[]{:S(2)}, u32[]{:S(2)}) collective-permute-start(bf16[128,1024]{1,0:T(8,128)(2,1)S(1)} %get-tuple-element.129), channel_id=1, source_target_pairs={{0,3},{1,2},{2,1},{3,0},{4,7},{5,6},{6,5},{7,4},{8,11},{9,10},{10,... | collective-permute-start | bytes 786440 | tf_op jit(solution)/shard_map/ppermute | solution.py:502
  17.8 15.8 %collective-permute-start.12 = (bf16[128,1024]{1,0:T(8,128)(2,1)S(1)}, bf16[128,1024]{1,0:T(8,128)(2,1)S(1)}, u32[]{:S(2)}, u32[]{:S(2)}) collective-permute-start(bf16[128,1024]{1,0:T(8,128)(2,1)S(1)} %collective-permute-done.7.rest_0_), channel_id=1, source_target_pairs={{0,8},{8,0},{16,24},{24,16},{1,9},{9,1},{17,25},{25,17},{2,10},{10... | collective-permute-start | bytes 786440 | tf_op jit(solution)/shard_map/ppermute | solution.py:456
  20.2 16.9 %collective-permute-start.13 = (bf16[128,1024]{1,0:T(8,128)(2,1)S(1)}, bf16[128,1024]{1,0:T(8,128)(2,1)S(1)}, u32[]{:S(2)}, u32[]{:S(2)}) collective-permute-start(bf16[128,1024]{1,0:T(8,128)(2,1)S(1)} %collective-permute-done.8.rest_1_), channel_id=1, source_target_pairs={{0,8},{8,0},{16,24},{24,16},{1,9},{9,1},{17,25},{25,17},{2,10},{10... | collective-permute-start | bytes 786440 | tf_op jit(solution)/shard_map/ppermute | solution.py:456
  33.1 5.4 %collective-permute-start.15 = (bf16[128,1024]{1,0:T(8,128)(2,1)}, bf16[128,1024]{1,0:T(8,128)(2,1)S(1)}, u32[]{:S(2)}, u32[]{:S(2)}) collective-permute-start(bf16[128,1024]{1,0:T(8,128)(2,1)} %collective-permute-done.10.rest_3_), channel_id=1, source_target_pairs={{0,8},{8,0},{16,24},{24,16},{1,9},{9,1},{17,25},{25,17},{2,10},{10... | collective-permute-start | bytes 786440 | tf_op jit(solution)/shard_map/ppermute | solution.py:456
  33.1 5.4 %collective-permute-start.16 = (bf16[128,1024]{1,0:T(8,128)(2,1)}, bf16[128,1024]{1,0:T(8,128)(2,1)S(1)}, u32[]{:S(2)}, u32[]{:S(2)}) collective-permute-start(bf16[128,1024]{1,0:T(8,128)(2,1)} %collective-permute-done.11.rest_4_), channel_id=1, source_target_pairs={{0,8},{8,0},{16,24},{24,16},{1,9},{9,1},{17,25},{25,17},{2,10},{10... | collective-permute-start | bytes 786440 | tf_op jit(solution)/shard_map/ppermute | solution.py:456
  33.6 4.8 %collective-permute-start.14 = (bf16[128,1024]{1,0:T(8,128)(2,1)}, bf16[128,1024]{1,0:T(8,128)(2,1)S(1)}, u32[]{:S(2)}, u32[]{:S(2)}) collective-permute-start(bf16[128,1024]{1,0:T(8,128)(2,1)} %collective-permute-done.9.rest_2_), channel_id=1, source_target_pairs={{0,8},{8,0},{16,24},{24,16},{1,9},{9,1},{17,25},{25,17},{2,10},{10... | collective-permute-start | bytes 786440 | tf_op jit(solution)/shard_map/ppermute | solution.py:456
  33.6 27.5 %collective-permute-start.18 = (bf16[128,1024]{1,0:T(8,128)(2,1)S(1)}, bf16[128,1024]{1,0:T(8,128)(2,1)S(1)}, u32[]{:S(2)}, u32[]{:S(2)}) collective-permute-start(bf16[128,1024]{1,0:T(8,128)(2,1)S(1)} %get-tuple-element.141), channel_id=1, source_target_pairs={{0,7},{1,6},{2,5},{3,4},{4,3},{5,2},{6,1},{7,0},{8,15},{9,14},{10,... | collective-permute-start | bytes 786440 | tf_op jit(solution)/shard_map/ppermute | solution.py:502
  37.1 24.1 %collective-permute-start.17 = (bf16[128,1024]{1,0:T(8,128)(2,1)S(1)}, bf16[128,1024]{1,0:T(8,128)(2,1)S(1)}, u32[]{:S(2)}, u32[]{:S(2)}) collective-permute-start(bf16[128,1024]{1,0:T(8,128)(2,1)S(1)} %get-tuple-element.139), channel_id=1, source_target_pairs={{0,6},{1,7},{2,4},{3,5},{4,2},{5,3},{6,0},{7,1},{8,14},{9,15},{10,... | collective-permute-start | bytes 786440 | tf_op jit(solution)/shard_map/ppermute | solution.py:502
  39.3 6.7 %collective-permute-start.2 = (bf16[5,144,128]{2,1,0:T(8,128)(2,1)}, bf16[5,144,128]{2,1,0:T(8,128)(2,1)}, u32[]{:S(2)}, u32[]{:S(2)}) collective-permute-start(bf16[5,144,128]{2,1,0:T(8,128)(2,1)} %get-tuple-element.54), channel_id=1, source_target_pairs={{0,16},{8,24},{16,0},{24,8},{1,17},{9,25},{17,1},{25,9},{2,18},{10... | collective-permute-start | bytes 552968 | tf_op jit(solution)/shard_map/cond/branch_1_fun/ppermute | solution.py:456
  46.0 12.9 %collective-permute-start.3 = (bf16[5,400,128]{2,1,0:T(8,128)(2,1)}, bf16[5,400,128]{2,1,0:T(8,128)(2,1)}, u32[]{:S(2)}, u32[]{:S(2)}) collective-permute-start(bf16[5,400,128]{2,1,0:T(8,128)(2,1)} %branch_1_fun.7), channel_id=1, source_target_pairs={{0,16},{8,24},{16,0},{24,8},{1,17},{9,25},{17,1},{25,9},{2,18},{10... | collective-permute-start | bytes 1536008 | tf_op jit(solution)/shard_map/cond/branch_1_fun/ppermute | solution.py:456
  53.9 5.1 %collective-permute-start.4 = (bf16[5,400,128]{2,1,0:T(8,128)(2,1)}, bf16[5,400,128]{2,1,0:T(8,128)(2,1)}, u32[]{:S(2)}, u32[]{:S(2)}) collective-permute-start(bf16[5,400,128]{2,1,0:T(8,128)(2,1)} %branch_1_fun.7), channel_id=1, source_target_pairs={{0,8},{8,0},{16,24},{24,16},{1,9},{9,1},{17,25},{25,17},{2,10},{10... | collective-permute-start | bytes 1536008 | tf_op jit(solution)/shard_map/cond/branch_1_fun/ppermute | solution.py:456
  58.9 2.2 %collective-permute-start.5 = (bf16[5,400,128]{2,1,0:T(8,128)(2,1)}, bf16[5,400,128]{2,1,0:T(8,128)(2,1)}, u32[]{:S(2)}, u32[]{:S(2)}) collective-permute-start(bf16[5,400,128]{2,1,0:T(8,128)(2,1)} %collective-permute-done.3), channel_id=1, source_target_pairs={{0,8},{8,0},{16,24},{24,16},{1,9},{9,1},{17,25},{25,17},{2,10},{10... | collective-permute-start | bytes 1536008 | tf_op jit(solution)/shard_map/cond/branch_1_fun/ppermute | solution.py:456
  65.7 7.2 %collective-permute-start.21 = (bf16[2,400,128]{2,1,0:T(8,128)(2,1)S(1)}, bf16[2,400,128]{2,1,0:T(8,128)(2,1)S(1)}, u32[]{:S(2)}, u32[]{:S(2)}) collective-permute-start(bf16[2,400,128]{2,1,0:T(8,128)(2,1)S(1)} %shard_map.38.rest_0_), channel_id=1, source_target_pairs={{0,16},{8,24},{16,0},{24,8},{1,17},{9,25},{17,1},{25,9},{2,18},{10... | collective-permute-start | bytes 614408 | tf_op jit(solution)/shard_map/ppermute | solution.py:456
  67.3 5.6 %collective-permute-start.22 = (bf16[2,400,128]{2,1,0:T(8,128)(2,1)S(1)}, bf16[2,400,128]{2,1,0:T(8,128)(2,1)S(1)}, u32[]{:S(2)}, u32[]{:S(2)}) collective-permute-start(bf16[2,400,128]{2,1,0:T(8,128)(2,1)S(1)} %shard_map.38.rest_0_), channel_id=1, source_target_pairs={{0,8},{8,0},{16,24},{24,16},{1,9},{9,1},{17,25},{25,17},{2,10},{10... | collective-permute-start | bytes 614408 | tf_op jit(solution)/shard_map/ppermute | solution.py:456
  77.2 4.2 %collective-permute-start.24 = (bf16[128,128]{1,0:T(8,128)(2,1)S(1)}, bf16[128,128]{1,0:T(8,128)(2,1)S(1)}, u32[]{:S(2)}, u32[]{:S(2)}) collective-permute-start(bf16[128,128]{1,0:T(8,128)(2,1)S(1)} %get-tuple-element.154), channel_id=1, source_target_pairs={{0,2},{1,3},{2,0},{3,1},{4,6},{5,7},{6,4},{7,5},{8,15},{9,14},{10,... | collective-permute-start | bytes 98312 | tf_op jit(solution)/shard_map/ppermute | solution.py:615
  77.2 6.2 %collective-permute-start.25 = (bf16[128,128]{1,0:T(8,128)(2,1)S(1)}, bf16[128,128]{1,0:T(8,128)(2,1)S(1)}, u32[]{:S(2)}, u32[]{:S(2)}) collective-permute-start(bf16[128,128]{1,0:T(8,128)(2,1)S(1)} %get-tuple-element.155), channel_id=1, source_target_pairs={{0,3},{1,2},{2,1},{3,0},{4,7},{5,6},{6,5},{7,4},{8,13},{9,12},{10,... | collective-permute-start | bytes 98312 | tf_op jit(solution)/shard_map/ppermute | solution.py:615
  80.8 3.9 %collective-permute-start.26 = (bf16[128,128]{1,0:T(8,128)(2,1)S(1)}, bf16[128,128]{1,0:T(8,128)(2,1)S(1)}, u32[]{:S(2)}, u32[]{:S(2)}) collective-permute-start(bf16[128,128]{1,0:T(8,128)(2,1)S(1)} %get-tuple-element.156), channel_id=1, source_target_pairs={{0,2},{1,3},{2,0},{3,1},{4,6},{5,7},{6,4},{7,5},{8,14},{9,15},{10,... | collective-permute-start | bytes 98312 | tf_op jit(solution)/shard_map/ppermute | solution.py:615
  80.9 3.9 %collective-permute-start.27 = (bf16[128,128]{1,0:T(8,128)(2,1)S(1)}, bf16[128,128]{1,0:T(8,128)(2,1)S(1)}, u32[]{:S(2)}, u32[]{:S(2)}) collective-permute-start(bf16[128,128]{1,0:T(8,128)(2,1)S(1)} %get-tuple-element.157), channel_id=1, source_target_pairs={{0,1},{1,0},{2,3},{3,2},{4,5},{5,4},{6,7},{7,6},{8,12},{9,13},{10,... | collective-permute-start | bytes 98312 | tf_op jit(solution)/shard_map/ppermute | solution.py:615
  84.8 2.5 %collective-permute-start.28 = (bf16[4,128,128]{2,1,0:T(8,128)(2,1)S(1)}, bf16[4,128,128]{2,1,0:T(8,128)(2,1)S(1)}, u32[]{:S(2)}, u32[]{:S(2)}) collective-permute-start(bf16[4,128,128]{2,1,0:T(8,128)(2,1)S(1)} %pad_maximum_fusion.rest_0_), channel_id=1, source_target_pairs={{0,8},{8,0},{16,24},{24,16},{1,9},{9,1},{17,25},{25,17},{2,10},{10... | collective-permute-start | bytes 393224 | tf_op jit(solution)/shard_map/ppermute | solution.py:456
  89.8 4.7 %collective-permute-start.29 = (bf16[128,128]{1,0:T(8,128)(2,1)S(1)}, bf16[128,128]{1,0:T(8,128)(2,1)S(1)}, u32[]{:S(2)}, u32[]{:S(2)}) collective-permute-start(bf16[128,128]{1,0:T(8,128)(2,1)S(1)} %get-tuple-element.162), channel_id=1, source_target_pairs={{0,2},{1,3},{2,0},{3,1},{4,6},{5,7},{6,4},{7,5},{8,15},{9,14},{10,... | collective-permute-start | bytes 98312 | tf_op jit(solution)/shard_map/ppermute | solution.py:615
  91.1 4.8 %collective-permute-start.30 = (bf16[128,128]{1,0:T(8,128)(2,1)S(1)}, bf16[128,128]{1,0:T(8,128)(2,1)S(1)}, u32[]{:S(2)}, u32[]{:S(2)}) collective-permute-start(bf16[128,128]{1,0:T(8,128)(2,1)S(1)} %get-tuple-element.163), channel_id=1, source_target_pairs={{0,3},{1,2},{2,1},{3,0},{4,7},{5,6},{6,5},{7,4},{8,13},{9,12},{10,... | collective-permute-start | bytes 98312 | tf_op jit(solution)/shard_map/ppermute | solution.py:615
  92.3 4.0 %collective-permute-start.31 = (bf16[128,128]{1,0:T(8,128)(2,1)S(1)}, bf16[128,128]{1,0:T(8,128)(2,1)S(1)}, u32[]{:S(2)}, u32[]{:S(2)}) collective-permute-start(bf16[128,128]{1,0:T(8,128)(2,1)S(1)} %get-tuple-element.164), channel_id=1, source_target_pairs={{0,2},{1,3},{2,0},{3,1},{4,6},{5,7},{6,4},{7,5},{8,14},{9,15},{10,... | collective-permute-start | bytes 98312 | tf_op jit(solution)/shard_map/ppermute | solution.py:615
  94.0 3.9 %collective-permute-start.32 = (bf16[128,128]{1,0:T(8,128)(2,1)S(1)}, bf16[128,128]{1,0:T(8,128)(2,1)S(1)}, u32[]{:S(2)}, u32[]{:S(2)}) collective-permute-start(bf16[128,128]{1,0:T(8,128)(2,1)S(1)} %get-tuple-element.165), channel_id=1, source_target_pairs={{0,1},{1,0},{2,3},{3,2},{4,5},{5,4},{6,7},{7,6},{8,12},{9,13},{10,... | collective-permute-start | bytes 98312 | tf_op jit(solution)/shard_map/ppermute | solution.py:615
  102.3 4.5 %collective-permute-start.34 = (bf16[128,128]{1,0:T(8,128)(2,1)S(1)}, bf16[128,128]{1,0:T(8,128)(2,1)S(1)}, u32[]{:S(2)}, u32[]{:S(2)}) collective-permute-start(bf16[128,128]{1,0:T(8,128)(2,1)S(1)} %get-tuple-element.168), channel_id=1, source_target_pairs={{0,2},{1,3},{2,0},{3,1},{4,6},{5,7},{6,4},{7,5},{8,15},{9,14},{10,... | collective-permute-start | bytes 98312 | tf_op jit(solution)/shard_map/ppermute | solution.py:615
  103.3 5.2 %collective-permute-start.35 = (bf16[128,128]{1,0:T(8,128)(2,1)S(1)}, bf16[128,128]{1,0:T(8,128)(2,1)S(1)}, u32[]{:S(2)}, u32[]{:S(2)}) collective-permute-start(bf16[128,128]{1,0:T(8,128)(2,1)S(1)} %get-tuple-element.169), channel_id=1, source_target_pairs={{0,3},{1,2},{2,1},{3,0},{4,7},{5,6},{6,5},{7,4},{8,13},{9,12},{10,... | collective-permute-start | bytes 98312 | tf_op jit(solution)/shard_map/ppermute | solution.py:615
  105.3 4.3 %collective-permute-start.36 = (bf16[128,128]{1,0:T(8,128)(2,1)S(1)}, bf16[128,128]{1,0:T(8,128)(2,1)S(1)}, u32[]{:S(2)}, u32[]{:S(2)}) collective-permute-start(bf16[128,128]{1,0:T(8,128)(2,1)S(1)} %get-tuple-element.170), channel_id=1, source_target_pairs={{0,2},{1,3},{2,0},{3,1},{4,6},{5,7},{6,4},{7,5},{8,14},{9,15},{10,... | collective-permute-start | bytes 98312 | tf_op jit(solution)/shard_map/ppermute | solution.py:615
  105.4 4.2 %collective-permute-start.37 = (bf16[128,128]{1,0:T(8,128)(2,1)S(1)}, bf16[128,128]{1,0:T(8,128)(2,1)S(1)}, u32[]{:S(2)}, u32[]{:S(2)}) collective-permute-start(bf16[128,128]{1,0:T(8,128)(2,1)S(1)} %get-tuple-element.171), channel_id=1, source_target_pairs={{0,1},{1,0},{2,3},{3,2},{4,5},{5,4},{6,7},{7,6},{8,12},{9,13},{10,... | collective-permute-start | bytes 98312 | tf_op jit(solution)/shard_map/ppermute | solution.py:615
  (12 other events, 24.8 us)

commit v7 on v6

--- a/solution.py
+++ b/solution.py
@@ -356,20 +356,26 @@
             stepped_ref[j, k] = omega - scale * (v_ref[j, :, span(k, block)] + mirrored)
 
 
-def first_kernel(group, ways, table_ref, prec_ref, gram_in_ref, low_in_ref, *rest):
+def weights_kernel(table_ref, prec_ref, w_ref):
+    block_rows, slots, block, _ = prec_ref.shape
+    here = Pattern(table_ref, block_rows, slots)
+
+    @pl.loop(0, block_rows)
+    def _(j):
+        for k in range(slots):
+            value = jnp.where(here.source(j, k) >= 0, prec_ref[j, k], 0.0)
+            w_ref[j, :, span(k, block)] = value.astype(jnp.bfloat16)
+
+
+def first_kernel(group, ways, table_ref, w_ref, gram_in_ref, low_in_ref, *rest):
     parts, rest = rest[: 2 * ways], rest[2 * ways :]
-    gram_ref, low_ref, v_ref, *out_refs, w_ref, sem = rest
+    gram_ref, low_ref, v_ref, *out_refs, sem = rest
     copy = pltpu.make_async_copy(gram_in_ref, gram_ref, sem)
     copy.start()
     low_ref[...] = low_in_ref[...]
-    block_rows, slots, block, _ = prec_ref.shape
+    block_rows, block, width = w_ref.shape
+    slots = width // block
     here = Pattern(table_ref, block_rows, slots)
-
-    @pl.loop(0, block_rows)
-    def _(j):
-        for k in range(slots):
-            value = jnp.where(here.source(j, k) >= 0, prec_ref[j, k], 0.0)
-            w_ref[j, :, span(k, block)] = value.astype(jnp.bfloat16)
 
     copy.wait()
     place_arrivals(here, *group, parts, gram_ref, low_ref)
@@ -618,11 +624,14 @@
 
     weights = pltpu.VMEM((block_rows, block, slots * block), bf16)
     wide = shape((block_rows, block, (slots + 1) * block), f32)
+    (first_weights,) = call(
+        weights_kernel, (table, precision), [shape(weights.shape, bf16)], []
+    )
     gram, low, v, *out = call(
         functools.partial(first_kernel, groups[-1], ways),
-        (table, precision, gram, low, *last_list),
+        (table, first_weights, gram, low, *last_list),
         [*grams, wide, *swapped],
-        [weights],
+        [],
         left=[2],
         sems=[sem],
     )

time: 114 us -> 116 us (1.018)
  starting transfers between devices: 36.1 us -> 38.9 us
  waiting for transfers between devices: 37.6 us -> 36.4 us
    ppermute x20, starting transfers between devices: 9.36 us -> 12.7 us  [swap(): return lax.ppermute(x, 'samp', [(i, i ^ bit) for i in range(count)])]
    ppermute x7, waiting for transfers between devices: 15.2 us -> 13.7 us  [exchange(): return lax.ppermute(x, 'feat', [(i, i ^ r) for i in range(peers)])]
    pallas_call x14 -> x15, Pallas kernels: 35.7 us -> 36.3 us  [call(): pl.pallas_call(kernel, out_shape=outs, in_specs=specs, out_specs=[out_spa...]
  transfers between devices with their start and end apart: 39 -> 39, of which waited for: 19 -> 20; matrix products, arithmetic and copies ran while one was open for 1% -> 1% of each run, Pallas kernels for 19% -> 19%
where the time goes in v7:
time: 116 us
  starting transfers between devices  38.9 us (34%)
  waiting for transfers between devices  36.4 us (31%)
  Pallas kernels  36.3 us (31%)
  local copies, waits for them, and re-layouts  3.23 us (3%)
    pallas_call x15, Pallas kernels, call(): pl.pallas_call(kernel, out_shape=outs, in_specs=specs, out_specs=[out_spa...  36.3 us
    ppermute x20, waiting for transfers between devices, swap(): return lax.ppermute(x, 'samp', [(i, i ^ bit) for i in range(count)])  13.8 us
    ppermute x7, waiting for transfers between devices, exchange(): return lax.ppermute(x, 'feat', [(i, i ^ r) for i in range(peers)])  13.7 us
    ppermute x7, starting transfers between devices, exchange(): return lax.ppermute(x, 'feat', [(i, i ^ r) for i in range(peers)])  13.3 us
    ppermute x12, starting transfers between devices, trade(): got.append(lax.ppermute(x, ('samp', 'feat'), pairs))  12.9 us
    ppermute x20, starting transfers between devices, swap(): return lax.ppermute(x, 'samp', [(i, i ^ bit) for i in range(count)])  12.7 us
    ppermute x12, waiting for transfers between devices, trade(): got.append(lax.ppermute(x, ('samp', 'feat'), pairs))  8.92 us
  transfers between devices with their start and end apart: 39, of which 20 were waited for; matrix products, arithmetic and copies ran while one was open for 1% of the time, Pallas kernels for 19%

profile of v7, /device:TPU:0, one launch (start us, length us, event | category | flops | bytes accessed | tf_op | source)
XLA Modules:
  0.0 115.9 jit_solution(17493523770748437887)
XLA Ops:
  3.0 4.6 %collective-permute-start.11 = (bf16[128,1024]{1,0:T(8,128)(2,1)S(1)}, bf16[128,1024]{1,0:T(8,128)(2,1)S(1)}, u32[]{:S(2)}, u32[]{:S(2)}) collective-permute-start(bf16[128,1024]{1,0:T(8,128)(2,1)S(1)} %get-tuple-element.131), channel_id=1, source_target_pairs={{0,5},{1,4},{2,7},{3,6},{4,1},{5,0},{6,3},{7,2},{8,13},{9,12},{10,... | collective-permute-start | bytes 786440 | tf_op jit(solution)/shard_map/ppermute | solution.py:508
  7.9 1.6 %collective-permute-start.8 = (bf16[128,1024]{1,0:T(8,128)(2,1)S(1)}, bf16[128,1024]{1,0:T(8,128)(2,1)}, u32[]{:S(2)}, u32[]{:S(2)}) collective-permute-start(bf16[128,1024]{1,0:T(8,128)(2,1)S(1)} %get-tuple-element.127), channel_id=1, source_target_pairs={{0,2},{1,3},{2,0},{3,1},{4,6},{5,7},{6,4},{7,5},{8,10},{9,11},{10,... | collective-permute-start | bytes 786440 | tf_op jit(solution)/shard_map/ppermute | solution.py:508
  11.9 1.4 %collective-permute-start.9 = (bf16[128,1024]{1,0:T(8,128)(2,1)S(1)}, bf16[128,1024]{1,0:T(8,128)(2,1)}, u32[]{:S(2)}, u32[]{:S(2)}) collective-permute-start(bf16[128,1024]{1,0:T(8,128)(2,1)S(1)} %get-tuple-element.129), channel_id=1, source_target_pairs={{0,3},{1,2},{2,1},{3,0},{4,7},{5,6},{6,5},{7,4},{8,11},{9,10},{10,... | collective-permute-start | bytes 786440 | tf_op jit(solution)/shard_map/ppermute | solution.py:508
  13.3 4.5 %conditional.3 = (bf16[5,144,128]{2,1,0:T(8,128)(2,1)}, s32[8,24]{1,0:T(8,128)S(1)}) conditional(s32[]{:T(128)} %convert_element_type.7, () %tuple.44, (bf16[4,128,1024]{2,1,0:T(8,128)(2,1)S(1)}, bf16[4,128,1024]{2,1,0:T(8,128)(2,1)}, s32[4,6]{1,0:T(4,128)}) %tuple.45), branch_computations={%region_0.0_spmd, %region_1.0_spmd} | conditional | flops 2 | bytes 185110 | solution.py:481
  13.3 2.8 %branch_1_fun.4 = bf16[5,144,128]{2,1,0:T(8,128)(2,1)} custom-call(bf16[4,128,1024]{2,1,0:T(8,128)(2,1)S(1)} %get-tuple-element.47.mine_ref, bf16[4,128,1024]{2,1,0:T(8,128)(2,1)} %get-tuple-element.48.other_ref), custom_call_target="tpu_custom_call" | custom-call | flops 1 | bytes 1 | tf_op jit(solution)/shard_map/cond/branch_1_fun/pallas_call | solution.py:449
  16.1 1.7 %branch_1_fun.5 = s32[8,24]{1,0:T(8,128)S(1)} custom-call(s32[4,6]{1,0:T(4,128)S(1)} %copy-done.4), custom_call_target="tpu_custom_call" | custom-call | flops 1 | bytes 1 | tf_op jit(solution)/shard_map/cond/branch_1_fun/pallas_call | solution.py:449
  17.8 8.3 %collective-permute-done.11.rest_4_ = bf16[128,1024]{1,0:T(8,128)(2,1)S(1)} collective-permute-done((bf16[128,1024]{1,0:T(8,128)(2,1)S(1)}, bf16[128,1024]{1,0:T(8,128)(2,1)S(1)}, u32[]{:S(2)}, u32[]{:S(2)}) %collective-permute-start.11) | collective-permute-done | bytes 262176 | tf_op jit(solution)/shard_map/ppermute | solution.py:508
  26.1 5.4 %collective-permute-done.10.rest_3_ = bf16[128,1024]{1,0:T(8,128)(2,1)S(1)} collective-permute-done((bf16[128,1024]{1,0:T(8,128)(2,1)S(1)}, bf16[128,1024]{1,0:T(8,128)(2,1)S(1)}, u32[]{:S(2)}, u32[]{:S(2)}) %collective-permute-start.10) | collective-permute-done | bytes 262176 | tf_op jit(solution)/shard_map/ppermute | solution.py:508
  32.5 4.8 %collective-permute-start.18 = (bf16[128,1024]{1,0:T(8,128)(2,1)S(1)}, bf16[128,1024]{1,0:T(8,128)(2,1)S(1)}, u32[]{:S(2)}, u32[]{:S(2)}) collective-permute-start(bf16[128,1024]{1,0:T(8,128)(2,1)S(1)} %get-tuple-element.141), channel_id=1, source_target_pairs={{0,7},{1,6},{2,5},{3,4},{4,3},{5,2},{6,1},{7,0},{8,15},{9,14},{10,... | collective-permute-start | bytes 786440 | tf_op jit(solution)/shard_map/ppermute | solution.py:508
  38.2 22.6 %conditional.4 = (bf16[4,768,768]{2,1,0:T(8,128)(2,1)}, f32[4,8,128]{2,1,0:T(8,128)}, bf16[5,400,128]{2,1,0:T(8,128)(2,1)}, bf16[5,400,128]{2,1,0:T(8,128)(2,1)}...) conditional(s32[]{:T(128)} %convert_element_type.7, () %tuple.46, (pred[]{:T(512)}, ...), branch_computations={%region_2.0_spmd, %region_3.0_spmd} | conditional | flops 3 | bytes 11616524 | solution.py:481
  38.2 1.5 %collective-permute-start.2 = (bf16[5,144,128]{2,1,0:T(8,128)(2,1)}, bf16[5,144,128]{2,1,0:T(8,128)(2,1)}, u32[]{:S(2)}, u32[]{:S(2)}) collective-permute-start(bf16[5,144,128]{2,1,0:T(8,128)(2,1)} %get-tuple-element.54), channel_id=1, source_target_pairs={{0,16},{8,24},{16,0},{24,8},{1,17},{9,25},{17,1},{25,9},{2,18},{10... | collective-permute-start | bytes 552968 | tf_op jit(solution)/shard_map/cond/branch_1_fun/ppermute | solution.py:462
  39.8 3.8 %branch_1_fun.7 = bf16[5,400,128]{2,1,0:T(8,128)(2,1)} custom-call(s32[8,24]{1,0:T(8,128)S(1)} %get-tuple-element.55.table_ref, bf16[4,128,1024]{2,1,0:T(8,128)(2,1)S(1)} %get-tuple-element.56.mine_ref, bf16[4,128,1024]{2,1,0:T(8,128)(2,1)} %get-tuple-element.57.other_ref, bf16[128,1024]{1,0:T(8,128)(2,1)} %get-tuple-element.58.rest_0_, ...), custom_call_target="tpu_custom_call" | custom-call | flops 1 | bytes 1 | tf_op jit(solution)/shard_map/cond/branch_1_fun/pallas_call | solution.py:449
  43.6 1.7 %collective-permute-done.2 = bf16[5,144,128]{2,1,0:T(8,128)(2,1)} collective-permute-done((bf16[5,144,128]{2,1,0:T(8,128)(2,1)}, bf16[5,144,128]{2,1,0:T(8,128)(2,1)}, u32[]{:S(2)}, u32[]{:S(2)}) %collective-permute-start.2) | collective-permute-done | bytes 184352 | tf_op jit(solution)/shard_map/cond/branch_1_fun/ppermute | solution.py:462
  45.3 1.5 %collective-permute-start.3 = (bf16[5,400,128]{2,1,0:T(8,128)(2,1)}, bf16[5,400,128]{2,1,0:T(8,128)(2,1)}, u32[]{:S(2)}, u32[]{:S(2)}) collective-permute-start(bf16[5,400,128]{2,1,0:T(8,128)(2,1)} %branch_1_fun.7), channel_id=1, source_target_pairs={{0,16},{8,24},{16,0},{24,8},{1,17},{9,25},{17,1},{25,9},{2,18},{10... | collective-permute-start | bytes 1536008 | tf_op jit(solution)/shard_map/cond/branch_1_fun/ppermute | solution.py:462
  46.8 6.3 %conditional = ((bf16[4,768,768]{2,1,0:T(8,128)(2,1)}, f32[4,8,128]{2,1,0:T(8,128)})) conditional(s32[]{:T(128)} %convert_element_type.1, () %tuple.21, (bf16[5,144,128]{2,1,0:T(8,128)(2,1)}, bf16[5,144,128]{2,1,0:T(8,128)(2,1)}, s32[8,24]{1,0:T(8,128)S(1)}) %tuple.24), branch_computations={%region_4.0_spmd, %region_5.0_spmd} | conditional | flops 1 | bytes 4735006 | solution.py:481
  48.7 4.4 %branch_1_fun.6 = (bf16[4,768,768]{2,1,0:T(8,128)(2,1)}, f32[4,8,128]{2,1,0:T(8,128)}) custom-call(s32[8,24]{1,0:T(8,128)S(1)} %get-tuple-element.50.table_ref, bf16[5,144,128]{2,1,0:T(8,128)(2,1)} %get-tuple-element.51.rest_0_, bf16[5,144,128]{2,1,0:T(8,128)(2,1)} %get-tuple-element.52.rest_1_, bf16[5,144,128]{2,1,0:T(8,128)(2,1)S(1)} %collective-permute-done.rest_2_, ...), custom_call_target="tpu_custom_call" | custom-call | flops 1 | bytes 1 | tf_op jit(solution)/shard_map/cond/branch_1_fun/cond/branch_1_fun/pallas_call | solution.py:449
  53.4 5.2 %collective-permute-done.3 = bf16[5,400,128]{2,1,0:T(8,128)(2,1)} collective-permute-done((bf16[5,400,128]{2,1,0:T(8,128)(2,1)}, bf16[5,400,128]{2,1,0:T(8,128)(2,1)}, u32[]{:S(2)}, u32[]{:S(2)}) %collective-permute-start.3) | collective-permute-done | bytes 512032 | tf_op jit(solution)/shard_map/cond/branch_1_fun/ppermute | solution.py:462
  58.6 2.2 %collective-permute-done.5 = bf16[5,400,128]{2,1,0:T(8,128)(2,1)} collective-permute-done((bf16[5,400,128]{2,1,0:T(8,128)(2,1)}, bf16[5,400,128]{2,1,0:T(8,128)(2,1)}, u32[]{:S(2)}, u32[]{:S(2)}) %collective-permute-start.5) | collective-permute-done | bytes 512032 | tf_op jit(solution)/shard_map/cond/branch_1_fun/ppermute | solution.py:462
  62.8 3.4 %shard_map.39.rest_0_ = bf16[2,400,128]{2,1,0:T(8,128)(2,1)S(1)} custom-call(s32[8,24]{1,0:T(8,128)S(1)} %get-tuple-element.124.table_ref, bf16[4,128,1024]{2,1,0:T(8,128)(2,1)S(1)} %get-tuple-element.123.mine_ref, bf16[4,128,1024]{2,1,0:T(8,128)(2,1)} %collective-permute-done.6.other_ref, bf16[128,1024]{1,0:T(8,128)(2,1)} %collective-permute-done.7.rest_0_, ...), custom_call_target="tpu_custom_call" | custom-call | flops 1 | bytes 1 | tf_op jit(solution)/shard_map/pallas_call | solution.py:449
  66.2 1.6 %collective-permute-start.21 = (bf16[2,400,128]{2,1,0:T(8,128)(2,1)S(1)}, bf16[2,400,128]{2,1,0:T(8,128)(2,1)S(1)}, u32[]{:S(2)}, u32[]{:S(2)}) collective-permute-start(bf16[2,400,128]{2,1,0:T(8,128)(2,1)S(1)} %shard_map.39.rest_0_), channel_id=1, source_target_pairs={{0,16},{8,24},{16,0},{24,8},{1,17},{9,25},{17,1},{25,9},{2,18},{10... | collective-permute-start | bytes 614408 | tf_op jit(solution)/shard_map/ppermute | solution.py:462
  67.8 4.4 %shard_map.40 = (bf16[4,768,768]{2,1,0:T(8,128)(2,1)S(1)}, f32[4,8,128]{2,1,0:T(8,128)S(1)}) custom-call(s32[8,24]{1,0:T(8,128)S(1)} %get-tuple-element.124.table_ref, bf16[4,768,768]{2,1,0:T(8,128)(2,1)} %get-tuple-element.144.gram_in_ref, f32[4,8,128]{2,1,0:T(8,128)} %get-tuple-element.145.low_in_ref, bf16[5,400,128]{2,1,0:T(8,128)(2,1)} %get-tuple-element.146.rest_0_, ...), custom_call_target="tpu_custom_call" | custom-call | flops 1 | bytes 1 | tf_op jit(solution)/shard_map/pallas_call | solution.py:449
  74.8 2.8 %shard_map.41 = (bf16[4,768,768]{2,1,0:T(8,128)(2,1)S(1)}, f32[4,8,128]{2,1,0:T(8,128)S(1)}, f32[4,128,896]{2,1,0:T(8,128)S(1)}, bf16[128,128]{1,0:T(8,128)(2,1)...) custom-call(s32[8,24]{1,0:T(8,128)S(1)} %get-tuple-element.124.table_ref, ...), custom_call_target="tpu_custom_call" | custom-call | flops 1 | bytes 1 | tf_op jit(solution)/shard_map/pallas_call | solution.py:449
  79.7 1.5 %collective-permute-start.27 = (bf16[128,128]{1,0:T(8,128)(2,1)S(1)}, bf16[128,128]{1,0:T(8,128)(2,1)S(1)}, u32[]{:S(2)}, u32[]{:S(2)}) collective-permute-start(bf16[128,128]{1,0:T(8,128)(2,1)S(1)} %get-tuple-element.157), channel_id=1, source_target_pairs={{0,1},{1,0},{2,3},{3,2},{4,5},{5,4},{6,7},{7,6},{8,12},{9,13},{10,... | collective-permute-start | bytes 98312 | tf_op jit(solution)/shard_map/ppermute | solution.py:621
  83.8 2.6 %collective-permute-start.28 = (bf16[4,128,128]{2,1,0:T(8,128)(2,1)S(1)}, bf16[4,128,128]{2,1,0:T(8,128)(2,1)S(1)}, u32[]{:S(2)}, u32[]{:S(2)}) collective-permute-start(bf16[4,128,128]{2,1,0:T(8,128)(2,1)S(1)} %pad_maximum_fusion.rest_0_), channel_id=1, source_target_pairs={{0,8},{8,0},{16,24},{24,16},{1,9},{9,1},{17,25},{25,17},{2,10},{10... | collective-permute-start | bytes 393224 | tf_op jit(solution)/shard_map/ppermute | solution.py:462
  87.7 2.5 %shard_map.43 = (f32[4,6,128,128]{3,2,1,0:T(8,128)S(1)}, f32[4,128,896]{2,1,0:T(8,128)S(1)}, bf16[128,128]{1,0:T(8,128)(2,1)S(1)}, bf16[128,128]{1,0:T(8,128)(2,...) custom-call(s32[8,24]{1,0:T(8,128)S(1)} %get-tuple-element.124.table_ref, ...), custom_call_target="tpu_custom_call" | custom-call | flops 1 | bytes 1 | tf_op jit(solution)/shard_map/pallas_call | solution.py:449
  90.3 1.9 %collective-permute-start.29 = (bf16[128,128]{1,0:T(8,128)(2,1)S(1)}, bf16[128,128]{1,0:T(8,128)(2,1)S(1)}, u32[]{:S(2)}, u32[]{:S(2)}) collective-permute-start(bf16[128,128]{1,0:T(8,128)(2,1)S(1)} %get-tuple-element.162), channel_id=1, source_target_pairs={{0,2},{1,3},{2,0},{3,1},{4,6},{5,7},{6,4},{7,5},{8,15},{9,14},{10,... | collective-permute-start | bytes 98312 | tf_op jit(solution)/shard_map/ppermute | solution.py:621
  92.6 1.9 %collective-permute-start.31 = (bf16[128,128]{1,0:T(8,128)(2,1)S(1)}, bf16[128,128]{1,0:T(8,128)(2,1)S(1)}, u32[]{:S(2)}, u32[]{:S(2)}) collective-permute-start(bf16[128,128]{1,0:T(8,128)(2,1)S(1)} %get-tuple-element.164), channel_id=1, source_target_pairs={{0,2},{1,3},{2,0},{3,1},{4,6},{5,7},{6,4},{7,5},{8,14},{9,15},{10,... | collective-permute-start | bytes 98312 | tf_op jit(solution)/shard_map/ppermute | solution.py:621
  100.7 2.5 %shard_map.45 = (f32[4,6,128,128]{3,2,1,0:T(8,128)S(1)}, f32[4,128,896]{2,1,0:T(8,128)S(1)}, bf16[128,128]{1,0:T(8,128)(2,1)S(1)}, bf16[128,128]{1,0:T(8,128)(2,...) custom-call(s32[8,24]{1,0:T(8,128)S(1)} %get-tuple-element.124.table_ref, ...), custom_call_target="tpu_custom_call" | custom-call | flops 1 | bytes 1 | tf_op jit(solution)/shard_map/pallas_call | solution.py:449
  104.2 1.6 %collective-permute-start.36 = (bf16[128,128]{1,0:T(8,128)(2,1)S(1)}, bf16[128,128]{1,0:T(8,128)(2,1)S(1)}, u32[]{:S(2)}, u32[]{:S(2)}) collective-permute-start(bf16[128,128]{1,0:T(8,128)(2,1)S(1)} %get-tuple-element.170), channel_id=1, source_target_pairs={{0,2},{1,3},{2,0},{3,1},{4,6},{5,7},{6,4},{7,5},{8,14},{9,15},{10,... | collective-permute-start | bytes 98312 | tf_op jit(solution)/shard_map/ppermute | solution.py:621
  107.1 1.4 %collective-permute-done.35 = bf16[128,128]{1,0:T(8,128)(2,1)S(1)} collective-permute-done((bf16[128,128]{1,0:T(8,128)(2,1)S(1)}, bf16[128,128]{1,0:T(8,128)(2,1)S(1)}, u32[]{:S(2)}, u32[]{:S(2)}) %collective-permute-start.35) | collective-permute-done | bytes 32800 | tf_op jit(solution)/shard_map/ppermute | solution.py:621
  110.8 1.7 %collective-permute-start.38 = (bf16[4,128,128]{2,1,0:T(8,128)(2,1)S(1)}, bf16[4,128,128]{2,1,0:T(8,128)(2,1)S(1)}, u32[]{:S(2)}, u32[]{:S(2)}) collective-permute-start(bf16[4,128,128]{2,1,0:T(8,128)(2,1)S(1)} %pad_maximum_fusion.2.rest_0_), channel_id=1, source_target_pairs={{0,8},{8,0},{16,24},{24,16},{1,9},{9,1},{17,25},{25,17},{2,10},{10... | collective-permute-start | bytes 393224 | tf_op jit(solution)/shard_map/ppermute | solution.py:462
  113.8 1.9 %shard_map.47 = f32[4,6,128,128]{3,2,1,0:T(8,128)} custom-call(s32[8,24]{1,0:T(8,128)S(1)} %get-tuple-element.124.table_ref, f32[4,6,128,128]{3,2,1,0:T(8,128)S(1)} %shard_map.46.stepped_ref, bf16[4,128,128]{2,1,0:T(8,128)(2,1)S(1)} %pad_maximum_fusion.2.rest_0_, bf16[4,128,128]{2,1,0:T(8,128)(2,1)S(1)} %collective-permute-done.38.rest_1_), custom_call_target="tpu_custom_call" | custom-call | flops 1 | bytes 1 | tf_op jit(solution)/shard_map/pallas_call | solution.py:449
  (78 shorter events, 32.0 us)
Async XLA Ops:
  2.5 9.4 %collective-permute-start.6 = (bf16[4,128,1024]{2,1,0:T(8,128)(2,1)S(1)}, bf16[4,128,1024]{2,1,0:T(8,128)(2,1)}, u32[]{:S(2)}, u32[]{:S(2)}) collective-permute-start(bf16[4,128,1024]{2,1,0:T(8,128)(2,1)S(1)} %get-tuple-element.123.mine_ref), channel_id=1, source_target_pairs={{0,8},{8,0},{16,24},{24,16},{1,9},{9,1},{17,25},{25,17},{2,10},{10... | collective-permute-start | bytes 3145736 | tf_op jit(solution)/shard_map/ppermute | solution.py:462
  3.0 23.1 %collective-permute-start.11 = (bf16[128,1024]{1,0:T(8,128)(2,1)S(1)}, bf16[128,1024]{1,0:T(8,128)(2,1)S(1)}, u32[]{:S(2)}, u32[]{:S(2)}) collective-permute-start(bf16[128,1024]{1,0:T(8,128)(2,1)S(1)} %get-tuple-element.131), channel_id=1, source_target_pairs={{0,5},{1,4},{2,7},{3,6},{4,1},{5,0},{6,3},{7,2},{8,13},{9,12},{10,... | collective-permute-start | bytes 786440 | tf_op jit(solution)/shard_map/ppermute | solution.py:508
  7.6 23.9 %collective-permute-start.10 = (bf16[128,1024]{1,0:T(8,128)(2,1)S(1)}, bf16[128,1024]{1,0:T(8,128)(2,1)S(1)}, u32[]{:S(2)}, u32[]{:S(2)}) collective-permute-start(bf16[128,1024]{1,0:T(8,128)(2,1)S(1)} %get-tuple-element.130), channel_id=1, source_target_pairs={{0,4},{1,5},{2,6},{3,7},{4,0},{5,1},{6,2},{7,3},{8,12},{9,13},{10,... | collective-permute-start | bytes 786440 | tf_op jit(solution)/shard_map/ppermute | solution.py:508
  7.9 23.6 %collective-permute-start.8 = (bf16[128,1024]{1,0:T(8,128)(2,1)S(1)}, bf16[128,1024]{1,0:T(8,128)(2,1)}, u32[]{:S(2)}, u32[]{:S(2)}) collective-permute-start(bf16[128,1024]{1,0:T(8,128)(2,1)S(1)} %get-tuple-element.127), channel_id=1, source_target_pairs={{0,2},{1,3},{2,0},{3,1},{4,6},{5,7},{6,4},{7,5},{8,10},{9,11},{10,... | collective-permute-start | bytes 786440 | tf_op jit(solution)/shard_map/ppermute | solution.py:508
  9.5 22.5 %collective-permute-start.7 = (bf16[128,1024]{1,0:T(8,128)(2,1)S(1)}, bf16[128,1024]{1,0:T(8,128)(2,1)}, u32[]{:S(2)}, u32[]{:S(2)}) collective-permute-start(bf16[128,1024]{1,0:T(8,128)(2,1)S(1)} %get-tuple-element.126), channel_id=1, source_target_pairs={{0,1},{1,0},{2,3},{3,2},{4,5},{5,4},{6,7},{7,6},{8,9},{9,8},{10,11... | collective-permute-start | bytes 786440 | tf_op jit(solution)/shard_map/ppermute | solution.py:508
  11.9 20.2 %collective-permute-start.9 = (bf16[128,1024]{1,0:T(8,128)(2,1)S(1)}, bf16[128,1024]{1,0:T(8,128)(2,1)}, u32[]{:S(2)}, u32[]{:S(2)}) collective-permute-start(bf16[128,1024]{1,0:T(8,128)(2,1)S(1)} %get-tuple-element.129), channel_id=1, source_target_pairs={{0,3},{1,2},{2,1},{3,0},{4,7},{5,6},{6,5},{7,4},{8,11},{9,10},{10,... | collective-permute-start | bytes 786440 | tf_op jit(solution)/shard_map/ppermute | solution.py:508
  26.1 6.5 %collective-permute-start.16 = (bf16[128,1024]{1,0:T(8,128)(2,1)S(1)}, bf16[128,1024]{1,0:T(8,128)(2,1)S(1)}, u32[]{:S(2)}, u32[]{:S(2)}) collective-permute-start(bf16[128,1024]{1,0:T(8,128)(2,1)S(1)} %collective-permute-done.11.rest_4_), channel_id=1, source_target_pairs={{0,8},{8,0},{16,24},{24,16},{1,9},{9,1},{17,25},{25,17},{2,10},{10... | collective-permute-start | bytes 786440 | tf_op jit(solution)/shard_map/ppermute | solution.py:462
  31.5 5.9 %collective-permute-start.15 = (bf16[128,1024]{1,0:T(8,128)(2,1)S(1)}, bf16[128,1024]{1,0:T(8,128)(2,1)S(1)}, u32[]{:S(2)}, u32[]{:S(2)}) collective-permute-start(bf16[128,1024]{1,0:T(8,128)(2,1)S(1)} %collective-permute-done.10.rest_3_), channel_id=1, source_target_pairs={{0,8},{8,0},{16,24},{24,16},{1,9},{9,1},{17,25},{25,17},{2,10},{10... | collective-permute-start | bytes 786440 | tf_op jit(solution)/shard_map/ppermute | solution.py:462
  31.5 5.9 %collective-permute-start.13 = (bf16[128,1024]{1,0:T(8,128)(2,1)}, bf16[128,1024]{1,0:T(8,128)(2,1)S(1)}, u32[]{:S(2)}, u32[]{:S(2)}) collective-permute-start(bf16[128,1024]{1,0:T(8,128)(2,1)} %collective-permute-done.8.rest_1_), channel_id=1, source_target_pairs={{0,8},{8,0},{16,24},{24,16},{1,9},{9,1},{17,25},{25,17},{2,10},{10... | collective-permute-start | bytes 786440 | tf_op jit(solution)/shard_map/ppermute | solution.py:462
  32.0 5.4 %collective-permute-start.12 = (bf16[128,1024]{1,0:T(8,128)(2,1)}, bf16[128,1024]{1,0:T(8,128)(2,1)S(1)}, u32[]{:S(2)}, u32[]{:S(2)}) collective-permute-start(bf16[128,1024]{1,0:T(8,128)(2,1)} %collective-permute-done.7.rest_0_), channel_id=1, source_target_pairs={{0,8},{8,0},{16,24},{24,16},{1,9},{9,1},{17,25},{25,17},{2,10},{10... | collective-permute-start | bytes 786440 | tf_op jit(solution)/shard_map/ppermute | solution.py:462
  32.1 5.3 %collective-permute-start.14 = (bf16[128,1024]{1,0:T(8,128)(2,1)}, bf16[128,1024]{1,0:T(8,128)(2,1)S(1)}, u32[]{:S(2)}, u32[]{:S(2)}) collective-permute-start(bf16[128,1024]{1,0:T(8,128)(2,1)} %collective-permute-done.9.rest_2_), channel_id=1, source_target_pairs={{0,8},{8,0},{16,24},{24,16},{1,9},{9,1},{17,25},{25,17},{2,10},{10... | collective-permute-start | bytes 786440 | tf_op jit(solution)/shard_map/ppermute | solution.py:462
  32.5 28.3 %collective-permute-start.18 = (bf16[128,1024]{1,0:T(8,128)(2,1)S(1)}, bf16[128,1024]{1,0:T(8,128)(2,1)S(1)}, u32[]{:S(2)}, u32[]{:S(2)}) collective-permute-start(bf16[128,1024]{1,0:T(8,128)(2,1)S(1)} %get-tuple-element.141), channel_id=1, source_target_pairs={{0,7},{1,6},{2,5},{3,4},{4,3},{5,2},{6,1},{7,0},{8,15},{9,14},{10,... | collective-permute-start | bytes 786440 | tf_op jit(solution)/shard_map/ppermute | solution.py:508
  37.4 23.6 %collective-permute-start.17 = (bf16[128,1024]{1,0:T(8,128)(2,1)S(1)}, bf16[128,1024]{1,0:T(8,128)(2,1)S(1)}, u32[]{:S(2)}, u32[]{:S(2)}) collective-permute-start(bf16[128,1024]{1,0:T(8,128)(2,1)S(1)} %get-tuple-element.139), channel_id=1, source_target_pairs={{0,6},{1,7},{2,4},{3,5},{4,2},{5,3},{6,0},{7,1},{8,14},{9,15},{10,... | collective-permute-start | bytes 786440 | tf_op jit(solution)/shard_map/ppermute | solution.py:508
  38.2 7.1 %collective-permute-start.2 = (bf16[5,144,128]{2,1,0:T(8,128)(2,1)}, bf16[5,144,128]{2,1,0:T(8,128)(2,1)}, u32[]{:S(2)}, u32[]{:S(2)}) collective-permute-start(bf16[5,144,128]{2,1,0:T(8,128)(2,1)} %get-tuple-element.54), channel_id=1, source_target_pairs={{0,16},{8,24},{16,0},{24,8},{1,17},{9,25},{17,1},{25,9},{2,18},{10... | collective-permute-start | bytes 552968 | tf_op jit(solution)/shard_map/cond/branch_1_fun/ppermute | solution.py:462
  45.3 13.3 %collective-permute-start.3 = (bf16[5,400,128]{2,1,0:T(8,128)(2,1)}, bf16[5,400,128]{2,1,0:T(8,128)(2,1)}, u32[]{:S(2)}, u32[]{:S(2)}) collective-permute-start(bf16[5,400,128]{2,1,0:T(8,128)(2,1)} %branch_1_fun.7), channel_id=1, source_target_pairs={{0,16},{8,24},{16,0},{24,8},{1,17},{9,25},{17,1},{25,9},{2,18},{10... | collective-permute-start | bytes 1536008 | tf_op jit(solution)/shard_map/cond/branch_1_fun/ppermute | solution.py:462
  53.2 5.5 %collective-permute-start.4 = (bf16[5,400,128]{2,1,0:T(8,128)(2,1)}, bf16[5,400,128]{2,1,0:T(8,128)(2,1)}, u32[]{:S(2)}, u32[]{:S(2)}) collective-permute-start(bf16[5,400,128]{2,1,0:T(8,128)(2,1)} %branch_1_fun.7), channel_id=1, source_target_pairs={{0,8},{8,0},{16,24},{24,16},{1,9},{9,1},{17,25},{25,17},{2,10},{10... | collective-permute-start | bytes 1536008 | tf_op jit(solution)/shard_map/cond/branch_1_fun/ppermute | solution.py:462
  66.2 7.2 %collective-permute-start.21 = (bf16[2,400,128]{2,1,0:T(8,128)(2,1)S(1)}, bf16[2,400,128]{2,1,0:T(8,128)(2,1)S(1)}, u32[]{:S(2)}, u32[]{:S(2)}) collective-permute-start(bf16[2,400,128]{2,1,0:T(8,128)(2,1)S(1)} %shard_map.39.rest_0_), channel_id=1, source_target_pairs={{0,16},{8,24},{16,0},{24,8},{1,17},{9,25},{17,1},{25,9},{2,18},{10... | collective-permute-start | bytes 614408 | tf_op jit(solution)/shard_map/ppermute | solution.py:462
  67.8 6.4 %collective-permute-start.22 = (bf16[2,400,128]{2,1,0:T(8,128)(2,1)S(1)}, bf16[2,400,128]{2,1,0:T(8,128)(2,1)S(1)}, u32[]{:S(2)}, u32[]{:S(2)}) collective-permute-start(bf16[2,400,128]{2,1,0:T(8,128)(2,1)S(1)} %shard_map.39.rest_0_), channel_id=1, source_target_pairs={{0,8},{8,0},{16,24},{24,16},{1,9},{9,1},{17,25},{25,17},{2,10},{10... | collective-permute-start | bytes 614408 | tf_op jit(solution)/shard_map/ppermute | solution.py:462
  77.6 4.0 %collective-permute-start.24 = (bf16[128,128]{1,0:T(8,128)(2,1)S(1)}, bf16[128,128]{1,0:T(8,128)(2,1)S(1)}, u32[]{:S(2)}, u32[]{:S(2)}) collective-permute-start(bf16[128,128]{1,0:T(8,128)(2,1)S(1)} %get-tuple-element.154), channel_id=1, source_target_pairs={{0,2},{1,3},{2,0},{3,1},{4,6},{5,7},{6,4},{7,5},{8,15},{9,14},{10,... | collective-permute-start | bytes 98312 | tf_op jit(solution)/shard_map/ppermute | solution.py:621
  77.7 4.9 %collective-permute-start.25 = (bf16[128,128]{1,0:T(8,128)(2,1)S(1)}, bf16[128,128]{1,0:T(8,128)(2,1)S(1)}, u32[]{:S(2)}, u32[]{:S(2)}) collective-permute-start(bf16[128,128]{1,0:T(8,128)(2,1)S(1)} %get-tuple-element.155), channel_id=1, source_target_pairs={{0,3},{1,2},{2,1},{3,0},{4,7},{5,6},{6,5},{7,4},{8,13},{9,12},{10,... | collective-permute-start | bytes 98312 | tf_op jit(solution)/shard_map/ppermute | solution.py:621
  78.7 3.9 %collective-permute-start.26 = (bf16[128,128]{1,0:T(8,128)(2,1)S(1)}, bf16[128,128]{1,0:T(8,128)(2,1)S(1)}, u32[]{:S(2)}, u32[]{:S(2)}) collective-permute-start(bf16[128,128]{1,0:T(8,128)(2,1)S(1)} %get-tuple-element.156), channel_id=1, source_target_pairs={{0,2},{1,3},{2,0},{3,1},{4,6},{5,7},{6,4},{7,5},{8,14},{9,15},{10,... | collective-permute-start | bytes 98312 | tf_op jit(solution)/shard_map/ppermute | solution.py:621
  79.7 4.1 %collective-permute-start.27 = (bf16[128,128]{1,0:T(8,128)(2,1)S(1)}, bf16[128,128]{1,0:T(8,128)(2,1)S(1)}, u32[]{:S(2)}, u32[]{:S(2)}) collective-permute-start(bf16[128,128]{1,0:T(8,128)(2,1)S(1)} %get-tuple-element.157), channel_id=1, source_target_pairs={{0,1},{1,0},{2,3},{3,2},{4,5},{5,4},{6,7},{7,6},{8,12},{9,13},{10,... | collective-permute-start | bytes 98312 | tf_op jit(solution)/shard_map/ppermute | solution.py:621
  83.8 3.9 %collective-permute-start.28 = (bf16[4,128,128]{2,1,0:T(8,128)(2,1)S(1)}, bf16[4,128,128]{2,1,0:T(8,128)(2,1)S(1)}, u32[]{:S(2)}, u32[]{:S(2)}) collective-permute-start(bf16[4,128,128]{2,1,0:T(8,128)(2,1)S(1)} %pad_maximum_fusion.rest_0_), channel_id=1, source_target_pairs={{0,8},{8,0},{16,24},{24,16},{1,9},{9,1},{17,25},{25,17},{2,10},{10... | collective-permute-start | bytes 393224 | tf_op jit(solution)/shard_map/ppermute | solution.py:462
  90.3 5.4 %collective-permute-start.29 = (bf16[128,128]{1,0:T(8,128)(2,1)S(1)}, bf16[128,128]{1,0:T(8,128)(2,1)S(1)}, u32[]{:S(2)}, u32[]{:S(2)}) collective-permute-start(bf16[128,128]{1,0:T(8,128)(2,1)S(1)} %get-tuple-element.162), channel_id=1, source_target_pairs={{0,2},{1,3},{2,0},{3,1},{4,6},{5,7},{6,4},{7,5},{8,15},{9,14},{10,... | collective-permute-start | bytes 98312 | tf_op jit(solution)/shard_map/ppermute | solution.py:621
  92.2 4.9 %collective-permute-start.30 = (bf16[128,128]{1,0:T(8,128)(2,1)S(1)}, bf16[128,128]{1,0:T(8,128)(2,1)S(1)}, u32[]{:S(2)}, u32[]{:S(2)}) collective-permute-start(bf16[128,128]{1,0:T(8,128)(2,1)S(1)} %get-tuple-element.163), channel_id=1, source_target_pairs={{0,3},{1,2},{2,1},{3,0},{4,7},{5,6},{6,5},{7,4},{8,13},{9,12},{10,... | collective-permute-start | bytes 98312 | tf_op jit(solution)/shard_map/ppermute | solution.py:621
  92.6 4.5 %collective-permute-start.31 = (bf16[128,128]{1,0:T(8,128)(2,1)S(1)}, bf16[128,128]{1,0:T(8,128)(2,1)S(1)}, u32[]{:S(2)}, u32[]{:S(2)}) collective-permute-start(bf16[128,128]{1,0:T(8,128)(2,1)S(1)} %get-tuple-element.164), channel_id=1, source_target_pairs={{0,2},{1,3},{2,0},{3,1},{4,6},{5,7},{6,4},{7,5},{8,14},{9,15},{10,... | collective-permute-start | bytes 98312 | tf_op jit(solution)/shard_map/ppermute | solution.py:621
  94.5 3.9 %collective-permute-start.32 = (bf16[128,128]{1,0:T(8,128)(2,1)S(1)}, bf16[128,128]{1,0:T(8,128)(2,1)S(1)}, u32[]{:S(2)}, u32[]{:S(2)}) collective-permute-start(bf16[128,128]{1,0:T(8,128)(2,1)S(1)} %get-tuple-element.165), channel_id=1, source_target_pairs={{0,1},{1,0},{2,3},{3,2},{4,5},{5,4},{6,7},{7,6},{8,12},{9,13},{10,... | collective-permute-start | bytes 98312 | tf_op jit(solution)/shard_map/ppermute | solution.py:621
  103.3 5.2 %collective-permute-start.35 = (bf16[128,128]{1,0:T(8,128)(2,1)S(1)}, bf16[128,128]{1,0:T(8,128)(2,1)S(1)}, u32[]{:S(2)}, u32[]{:S(2)}) collective-permute-start(bf16[128,128]{1,0:T(8,128)(2,1)S(1)} %get-tuple-element.169), channel_id=1, source_target_pairs={{0,3},{1,2},{2,1},{3,0},{4,7},{5,6},{6,5},{7,4},{8,13},{9,12},{10,... | collective-permute-start | bytes 98312 | tf_op jit(solution)/shard_map/ppermute | solution.py:621
  104.2 4.3 %collective-permute-start.36 = (bf16[128,128]{1,0:T(8,128)(2,1)S(1)}, bf16[128,128]{1,0:T(8,128)(2,1)S(1)}, u32[]{:S(2)}, u32[]{:S(2)}) collective-permute-start(bf16[128,128]{1,0:T(8,128)(2,1)S(1)} %get-tuple-element.170), channel_id=1, source_target_pairs={{0,2},{1,3},{2,0},{3,1},{4,6},{5,7},{6,4},{7,5},{8,14},{9,15},{10,... | collective-permute-start | bytes 98312 | tf_op jit(solution)/shard_map/ppermute | solution.py:621
  105.8 3.9 %collective-permute-start.37 = (bf16[128,128]{1,0:T(8,128)(2,1)S(1)}, bf16[128,128]{1,0:T(8,128)(2,1)S(1)}, u32[]{:S(2)}, u32[]{:S(2)}) collective-permute-start(bf16[128,128]{1,0:T(8,128)(2,1)S(1)} %get-tuple-element.171), channel_id=1, source_target_pairs={{0,1},{1,0},{2,3},{3,2},{4,5},{5,4},{6,7},{7,6},{8,12},{9,13},{10,... | collective-permute-start | bytes 98312 | tf_op jit(solution)/shard_map/ppermute | solution.py:621
  106.8 3.9 %collective-permute-start.34 = (bf16[128,128]{1,0:T(8,128)(2,1)S(1)}, bf16[128,128]{1,0:T(8,128)(2,1)S(1)}, u32[]{:S(2)}, u32[]{:S(2)}) collective-permute-start(bf16[128,128]{1,0:T(8,128)(2,1)S(1)} %get-tuple-element.168), channel_id=1, source_target_pairs={{0,2},{1,3},{2,0},{3,1},{4,6},{5,7},{6,4},{7,5},{8,15},{9,14},{10,... | collective-permute-start | bytes 98312 | tf_op jit(solution)/shard_map/ppermute | solution.py:621
  110.8 3.0 %collective-permute-start.38 = (bf16[4,128,128]{2,1,0:T(8,128)(2,1)S(1)}, bf16[4,128,128]{2,1,0:T(8,128)(2,1)S(1)}, u32[]{:S(2)}, u32[]{:S(2)}) collective-permute-start(bf16[4,128,128]{2,1,0:T(8,128)(2,1)S(1)} %pad_maximum_fusion.2.rest_0_), channel_id=1, source_target_pairs={{0,8},{8,0},{16,24},{24,16},{1,9},{9,1},{17,25},{25,17},{2,10},{10... | collective-permute-start | bytes 393224 | tf_op jit(solution)/shard_map/ppermute | solution.py:462
  (12 other events, 23.9 us)

commit v8 on v6

--- a/solution.py
+++ b/solution.py
@@ -557,12 +557,13 @@
     def over_of(blocks, earlier):
         return [swap(after(x, earlier), 1) for x in blocks]
 
-    always = col_blocks[0, 0] >= 0
     if rounds:
         other = swap(own, 1)
         own_pair = (own, other)
         ready = [*sends[:2], after(sends[2], other), *sends[3:]]
         arrived = [exchange(ready[r - 1], r) for r in (1, 2, 3, 4, 5)]
+
+        always = after(col_blocks, arrived[0])[0, 0] >= 0
 
         def begin(own, other):
             return own_list(own, other), pattern()

time: 114 us -> 113 us (level)
  waiting for transfers between devices: 37.6 us -> 35.4 us
  starting transfers between devices: 36.1 us -> 37.5 us
    ppermute x7, waiting for transfers between devices: 15.2 us -> 13.3 us  [exchange(): return lax.ppermute(x, 'feat', [(i, i ^ r) for i in range(peers)])]
    ppermute x7, starting transfers between devices: 13.3 us -> 14.7 us  [exchange(): return lax.ppermute(x, 'feat', [(i, i ^ r) for i in range(peers)])]
    ppermute x20, starting transfers between devices: 9.36 us -> 10.5 us  [swap(): return lax.ppermute(x, 'samp', [(i, i ^ bit) for i in range(count)])]
    ppermute x12, starting transfers between devices: 13.4 us -> 12.3 us  [trade(): got.append(lax.ppermute(x, ('samp', 'feat'), pairs))]
  transfers between devices with their start and end apart: 39 -> 39, of which waited for: 19 -> 21; matrix products, arithmetic and copies ran while one was open for 1% -> 1% of each run, Pallas kernels for 19% -> 19%
where the time goes in v8:
time: 113 us
  starting transfers between devices  37.5 us (33%)
  Pallas kernels  35.6 us (32%)
  waiting for transfers between devices  35.4 us (31%)
  local copies, waits for them, and re-layouts  3.26 us (3%)
    pallas_call x14, Pallas kernels, call(): pl.pallas_call(kernel, out_shape=outs, in_specs=specs, out_specs=[out_spa...  35.6 us
    ppermute x7, starting transfers between devices, exchange(): return lax.ppermute(x, 'feat', [(i, i ^ r) for i in range(peers)])  14.7 us
    ppermute x7, waiting for transfers between devices, exchange(): return lax.ppermute(x, 'feat', [(i, i ^ r) for i in range(peers)])  13.3 us
    ppermute x20, waiting for transfers between devices, swap(): return lax.ppermute(x, 'samp', [(i, i ^ bit) for i in range(count)])  13 us
    ppermute x12, starting transfers between devices, trade(): got.append(lax.ppermute(x, ('samp', 'feat'), pairs))  12.3 us
    ppermute x20, starting transfers between devices, swap(): return lax.ppermute(x, 'samp', [(i, i ^ bit) for i in range(count)])  10.5 us
    ppermute x12, waiting for transfers between devices, trade(): got.append(lax.ppermute(x, ('samp', 'feat'), pairs))  9.07 us
  transfers between devices with their start and end apart: 39, of which 21 were waited for; matrix products, arithmetic and copies ran while one was open for 1% of the time, Pallas kernels for 19%

profile of v8, /device:TPU:0, one launch (start us, length us, event | category | flops | bytes accessed | tf_op | source)
XLA Modules:
  0.0 112.9 jit_solution(8754846779504856563)
XLA Ops:
  3.0 2.6 %collective-permute-start.6 = (bf16[128,1024]{1,0:T(8,128)(2,1)S(1)}, bf16[128,1024]{1,0:T(8,128)(2,1)S(1)}, u32[]{:S(2)}, u32[]{:S(2)}) collective-permute-start(bf16[128,1024]{1,0:T(8,128)(2,1)S(1)} %get-tuple-element.124), channel_id=1, source_target_pairs={{0,1},{1,0},{2,3},{3,2},{4,5},{5,4},{6,7},{7,6},{8,9},{9,8},{10,11... | collective-permute-start | bytes 786440 | tf_op jit(solution)/shard_map/ppermute | solution.py:502
  5.6 1.6 %collective-permute-start.8 = (bf16[128,1024]{1,0:T(8,128)(2,1)S(1)}, bf16[128,1024]{1,0:T(8,128)(2,1)S(1)}, u32[]{:S(2)}, u32[]{:S(2)}) collective-permute-start(bf16[128,1024]{1,0:T(8,128)(2,1)S(1)} %get-tuple-element.129), channel_id=1, source_target_pairs={{0,2},{1,3},{2,0},{3,1},{4,6},{5,7},{6,4},{7,5},{8,10},{9,11},{10,... | collective-permute-start | bytes 786440 | tf_op jit(solution)/shard_map/ppermute | solution.py:502
  7.1 2.6 %collective-permute-start.10 = (bf16[128,1024]{1,0:T(8,128)(2,1)S(1)}, bf16[128,1024]{1,0:T(8,128)(2,1)S(1)}, u32[]{:S(2)}, u32[]{:S(2)}) collective-permute-start(bf16[128,1024]{1,0:T(8,128)(2,1)S(1)} %get-tuple-element.132), channel_id=1, source_target_pairs={{0,4},{1,5},{2,6},{3,7},{4,0},{5,1},{6,2},{7,3},{8,12},{9,13},{10,... | collective-permute-start | bytes 786440 | tf_op jit(solution)/shard_map/ppermute | solution.py:502
  10.0 2.4 %collective-permute-done.6.rest_0_ = bf16[128,1024]{1,0:T(8,128)(2,1)S(1)} collective-permute-done((bf16[128,1024]{1,0:T(8,128)(2,1)S(1)}, bf16[128,1024]{1,0:T(8,128)(2,1)S(1)}, u32[]{:S(2)}, u32[]{:S(2)}) %collective-permute-start.6) | collective-permute-done | bytes 262176 | tf_op jit(solution)/shard_map/ppermute | solution.py:502
  14.3 2.8 %collective-permute-start.9 = (bf16[128,1024]{1,0:T(8,128)(2,1)S(1)}, bf16[128,1024]{1,0:T(8,128)(2,1)}, u32[]{:S(2)}, u32[]{:S(2)}) collective-permute-start(bf16[128,1024]{1,0:T(8,128)(2,1)S(1)} %get-tuple-element.131), channel_id=1, source_target_pairs={{0,3},{1,2},{2,1},{3,0},{4,7},{5,6},{6,5},{7,4},{8,11},{9,10},{10,... | collective-permute-start | bytes 786440 | tf_op jit(solution)/shard_map/ppermute | solution.py:502
  17.2 4.5 %conditional.3 = (bf16[5,144,128]{2,1,0:T(8,128)(2,1)}, s32[8,24]{1,0:T(8,128)S(1)}) conditional(s32[]{:T(128)} %convert_element_type.7, () %tuple.46, (bf16[4,128,1024]{2,1,0:T(8,128)(2,1)S(1)}, bf16[4,128,1024]{2,1,0:T(8,128)(2,1)}, s32[4,6]{1,0:T(4,128)}) %tuple.47), branch_computations={%region_0.0_spmd, %region_1.0_spmd} | conditional | flops 2 | bytes 185110 | solution.py:475
  17.2 2.8 %branch_1_fun.4 = bf16[5,144,128]{2,1,0:T(8,128)(2,1)} custom-call(bf16[4,128,1024]{2,1,0:T(8,128)(2,1)S(1)} %get-tuple-element.47.mine_ref, bf16[4,128,1024]{2,1,0:T(8,128)(2,1)} %get-tuple-element.48.other_ref), custom_call_target="tpu_custom_call" | custom-call | flops 1 | bytes 1 | tf_op jit(solution)/shard_map/cond/branch_1_fun/pallas_call | solution.py:443
  19.9 1.7 %branch_1_fun.5 = s32[8,24]{1,0:T(8,128)S(1)} custom-call(s32[4,6]{1,0:T(4,128)S(1)} %copy-done.5), custom_call_target="tpu_custom_call" | custom-call | flops 1 | bytes 1 | tf_op jit(solution)/shard_map/cond/branch_1_fun/pallas_call | solution.py:443
  22.2 10.9 %collective-permute-done.11.rest_4_ = bf16[128,1024]{1,0:T(8,128)(2,1)} collective-permute-done((bf16[128,1024]{1,0:T(8,128)(2,1)S(1)}, bf16[128,1024]{1,0:T(8,128)(2,1)}, u32[]{:S(2)}, u32[]{:S(2)}) %collective-permute-start.11) | collective-permute-done | bytes 262176 | tf_op jit(solution)/shard_map/ppermute | solution.py:502
  33.6 3.5 %collective-permute-start.18 = (bf16[128,1024]{1,0:T(8,128)(2,1)S(1)}, bf16[128,1024]{1,0:T(8,128)(2,1)S(1)}, u32[]{:S(2)}, u32[]{:S(2)}) collective-permute-start(bf16[128,1024]{1,0:T(8,128)(2,1)S(1)} %get-tuple-element.143), channel_id=1, source_target_pairs={{0,7},{1,6},{2,5},{3,4},{4,3},{5,2},{6,1},{7,0},{8,15},{9,14},{10,... | collective-permute-start | bytes 786440 | tf_op jit(solution)/shard_map/ppermute | solution.py:502
  39.3 21.9 %conditional.4 = (bf16[4,768,768]{2,1,0:T(8,128)(2,1)}, f32[4,8,128]{2,1,0:T(8,128)}, bf16[5,400,128]{2,1,0:T(8,128)(2,1)}, bf16[5,400,128]{2,1,0:T(8,128)(2,1)}...) conditional(s32[]{:T(128)} %convert_element_type.7, () %tuple.48, (pred[]{:T(512)}, ...), branch_computations={%region_2.0_spmd, %region_3.0_spmd} | conditional | flops 3 | bytes 11616524 | solution.py:475
  39.3 1.5 %collective-permute-start.2 = (bf16[5,144,128]{2,1,0:T(8,128)(2,1)}, bf16[5,144,128]{2,1,0:T(8,128)(2,1)}, u32[]{:S(2)}, u32[]{:S(2)}) collective-permute-start(bf16[5,144,128]{2,1,0:T(8,128)(2,1)} %get-tuple-element.54), channel_id=1, source_target_pairs={{0,16},{8,24},{16,0},{24,8},{1,17},{9,25},{17,1},{25,9},{2,18},{10... | collective-permute-start | bytes 552968 | tf_op jit(solution)/shard_map/cond/branch_1_fun/ppermute | solution.py:456
  40.9 4.5 %branch_1_fun.7 = bf16[5,400,128]{2,1,0:T(8,128)(2,1)} custom-call(s32[8,24]{1,0:T(8,128)S(1)} %get-tuple-element.55.table_ref, bf16[4,128,1024]{2,1,0:T(8,128)(2,1)S(1)} %get-tuple-element.56.mine_ref, bf16[4,128,1024]{2,1,0:T(8,128)(2,1)} %get-tuple-element.57.other_ref, bf16[128,1024]{1,0:T(8,128)(2,1)S(1)} %get-tuple-element.58.rest_0_, ...), custom_call_target="tpu_custom_call" | custom-call | flops 1 | bytes 1 | tf_op jit(solution)/shard_map/cond/branch_1_fun/pallas_call | solution.py:443
  46.1 1.5 %collective-permute-start.3 = (bf16[5,400,128]{2,1,0:T(8,128)(2,1)}, bf16[5,400,128]{2,1,0:T(8,128)(2,1)}, u32[]{:S(2)}, u32[]{:S(2)}) collective-permute-start(bf16[5,400,128]{2,1,0:T(8,128)(2,1)} %branch_1_fun.7), channel_id=1, source_target_pairs={{0,16},{8,24},{16,0},{24,8},{1,17},{9,25},{17,1},{25,9},{2,18},{10... | collective-permute-start | bytes 1536008 | tf_op jit(solution)/shard_map/cond/branch_1_fun/ppermute | solution.py:456
  47.6 6.3 %conditional = ((bf16[4,768,768]{2,1,0:T(8,128)(2,1)}, f32[4,8,128]{2,1,0:T(8,128)})) conditional(s32[]{:T(128)} %convert_element_type.1, () %tuple.21, (bf16[5,144,128]{2,1,0:T(8,128)(2,1)}, bf16[5,144,128]{2,1,0:T(8,128)(2,1)}, s32[8,24]{1,0:T(8,128)S(1)}) %tuple.24), branch_computations={%region_4.0_spmd, %region_5.0_spmd} | conditional | flops 1 | bytes 4735006 | solution.py:475
  49.5 4.4 %branch_1_fun.6 = (bf16[4,768,768]{2,1,0:T(8,128)(2,1)}, f32[4,8,128]{2,1,0:T(8,128)}) custom-call(s32[8,24]{1,0:T(8,128)S(1)} %get-tuple-element.50.table_ref, bf16[5,144,128]{2,1,0:T(8,128)(2,1)} %get-tuple-element.51.rest_0_, bf16[5,144,128]{2,1,0:T(8,128)(2,1)} %get-tuple-element.52.rest_1_, bf16[5,144,128]{2,1,0:T(8,128)(2,1)S(1)} %collective-permute-done.rest_2_, ...), custom_call_target="tpu_custom_call" | custom-call | flops 1 | bytes 1 | tf_op jit(solution)/shard_map/cond/branch_1_fun/cond/branch_1_fun/pallas_call | solution.py:443
  54.2 4.8 %collective-permute-done.3 = bf16[5,400,128]{2,1,0:T(8,128)(2,1)} collective-permute-done((bf16[5,400,128]{2,1,0:T(8,128)(2,1)}, bf16[5,400,128]{2,1,0:T(8,128)(2,1)}, u32[]{:S(2)}, u32[]{:S(2)}) %collective-permute-start.3) | collective-permute-done | bytes 512032 | tf_op jit(solution)/shard_map/cond/branch_1_fun/ppermute | solution.py:456
  59.0 2.2 %collective-permute-done.5 = bf16[5,400,128]{2,1,0:T(8,128)(2,1)} collective-permute-done((bf16[5,400,128]{2,1,0:T(8,128)(2,1)}, bf16[5,400,128]{2,1,0:T(8,128)(2,1)}, u32[]{:S(2)}, u32[]{:S(2)}) %collective-permute-start.5) | collective-permute-done | bytes 512032 | tf_op jit(solution)/shard_map/cond/branch_1_fun/ppermute | solution.py:456
  63.1 2.6 %shard_map.38.rest_0_ = bf16[2,400,128]{2,1,0:T(8,128)(2,1)S(1)} custom-call(s32[8,24]{1,0:T(8,128)S(1)} %get-tuple-element.127.table_ref, bf16[4,128,1024]{2,1,0:T(8,128)(2,1)S(1)} %get-tuple-element.126.mine_ref, bf16[4,128,1024]{2,1,0:T(8,128)(2,1)} %collective-permute-done.7.other_ref, bf16[128,1024]{1,0:T(8,128)(2,1)S(1)} %collective-permute-done.6.rest_0_, ...), custom_call_target="tpu_custom_call" | custom-call | flops 1 | bytes 1 | tf_op jit(solution)/shard_map/pallas_call | solution.py:443
  65.8 1.6 %collective-permute-start.21 = (bf16[2,400,128]{2,1,0:T(8,128)(2,1)S(1)}, bf16[2,400,128]{2,1,0:T(8,128)(2,1)S(1)}, u32[]{:S(2)}, u32[]{:S(2)}) collective-permute-start(bf16[2,400,128]{2,1,0:T(8,128)(2,1)S(1)} %shard_map.38.rest_0_), channel_id=1, source_target_pairs={{0,16},{8,24},{16,0},{24,8},{1,17},{9,25},{17,1},{25,9},{2,18},{10... | collective-permute-start | bytes 614408 | tf_op jit(solution)/shard_map/ppermute | solution.py:456
  67.4 4.5 %shard_map.39 = (bf16[4,768,768]{2,1,0:T(8,128)(2,1)S(1)}, f32[4,8,128]{2,1,0:T(8,128)S(1)}) custom-call(s32[8,24]{1,0:T(8,128)S(1)} %get-tuple-element.127.table_ref, bf16[4,768,768]{2,1,0:T(8,128)(2,1)} %get-tuple-element.146.gram_in_ref, f32[4,8,128]{2,1,0:T(8,128)} %get-tuple-element.147.low_in_ref, bf16[5,400,128]{2,1,0:T(8,128)(2,1)} %get-tuple-element.148.rest_0_, ...), custom_call_target="tpu_custom_call" | custom-call | flops 1 | bytes 1 | tf_op jit(solution)/shard_map/pallas_call | solution.py:443
  72.9 1.4 %collective-permute-done.23.rest_3_ = bf16[2,400,128]{2,1,0:T(8,128)(2,1)S(1)} collective-permute-done((bf16[2,400,128]{2,1,0:T(8,128)(2,1)S(1)}, bf16[2,400,128]{2,1,0:T(8,128)(2,1)S(1)}, u32[]{:S(2)}, u32[]{:S(2)}) %collective-permute-start.23) | collective-permute-done | bytes 204832 | tf_op jit(solution)/shard_map/ppermute | solution.py:456
  74.4 2.8 %shard_map.40 = (bf16[4,768,768]{2,1,0:T(8,128)(2,1)S(1)}, f32[4,8,128]{2,1,0:T(8,128)S(1)}, f32[4,128,896]{2,1,0:T(8,128)S(1)}, bf16[128,128]{1,0:T(8,128)(2,1)...) custom-call(s32[8,24]{1,0:T(8,128)S(1)} %get-tuple-element.127.table_ref, ...), custom_call_target="tpu_custom_call" | custom-call | flops 1 | bytes 1 | tf_op jit(solution)/shard_map/pallas_call | solution.py:443
  79.3 1.5 %collective-permute-start.27 = (bf16[128,128]{1,0:T(8,128)(2,1)S(1)}, bf16[128,128]{1,0:T(8,128)(2,1)S(1)}, u32[]{:S(2)}, u32[]{:S(2)}) collective-permute-start(bf16[128,128]{1,0:T(8,128)(2,1)S(1)} %get-tuple-element.159), channel_id=1, source_target_pairs={{0,1},{1,0},{2,3},{3,2},{4,5},{5,4},{6,7},{7,6},{8,12},{9,13},{10,... | collective-permute-start | bytes 98312 | tf_op jit(solution)/shard_map/ppermute | solution.py:616
  83.4 1.5 %collective-permute-start.28 = (bf16[4,128,128]{2,1,0:T(8,128)(2,1)S(1)}, bf16[4,128,128]{2,1,0:T(8,128)(2,1)S(1)}, u32[]{:S(2)}, u32[]{:S(2)}) collective-permute-start(bf16[4,128,128]{2,1,0:T(8,128)(2,1)S(1)} %pad_maximum_fusion.rest_0_), channel_id=1, source_target_pairs={{0,8},{8,0},{16,24},{24,16},{1,9},{9,1},{17,25},{25,17},{2,10},{10... | collective-permute-start | bytes 393224 | tf_op jit(solution)/shard_map/ppermute | solution.py:456
  86.3 2.5 %shard_map.42 = (f32[4,6,128,128]{3,2,1,0:T(8,128)S(1)}, f32[4,128,896]{2,1,0:T(8,128)S(1)}, bf16[128,128]{1,0:T(8,128)(2,1)S(1)}, bf16[128,128]{1,0:T(8,128)(2,...) custom-call(s32[8,24]{1,0:T(8,128)S(1)} %get-tuple-element.127.table_ref, ...), custom_call_target="tpu_custom_call" | custom-call | flops 1 | bytes 1 | tf_op jit(solution)/shard_map/pallas_call | solution.py:443
  88.8 1.4 %collective-permute-start.29 = (bf16[128,128]{1,0:T(8,128)(2,1)S(1)}, bf16[128,128]{1,0:T(8,128)(2,1)S(1)}, u32[]{:S(2)}, u32[]{:S(2)}) collective-permute-start(bf16[128,128]{1,0:T(8,128)(2,1)S(1)} %get-tuple-element.164), channel_id=1, source_target_pairs={{0,2},{1,3},{2,0},{3,1},{4,6},{5,7},{6,4},{7,5},{8,15},{9,14},{10,... | collective-permute-start | bytes 98312 | tf_op jit(solution)/shard_map/ppermute | solution.py:616
  91.3 1.8 %collective-permute-start.31 = (bf16[128,128]{1,0:T(8,128)(2,1)S(1)}, bf16[128,128]{1,0:T(8,128)(2,1)S(1)}, u32[]{:S(2)}, u32[]{:S(2)}) collective-permute-start(bf16[128,128]{1,0:T(8,128)(2,1)S(1)} %get-tuple-element.166), channel_id=1, source_target_pairs={{0,2},{1,3},{2,0},{3,1},{4,6},{5,7},{6,4},{7,5},{8,14},{9,15},{10,... | collective-permute-start | bytes 98312 | tf_op jit(solution)/shard_map/ppermute | solution.py:616
  99.3 2.5 %shard_map.44 = (f32[4,6,128,128]{3,2,1,0:T(8,128)S(1)}, f32[4,128,896]{2,1,0:T(8,128)S(1)}, bf16[128,128]{1,0:T(8,128)(2,1)S(1)}, bf16[128,128]{1,0:T(8,128)(2,...) custom-call(s32[8,24]{1,0:T(8,128)S(1)} %get-tuple-element.127.table_ref, ...), custom_call_target="tpu_custom_call" | custom-call | flops 1 | bytes 1 | tf_op jit(solution)/shard_map/pallas_call | solution.py:443
  102.2 2.1 %collective-permute-start.35 = (bf16[128,128]{1,0:T(8,128)(2,1)S(1)}, bf16[128,128]{1,0:T(8,128)(2,1)S(1)}, u32[]{:S(2)}, u32[]{:S(2)}) collective-permute-start(bf16[128,128]{1,0:T(8,128)(2,1)S(1)} %get-tuple-element.171), channel_id=1, source_target_pairs={{0,3},{1,2},{2,1},{3,0},{4,7},{5,6},{6,5},{7,4},{8,13},{9,12},{10,... | collective-permute-start | bytes 98312 | tf_op jit(solution)/shard_map/ppermute | solution.py:616
  107.0 1.7 %collective-permute-done.36 = bf16[128,128]{1,0:T(8,128)(2,1)S(1)} collective-permute-done((bf16[128,128]{1,0:T(8,128)(2,1)S(1)}, bf16[128,128]{1,0:T(8,128)(2,1)S(1)}, u32[]{:S(2)}, u32[]{:S(2)}) %collective-permute-start.36) | collective-permute-done | bytes 32800 | tf_op jit(solution)/shard_map/ppermute | solution.py:616
  110.8 1.9 %shard_map.46 = f32[4,6,128,128]{3,2,1,0:T(8,128)} custom-call(s32[8,24]{1,0:T(8,128)S(1)} %get-tuple-element.127.table_ref, f32[4,6,128,128]{3,2,1,0:T(8,128)S(1)} %shard_map.45.stepped_ref, bf16[4,128,128]{2,1,0:T(8,128)(2,1)S(1)} %pad_maximum_fusion.2.rest_0_, bf16[4,128,128]{2,1,0:T(8,128)(2,1)S(1)} %collective-permute-done.38.rest_1_), custom_call_target="tpu_custom_call" | custom-call | flops 1 | bytes 1 | tf_op jit(solution)/shard_map/pallas_call | solution.py:443
  (79 shorter events, 32.0 us)
Async XLA Ops:
  2.5 11.8 %collective-permute-start.7 = (bf16[4,128,1024]{2,1,0:T(8,128)(2,1)S(1)}, bf16[4,128,1024]{2,1,0:T(8,128)(2,1)}, u32[]{:S(2)}, u32[]{:S(2)}) collective-permute-start(bf16[4,128,1024]{2,1,0:T(8,128)(2,1)S(1)} %get-tuple-element.126.mine_ref), channel_id=1, source_target_pairs={{0,8},{8,0},{16,24},{24,16},{1,9},{9,1},{17,25},{25,17},{2,10},{10... | collective-permute-start | bytes 3145736 | tf_op jit(solution)/shard_map/ppermute | solution.py:456
  3.0 9.5 %collective-permute-start.6 = (bf16[128,1024]{1,0:T(8,128)(2,1)S(1)}, bf16[128,1024]{1,0:T(8,128)(2,1)S(1)}, u32[]{:S(2)}, u32[]{:S(2)}) collective-permute-start(bf16[128,1024]{1,0:T(8,128)(2,1)S(1)} %get-tuple-element.124), channel_id=1, source_target_pairs={{0,1},{1,0},{2,3},{3,2},{4,5},{5,4},{6,7},{7,6},{8,9},{9,8},{10,11... | collective-permute-start | bytes 786440 | tf_op jit(solution)/shard_map/ppermute | solution.py:502
  5.6 16.2 %collective-permute-start.8 = (bf16[128,1024]{1,0:T(8,128)(2,1)S(1)}, bf16[128,1024]{1,0:T(8,128)(2,1)S(1)}, u32[]{:S(2)}, u32[]{:S(2)}) collective-permute-start(bf16[128,1024]{1,0:T(8,128)(2,1)S(1)} %get-tuple-element.129), channel_id=1, source_target_pairs={{0,2},{1,3},{2,0},{3,1},{4,6},{5,7},{6,4},{7,5},{8,10},{9,11},{10,... | collective-permute-start | bytes 786440 | tf_op jit(solution)/shard_map/ppermute | solution.py:502
  7.1 26.0 %collective-permute-start.10 = (bf16[128,1024]{1,0:T(8,128)(2,1)S(1)}, bf16[128,1024]{1,0:T(8,128)(2,1)S(1)}, u32[]{:S(2)}, u32[]{:S(2)}) collective-permute-start(bf16[128,1024]{1,0:T(8,128)(2,1)S(1)} %get-tuple-element.132), channel_id=1, source_target_pairs={{0,4},{1,5},{2,6},{3,7},{4,0},{5,1},{6,2},{7,3},{8,12},{9,13},{10,... | collective-permute-start | bytes 786440 | tf_op jit(solution)/shard_map/ppermute | solution.py:502
  9.7 23.4 %collective-permute-start.11 = (bf16[128,1024]{1,0:T(8,128)(2,1)S(1)}, bf16[128,1024]{1,0:T(8,128)(2,1)}, u32[]{:S(2)}, u32[]{:S(2)}) collective-permute-start(bf16[128,1024]{1,0:T(8,128)(2,1)S(1)} %get-tuple-element.133), channel_id=1, source_target_pairs={{0,5},{1,4},{2,7},{3,6},{4,1},{5,0},{6,3},{7,2},{8,13},{9,12},{10,... | collective-permute-start | bytes 786440 | tf_op jit(solution)/shard_map/ppermute | solution.py:502
  14.3 19.3 %collective-permute-start.9 = (bf16[128,1024]{1,0:T(8,128)(2,1)S(1)}, bf16[128,1024]{1,0:T(8,128)(2,1)}, u32[]{:S(2)}, u32[]{:S(2)}) collective-permute-start(bf16[128,1024]{1,0:T(8,128)(2,1)S(1)} %get-tuple-element.131), channel_id=1, source_target_pairs={{0,3},{1,2},{2,1},{3,0},{4,7},{5,6},{6,5},{7,4},{8,11},{9,10},{10,... | collective-permute-start | bytes 786440 | tf_op jit(solution)/shard_map/ppermute | solution.py:502
  21.6 12.0 %collective-permute-start.12 = (bf16[128,1024]{1,0:T(8,128)(2,1)S(1)}, bf16[128,1024]{1,0:T(8,128)(2,1)S(1)}, u32[]{:S(2)}, u32[]{:S(2)}) collective-permute-start(bf16[128,1024]{1,0:T(8,128)(2,1)S(1)} %collective-permute-done.6.rest_0_), channel_id=1, source_target_pairs={{0,8},{8,0},{16,24},{24,16},{1,9},{9,1},{17,25},{25,17},{2,10},{10... | collective-permute-start | bytes 786440 | tf_op jit(solution)/shard_map/ppermute | solution.py:456
  21.7 15.4 %collective-permute-start.13 = (bf16[128,1024]{1,0:T(8,128)(2,1)S(1)}, bf16[128,1024]{1,0:T(8,128)(2,1)S(1)}, u32[]{:S(2)}, u32[]{:S(2)}) collective-permute-start(bf16[128,1024]{1,0:T(8,128)(2,1)S(1)} %collective-permute-done.8.rest_1_), channel_id=1, source_target_pairs={{0,8},{8,0},{16,24},{24,16},{1,9},{9,1},{17,25},{25,17},{2,10},{10... | collective-permute-start | bytes 786440 | tf_op jit(solution)/shard_map/ppermute | solution.py:456
  33.1 5.4 %collective-permute-start.15 = (bf16[128,1024]{1,0:T(8,128)(2,1)S(1)}, bf16[128,1024]{1,0:T(8,128)(2,1)S(1)}, u32[]{:S(2)}, u32[]{:S(2)}) collective-permute-start(bf16[128,1024]{1,0:T(8,128)(2,1)S(1)} %collective-permute-done.10.rest_3_), channel_id=1, source_target_pairs={{0,8},{8,0},{16,24},{24,16},{1,9},{9,1},{17,25},{25,17},{2,10},{10... | collective-permute-start | bytes 786440 | tf_op jit(solution)/shard_map/ppermute | solution.py:456
  33.1 5.4 %collective-permute-start.16 = (bf16[128,1024]{1,0:T(8,128)(2,1)}, bf16[128,1024]{1,0:T(8,128)(2,1)S(1)}, u32[]{:S(2)}, u32[]{:S(2)}) collective-permute-start(bf16[128,1024]{1,0:T(8,128)(2,1)} %collective-permute-done.11.rest_4_), channel_id=1, source_target_pairs={{0,8},{8,0},{16,24},{24,16},{1,9},{9,1},{17,25},{25,17},{2,10},{10... | collective-permute-start | bytes 786440 | tf_op jit(solution)/shard_map/ppermute | solution.py:456
  33.6 4.9 %collective-permute-start.14 = (bf16[128,1024]{1,0:T(8,128)(2,1)}, bf16[128,1024]{1,0:T(8,128)(2,1)S(1)}, u32[]{:S(2)}, u32[]{:S(2)}) collective-permute-start(bf16[128,1024]{1,0:T(8,128)(2,1)} %collective-permute-done.9.rest_2_), channel_id=1, source_target_pairs={{0,8},{8,0},{16,24},{24,16},{1,9},{9,1},{17,25},{25,17},{2,10},{10... | collective-permute-start | bytes 786440 | tf_op jit(solution)/shard_map/ppermute | solution.py:456
  33.6 27.6 %collective-permute-start.18 = (bf16[128,1024]{1,0:T(8,128)(2,1)S(1)}, bf16[128,1024]{1,0:T(8,128)(2,1)S(1)}, u32[]{:S(2)}, u32[]{:S(2)}) collective-permute-start(bf16[128,1024]{1,0:T(8,128)(2,1)S(1)} %get-tuple-element.143), channel_id=1, source_target_pairs={{0,7},{1,6},{2,5},{3,4},{4,3},{5,2},{6,1},{7,0},{8,15},{9,14},{10,... | collective-permute-start | bytes 786440 | tf_op jit(solution)/shard_map/ppermute | solution.py:502
  37.1 24.1 %collective-permute-start.17 = (bf16[128,1024]{1,0:T(8,128)(2,1)S(1)}, bf16[128,1024]{1,0:T(8,128)(2,1)S(1)}, u32[]{:S(2)}, u32[]{:S(2)}) collective-permute-start(bf16[128,1024]{1,0:T(8,128)(2,1)S(1)} %get-tuple-element.141), channel_id=1, source_target_pairs={{0,6},{1,7},{2,4},{3,5},{4,2},{5,3},{6,0},{7,1},{8,14},{9,15},{10,... | collective-permute-start | bytes 786440 | tf_op jit(solution)/shard_map/ppermute | solution.py:502
  39.3 6.7 %collective-permute-start.2 = (bf16[5,144,128]{2,1,0:T(8,128)(2,1)}, bf16[5,144,128]{2,1,0:T(8,128)(2,1)}, u32[]{:S(2)}, u32[]{:S(2)}) collective-permute-start(bf16[5,144,128]{2,1,0:T(8,128)(2,1)} %get-tuple-element.54), channel_id=1, source_target_pairs={{0,16},{8,24},{16,0},{24,8},{1,17},{9,25},{17,1},{25,9},{2,18},{10... | collective-permute-start | bytes 552968 | tf_op jit(solution)/shard_map/cond/branch_1_fun/ppermute | solution.py:456
  46.1 12.9 %collective-permute-start.3 = (bf16[5,400,128]{2,1,0:T(8,128)(2,1)}, bf16[5,400,128]{2,1,0:T(8,128)(2,1)}, u32[]{:S(2)}, u32[]{:S(2)}) collective-permute-start(bf16[5,400,128]{2,1,0:T(8,128)(2,1)} %branch_1_fun.7), channel_id=1, source_target_pairs={{0,16},{8,24},{16,0},{24,8},{1,17},{9,25},{17,1},{25,9},{2,18},{10... | collective-permute-start | bytes 1536008 | tf_op jit(solution)/shard_map/cond/branch_1_fun/ppermute | solution.py:456
  53.9 5.0 %collective-permute-start.4 = (bf16[5,400,128]{2,1,0:T(8,128)(2,1)}, bf16[5,400,128]{2,1,0:T(8,128)(2,1)}, u32[]{:S(2)}, u32[]{:S(2)}) collective-permute-start(bf16[5,400,128]{2,1,0:T(8,128)(2,1)} %branch_1_fun.7), channel_id=1, source_target_pairs={{0,8},{8,0},{16,24},{24,16},{1,9},{9,1},{17,25},{25,17},{2,10},{10... | collective-permute-start | bytes 1536008 | tf_op jit(solution)/shard_map/cond/branch_1_fun/ppermute | solution.py:456
  65.8 7.2 %collective-permute-start.21 = (bf16[2,400,128]{2,1,0:T(8,128)(2,1)S(1)}, bf16[2,400,128]{2,1,0:T(8,128)(2,1)S(1)}, u32[]{:S(2)}, u32[]{:S(2)}) collective-permute-start(bf16[2,400,128]{2,1,0:T(8,128)(2,1)S(1)} %shard_map.38.rest_0_), channel_id=1, source_target_pairs={{0,16},{8,24},{16,0},{24,8},{1,17},{9,25},{17,1},{25,9},{2,18},{10... | collective-permute-start | bytes 614408 | tf_op jit(solution)/shard_map/ppermute | solution.py:456
  67.4 5.6 %collective-permute-start.22 = (bf16[2,400,128]{2,1,0:T(8,128)(2,1)S(1)}, bf16[2,400,128]{2,1,0:T(8,128)(2,1)S(1)}, u32[]{:S(2)}, u32[]{:S(2)}) collective-permute-start(bf16[2,400,128]{2,1,0:T(8,128)(2,1)S(1)} %shard_map.38.rest_0_), channel_id=1, source_target_pairs={{0,8},{8,0},{16,24},{24,16},{1,9},{9,1},{17,25},{25,17},{2,10},{10... | collective-permute-start | bytes 614408 | tf_op jit(solution)/shard_map/ppermute | solution.py:456
  77.2 4.3 %collective-permute-start.24 = (bf16[128,128]{1,0:T(8,128)(2,1)S(1)}, bf16[128,128]{1,0:T(8,128)(2,1)S(1)}, u32[]{:S(2)}, u32[]{:S(2)}) collective-permute-start(bf16[128,128]{1,0:T(8,128)(2,1)S(1)} %get-tuple-element.156), channel_id=1, source_target_pairs={{0,2},{1,3},{2,0},{3,1},{4,6},{5,7},{6,4},{7,5},{8,15},{9,14},{10,... | collective-permute-start | bytes 98312 | tf_op jit(solution)/shard_map/ppermute | solution.py:616
  77.3 4.9 %collective-permute-start.25 = (bf16[128,128]{1,0:T(8,128)(2,1)S(1)}, bf16[128,128]{1,0:T(8,128)(2,1)S(1)}, u32[]{:S(2)}, u32[]{:S(2)}) collective-permute-start(bf16[128,128]{1,0:T(8,128)(2,1)S(1)} %get-tuple-element.157), channel_id=1, source_target_pairs={{0,3},{1,2},{2,1},{3,0},{4,7},{5,6},{6,5},{7,4},{8,13},{9,12},{10,... | collective-permute-start | bytes 98312 | tf_op jit(solution)/shard_map/ppermute | solution.py:616
  78.3 3.9 %collective-permute-start.26 = (bf16[128,128]{1,0:T(8,128)(2,1)S(1)}, bf16[128,128]{1,0:T(8,128)(2,1)S(1)}, u32[]{:S(2)}, u32[]{:S(2)}) collective-permute-start(bf16[128,128]{1,0:T(8,128)(2,1)S(1)} %get-tuple-element.158), channel_id=1, source_target_pairs={{0,2},{1,3},{2,0},{3,1},{4,6},{5,7},{6,4},{7,5},{8,14},{9,15},{10,... | collective-permute-start | bytes 98312 | tf_op jit(solution)/shard_map/ppermute | solution.py:616
  79.3 4.1 %collective-permute-start.27 = (bf16[128,128]{1,0:T(8,128)(2,1)S(1)}, bf16[128,128]{1,0:T(8,128)(2,1)S(1)}, u32[]{:S(2)}, u32[]{:S(2)}) collective-permute-start(bf16[128,128]{1,0:T(8,128)(2,1)S(1)} %get-tuple-element.159), channel_id=1, source_target_pairs={{0,1},{1,0},{2,3},{3,2},{4,5},{5,4},{6,7},{7,6},{8,12},{9,13},{10,... | collective-permute-start | bytes 98312 | tf_op jit(solution)/shard_map/ppermute | solution.py:616
  83.4 2.8 %collective-permute-start.28 = (bf16[4,128,128]{2,1,0:T(8,128)(2,1)S(1)}, bf16[4,128,128]{2,1,0:T(8,128)(2,1)S(1)}, u32[]{:S(2)}, u32[]{:S(2)}) collective-permute-start(bf16[4,128,128]{2,1,0:T(8,128)(2,1)S(1)} %pad_maximum_fusion.rest_0_), channel_id=1, source_target_pairs={{0,8},{8,0},{16,24},{24,16},{1,9},{9,1},{17,25},{25,17},{2,10},{10... | collective-permute-start | bytes 393224 | tf_op jit(solution)/shard_map/ppermute | solution.py:456
  88.8 4.9 %collective-permute-start.29 = (bf16[128,128]{1,0:T(8,128)(2,1)S(1)}, bf16[128,128]{1,0:T(8,128)(2,1)S(1)}, u32[]{:S(2)}, u32[]{:S(2)}) collective-permute-start(bf16[128,128]{1,0:T(8,128)(2,1)S(1)} %get-tuple-element.164), channel_id=1, source_target_pairs={{0,2},{1,3},{2,0},{3,1},{4,6},{5,7},{6,4},{7,5},{8,15},{9,14},{10,... | collective-permute-start | bytes 98312 | tf_op jit(solution)/shard_map/ppermute | solution.py:616
  90.2 4.8 %collective-permute-start.30 = (bf16[128,128]{1,0:T(8,128)(2,1)S(1)}, bf16[128,128]{1,0:T(8,128)(2,1)S(1)}, u32[]{:S(2)}, u32[]{:S(2)}) collective-permute-start(bf16[128,128]{1,0:T(8,128)(2,1)S(1)} %get-tuple-element.165), channel_id=1, source_target_pairs={{0,3},{1,2},{2,1},{3,0},{4,7},{5,6},{6,5},{7,4},{8,13},{9,12},{10,... | collective-permute-start | bytes 98312 | tf_op jit(solution)/shard_map/ppermute | solution.py:616
  91.3 4.4 %collective-permute-start.31 = (bf16[128,128]{1,0:T(8,128)(2,1)S(1)}, bf16[128,128]{1,0:T(8,128)(2,1)S(1)}, u32[]{:S(2)}, u32[]{:S(2)}) collective-permute-start(bf16[128,128]{1,0:T(8,128)(2,1)S(1)} %get-tuple-element.166), channel_id=1, source_target_pairs={{0,2},{1,3},{2,0},{3,1},{4,6},{5,7},{6,4},{7,5},{8,14},{9,15},{10,... | collective-permute-start | bytes 98312 | tf_op jit(solution)/shard_map/ppermute | solution.py:616
  93.1 3.9 %collective-permute-start.32 = (bf16[128,128]{1,0:T(8,128)(2,1)S(1)}, bf16[128,128]{1,0:T(8,128)(2,1)S(1)}, u32[]{:S(2)}, u32[]{:S(2)}) collective-permute-start(bf16[128,128]{1,0:T(8,128)(2,1)S(1)} %get-tuple-element.167), channel_id=1, source_target_pairs={{0,1},{1,0},{2,3},{3,2},{4,5},{5,4},{6,7},{7,6},{8,12},{9,13},{10,... | collective-permute-start | bytes 98312 | tf_op jit(solution)/shard_map/ppermute | solution.py:616
  97.1 2.3 %collective-permute-start.33 = (bf16[4,128,128]{2,1,0:T(8,128)(2,1)S(1)}, bf16[4,128,128]{2,1,0:T(8,128)(2,1)S(1)}, u32[]{:S(2)}, u32[]{:S(2)}) collective-permute-start(bf16[4,128,128]{2,1,0:T(8,128)(2,1)S(1)} %pad_maximum_fusion.1.rest_0_), channel_id=1, source_target_pairs={{0,8},{8,0},{16,24},{24,16},{1,9},{9,1},{17,25},{25,17},{2,10},{10... | collective-permute-start | bytes 393224 | tf_op jit(solution)/shard_map/ppermute | solution.py:456
  101.9 4.0 %collective-permute-start.34 = (bf16[128,128]{1,0:T(8,128)(2,1)S(1)}, bf16[128,128]{1,0:T(8,128)(2,1)S(1)}, u32[]{:S(2)}, u32[]{:S(2)}) collective-permute-start(bf16[128,128]{1,0:T(8,128)(2,1)S(1)} %get-tuple-element.170), channel_id=1, source_target_pairs={{0,2},{1,3},{2,0},{3,1},{4,6},{5,7},{6,4},{7,5},{8,15},{9,14},{10,... | collective-permute-start | bytes 98312 | tf_op jit(solution)/shard_map/ppermute | solution.py:616
  102.2 4.8 %collective-permute-start.35 = (bf16[128,128]{1,0:T(8,128)(2,1)S(1)}, bf16[128,128]{1,0:T(8,128)(2,1)S(1)}, u32[]{:S(2)}, u32[]{:S(2)}) collective-permute-start(bf16[128,128]{1,0:T(8,128)(2,1)S(1)} %get-tuple-element.171), channel_id=1, source_target_pairs={{0,3},{1,2},{2,1},{3,0},{4,7},{5,6},{6,5},{7,4},{8,13},{9,12},{10,... | collective-permute-start | bytes 98312 | tf_op jit(solution)/shard_map/ppermute | solution.py:616
  104.3 4.5 %collective-permute-start.36 = (bf16[128,128]{1,0:T(8,128)(2,1)S(1)}, bf16[128,128]{1,0:T(8,128)(2,1)S(1)}, u32[]{:S(2)}, u32[]{:S(2)}) collective-permute-start(bf16[128,128]{1,0:T(8,128)(2,1)S(1)} %get-tuple-element.172), channel_id=1, source_target_pairs={{0,2},{1,3},{2,0},{3,1},{4,6},{5,7},{6,4},{7,5},{8,14},{9,15},{10,... | collective-permute-start | bytes 98312 | tf_op jit(solution)/shard_map/ppermute | solution.py:616
  104.6 4.3 %collective-permute-start.37 = (bf16[128,128]{1,0:T(8,128)(2,1)S(1)}, bf16[128,128]{1,0:T(8,128)(2,1)S(1)}, u32[]{:S(2)}, u32[]{:S(2)}) collective-permute-start(bf16[128,128]{1,0:T(8,128)(2,1)S(1)} %get-tuple-element.173), channel_id=1, source_target_pairs={{0,1},{1,0},{2,3},{3,2},{4,5},{5,4},{6,7},{7,6},{8,12},{9,13},{10,... | collective-permute-start | bytes 98312 | tf_op jit(solution)/shard_map/ppermute | solution.py:616
  (13 other events, 29.9 us)
